TPU v7x, 32 devices: a whole 2x2x4 slice. The times are simulated.
32 devices in a mesh: groups: 2 (over x), nodes: 16 (over z, y, core).
Axes of the slice: x: 2, y: 2, z: 4, core: 2. Of those that a mesh axis runs over, the one named last changes fastest.
Arguments:
- features: bfloat16 [65536, 128], P(('groups', 'nodes')), parts along dimension 0, may hold values from -6 to 6
- fine_cotangent: bfloat16 [65536, 128], P(('groups', 'nodes')), parts along dimension 0, may hold values from -6 to 6
- mid_cotangent: bfloat16 [16384, 128], P(('groups', 'nodes')), parts along dimension 0, may hold values from -6 to 6
- coarse_cotangent: bfloat16 [512, 128], P(('groups', 'nodes')), parts along dimension 0, may hold values from -6 to 6
- weights: bfloat16 [3, 4, 128, 128], replicated, may hold values from -0.5 to 0.5
- fine_offsets: int32 [16, 32768], P('groups', 'nodes'), parts along dimension 0, may hold values from -256 to 256
- fine_edge_w: float32 [16, 32768], P('groups', 'nodes'), parts along dimension 0, may hold values from -2 to 2
- pool_fine: bfloat16 [16, 32768], P('groups', 'nodes'), parts along dimension 0, may hold values from -1 to 1
- owner_dev: int32 [2048, 1], P(('groups', 'nodes')), parts along dimension 0, may hold values from 0 to 15; in each aligned block of 64 rows (0 to 63, 64 to 127, ...) at most 8 rows name the same one
- coarse_slot: int32 [2048], P(('groups', 'nodes')), parts along dimension 0, may hold values from 0 to 63
- mid_nbrs: int32 [16, 8192], P('groups', 'nodes'), parts along dimension 0, may hold values from 0 to 511
- mid_edge_w: float32 [16, 8192], P('groups', 'nodes'), parts along dimension 0, may hold values from -2 to 2
- pool_mid: bfloat16 [512, 512], P(('groups', 'nodes')), parts along dimension 0, may hold values from -0.25 to 0.25
- coarse_nbrs: int32 [16, 256], P('groups', 'nodes'), parts along dimension 0, may hold values from 0 to 255
- coarse_edge_w: float32 [16, 256], P('groups', 'nodes'), parts along dimension 0, may hold values from -2 to 2
Outputs:
- feature_grads: bfloat16 [65536, 128], P(('groups', 'nodes')), parts along dimension 0
- weight_grads: float32 [6, 4, 128, 128], P('groups'), parts along dimension 0
There are 2 independent parts, one for each index of `groups`. A program takes and returns all parts, laid end to end along the dimension named above; an argument that names none is the same for every part. Nothing has to cross between parts.
Inputs may be any that keep to these rules, and one draw needn't show every extreme that they name: `owner_dev`: within the 64 tiles of one device no owner is named more than 8 times, a bound that some block reaches.
All inputs are finite; a program needn't handle non-finite values.
Results may differ from a plain program's by a relative error of at most 0.014.
Values may be sent and summed in bfloat16 or wider, within the bound.
No kernel may reach another device: no remote copies, remote signals or barrier semaphores. Data moves between devices by JAX's collectives and lax.ppermute only.
A program may use at most 128 MiB of HBM per device.

v0:
```python
import math

import jax
import jax.numpy as jnp
from jax import lax
from jax.sharding import PartitionSpec as P

HALO = 256


def padded(cells, sides, width):
    for axis, dim in sides:
        count = lax.axis_size(axis)
        ends = count - 1
        head = lax.slice_in_dim(cells, 0, width, axis=dim)
        tail = lax.slice_in_dim(cells, cells.shape[dim] - width, cells.shape[dim], axis=dim)
        cells = jnp.concatenate(
            [
                lax.ppermute(tail, axis, [(i, (i + 1) % count) for i in range(ends)]),
                cells,
                lax.ppermute(head, axis, [((i + 1) % count, i) for i in range(ends)]),
            ],
            axis=dim,
        )
    return cells


def silu_slope(values):
    logistic = jax.nn.sigmoid(values)
    return logistic * (1.0 + values * (1.0 - logistic))


def gather_rows(source, neighbour_index, edge_weight):
    summed = jnp.zeros((neighbour_index.shape[1], source.shape[1]), jnp.float32)
    for neighbour in range(neighbour_index.shape[0]):
        picked = source[neighbour_index[neighbour]].astype(jnp.float32)
        summed = summed + edge_weight[neighbour][:, None] * picked
    return summed.astype(jnp.bfloat16)


def spread_rows(gradient, neighbour_index, edge_weight, row_count):
    summed = jnp.zeros((row_count, gradient.shape[1]), jnp.float32)
    for neighbour in range(neighbour_index.shape[0]):
        summed = summed.at[neighbour_index[neighbour]].add(
            edge_weight[neighbour][:, None] * gradient
        )
    return summed


def node_forward(hidden, gathered, level_weights):
    first = jnp.dot(hidden, level_weights[0], preferred_element_type=jnp.float32)
    first = first + jnp.dot(gathered, level_weights[1], preferred_element_type=jnp.float32)
    middle = jax.nn.silu(first).astype(jnp.bfloat16)
    second = jnp.dot(middle, level_weights[2], preferred_element_type=jnp.float32)
    outer = jax.nn.silu(second).astype(jnp.bfloat16)
    return (first, middle, second, outer)


def node_output(hidden, saved, level_weights):
    added = hidden.astype(jnp.float32) + jnp.dot(
        saved[3], level_weights[3], preferred_element_type=jnp.float32
    )
    return added.astype(jnp.bfloat16)


def node_backward(out_grad, hidden, gathered, saved, level_weights):
    first, middle, second, outer = saved
    grad_outer = jnp.dot(outer.T, out_grad, preferred_element_type=jnp.float32)
    second_grad = jnp.dot(out_grad, level_weights[3].T, preferred_element_type=jnp.float32)
    second_grad = (second_grad * silu_slope(second)).astype(jnp.bfloat16)
    grad_middle = jnp.dot(middle.T, second_grad, preferred_element_type=jnp.float32)
    first_grad = jnp.dot(second_grad, level_weights[2].T, preferred_element_type=jnp.float32)
    first_grad = (first_grad * silu_slope(first)).astype(jnp.bfloat16)
    grad_hidden = jnp.dot(hidden.T, first_grad, preferred_element_type=jnp.float32)
    grad_gathered = jnp.dot(gathered.T, first_grad, preferred_element_type=jnp.float32)
    direct = out_grad.astype(jnp.float32) + jnp.dot(
        first_grad, level_weights[0].T, preferred_element_type=jnp.float32
    )
    spill = jnp.dot(first_grad, level_weights[1].T, preferred_element_type=jnp.float32)
    return (direct, spill, jnp.stack([grad_hidden, grad_gathered, grad_middle, grad_outer]))


def per_device(
    features,
    fine_cotangent,
    mid_cotangent,
    coarse_cotangent,
    weights,
    fine_offsets,
    fine_edge_w,
    pool_fine,
    owner_dev,
    coarse_slot,
    mid_nbrs,
    mid_edge_w,
    pool_mid,
    coarse_nbrs,
    coarse_edge_w,
):
    row_count = features.shape[0]
    feature_width = features.shape[1]
    tile_count = owner_dev.shape[0]
    tile_rows = row_count // tile_count
    block_rows = pool_fine.shape[0]
    mid_count = mid_cotangent.shape[0]
    coarse_count = coarse_cotangent.shape[0]
    peer_count = lax.axis_size("nodes")
    capacity = max(2, 2 * tile_count // peer_count)
    extended = padded(features, (("nodes", 0),), HALO)
    fine_index = fine_offsets + HALO + jnp.arange(row_count, dtype=jnp.int32)[None, :]
    fine_agg = gather_rows(extended, fine_index, fine_edge_w)
    fine_saved = node_forward(features, fine_agg, weights[0])
    fine_out = node_output(features, fine_saved, weights[0])
    pool_tiles = pool_fine.reshape(block_rows, tile_count, tile_rows)
    blocks = jnp.einsum(
        "rtj,tjd->trd",
        pool_tiles,
        fine_out.reshape(tile_count, tile_rows, feature_width),
        preferred_element_type=jnp.float32,
    ).astype(jnp.bfloat16)
    owners = owner_dev[:, 0]
    tile_order = jnp.arange(tile_count, dtype=jnp.int32)
    earlier = jnp.sum(
        ((owners[None, :] == owners[:, None]) & (tile_order[None, :] < tile_order[:, None])).astype(
            jnp.int32
        ),
        axis=1,
    )
    slot_of_tile = owners * capacity + earlier
    send_match = (
        slot_of_tile[None, :] == jnp.arange(peer_count * capacity, dtype=jnp.int32)[:, None]
    )
    send_map = send_match.astype(jnp.bfloat16)
    send_blocks = jnp.dot(
        send_map,
        blocks.reshape(tile_count, block_rows * feature_width),
        preferred_element_type=jnp.float32,
    )
    send_blocks = send_blocks.astype(jnp.bfloat16).reshape(
        peer_count, capacity, block_rows, feature_width
    )
    send_ids = jnp.sum(send_match.astype(jnp.int32) * (coarse_slot[None, :] + 1), axis=1) - 1
    got_blocks, got_ids = (
        lax.all_to_all(send_blocks, "nodes", split_axis=0, concat_axis=0, tiled=True),
        lax.all_to_all(
            send_ids.reshape(peer_count, capacity), "nodes", split_axis=0, concat_axis=0, tiled=True
        ),
    )
    owned_blocks = mid_count // block_rows
    recv_map = (
        got_ids.reshape(-1)[None, :] == jnp.arange(owned_blocks, dtype=jnp.int32)[:, None]
    ).astype(jnp.bfloat16)
    mid_sum = jnp.dot(
        recv_map,
        got_blocks.reshape(peer_count * capacity, block_rows * feature_width),
        preferred_element_type=jnp.float32,
    )
    mid_in = mid_sum.reshape(mid_count, feature_width).astype(jnp.bfloat16)
    mid_agg = gather_rows(mid_in, mid_nbrs, mid_edge_w)
    mid_saved = node_forward(mid_in, mid_agg, weights[1])
    mid_out = node_output(mid_in, mid_saved, weights[1])
    coarse_in = jnp.dot(pool_mid, mid_out, preferred_element_type=jnp.float32).astype(jnp.bfloat16)
    all_coarse, all_cotangent, all_nbrs, all_edge_w = (
        lax.all_gather(coarse_in.astype(jnp.float32), "nodes", axis=0, tiled=True),
        lax.all_gather(coarse_cotangent.astype(jnp.float32), "nodes", axis=0, tiled=True),
        lax.all_gather(coarse_nbrs, "nodes", axis=1, tiled=True),
        lax.all_gather(coarse_edge_w, "nodes", axis=1, tiled=True),
    )
    all_coarse = all_coarse.astype(jnp.bfloat16)
    all_cotangent = all_cotangent.astype(jnp.bfloat16)
    coarse_agg = gather_rows(all_coarse, all_nbrs, all_edge_w)
    coarse_saved = node_forward(all_coarse, coarse_agg, weights[2])
    coarse_direct, coarse_spill, coarse_wgrad = node_backward(
        all_cotangent, all_coarse, coarse_agg, coarse_saved, weights[2]
    )
    coarse_total = coarse_direct + spread_rows(
        coarse_spill, all_nbrs, all_edge_w, all_coarse.shape[0]
    )
    coarse_start = lax.axis_index("nodes") * coarse_count
    coarse_grad = lax.dynamic_slice_in_dim(coarse_total, coarse_start, coarse_count, 0).astype(
        jnp.bfloat16
    )
    back_mid = jnp.dot(pool_mid.T, coarse_grad, preferred_element_type=jnp.float32)
    mid_out_grad = (mid_cotangent.astype(jnp.float32) + back_mid).astype(jnp.bfloat16)
    mid_direct, mid_spill, mid_wgrad = node_backward(
        mid_out_grad, mid_in, mid_agg, mid_saved, weights[1]
    )
    mid_grad = (mid_direct + spread_rows(mid_spill, mid_nbrs, mid_edge_w, mid_count)).astype(
        jnp.bfloat16
    )
    slot_grads = jnp.dot(
        recv_map.T,
        mid_grad.reshape(owned_blocks, block_rows * feature_width),
        preferred_element_type=jnp.float32,
    )
    slot_grads = slot_grads.astype(jnp.bfloat16).reshape(
        peer_count, capacity, block_rows, feature_width
    )
    returned = lax.all_to_all(slot_grads, "nodes", split_axis=0, concat_axis=0, tiled=True)
    block_grads = jnp.dot(
        send_map.T,
        returned.reshape(peer_count * capacity, block_rows * feature_width),
        preferred_element_type=jnp.float32,
    )
    block_grads = block_grads.astype(jnp.bfloat16).reshape(tile_count, block_rows, feature_width)
    back_fine = jnp.einsum(
        "rtj,trd->tjd", pool_tiles, block_grads, preferred_element_type=jnp.float32
    ).reshape(row_count, feature_width)
    fine_out_grad = (fine_cotangent.astype(jnp.float32) + back_fine).astype(jnp.bfloat16)
    fine_direct, fine_spill, fine_wgrad = node_backward(
        fine_out_grad, features, fine_agg, fine_saved, weights[0]
    )
    spread_fine = spread_rows(fine_spill, fine_index, fine_edge_w, row_count + 2 * HALO)
    spill_rims = jnp.concatenate([spread_fine[:HALO], spread_fine[HALO + row_count :]], axis=0)
    rim_inflow = padded(spill_rims.astype(jnp.bfloat16), (("nodes", 0),), HALO).astype(
        spill_rims.dtype
    )
    inner = spread_fine[HALO : HALO + row_count]
    inner = inner.at[:HALO].add(rim_inflow[:HALO])
    inner = inner.at[row_count - HALO :].add(rim_inflow[3 * HALO :])
    feature_grads = (fine_direct + inner).astype(jnp.bfloat16)
    fine_scale = 1.0 / math.sqrt(row_count * peer_count)
    mid_scale = 1.0 / math.sqrt(mid_count * peer_count)
    coarse_scale = 1.0 / math.sqrt(coarse_count * peer_count)
    fine_summed, mid_summed = lax.psum((fine_wgrad, mid_wgrad), "nodes")
    weight_grads = jnp.stack(
        [fine_summed * fine_scale, mid_summed * mid_scale, coarse_wgrad * coarse_scale]
    )
    return (feature_grads, weight_grads)


def solution(mesh):
    in_specs = (
        P(("groups", "nodes"), None),
        P(("groups", "nodes"), None),
        P(("groups", "nodes"), None),
        P(("groups", "nodes"), None),
        P(),
        P("groups", "nodes"),
        P("groups", "nodes"),
        P("groups", "nodes"),
        P(("groups", "nodes"), None),
        P(("groups", "nodes")),
        P("groups", "nodes"),
        P("groups", "nodes"),
        P(("groups", "nodes"), None),
        P("groups", "nodes"),
        P("groups", "nodes"),
    )
    out_specs = (P(("groups", "nodes"), None), P("groups", None, None, None))
    return jax.shard_map(
        per_device, mesh=mesh, in_specs=in_specs, out_specs=out_specs, check_vma=False
    )
```

profile of v0, /device:TPU:1, one launch (start us, length us, event | category | flops | bytes accessed | tf_op | source)
XLA Modules:
  0.0 502.6 jit_solution(12995572061017026529)
XLA Ops:
  9.6 7.3 %all-to-all-start = ((s32[16,1,8]{2,1,0:T(1,128)}), s32[16,1,8]{2,1,0:T(1,128)}, u32[]{:S(2)}, u32[]{:S(2)}) async-start(s32[16,1,8]{2,1,0:T(1,128)} %bitcast.1), calls=%async_computation | async-start | bytes 16384 | tf_op jit(solution)/shard_map/all_to_all | solution.py:145
  25.6 20.8 %all-gather.1 = s32[16,16,8]{1,2,0:T(8,128)S(1)} all-gather(s32[1,16,8]{1,2,0:T(8,128)} %bitcast.403), channel_id=1, replica_groups=mesh['groups'=2,'nodes'=16] {'nodes'}, dimensions={0}, use_global_device_ids=true | all-gather | bytes 8704 | tf_op jit(solution)/shard_map/all_gather | solution.py:166
  57.7 6.2 %gather_fusion.7 = bf16[2048,128]{1,0:T(8,128)(2,1)S(1)} fusion(bf16[2560,128]{1,0:T(8,128)(2,1)S(1)} %constant_dynamic-update-slice_fusion, s32[2048]{0:T(1024)S(1)} %get-tuple-element.110), kind=kCustom, calls=%fused_computation.7 | custom fusion | bytes 1056768 | tf_op jit(solution)/shard_map/gather | solution.py:36
  63.9 6.2 %gather_fusion.6 = bf16[2048,128]{1,0:T(8,128)(2,1)S(1)} fusion(bf16[2560,128]{1,0:T(8,128)(2,1)S(1)} %constant_dynamic-update-slice_fusion, s32[2048]{0:T(1024)S(1)} %get-tuple-element.111), kind=kCustom, calls=%fused_computation.6 | custom fusion | bytes 1056768 | tf_op jit(solution)/shard_map/gather | solution.py:36
  70.1 6.2 %gather_fusion.5 = bf16[2048,128]{1,0:T(8,128)(2,1)S(1)} fusion(bf16[2560,128]{1,0:T(8,128)(2,1)S(1)} %constant_dynamic-update-slice_fusion, s32[2048]{0:T(1024)S(1)} %get-tuple-element.112), kind=kCustom, calls=%fused_computation.5 | custom fusion | bytes 1056768 | tf_op jit(solution)/shard_map/gather | solution.py:36
  76.3 6.2 %gather_fusion.4 = bf16[2048,128]{1,0:T(8,128)(2,1)S(1)} fusion(bf16[2560,128]{1,0:T(8,128)(2,1)S(1)} %constant_dynamic-update-slice_fusion, s32[2048]{0:T(1024)S(1)} %copy-done.19), kind=kCustom, calls=%fused_computation.4 | custom fusion | bytes 1056768 | tf_op jit(solution)/shard_map/gather | solution.py:36
  82.6 8.1 %gather_fusion.3 = bf16[2048,128]{1,0:T(8,128)(2,1)} fusion(bf16[2560,128]{1,0:T(8,128)(2,1)S(1)} %constant_dynamic-update-slice_fusion, s32[2048]{0:T(1024)S(1)} %copy-done.20), kind=kCustom, calls=%fused_computation.3 | custom fusion | bytes 1056768 | tf_op jit(solution)/shard_map/gather | solution.py:36
  90.6 8.0 %gather_fusion.2 = bf16[2048,128]{1,0:T(8,128)(2,1)} fusion(bf16[2560,128]{1,0:T(8,128)(2,1)S(1)} %constant_dynamic-update-slice_fusion, s32[2048]{0:T(1024)S(1)} %copy-done.18), kind=kCustom, calls=%fused_computation.2 | custom fusion | bytes 1056768 | tf_op jit(solution)/shard_map/gather | solution.py:36
  98.7 8.0 %gather_fusion.1 = bf16[2048,128]{1,0:T(8,128)(2,1)} fusion(bf16[2560,128]{1,0:T(8,128)(2,1)S(1)} %constant_dynamic-update-slice_fusion, s32[2048]{0:T(1024)S(1)} %copy-done.17), kind=kCustom, calls=%fused_computation.1 | custom fusion | bytes 1056768 | tf_op jit(solution)/shard_map/gather | solution.py:36
  106.7 8.0 %gather_fusion = bf16[2048,128]{1,0:T(8,128)(2,1)} fusion(bf16[2560,128]{1,0:T(8,128)(2,1)S(1)} %constant_dynamic-update-slice_fusion, s32[2048]{0:T(1024)S(1)} %copy-done.16), kind=kCustom, calls=%fused_computation | custom fusion | bytes 1056768 | tf_op jit(solution)/shard_map/gather | solution.py:36
  114.7 5.1 %add_convert_fusion = bf16[2048,128]{1,0:T(8,128)(2,1)S(1)} fusion(bf16[2048,128]{1,0:T(8,128)(2,1)S(1)} %gather_fusion.7, bf16[2048,128]{1,0:T(8,128)(2,1)S(1)} %gather_fusion.6, bf16[2048,128]{1,0:T(8,128)(2,1)S(1)} %gather_fusion.5, bf16[2048,128]{1,0:T(8,128)(2,1)S(1)} %gather_fusion.4, bf16[2048,128]{1,0:T(8,128)(2,1)} %gather_fusion.3, ...), kind=kLoop, calls=%fused_computation.121 | loop fusion | flops 6291456 | bytes 4784128 | tf_op jit(solution)/shard_map/convert_element_type | solution.py:38
  130.6 21.9 %all-gather = f32[16,16,8]{1,2,0:T(8,128)S(1)} all-gather(f32[1,16,8]{1,2,0:T(8,128)S(1)} %bitcast.404), channel_id=1, replica_groups=mesh['groups'=2,'nodes'=16] {'nodes'}, dimensions={0}, use_global_device_ids=true | all-gather | bytes 8704 | tf_op jit(solution)/shard_map/all_gather | solution.py:167
  152.7 17.6 %all_gather.12 = bf16[256,128]{1,0:T(8,128)(2,1)S(1)} all-gather(bf16[16,128]{1,0:T(8,128)(2,1)S(1)} %copy-done.76), channel_id=1, replica_groups=mesh['groups'=2,'nodes'=16] {'nodes'}, dimensions={0}, use_global_device_ids=true | all-gather | bytes 69632 | tf_op jit(solution)/shard_map/all_gather | solution.py:165
  186.5 19.1 %all_gather.13 = bf16[256,128]{1,0:T(8,128)(2,1)S(1)} all-gather(bf16[16,128]{1,0:T(8,128)(2,1)S(1)} %fusion.18), channel_id=1, replica_groups=mesh['groups'=2,'nodes'=16] {'nodes'}, dimensions={0}, use_global_device_ids=true | all-gather | bytes 69632 | tf_op jit(solution)/shard_map/all_gather | solution.py:164
  273.4 7.6 %all-to-all-done.2 = bf16[16,8,8,128]{3,1,2,0:T(8,128)(2,1)S(1)} async-done(((bf16[16,8,8,128]{3,1,2,0:T(8,128)(2,1)}), bf16[16,8,8,128]{3,1,2,0:T(8,128)(2,1)S(1)}, u32[]{:S(2)}, u32[]{:S(2)}) %all-to-all-start.2) | async-done | bytes 262176 | tf_op jit(solution)/shard_map/all_to_all | solution.py:199
  290.6 12.9 %scatter_custom_fusion.16 = f32[2560,128]{1,0:T(8,128)S(1)} fusion(s32[2048]{0:T(1024)} %bitcast.354, f32[2048,128]{1,0:T(8,128)S(1)} %fusion.130, f32[]{:T(128)} %constant.100.clone.1, f32[2048]{0:T(1024)S(1)} %bitcast.336), kind=kCustom, calls=%fused_computation.115 | custom fusion | flops 524288 | bytes 2368000 | tf_op jit(solution)/shard_map/scatter-add | solution.py:44
  303.5 13.1 %scatter_custom_fusion.17 = f32[2560,128]{1,0:T(8,128)S(1)} fusion(f32[2560,128]{1,0:T(8,128)S(1)} %scatter_custom_fusion.16, s32[2048]{0:T(1024)} %bitcast.352, f32[2048,128]{1,0:T(8,128)S(1)} %fusion.130, f32[2048]{0:T(1024)S(1)} %bitcast.334), kind=kCustom, calls=%fused_computation.113 | custom fusion | flops 524288 | bytes 2367488 | tf_op jit(solution)/shard_map/scatter-add | solution.py:44
  316.7 13.4 %scatter_custom_fusion.18 = f32[2560,128]{1,0:T(8,128)S(1)} fusion(f32[2560,128]{1,0:T(8,128)S(1)} %scatter_custom_fusion.17, s32[2048]{0:T(1024)} %bitcast.350, f32[2048,128]{1,0:T(8,128)S(1)} %fusion.130, f32[2048]{0:T(1024)S(1)} %bitcast.332), kind=kCustom, calls=%fused_computation.111 | custom fusion | flops 524288 | bytes 2367488 | tf_op jit(solution)/shard_map/scatter-add | solution.py:44
  330.0 13.1 %scatter_custom_fusion.19 = f32[2560,128]{1,0:T(8,128)S(1)} fusion(f32[2560,128]{1,0:T(8,128)S(1)} %scatter_custom_fusion.18, s32[2048]{0:T(1024)} %bitcast.348, f32[2048,128]{1,0:T(8,128)S(1)} %fusion.130, f32[2048]{0:T(1024)S(1)} %bitcast.330), kind=kCustom, calls=%fused_computation.109 | custom fusion | flops 524288 | bytes 2367488 | tf_op jit(solution)/shard_map/scatter-add | solution.py:44
  343.1 13.1 %scatter_custom_fusion.20 = f32[2560,128]{1,0:T(8,128)S(1)} fusion(f32[2560,128]{1,0:T(8,128)S(1)} %scatter_custom_fusion.19, s32[2048]{0:T(1024)} %bitcast.346, f32[2048,128]{1,0:T(8,128)S(1)} %fusion.130, f32[2048]{0:T(1024)S(1)} %bitcast.328), kind=kCustom, calls=%fused_computation.107 | custom fusion | flops 524288 | bytes 2367488 | tf_op jit(solution)/shard_map/scatter-add | solution.py:44
  356.3 13.1 %scatter_custom_fusion.21 = f32[2560,128]{1,0:T(8,128)S(1)} fusion(f32[2560,128]{1,0:T(8,128)S(1)} %scatter_custom_fusion.20, s32[2048]{0:T(1024)} %bitcast.344, f32[2048,128]{1,0:T(8,128)S(1)} %fusion.130, f32[2048]{0:T(1024)S(1)} %bitcast.326), kind=kCustom, calls=%fused_computation.105 | custom fusion | flops 524288 | bytes 2367488 | tf_op jit(solution)/shard_map/scatter-add | solution.py:44
  369.4 13.1 %scatter_custom_fusion.22 = f32[2560,128]{1,0:T(8,128)S(1)} fusion(f32[2560,128]{1,0:T(8,128)S(1)} %scatter_custom_fusion.21, s32[2048]{0:T(1024)} %bitcast.342, f32[2048,128]{1,0:T(8,128)S(1)} %fusion.130, f32[2048]{0:T(1024)S(1)} %bitcast.324), kind=kCustom, calls=%fused_computation.103 | custom fusion | flops 524288 | bytes 2367488 | tf_op jit(solution)/shard_map/scatter-add | solution.py:44
  382.5 13.4 %scatter_custom_fusion.23 = f32[2560,128]{1,0:T(8,128)S(1)} fusion(f32[2560,128]{1,0:T(8,128)S(1)} %scatter_custom_fusion.22, s32[2048]{0:T(1024)} %bitcast.340, f32[2048,128]{1,0:T(8,128)S(1)} %fusion.130, f32[2048]{0:T(1024)S(1)} %bitcast.322), kind=kCustom, calls=%fused_computation.101 | custom fusion | flops 524288 | bytes 2367488 | tf_op jit(solution)/shard_map/scatter-add | solution.py:44
  407.4 84.7 %all-reduce.3.cloned.1.call-done = (f32[4,128,128]{1,2,0:T(8,128)}, f32[4,128,128]{1,2,0:T(8,128)}) async-done(((f32[4,128,128]{1,2,0:T(8,128)}, f32[4,128,128]{1,2,0:T(8,128)}), (f32[4,128,128]{1,2,0:T(8,128)}, f32[4,128,128]{1,2,0:T(8,128)})) %all-reduce.3.cloned.1.call-update) | async-done | bytes 524304 | tf_op jit(solution)/shard_map/psum | solution.py:225
  (319 shorter events, 139.9 us)
Async XLA Ops:
  7.2 179.0 %copy-start = (bf16[16,512]{1,0:T(8,128)(2,1)S(1)}, bf16[16,512]{1,0:T(8,128)(2,1)}, u32[]{:S(2)}) copy-start(bf16[16,512]{1,0:T(8,128)(2,1)} %param.31) | copy-start | bytes 49156
  7.2 42.2 %copy-start.1 = (bf16[2048,128]{1,0:T(8,128)(2,1)S(1)}, bf16[2048,128]{1,0:T(8,128)(2,1)}, u32[]{:S(2)}) copy-start(bf16[2048,128]{1,0:T(8,128)(2,1)} %param.19) | copy-start | bytes 1572868
  9.6 116.9 %all-to-all-start = ((s32[16,1,8]{2,1,0:T(1,128)}), s32[16,1,8]{2,1,0:T(1,128)}, u32[]{:S(2)}, u32[]{:S(2)}) async-start(s32[16,1,8]{2,1,0:T(1,128)} %bitcast.1), calls=%async_computation | async-start | bytes 16384 | tf_op jit(solution)/shard_map/all_to_all | solution.py:145
  17.8 39.9 %collective-permute-start.1 = (bf16[256,128]{1,0:T(8,128)(2,1)S(1)}, bf16[256,128]{1,0:T(8,128)(2,1)S(1)}, u32[]{:S(2)}, u32[]{:S(2)}) collective-permute-start(bf16[256,128]{1,0:T(8,128)(2,1)S(1)} %get-tuple-element.38), channel_id=1, source_target_pairs={{1,0},{2,1},{3,2},{4,3},{5,4},{6,5},{7,6},{8,7},{9,8},{10,9},{11,1... | collective-permute-start | bytes 196616 | tf_op jit(solution)/shard_map/ppermute | solution.py:21
  19.9 37.6 %collective-permute-start = (bf16[256,128]{1,0:T(8,128)(2,1)S(1)}, bf16[256,128]{1,0:T(8,128)(2,1)S(1)}, u32[]{:S(2)}, u32[]{:S(2)}) collective-permute-start(bf16[256,128]{1,0:T(8,128)(2,1)S(1)} %get-tuple-element.39), channel_id=1, source_target_pairs={{0,1},{1,2},{2,3},{3,4},{4,5},{5,6},{6,7},{7,8},{8,9},{9,10},{10,1... | collective-permute-start | bytes 196616 | tf_op jit(solution)/shard_map/ppermute | solution.py:19
  24.4 30.0 %copy-start.62 = (s32[512,1]{0,1:T(1,128)}, s32[512,1]{0,1:T(1,128)S(1)}, u32[]{:S(2)}) copy-start(s32[512,1]{0,1:T(1,128)S(1)} %get-tuple-element.70) | copy-start | bytes 6148
  25.5 32.1 %copy-start.21 = (s32[2048,1]{0,1:T(1,128)}, s32[2048,1]{0,1:T(1,128)S(1)}, u32[]{:S(2)}) copy-start(s32[2048,1]{0,1:T(1,128)S(1)} %get-tuple-element.49) | copy-start | bytes 24580
  25.5 32.1 %copy-start.22 = (s32[2048,1]{0,1:T(1,128)}, s32[2048,1]{0,1:T(1,128)S(1)}, u32[]{:S(2)}) copy-start(s32[2048,1]{0,1:T(1,128)S(1)} %get-tuple-element.50) | copy-start | bytes 24580
  25.5 32.1 %copy-start.23 = (s32[2048,1]{0,1:T(1,128)}, s32[2048,1]{0,1:T(1,128)S(1)}, u32[]{:S(2)}) copy-start(s32[2048,1]{0,1:T(1,128)S(1)} %get-tuple-element.51) | copy-start | bytes 24580
  25.5 32.1 %copy-start.24 = (s32[2048,1]{0,1:T(1,128)}, s32[2048,1]{0,1:T(1,128)S(1)}, u32[]{:S(2)}) copy-start(s32[2048,1]{0,1:T(1,128)S(1)} %get-tuple-element.52) | copy-start | bytes 24580
  25.5 32.1 %copy-start.25 = (s32[2048,1]{0,1:T(1,128)}, s32[2048,1]{0,1:T(1,128)S(1)}, u32[]{:S(2)}) copy-start(s32[2048,1]{0,1:T(1,128)S(1)} %get-tuple-element.53) | copy-start | bytes 24580
  25.5 32.1 %copy-start.26 = (s32[2048,1]{0,1:T(1,128)}, s32[2048,1]{0,1:T(1,128)S(1)}, u32[]{:S(2)}) copy-start(s32[2048,1]{0,1:T(1,128)S(1)} %get-tuple-element.54) | copy-start | bytes 24580
  25.5 32.1 %copy-start.27 = (s32[2048,1]{0,1:T(1,128)}, s32[2048,1]{0,1:T(1,128)S(1)}, u32[]{:S(2)}) copy-start(s32[2048,1]{0,1:T(1,128)S(1)} %get-tuple-element.48) | copy-start | bytes 24580
  25.5 32.1 %copy-start.28 = (s32[2048,1]{0,1:T(1,128)}, s32[2048,1]{0,1:T(1,128)S(1)}, u32[]{:S(2)}) copy-start(s32[2048,1]{0,1:T(1,128)S(1)} %get-tuple-element.55) | copy-start | bytes 24580
  125.2 45.8 %copy-start.45 = (f32[8,512]{1,0:T(8,128)S(1)}, f32[8,512]{1,0:T(8,128)}, u32[]{:S(2)}) copy-start(f32[8,512]{1,0:T(8,128)} %param.30) | copy-start | bytes 49156
  125.4 47.8 %copy-start.8 = (bf16[3,4,128,128]{3,2,1,0:T(8,128)(2,1)S(1)}, bf16[3,4,128,128]{3,2,1,0:T(8,128)(2,1)}, u32[]{:S(2)}) copy-start(bf16[3,4,128,128]{3,2,1,0:T(8,128)(2,1)} %param.23) | copy-start | bytes 1179652
  125.5 48.0 %copy-start.61 = (s32[1024]{0:T(1024)S(1)}, s32[1024]{0:T(1024)}, u32[]{:S(2)}) copy-start(s32[1024]{0:T(1024)} %get-tuple-element.102) | copy-start | bytes 12292
  126.5 46.5 %all-to-all-start.1 = ((bf16[16,8,8,128]{3,1,2,0:T(8,128)(2,1)}), bf16[16,8,8,128]{3,1,2,0:T(8,128)(2,1)S(1)}, u32[]{:S(2)}, u32[]{:S(2)}) async-start(bf16[16,8,8,128]{3,1,2,0:T(8,128)(2,1)} %fusion.5), calls=%async_computation.1 | async-start | bytes 524288 | tf_op jit(solution)/shard_map/all_to_all | solution.py:144
  185.2 50.8 %copy-start.9 = (f32[512,128]{1,0:T(8,128)}, f32[512,128]{1,0:T(8,128)S(1)}, u32[]{:S(2)}) copy-start(f32[512,128]{1,0:T(8,128)S(1)} %convolution_add_fusion.5) | copy-start | bytes 786436
  268.0 13.0 %all-to-all-start.2 = ((bf16[16,8,8,128]{3,1,2,0:T(8,128)(2,1)}), bf16[16,8,8,128]{3,1,2,0:T(8,128)(2,1)S(1)}, u32[]{:S(2)}, u32[]{:S(2)}) async-start(bf16[16,8,8,128]{3,1,2,0:T(8,128)(2,1)} %fusion.6), calls=%async_computation.2 | async-start | bytes 524288 | tf_op jit(solution)/shard_map/all_to_all | solution.py:199
  271.5 220.6 %all-reduce.3.cloned.1.call-start = ((), (), s32[]{:S(2)}) async-start(), calls=%async_computation.3 | async-start | bytes 1048576 | tf_op jit(solution)/shard_map/psum | solution.py:225
  396.1 5.7 %collective-permute-start.2 = (bf16[256,128]{1,0:T(8,128)(2,1)S(1)}, bf16[256,128]{1,0:T(8,128)(2,1)}, u32[]{:S(2)}, u32[]{:S(2)}) collective-permute-start(bf16[256,128]{1,0:T(8,128)(2,1)S(1)} %get-tuple-element.36), channel_id=1, source_target_pairs={{0,1},{1,2},{2,3},{3,4},{4,5},{5,6},{6,7},{7,8},{8,9},{9,10},{10,1... | collective-permute-start | bytes 196616 | tf_op jit(solution)/shard_map/ppermute | solution.py:19
  398.0 5.7 %collective-permute-start.3 = (bf16[256,128]{1,0:T(8,128)(2,1)S(1)}, bf16[256,128]{1,0:T(8,128)(2,1)}, u32[]{:S(2)}, u32[]{:S(2)}) collective-permute-start(bf16[256,128]{1,0:T(8,128)(2,1)S(1)} %get-tuple-element.37), channel_id=1, source_target_pairs={{1,0},{2,1},{3,2},{4,3},{5,4},{6,5},{7,6},{8,7},{9,8},{10,9},{11,1... | collective-permute-start | bytes 196616 | tf_op jit(solution)/shard_map/ppermute | solution.py:21
  405.4 88.5 %copy-start.5 = (f32[1,4,128,128]{2,3,1,0:T(8,128)S(1)}, f32[1,4,128,128]{2,3,1,0:T(8,128)}, u32[]{:S(2)}) copy-start(f32[1,4,128,128]{2,3,1,0:T(8,128)} %maximum_multiply_fusion) | copy-start | bytes 786436
  (71 other events, 742.0 us)
Sparse Core Ops, SparseCore 0:
  401.9 90.0 all-reduce.2
where the time goes:
time: 513 us; the launch traced here: 503 us
  other arithmetic  179 us (35%)
  waiting for transfers between devices  94.1 us (18%)
  local copies, waits for them, and re-layouts  82.8 us (16%)
  blocking collectives  79.5 us (15%)
  matrix products  26.1 us (5%)
  starting transfers between devices  24.8 us (5%)
  between operations  16.4 us (3%)
    scatter-add x24, other arithmetic, spread_rows(): summed.at[neighbour_index[neighbour]]  153 us
    psum x1, waiting for transfers between devices, per_device(): fine_summed, mid_summed = lax.psum((fine_wgrad, mid_wgrad), 'nodes')  84.7 us
    gather x24, local copies, waits for them, and re-layouts, gather_rows(): picked = source[neighbour_index[neighbour]].astype(jnp.float32)  75.6 us
    all_gather x1, blocking collectives, per_device(): lax.all_gather(coarse_edge_w, 'nodes', axis=1, tiled=True)  21.9 us
    all_gather x1, blocking collectives, per_device(): lax.all_gather(coarse_nbrs, 'nodes', axis=1, tiled=True)  20.8 us
    all_gather x1, blocking collectives, per_device(): lax.all_gather(coarse_in.astype(jnp.float32), 'nodes', axis=0, tiled=True)  19.1 us
    all_gather x1, blocking collectives, per_device(): lax.all_gather(coarse_cotangent.astype(jnp.float32), 'nodes', axis=0, til...  17.6 us
  transfers between devices with their start and end apart: 8, of which 3 were waited for; matrix products, arithmetic and copies ran while one was open for 18% of the time, Pallas kernels for 0%

commit v1 on v0

v1 whole, which is shorter than its diff:
```python
import functools
import math

import jax
import jax.numpy as jnp
from jax import lax
from jax.experimental import pallas as pl
from jax.experimental.pallas import tpu as pltpu
from jax.sharding import PartitionSpec as P

HALO = 256
TILE = 256
BF = jnp.bfloat16
F32 = jnp.float32

VM = pl.BlockSpec(memory_space=pltpu.VMEM)
SM = pl.BlockSpec(memory_space=pltpu.SMEM)
ANY = pl.BlockSpec(memory_space=pl.ANY)


def dot(a, b):
    return jnp.dot(a, b, preferred_element_type=F32)


def dot_nt(a, b):
    return lax.dot_general(a, b, (((1,), (1,)), ((), ())), preferred_element_type=F32)


def dot_tn(a, b):
    return lax.dot_general(a, b, (((0,), (0,)), ((), ())), preferred_element_type=F32)


def silu(v):
    return v / (1.0 + jnp.exp(-v))


def silu_slope(v):
    s = 1.0 / (1.0 + jnp.exp(-v))
    return s * (1.0 + v * (1.0 - s))


def merged_weights(idx, ew):
    total = ew
    for r in range(1, idx.shape[0]):
        total = total + jnp.where(pltpu.roll(idx, r, 0) == idx, pltpu.roll(ew, r, 0), 0.0)
    return total.astype(BF)


def edge_columns(idx, ew, start, rows):
    count = idx.shape[0]
    lanes = idx.shape[1]
    position = lax.broadcasted_iota(jnp.int32, (rows, lanes), 0) + start
    position = position.astype(jnp.int16)
    picked = jnp.zeros((rows, lanes), BF)
    for k in range(count):
        picked = jnp.where(idx[k : k + 1, :] == position, ew[k : k + 1, :], picked)
    return picked


def fine_edges(off, ew, s_ref):
    for h in range(TILE // 128):
        lane = slice(128 * h, 128 * (h + 1))
        o = off[:, lane]
        weight = merged_weights(o, ew[:, lane])
        rel = o + lax.broadcasted_iota(jnp.int32, o.shape, 1) + HALO
        rel = rel.astype(jnp.int16)
        for c in range(2 * HALO // 128 + 1):
            s_ref[128 * (h + c) : 128 * (h + c + 1), lane] = edge_columns(
                rel, weight, 128 * c, 128
            )


def clear_corners(s_ref):
    for h in range(TILE // 128):
        lane = slice(128 * h, 128 * (h + 1))
        if h > 0:
            s_ref[: 128 * h, lane] = jnp.zeros((128 * h, 128), BF)
        last = 128 * h + 2 * HALO + 128
        if last < TILE + 2 * HALO:
            s_ref[last:, lane] = jnp.zeros((TILE + 2 * HALO - last, 128), BF)


def forward_weights(w):
    w01 = jnp.concatenate([jnp.transpose(w[0]), jnp.transpose(w[1])], axis=1)
    return w01, jnp.transpose(w[2]), jnp.transpose(w[3])


def pool_matrix(pool, tile_rows):
    lane = lax.broadcasted_iota(jnp.int32, pool.shape, 1) // tile_rows
    values = pool.astype(F32)
    parts = [jnp.where(lane == r, values, 0.0) for r in range(pool.shape[1] // tile_rows)]
    return jnp.concatenate(parts, axis=0).astype(BF)


def fine_tile(h_t, window_t, s, weights, pool, tile_rows):
    w01, w2t, w3t = weights
    agg = dot(window_t, s).astype(BF)
    first = dot(w01, jnp.concatenate([h_t, agg], axis=0))
    middle = silu(first).astype(BF)
    second = dot(w2t, middle)
    outer = silu(second).astype(BF)
    fine_out = (h_t.astype(F32) + dot(w3t, outer)).astype(BF)
    blocks = dot_nt(pool_matrix(pool, tile_rows), fine_out)
    return agg, blocks


def inner_kernel(
    tile_rows, feat_h, off_h, ew_h, w_h, pool_h, agg_ref, blocks_ref,
    feat, off, ew, w, pool, feat_t, s_ref, sems,
):
    copies = []
    for i, (src, dst) in enumerate(
        ((off_h, off), (ew_h, ew), (feat_h, feat), (w_h.at[0], w), (pool_h, pool))
    ):
        copy = pltpu.make_async_copy(src, dst, sems.at[i])
        copy.start()
        copies.append(copy)
    clear_corners(s_ref.at[0])
    clear_corners(s_ref.at[1])
    for copy in copies:
        copy.wait()
    feat_t[...] = jnp.transpose(feat[...])
    weights = forward_weights(w[...])
    tiles = feat.shape[0] // TILE
    per = TILE // tile_rows * pool.shape[0]
    for i in range(1, tiles - 1):
        cols = slice(i * TILE, (i + 1) * TILE)
        s = s_ref.at[i % 2]
        fine_edges(off[:, cols], ew[:, cols], s)
        agg, blocks = fine_tile(
            feat_t[:, cols],
            feat_t[:, i * TILE - HALO : (i + 1) * TILE + HALO],
            s[...],
            weights,
            pool[:, cols],
            tile_rows,
        )
        agg_ref[:, cols] = agg
        blocks_ref[i * per : (i + 1) * per, :] = blocks


def outer_kernel(
    tile_rows, peers, cap,
    left, right, feat, off, ew, w, pool, blocks_in, owner, slot, cot, nbrs, cew,
    agg_ref, send_ref, place_ref,
    s_ref, spread, ids, extra, counts,
):
    rows = feat.shape[0]
    block_rows = pool.shape[0]
    per_tile = TILE // tile_rows
    tile_count = rows // tile_rows
    n2 = cot.shape[0]
    clear_corners(s_ref.at[0])
    clear_corners(s_ref.at[1])
    weights = forward_weights(w[0])
    spread[...] = jnp.zeros(spread.shape, F32)
    ids[...] = jnp.full(ids.shape, -1.0, F32)
    for p in range(peers):
        counts[p] = 0
    lane_slot = lax.broadcasted_iota(jnp.int32, (1, 128), 1) // block_rows

    def place(t, values):
        o = owner[t]
        c = counts[o]
        counts[o] = c + 1
        q = o * cap + c
        place_ref[t] = q
        spread[pl.ds(pl.multiple_of(q * block_rows, 8), block_rows), :] = values
        row = ids[pl.ds(o, 1), :]
        ids[pl.ds(o, 1), :] = jnp.where(lane_slot == c, slot[t].astype(F32), row)

    results = {}
    for n, i in enumerate((0, rows // TILE - 1)):
        cols = slice(i * TILE, (i + 1) * TILE)
        s = s_ref.at[n]
        fine_edges(off[:, cols], ew[:, cols], s)
        if n == 0:
            window = jnp.concatenate([left[...], feat[: TILE + HALO, :]], axis=0)
            mine = slice(HALO, HALO + TILE)
        else:
            window = jnp.concatenate([feat[rows - TILE - HALO :, :], right[...]], axis=0)
            mine = slice(HALO, HALO + TILE)
        window_t = jnp.transpose(window)
        agg, blocks = fine_tile(
            window_t[:, mine], window_t, s[...], weights, pool[:, cols], tile_rows
        )
        agg_ref[:, n * TILE : (n + 1) * TILE] = agg
        results[i] = blocks
    for t in range(tile_count):
        i = t // per_tile
        if i in results:
            at = (t - i * per_tile) * block_rows
            values = results[i][at : at + block_rows, :]
        else:
            values = blocks_in[t * block_rows : (t + 1) * block_rows, :]
        place(t, values)
    nb = nbrs[...]
    extra[...] = jnp.zeros(extra.shape, F32)
    high = nb // 256
    extra[0:8, 0:n2] = high.astype(F32)
    extra[0:8, n2 : 2 * n2] = (nb - high * 256).astype(F32)
    ce = cew[...]
    ce_high = ce.astype(BF).astype(F32)
    extra[0:8, 2 * n2 : 3 * n2] = ce_high
    extra[0:8, 3 * n2 : 4 * n2] = ce - ce_high
    top = extra[0:8, :]
    last = lax.broadcasted_iota(jnp.int32, (8, 128), 0)
    chunk = cap * block_rows
    for p in range(peers):
        send_ref[p, 0:chunk, :] = spread[p * chunk : (p + 1) * chunk, :].astype(BF)
        send_ref[p, chunk : chunk + n2, :] = cot[...]
        below = jnp.where(last == 0, ids[p : p + 1, :], 0.0)
        send_ref[p, chunk + n2 : chunk + n2 + 16, :] = jnp.concatenate(
            [top, below], axis=0
        ).astype(BF)


def saved_kernel(
    feat, agg_in, agg_out, w, fine_cot, mid_nbrs, mid_ew, mid_cot,
    hid_ref, agg_ref, mid_ref, outer_ref, slope1_ref, slope2_ref, cot_ref,
    smid_ref, mcot_ref,
):
    rows = feat.shape[0]
    w01, w2t, _ = forward_weights(w[0])
    hid_ref[...] = jnp.transpose(feat[...])
    cot_ref[...] = jnp.transpose(fine_cot[...])
    mcot_ref[...] = jnp.transpose(mid_cot[...])
    tiles = rows // TILE
    for i in range(tiles):
        cols = slice(i * TILE, (i + 1) * TILE)
        if i == 0:
            agg = agg_out[:, :TILE]
        elif i == tiles - 1:
            agg = agg_out[:, TILE:]
        else:
            agg = agg_in[:, cols]
        agg_ref[:, cols] = agg
        first = dot(w01, jnp.concatenate([hid_ref[:, cols], agg], axis=0))
        s1 = 1.0 / (1.0 + jnp.exp(-first))
        middle = (first * s1).astype(BF)
        mid_ref[:, cols] = middle
        slope1_ref[:, cols] = s1 * (1.0 + first * (1.0 - s1))
        second = dot(w2t, middle)
        s2 = 1.0 / (1.0 + jnp.exp(-second))
        outer_ref[:, cols] = (second * s2).astype(BF)
        slope2_ref[:, cols] = s2 * (1.0 + second * (1.0 - s2))
    nodes = mid_nbrs.shape[1]
    for c in range(nodes // 128):
        lane = slice(128 * c, 128 * (c + 1))
        idx = mid_nbrs[:, lane]
        weight = merged_weights(idx, mid_ew[:, lane])
        idx = idx.astype(jnp.int16)
        for r in range(nodes // 128):
            smid_ref[128 * r : 128 * (r + 1), lane] = edge_columns(idx, weight, 128 * r, 128)


def mid_kernel(
    peers, cap, block_rows,
    got, smid, w, pool_mid,
    send_ref, hid_ref, agg_ref, mid_ref, outer_ref, slope1_ref, slope2_ref, sel_ref,
    blocks,
):
    chunk = cap * block_rows
    nodes = smid.shape[0]
    n2 = pool_mid.shape[0]
    rows = []
    for p in range(peers):
        rows.append(got[p, chunk + n2 : chunk + n2 + 16, :].astype(F32)[8:9, :])
    keys = jnp.transpose(jnp.concatenate(rows, axis=0))
    keys = keys * block_rows
    keys = keys + (lax.broadcasted_iota(jnp.int32, keys.shape, 0) % block_rows).astype(F32)
    keys = keys.astype(jnp.int32)
    lane = lax.broadcasted_iota(jnp.int32, (chunk, nodes), 1)
    for p in range(peers):
        sel_ref[p * chunk : (p + 1) * chunk, :] = jnp.where(
            keys[0:chunk, p : p + 1] == lane, 1.0, 0.0
        ).astype(BF)
        blocks[p * chunk : (p + 1) * chunk, :] = got[p, 0:chunk, :]
    w01, w2t, w3t = forward_weights(w[1])
    hidden = dot_tn(blocks[...], sel_ref[...]).astype(BF)
    hid_ref[...] = hidden
    agg = dot(hidden, smid[...]).astype(BF)
    agg_ref[...] = agg
    first = dot(w01, jnp.concatenate([hidden, agg], axis=0))
    s1 = 1.0 / (1.0 + jnp.exp(-first))
    middle = (first * s1).astype(BF)
    mid_ref[...] = middle
    second = dot(w2t, middle)
    s2 = 1.0 / (1.0 + jnp.exp(-second))
    outer = (second * s2).astype(BF)
    outer_ref[...] = outer
    mid_out = (hidden.astype(F32) + dot(w3t, outer)).astype(BF)
    coarse = dot_nt(pool_mid[...], mid_out).astype(BF)
    for p in range(peers):
        send_ref[p * n2 : (p + 1) * n2, :] = coarse
    slope1_ref[...] = s1 * (1.0 + first * (1.0 - s1))
    slope2_ref[...] = s2 * (1.0 + second * (1.0 - s2))


def coarse_edges_kernel(nbrs, ew, cot, s_ref, cot_ref):
    nodes = nbrs.shape[1]
    cot_ref[...] = jnp.transpose(cot[...])

    def column(c, _):
        lane = pl.ds(pl.multiple_of(c * 128, 128), 128)
        idx = nbrs[:, lane]
        weight = merged_weights(idx, ew[:, lane])
        idx = idx.astype(jnp.int16)
        for r in range(nodes // 128):
            s_ref[128 * r : 128 * (r + 1), lane] = edge_columns(idx, weight, 128 * r, 128)
        return 0

    lax.fori_loop(0, nodes // 128, column, 0)


def coarse_kernel(
    peers,
    got, sco, cot_all, w, cot_my, pool_mid, mcot, mhid, magg, mmid, mouter, msl1, msl2, smid, sel,
    send_ref, cwg_ref, gmid_ref, sg_ref, fg_ref,
):
    nodes = got.shape[0]
    n2 = cot_my.shape[0]
    me = lax.axis_index("nodes")
    width = min(TILE, nodes)
    hidden = jnp.transpose(got[...])
    w01, w2t, _ = forward_weights(w[2])
    mine = pl.ds(pl.multiple_of(me * n2, 16), n2)
    spread = jnp.zeros((n2, 128), F32)
    fg_mine = jnp.zeros((n2, 128), F32)
    grads = [jnp.zeros((128, 128), F32) for _ in range(4)]
    row = lax.broadcasted_iota(jnp.int32, (n2, width), 0) + me * n2
    lane = lax.broadcasted_iota(jnp.int32, (n2, width), 1)
    for i in range(nodes // width):
        cols = slice(i * width, (i + 1) * width)
        h = hidden[:, cols]
        agg = dot(hidden, sco[:, cols]).astype(BF)
        first = dot(w01, jnp.concatenate([h, agg], axis=0))
        s1 = 1.0 / (1.0 + jnp.exp(-first))
        middle = (first * s1).astype(BF)
        second = dot(w2t, middle)
        s2 = 1.0 / (1.0 + jnp.exp(-second))
        outer = (second * s2).astype(BF)
        g = cot_all[:, cols]
        sg = (dot(w[2, 3], g) * (s2 * (1.0 + second * (1.0 - s2)))).astype(BF)
        fg = (dot(w[2, 2], sg) * (s1 * (1.0 + first * (1.0 - s1)))).astype(BF)
        spill = dot(w[2, 1], fg).astype(BF)
        spread = spread + dot_nt(sco[mine, cols], spill)
        here = jnp.where(lane + i * width == row, 1.0, 0.0).astype(BF)
        fg_mine = fg_mine + dot_nt(here, fg)
        grads = [
            grads[0] + dot_nt(h, fg),
            grads[1] + dot_nt(agg, fg),
            grads[2] + dot_nt(middle, sg),
            grads[3] + dot_nt(outer, g),
        ]
    scale = 1.0 / math.sqrt(nodes)
    for m in range(4):
        cwg_ref[m] = grads[m] * scale
    direct = cot_my[...].astype(F32) + dot_nt(fg_mine.astype(BF), w[2, 0])
    coarse_grad = (direct + spread).astype(BF)
    back = dot_tn(coarse_grad, pool_mid[...])
    g = (mcot[...].astype(F32) + back).astype(BF)
    sg = (dot(w[1, 3], g) * msl2[...]).astype(BF)
    fg = (dot(w[1, 2], sg) * msl1[...]).astype(BF)
    spill = dot(w[1, 1], fg).astype(BF)
    mid_grad = (g.astype(F32) + dot(w[1, 0], fg) + dot_nt(spill, smid[...])).astype(BF)
    send_ref[...] = dot_nt(sel[...], mid_grad).astype(BF)
    gmid_ref[...] = g
    sg_ref[...] = sg
    fg_ref[...] = fg


def mid_wgrad_kernel(scale, hid, agg, mid, outer, g, sg, fg, out_ref):
    d = hid.shape[0]
    out_ref[0:d, :] = (dot_nt(hid[...], fg[...]) * scale).astype(BF)
    out_ref[d : 2 * d, :] = (dot_nt(agg[...], fg[...]) * scale).astype(BF)
    out_ref[2 * d : 3 * d, :] = (dot_nt(mid[...], sg[...]) * scale).astype(BF)
    out_ref[3 * d : 4 * d, :] = (dot_nt(outer[...], g[...]) * scale).astype(BF)


def fine_grad_kernel(
    tile_rows, scale,
    got, place, pool, w, hid, agg, mid, outer, slope1, slope2, cot, mid_wg,
    send_ref, g_ref, fg_ref,
    unpacked, blocks,
):
    rows = hid.shape[1]
    d = hid.shape[0]
    block_rows = pool.shape[0]
    unpacked[...] = got[...].astype(F32)
    for t in range(rows // tile_rows):
        at = pl.ds(pl.multiple_of(place[t] * block_rows, 8), block_rows)
        blocks[t * block_rows : (t + 1) * block_rows, :] = unpacked[at, :]
    per = TILE // tile_rows * block_rows
    grads = [jnp.zeros((d, d), F32) for _ in range(4)]
    for i in range(rows // TILE):
        cols = slice(i * TILE, (i + 1) * TILE)
        back = dot_tn(
            blocks[i * per : (i + 1) * per, :].astype(BF), pool_matrix(pool[:, cols], tile_rows)
        )
        g = (cot[:, cols].astype(F32) + back).astype(BF)
        sg = (dot(w[0, 3], g) * slope2[:, cols]).astype(BF)
        fg = (dot(w[0, 2], sg) * slope1[:, cols]).astype(BF)
        g_ref[:, cols] = g
        fg_ref[:, cols] = fg
        grads = [
            grads[0] + dot_nt(hid[:, cols], fg),
            grads[1] + dot_nt(agg[:, cols], fg),
            grads[2] + dot_nt(mid[:, cols], sg),
            grads[3] + dot_nt(outer[:, cols], g),
        ]
    for m in range(4):
        send_ref[m * d : (m + 1) * d, :] = (grads[m] * scale).astype(BF)
    send_ref[4 * d : 8 * d, :] = mid_wg[...]


def fine_spread_kernel(off, ew, w, g, fg, rim_l, rim_r, out_ref, s_ref, total):
    rows = g.shape[1]
    clear_corners(s_ref.at[0])
    clear_corners(s_ref.at[1])
    total[...] = jnp.zeros(total.shape, F32)
    for i in range(rows // TILE):
        cols = slice(i * TILE, (i + 1) * TILE)
        s = s_ref.at[i % 2]
        fine_edges(off[:, cols], ew[:, cols], s)
        fg_tile = fg[:, cols]
        direct = g[:, cols].astype(F32) + dot(w[0, 0], fg_tile)
        spill = dot(w[0, 1], fg_tile).astype(BF)
        window = slice(i * TILE, (i + 1) * TILE + 2 * HALO)
        total[window, :] = total[window, :] + dot_nt(s[...], spill)
        here = slice(HALO + i * TILE, HALO + (i + 1) * TILE)
        total[here, :] = total[here, :] + jnp.transpose(direct)
    rim_l[...] = total[:HALO, :].astype(BF)
    rim_r[...] = total[HALO + rows :, :].astype(BF)
    out_ref[...] = total[HALO : HALO + rows, :]


def join_kernel(total, from_left, from_right, out_ref):
    rows = total.shape[0]
    out_ref[:HALO, :] = (total[:HALO, :] + from_left[...].astype(F32)).astype(BF)
    out_ref[HALO : rows - HALO, :] = total[HALO : rows - HALO, :].astype(BF)
    out_ref[rows - HALO :, :] = (total[rows - HALO :, :] + from_right[...].astype(F32)).astype(BF)


def call(kernel, outs, args, in_specs=None, out_specs=None, scratch=(), us=3, mib=24):
    return pl.pallas_call(
        kernel,
        out_shape=outs,
        in_specs=in_specs or [VM] * len(args),
        out_specs=out_specs or jax.tree.map(lambda _: VM, outs),
        scratch_shapes=list(scratch),
        compiler_params=pltpu.CompilerParams(vmem_limit_bytes=mib << 20),
        cost_estimate=pl.CostEstimate(
            flops=0, bytes_accessed=int(us * 3_000_000), transcendentals=0
        ),
    )(*args)


def shape(dims, dtype=BF):
    return jax.ShapeDtypeStruct(dims, dtype)


def exchange(x):
    return lax.all_to_all(x, "nodes", split_axis=0, concat_axis=0, tiled=True)


def per_device(
    features,
    fine_cotangent,
    mid_cotangent,
    coarse_cotangent,
    weights,
    fine_offsets,
    fine_edge_w,
    pool_fine,
    owner_dev,
    coarse_slot,
    mid_nbrs,
    mid_edge_w,
    pool_mid,
    coarse_nbrs,
    coarse_edge_w,
):
    n, d = features.shape
    tile_count = owner_dev.shape[0]
    tile_rows = n // tile_count
    block_rows = pool_fine.shape[0]
    n1 = mid_cotangent.shape[0]
    n2 = coarse_cotangent.shape[0]
    edges = fine_offsets.shape[0]
    peers = lax.axis_size("nodes")
    cap = max(2, 2 * tile_count // peers)
    chunk = cap * block_rows
    window = TILE + 2 * HALO
    ends = peers - 1
    up = [(i, i + 1) for i in range(ends)]
    down = [(i + 1, i) for i in range(ends)]

    left = lax.ppermute(features[n - HALO :], "nodes", up)
    right = lax.ppermute(features[:HALO], "nodes", down)
    agg_in, blocks_in = call(
        functools.partial(inner_kernel, tile_rows),
        (shape((d, n)), shape((tile_count * block_rows, d), F32)),
        (features, fine_offsets, fine_edge_w, weights, pool_fine),
        in_specs=[ANY] * 5,
        scratch=(
            pltpu.VMEM((n, d), BF),
            pltpu.VMEM((edges, n), jnp.int32),
            pltpu.VMEM((edges, n), F32),
            pltpu.VMEM((4, d, d), BF),
            pltpu.VMEM((block_rows, n), BF),
            pltpu.VMEM((d, n), BF),
            pltpu.VMEM((2, window, TILE), BF),
            pltpu.SemaphoreType.DMA((5,)),
        ),
        us=6,
    )
    rows1 = chunk + n2 + 16
    agg_out, send1, place = call(
        functools.partial(outer_kernel, tile_rows, peers, cap),
        (shape((d, 2 * TILE)), shape((peers, rows1, d)), shape((tile_count,), jnp.int32)),
        (
            left, right, features, fine_offsets, fine_edge_w, weights, pool_fine, blocks_in,
            owner_dev.reshape(-1), coarse_slot, coarse_cotangent, coarse_nbrs, coarse_edge_w,
        ),
        in_specs=[VM] * 8 + [SM] * 2 + [VM] * 3,
        out_specs=(VM, VM, SM),
        scratch=(
            pltpu.VMEM((2, window, TILE), BF),
            pltpu.VMEM((peers * chunk, d), F32),
            pltpu.VMEM((peers, 128), F32),
            pltpu.VMEM((8, 128), F32),
            pltpu.SMEM((peers,), jnp.int32),
        ),
        us=3,
    )
    got1 = exchange(send1)
    hid, agg, mid, outer, slope1, slope2, cot, smid, mcot = call(
        saved_kernel,
        (
            shape((d, n)), shape((d, n)), shape((d, n)), shape((d, n)),
            shape((d, n), F32), shape((d, n), F32), shape((d, n)),
            shape((n1, n1)), shape((d, n1)),
        ),
        (
            features, agg_in, agg_out, weights, fine_cotangent, mid_nbrs, mid_edge_w,
            mid_cotangent,
        ),
        us=5,
    )
    send2, mhid, magg, mmid, mouter, mslope1, mslope2, sel = call(
        functools.partial(mid_kernel, peers, cap, block_rows),
        (
            shape((peers * n2, d)), shape((d, n1)), shape((d, n1)), shape((d, n1)),
            shape((d, n1)), shape((d, n1), F32), shape((d, n1), F32),
            shape((peers * chunk, n1)),
        ),
        (got1, smid, weights, pool_mid),
        scratch=(pltpu.VMEM((peers * chunk, d), BF),),
        us=3,
    )
    got2 = exchange(send2)
    extra = got1[:, chunk + n2 : chunk + n2 + edges, : 4 * n2].astype(F32)
    extra = extra.reshape(peers, edges, 4, n2).transpose(2, 1, 0, 3).reshape(4, edges, peers * n2)
    all_nbrs = (extra[0] * 256.0 + extra[1]).astype(jnp.int32)
    all_ew = extra[2] + extra[3]
    all_cot = got1[:, chunk : chunk + n2].reshape(peers * n2, d)
    total2 = peers * n2
    sco, cot_all = call(
        coarse_edges_kernel,
        (shape((total2, total2)), shape((d, total2))),
        (all_nbrs, all_ew, all_cot),
        us=2,
    )
    send3, coarse_wg, gmid, msg, mfg = call(
        functools.partial(coarse_kernel, peers),
        (
            shape((peers * chunk, d)), shape((4, d, d), F32), shape((d, n1)), shape((d, n1)),
            shape((d, n1)),
        ),
        (
            got2, sco, cot_all, weights, coarse_cotangent, pool_mid, mcot, mhid, magg, mmid,
            mouter, mslope1, mslope2, smid, sel,
        ),
        us=3,
    )
    got3 = exchange(send3)
    mid_wg = call(
        functools.partial(mid_wgrad_kernel, 1.0 / math.sqrt(n1 * peers)),
        shape((4 * d, d)),
        (mhid, magg, mmid, mouter, gmid, msg, mfg),
        us=2,
    )
    send4, g, fg = call(
        functools.partial(fine_grad_kernel, tile_rows, 1.0 / math.sqrt(n * peers)),
        (shape((8 * d, d)), shape((d, n)), shape((d, n))),
        (
            got3, place, pool_fine, weights, hid, agg, mid, outer, slope1, slope2, cot, mid_wg,
        ),
        in_specs=[VM, SM] + [VM] * 10,
        scratch=(
            pltpu.VMEM((peers * chunk, d), F32),
            pltpu.VMEM((tile_count * block_rows, d), F32),
        ),
        us=4,
    )
    got4 = exchange(send4)
    rim_l, rim_r, spread = call(
        fine_spread_kernel,
        (shape((HALO, d)), shape((HALO, d)), shape((n, d), F32)),
        (fine_offsets, fine_edge_w, weights, g, fg),
        scratch=(pltpu.VMEM((2, window, TILE), BF), pltpu.VMEM((n + 2 * HALO, d), F32)),
        us=6,
    )
    from_left = lax.ppermute(rim_r, "nodes", up)
    from_right = lax.ppermute(rim_l, "nodes", down)
    part = got4.astype(F32).reshape(peers, 8 * d // peers, d).sum(axis=0).astype(BF)
    got5 = exchange(jnp.tile(part, (peers, 1)))
    feature_grads = call(
        join_kernel, shape((n, d)), (spread, from_left, from_right), us=1
    )
    weight_grads = jnp.concatenate(
        [got5.reshape(2, 4, d, d).astype(F32), coarse_wg[None]], axis=0
    )
    return (feature_grads, weight_grads)


def solution(mesh):
    rows = P(("groups", "nodes"), None)
    cols = P("groups", "nodes")
    in_specs = (
        rows, rows, rows, rows, P(), cols, cols, cols, rows, P(("groups", "nodes")),
        cols, cols, rows, cols, cols,
    )
    out_specs = (rows, P("groups", None, None, None))
    return jax.shard_map(
        per_device, mesh=mesh, in_specs=in_specs, out_specs=out_specs, check_vma=False
    )
```

time: 513 us -> 125 us (0.24); the launches traced: 503 us -> 124 us
  other arithmetic: 179 us -> 2.62 us
  waiting for transfers between devices: 94.1 us -> 8.2 us
  blocking collectives: 79.5 us -> 12.9 us
  local copies, waits for them, and re-layouts: 82.8 us -> 41.7 us
  matrix products: 26.1 us -> 0 us
  Pallas kernels: 0 us -> 25 us
  between operations: 16.4 us -> 1 us
  starting transfers between devices: 24.8 us -> 32.3 us
    scatter-add x26 -> x0, other arithmetic: 155 us -> none  [the longest x24 153 us: spread_rows(): summed.at[neighbour_index[neighbour]]]
    psum x1 -> x0, waiting for transfers between devices: 84.7 us -> none  [per_device(): fine_summed, mid_summed = lax.psum((fine_wgrad, mid_wgrad), 'nodes')]
    all_gather x4 -> x0, blocking collectives: 79.5 us -> none  [the longest x1 21.9 us: per_device(): lax.all_gather(coarse_edge_w, 'nodes', axis=1, tiled=True)]
    gather x24 -> x0, local copies, waits for them, and re-layouts: 75.6 us -> none  [gather_rows(): picked = source[neighbour_index[neighbour]].astype(jnp.float32)]
    unnamed x181 -> x128, local copies, waits for them, and re-layouts: 1.92 us -> 36 us
    dot_general x42 -> x0, matrix products: 26.1 us -> none  [the longest x3 3.15 us: node_forward(): jnp.dot(middle, level_weights[2], preferred_element_type=jnp.float32)]
    pallas_call x0 -> x10, Pallas kernels: none -> 25 us  [call(): pl.pallas_call(kernel, out_shape=outs, in_specs=in_specs or [VM] * len(ar...]
    all_to_all x0 -> x1, blocking collectives: none -> 12.9 us  [exchange(): return lax.all_to_all(x, 'nodes', split_axis=0, concat_axis=0, tiled=True)]
  transfers between devices with their start and end apart: 8 -> 8, of which waited for: 3 -> 4; matrix products, arithmetic and copies ran while one was open for 18% -> 4% of each run, Pallas kernels for 0% -> 9%
where the time goes in v1:
time: 125 us; the launch traced here: 124 us
  local copies, waits for them, and re-layouts  41.7 us (33%)
  starting transfers between devices  32.3 us (26%)
  Pallas kernels  25 us (20%)
  blocking collectives  12.9 us (10%)
  waiting for transfers between devices  8.2 us (7%)
  other arithmetic  2.62 us (2%)
    unnamed x128, local copies, waits for them, and re-layouts  36 us
    pallas_call x10, Pallas kernels, call(): pl.pallas_call(kernel, out_shape=outs, in_specs=in_specs or [VM] * len(ar...  25 us
    all_to_all x4, starting transfers between devices, exchange(): return lax.all_to_all(x, 'nodes', split_axis=0, concat_axis=0, tiled=True)  20.4 us
    all_to_all x1, blocking collectives, exchange(): return lax.all_to_all(x, 'nodes', split_axis=0, concat_axis=0, tiled=True)  12.9 us
    all_to_all x4, waiting for transfers between devices, exchange(): return lax.all_to_all(x, 'nodes', split_axis=0, concat_axis=0, tiled=True)  4.55 us
    ppermute x1, starting transfers between devices, per_device(): left = lax.ppermute(features[n - HALO:], 'nodes', up)  4.49 us
    ppermute x1, waiting for transfers between devices, per_device(): from_right = lax.ppermute(rim_l, 'nodes', down)  3.65 us
    ppermute x1, starting transfers between devices, per_device(): from_left = lax.ppermute(rim_r, 'nodes', up)  3.55 us
  transfers between devices with their start and end apart: 8, of which 4 were waited for; matrix products, arithmetic and copies ran while one was open for 4% of the time, Pallas kernels for 9%

profile of v1, /device:TPU:1, one launch (start us, length us, event | category | flops | bytes accessed | tf_op | source)
XLA Modules:
  0.0 123.7 jit_solution(4500953599948630801)
XLA Ops:
  1.6 2.0 %collective-permute-start.1 = (bf16[256,128]{1,0:T(8,128)(2,1)S(1)}, bf16[256,128]{1,0:T(8,128)(2,1)S(1)}, u32[]{:S(2)}, u32[]{:S(2)}) collective-permute-start(bf16[256,128]{1,0:T(8,128)(2,1)S(1)} %get-tuple-element.72), channel_id=1, source_target_pairs={{1,0},{2,1},{3,2},{4,3},{5,4},{6,5},{7,6},{8,7},{9,8},{10,9},{11,1... | collective-permute-start | bytes 196616 | tf_op jit(solution)/shard_map/ppermute | solution.py:500
  3.6 4.5 %collective-permute-start = (bf16[256,128]{1,0:T(8,128)(2,1)S(1)}, bf16[256,128]{1,0:T(8,128)(2,1)S(1)}, u32[]{:S(2)}, u32[]{:S(2)}) collective-permute-start(bf16[256,128]{1,0:T(8,128)(2,1)S(1)} %get-tuple-element.73), channel_id=1, source_target_pairs={{0,1},{1,2},{2,3},{3,4},{4,5},{5,6},{6,7},{7,8},{8,9},{9,10},{10,1... | collective-permute-start | bytes 196616 | tf_op jit(solution)/shard_map/ppermute | solution.py:499
  9.1 1.0 copy-done.2
  10.1 5.3 %shard_map.158 = (bf16[128,2048]{1,0:T(8,128)(2,1)S(1)}, f32[512,128]{1,0:T(8,128)S(1)}) custom-call(bf16[2048,128]{1,0:T(8,128)(2,1)S(1)} %copy-done.2, s32[8,2048]{1,0:T(8,128)S(1)} %copy-done.8, f32[8,2048]{1,0:T(8,128)S(1)} %copy-done.9, bf16[3,4,128,128]{3,2,1,0:T(8,128)(2,1)S(1)} %copy-done, bf16[8,2048]{1,0:T(8,128)(2,1)S(1)} %copy-done.35), custom_call_target="tpu_custom_call" | custom-call | bytes 18000000 | tf_op jit(solution)/shard_map/pallas_call | solution.py:446
  16.9 3.2 %shard_map.159 = (bf16[128,512]{1,0:T(8,128)(2,1)S(1)}, bf16[16,96,128]{2,1,0:T(8,128)(2,1)}, s32[64]{0:T(128)S(1)}) custom-call(bf16[256,128]{1,0:T(8,128)(2,1)S(1)} %collective-permute-done.left, bf16[256,128]{1,0:T(8,128)(2,1)S(1)} %collective-permute-done.1.right, bf16[2048,128]{1,0:T(8,128)(2,1)S(1)} %copy-done.2, s32[8,2048]{1,0:T(8,128)S(1)} %copy-done.8, ...), custom_call_target="tpu_custom_call" | custom-call | bytes 9000000 | tf_op jit(solution)/shard_map/pallas_call | solution.py:446
  21.3 5.9 %all-to-all-start = ((bf16[16,96,128]{2,1,0:T(8,128)(2,1)}), bf16[16,96,128]{2,1,0:T(8,128)(2,1)S(1)}, u32[]{:S(2)}, u32[]{:S(2)}) async-start(bf16[16,96,128]{2,1,0:T(8,128)(2,1)} %get-tuple-element.38), calls=%async_computation | async-start | bytes 786432 | tf_op jit(solution)/shard_map/all_to_all | solution.py:464
  30.8 1.6 %shard_map.160 = (bf16[128,2048]{1,0:T(8,128)(2,1)S(1)}, bf16[128,2048]{1,0:T(8,128)(2,1)S(1)}, bf16[128,2048]{1,0:T(8,128)(2,1)S(1)}, bf16[128,2048]{1,0:T(8,12...) custom-call(bf16[2048,128]{1,0:T(8,128)(2,1)S(1)} %copy-done.3, ...), custom_call_target="tpu_custom_call" | custom-call | bytes 15000000 | tf_op jit(solution)/shard_map/pallas_call | solution.py:446
  38.0 1.1 all-to-all-done.got
  40.2 1.5 %shard_map.161 = (bf16[256,128]{1,0:T(8,128)(2,1)S(1)}, bf16[128,512]{1,0:T(8,128)(2,1)S(1)}, bf16[128,512]{1,0:T(8,128)(2,1)S(1)}, bf16[128,512]{1,0:T(8,128)(2...) custom-call(bf16[16,96,128]{2,1,0:T(8,128)(2,1)S(1)} %all-to-all-don, ...), custom_call_target="tpu_custom_call" | custom-call | bytes 9000000 | tf_op jit(solution)/shard_map/pallas_call | solution.py:446
  43.3 4.9 %all-to-all-start.1 = ((bf16[16,16,128]{2,1,0:T(8,128)(2,1)}), bf16[16,16,128]{2,1,0:T(8,128)(2,1)}, u32[]{:S(2)}, u32[]{:S(2)}) async-start(bf16[16,16,128]{2,1,0:T(8,128)(2,1)} %bitcast.21), calls=%async_computation.1 | async-start | bytes 131072 | tf_op jit(solution)/shard_map/all_to_all | solution.py:464
  48.3 1.6 %slice_add_fusion = (f32[1,8,16,16]{3,2,1,0:T(8,128)}, s32[1,8,16,16]{3,2,1,0:T(8,128)}) fusion(f32[4,8,16,16]{3,2,1,0:T(8,128)} %bitcast.24), kind=kLoop, calls=%fused_computation.2 | loop fusion | flops 8192 | bytes 49152 | tf_op jit(solution)/shard_map/add | solution.py:566
  49.9 1.5 %add.11.ew = f32[8,256]{1,0:T(8,128)} reshape(f32[1,8,16,16]{3,2,1,0:T(8,128)} %get-tuple-element.74) | data formatting | bytes 16384 | tf_op jit(solution)/shard_map/add | solution.py:566
  51.4 1.5 %convert_element_type.20.nbrs = s32[8,256]{1,0:T(8,128)} reshape(s32[1,8,16,16]{3,2,1,0:T(8,128)} %get-tuple-element.75) | data formatting | bytes 16384 | tf_op jit(solution)/shard_map/convert_element_type | solution.py:565
  55.1 1.2 copy-done.7
  57.2 3.9 %shard_map.163 = (bf16[1024,128]{1,0:T(8,128)(2,1)}, f32[4,128,128]{2,1,0:T(8,128)S(1)}, bf16[128,512]{1,0:T(8,128)(2,1)S(1)}, bf16[128,512]{1,0:T(8,128)(2,1)S(1)}, bf16[128,512]{1,0:T(8,128)(2,1)S(1)}) custom-call(bf16[256,128]{1,0:T(8,128)(2,1)} %bitcast.2.got, bf16[256,256]{1,0:T(8,128)(2,1)S(1)} %get-tuple-element.43.sco, ...), custom_call_target="tpu_custom_call" | custom-call | bytes 9000000 | tf_op jit(solution)/shard_map/pallas_call | solution.py:446
  63.8 5.5 %all-to-all-start.2 = ((bf16[16,64,128]{2,1,0:T(8,128)(2,1)}), bf16[16,64,128]{2,1,0:T(8,128)(2,1)S(1)}, u32[]{:S(2)}, u32[]{:S(2)}) async-start(bf16[16,64,128]{2,1,0:T(8,128)(2,1)} %bitcast.5), calls=%async_computation.2 | async-start | bytes 524288 | tf_op jit(solution)/shard_map/all_to_all | solution.py:464
  76.0 2.9 %all-to-all-done.2 = bf16[16,64,128]{2,1,0:T(8,128)(2,1)S(1)} async-done(((bf16[16,64,128]{2,1,0:T(8,128)(2,1)}), bf16[16,64,128]{2,1,0:T(8,128)(2,1)S(1)}, u32[]{:S(2)}, u32[]{:S(2)}) %all-to-all-start.2) | async-done | bytes 262176 | tf_op jit(solution)/shard_map/all_to_all | solution.py:464
  84.4 4.7 %shard_map.165 = (bf16[1024,128]{1,0:T(8,128)(2,1)S(1)}, bf16[128,2048]{1,0:T(8,128)(2,1)S(1)}, bf16[128,2048]{1,0:T(8,128)(2,1)S(1)}) custom-call(bf16[1024,128]{1,0:T(8,128)(2,1)S(1)} %bitcast.17, s32[64]{0:T(128)S(1)} %copy-done.63, bf16[8,2048]{1,0:T(8,128)(2,1)S(1)} %copy-done.36, bf16[3,4,128,128]{3,2,1,0:T(8,128)(2,1)S(1)} %copy-done.1, ...), custom_call_target="tpu_custom_call" | custom-call | bytes 12000000 | tf_op jit(solution)/shard_map/pallas_call | solution.py:446
  90.7 12.9 %all_to_all.42 = bf16[16,64,128]{2,1,0:T(8,128)(2,1)S(1)} all-to-all(bf16[16,64,128]{2,1,0:T(8,128)(2,1)S(1)} %bitcast.19), channel_id=1, replica_groups=mesh['groups'=2,'nodes'=16] {'nodes'}, dimensions={0} | all-to-all | bytes 524288 | tf_op jit(solution)/shard_map/all_to_all | solution.py:464
  104.4 4.0 %all-to-all-start.4 = ((bf16[16,64,128]{2,1,0:T(8,128)(2,1)}), bf16[16,64,128]{2,1,0:T(8,128)(2,1)S(1)}, u32[]{:S(2)}, u32[]{:S(2)}) async-start(bf16[16,64,128]{2,1,0:T(8,128)(2,1)} %tile.2), calls=%async_computation.4 | async-start | bytes 524288 | tf_op jit(solution)/shard_map/all_to_all | solution.py:464
  108.4 3.4 %shard_map.166 = (bf16[256,128]{1,0:T(8,128)(2,1)S(1)}, bf16[256,128]{1,0:T(8,128)(2,1)S(1)}, f32[2048,128]{1,0:T(8,128)S(1)}) custom-call(s32[8,2048]{1,0:T(8,128)S(1)} %copy-done.8, f32[8,2048]{1,0:T(8,128)S(1)} %copy-done.9, bf16[3,4,128,128]{3,2,1,0:T(8,128)(2,1)S(1)} %copy-done.1, bf16[128,2048]{1,0:T(8,128)(2,1)S(1)} %copy-done.24, ...), custom_call_target="tpu_custom_call" | custom-call | bytes 18000000 | tf_op jit(solution)/shard_map/pallas_call | solution.py:446
  111.8 3.5 %collective-permute-start.2 = (bf16[256,128]{1,0:T(8,128)(2,1)S(1)}, bf16[256,128]{1,0:T(8,128)(2,1)S(1)}, u32[]{:S(2)}, u32[]{:S(2)}) collective-permute-start(bf16[256,128]{1,0:T(8,128)(2,1)S(1)} %get-tuple-element.68), channel_id=1, source_target_pairs={{0,1},{1,2},{2,3},{3,4},{4,5},{5,6},{6,7},{7,8},{8,9},{9,10},{10,1... | collective-permute-start | bytes 196616 | tf_op jit(solution)/shard_map/ppermute | solution.py:615
  115.3 1.9 %collective-permute-start.3 = (bf16[256,128]{1,0:T(8,128)(2,1)S(1)}, bf16[256,128]{1,0:T(8,128)(2,1)S(1)}, u32[]{:S(2)}, u32[]{:S(2)}) collective-permute-start(bf16[256,128]{1,0:T(8,128)(2,1)S(1)} %get-tuple-element.69), channel_id=1, source_target_pairs={{1,0},{2,1},{3,2},{4,3},{5,4},{6,5},{7,6},{8,7},{9,8},{10,9},{11,1... | collective-permute-start | bytes 196616 | tf_op jit(solution)/shard_map/ppermute | solution.py:616
  117.3 3.6 %collective-permute-done.3.from_right = bf16[256,128]{1,0:T(8,128)(2,1)S(1)} collective-permute-done((bf16[256,128]{1,0:T(8,128)(2,1)S(1)}, bf16[256,128]{1,0:T(8,128)(2,1)S(1)}, u32[]{:S(2)}, u32[]{:S(2)}) %collective-permute-start.3) | collective-permute-done | bytes 65568 | tf_op jit(solution)/shard_map/ppermute | solution.py:616
  (143 shorter events, 39.4 us)
Async XLA Ops:
  0.6 7.4 %copy-start.35 = (bf16[8,2048]{1,0:T(8,128)(2,1)S(1)}, bf16[8,2048]{1,0:T(8,128)(2,1)}, u32[]{:S(2)}) copy-start(bf16[8,2048]{1,0:T(8,128)(2,1)} %pool.3) | copy-start | bytes 98308
  0.6 7.4 %copy-start.9 = (f32[8,2048]{1,0:T(8,128)S(1)}, f32[8,2048]{1,0:T(8,128)}, u32[]{:S(2)}) copy-start(f32[8,2048]{1,0:T(8,128)} %ew.3) | copy-start | bytes 196612
  0.7 7.4 %copy-start.8 = (s32[8,2048]{1,0:T(8,128)S(1)}, s32[8,2048]{1,0:T(8,128)}, u32[]{:S(2)}) copy-start(s32[8,2048]{1,0:T(8,128)} %off.3) | copy-start | bytes 196612
  1.6 14.7 %collective-permute-start.1 = (bf16[256,128]{1,0:T(8,128)(2,1)S(1)}, bf16[256,128]{1,0:T(8,128)(2,1)S(1)}, u32[]{:S(2)}, u32[]{:S(2)}) collective-permute-start(bf16[256,128]{1,0:T(8,128)(2,1)S(1)} %get-tuple-element.72), channel_id=1, source_target_pairs={{1,0},{2,1},{3,2},{4,3},{5,4},{6,5},{7,6},{8,7},{9,8},{10,9},{11,1... | collective-permute-start | bytes 196616 | tf_op jit(solution)/shard_map/ppermute | solution.py:500
  3.6 12.7 %collective-permute-start = (bf16[256,128]{1,0:T(8,128)(2,1)S(1)}, bf16[256,128]{1,0:T(8,128)(2,1)S(1)}, u32[]{:S(2)}, u32[]{:S(2)}) collective-permute-start(bf16[256,128]{1,0:T(8,128)(2,1)S(1)} %get-tuple-element.73), channel_id=1, source_target_pairs={{0,1},{1,2},{2,3},{3,4},{4,5},{5,6},{6,7},{7,8},{8,9},{9,10},{10,1... | collective-permute-start | bytes 196616 | tf_op jit(solution)/shard_map/ppermute | solution.py:499
  10.1 6.2 %copy-start.56 = (bf16[16,128]{1,0:T(8,128)(2,1)S(1)}, bf16[16,128]{1,0:T(8,128)(2,1)}, u32[]{:S(2)}) copy-start(bf16[16,128]{1,0:T(8,128)(2,1)} %cot_my.1) | copy-start | bytes 12292
  10.1 6.2 %copy-start.58 = (s32[8,16]{1,0:T(8,128)S(1)}, s32[8,16]{1,0:T(8,128)}, u32[]{:S(2)}) copy-start(s32[8,16]{1,0:T(8,128)} %nbrs.1) | copy-start | bytes 1540
  10.1 6.2 %copy-start.59 = (f32[8,16]{1,0:T(8,128)S(1)}, f32[8,16]{1,0:T(8,128)}, u32[]{:S(2)}) copy-start(f32[8,16]{1,0:T(8,128)} %cew.1) | copy-start | bytes 1540
  16.9 10.3 %copy-start.3 = (bf16[2048,128]{1,0:T(8,128)(2,1)S(1)}, bf16[2048,128]{1,0:T(8,128)(2,1)}, u32[]{:S(2)}) copy-start(bf16[2048,128]{1,0:T(8,128)(2,1)} %feat.3) | copy-start | bytes 1572868
  16.9 10.3 %copy-start.10 = (bf16[2048,128]{1,0:T(8,128)(2,1)S(1)}, bf16[2048,128]{1,0:T(8,128)(2,1)}, u32[]{:S(2)}) copy-start(bf16[2048,128]{1,0:T(8,128)(2,1)} %fine_cot.1) | copy-start | bytes 1572868
  21.3 5.9 %copy-start.1 = (bf16[3,4,128,128]{3,2,1,0:T(8,128)(2,1)S(1)}, bf16[3,4,128,128]{3,2,1,0:T(8,128)(2,1)}, u32[]{:S(2)}) copy-start(bf16[3,4,128,128]{3,2,1,0:T(8,128)(2,1)} %w.11) | copy-start | bytes 1179652
  21.3 5.9 %copy-start.54 = (s32[8,512]{1,0:T(8,128)S(1)}, s32[8,512]{1,0:T(8,128)}, u32[]{:S(2)}) copy-start(s32[8,512]{1,0:T(8,128)} %mid_nbrs.1) | copy-start | bytes 49156
  21.3 17.8 %all-to-all-start = ((bf16[16,96,128]{2,1,0:T(8,128)(2,1)}), bf16[16,96,128]{2,1,0:T(8,128)(2,1)S(1)}, u32[]{:S(2)}, u32[]{:S(2)}) async-start(bf16[16,96,128]{2,1,0:T(8,128)(2,1)} %get-tuple-element.38), calls=%async_computation | async-start | bytes 786432 | tf_op jit(solution)/shard_map/all_to_all | solution.py:464
  43.3 11.1 %copy-start.27 = (bf16[128,512]{1,0:T(8,128)(2,1)}, bf16[128,512]{1,0:T(8,128)(2,1)S(1)}, u32[]{:S(2)}) copy-start(bf16[128,512]{1,0:T(8,128)(2,1)S(1)} %get-tuple-element.46.mhid.hid) | copy-start | bytes 393220
  43.3 11.1 %copy-start.29 = (bf16[128,512]{1,0:T(8,128)(2,1)}, bf16[128,512]{1,0:T(8,128)(2,1)S(1)}, u32[]{:S(2)}) copy-start(bf16[128,512]{1,0:T(8,128)(2,1)S(1)} %get-tuple-element.47.magg.agg) | copy-start | bytes 393220
  43.3 11.1 %copy-start.31 = (bf16[128,512]{1,0:T(8,128)(2,1)}, bf16[128,512]{1,0:T(8,128)(2,1)S(1)}, u32[]{:S(2)}) copy-start(bf16[128,512]{1,0:T(8,128)(2,1)S(1)} %get-tuple-element.48.mmid.mid) | copy-start | bytes 393220
  43.3 11.1 %copy-start.33 = (bf16[128,512]{1,0:T(8,128)(2,1)}, bf16[128,512]{1,0:T(8,128)(2,1)S(1)}, u32[]{:S(2)}) copy-start(bf16[128,512]{1,0:T(8,128)(2,1)S(1)} %get-tuple-element.49.mouter.outer) | copy-start | bytes 393220
  43.3 11.1 %all-to-all-start.1 = ((bf16[16,16,128]{2,1,0:T(8,128)(2,1)}), bf16[16,16,128]{2,1,0:T(8,128)(2,1)}, u32[]{:S(2)}, u32[]{:S(2)}) async-start(bf16[16,16,128]{2,1,0:T(8,128)(2,1)} %bitcast.21), calls=%async_computation.1 | async-start | bytes 131072 | tf_op jit(solution)/shard_map/all_to_all | solution.py:464
  63.8 15.1 %copy-start.5 = (f32[128,2048]{1,0:T(8,128)S(1)}, f32[128,2048]{1,0:T(8,128)}, u32[]{:S(2)}) copy-start(f32[128,2048]{1,0:T(8,128)} %copy-done.4) | copy-start | bytes 3145732
  63.8 15.0 %all-to-all-start.2 = ((bf16[16,64,128]{2,1,0:T(8,128)(2,1)}), bf16[16,64,128]{2,1,0:T(8,128)(2,1)S(1)}, u32[]{:S(2)}, u32[]{:S(2)}) async-start(bf16[16,64,128]{2,1,0:T(8,128)(2,1)} %bitcast.5), calls=%async_computation.2 | async-start | bytes 524288 | tf_op jit(solution)/shard_map/all_to_all | solution.py:464
  103.6 4.8 %copy-start.26 = (bf16[128,2048]{1,0:T(8,128)(2,1)S(1)}, bf16[128,2048]{1,0:T(8,128)(2,1)}, u32[]{:S(2)}) copy-start(bf16[128,2048]{1,0:T(8,128)(2,1)} %copy-done.25) | copy-start | bytes 1572868
  104.4 17.4 %all-to-all-start.4 = ((bf16[16,64,128]{2,1,0:T(8,128)(2,1)}), bf16[16,64,128]{2,1,0:T(8,128)(2,1)S(1)}, u32[]{:S(2)}, u32[]{:S(2)}) async-start(bf16[16,64,128]{2,1,0:T(8,128)(2,1)} %tile.2), calls=%async_computation.4 | async-start | bytes 524288 | tf_op jit(solution)/shard_map/all_to_all | solution.py:464
  111.8 5.5 %collective-permute-start.2 = (bf16[256,128]{1,0:T(8,128)(2,1)S(1)}, bf16[256,128]{1,0:T(8,128)(2,1)S(1)}, u32[]{:S(2)}, u32[]{:S(2)}) collective-permute-start(bf16[256,128]{1,0:T(8,128)(2,1)S(1)} %get-tuple-element.68), channel_id=1, source_target_pairs={{0,1},{1,2},{2,3},{3,4},{4,5},{5,6},{6,7},{7,8},{8,9},{9,10},{10,1... | collective-permute-start | bytes 196616 | tf_op jit(solution)/shard_map/ppermute | solution.py:615
  115.3 5.6 %collective-permute-start.3 = (bf16[256,128]{1,0:T(8,128)(2,1)S(1)}, bf16[256,128]{1,0:T(8,128)(2,1)S(1)}, u32[]{:S(2)}, u32[]{:S(2)}) collective-permute-start(bf16[256,128]{1,0:T(8,128)(2,1)S(1)} %get-tuple-element.69), channel_id=1, source_target_pairs={{1,0},{2,1},{3,2},{4,3},{5,4},{6,5},{7,6},{8,7},{9,8},{10,9},{11,1... | collective-permute-start | bytes 196616 | tf_op jit(solution)/shard_map/ppermute | solution.py:616
  (48 other events, 46.3 us)

commit v2 on v1

v2 whole, which is shorter than its diff:
```python
import functools
import math

import jax
import jax.numpy as jnp
from jax import lax
from jax.experimental import pallas as pl
from jax.experimental.pallas import tpu as pltpu
from jax.sharding import PartitionSpec as P

HALO = 256
TILE = 256
BF = jnp.bfloat16
F32 = jnp.float32

VM = pl.BlockSpec(memory_space=pltpu.VMEM)
HB = pl.BlockSpec(memory_space=pltpu.HBM)
ANY = pl.BlockSpec(memory_space=pl.ANY)


def dot(a, b):
    return jnp.dot(a, b, preferred_element_type=F32)


def dot_nt(a, b):
    return lax.dot_general(a, b, (((1,), (1,)), ((), ())), preferred_element_type=F32)


def dot_tn(a, b):
    return lax.dot_general(a, b, (((0,), (0,)), ((), ())), preferred_element_type=F32)


def silu(v):
    return v / (1.0 + jnp.exp(-v))


def silu_slope(v):
    s = 1.0 / (1.0 + jnp.exp(-v))
    return s * (1.0 + v * (1.0 - s))


def merged_weights(idx, ew):
    total = ew
    for r in range(1, idx.shape[0]):
        total = total + jnp.where(pltpu.roll(idx, r, 0) == idx, pltpu.roll(ew, r, 0), 0.0)
    return total.astype(BF)


def edge_columns(idx, ew, start, rows):
    count = idx.shape[0]
    lanes = idx.shape[1]
    position = lax.broadcasted_iota(jnp.int32, (rows, lanes), 0) + start
    position = position.astype(jnp.int16)
    picked = jnp.zeros((rows, lanes), BF)
    for k in range(count):
        picked = jnp.where(idx[k : k + 1, :] == position, ew[k : k + 1, :], picked)
    return picked


def fine_edges(off, ew, s_ref):
    for h in range(TILE // 128):
        lane = slice(128 * h, 128 * (h + 1))
        o = off[:, lane]
        weight = merged_weights(o, ew[:, lane])
        rel = o + lax.broadcasted_iota(jnp.int32, o.shape, 1) + HALO
        rel = rel.astype(jnp.int16)
        for c in range(2 * HALO // 128 + 1):
            s_ref[128 * (h + c) : 128 * (h + c + 1), lane] = edge_columns(
                rel, weight, 128 * c, 128
            )


def clear_corners(s_ref):
    for h in range(TILE // 128):
        lane = slice(128 * h, 128 * (h + 1))
        if h > 0:
            s_ref[: 128 * h, lane] = jnp.zeros((128 * h, 128), BF)
        last = 128 * h + 2 * HALO + 128
        if last < TILE + 2 * HALO:
            s_ref[last:, lane] = jnp.zeros((TILE + 2 * HALO - last, 128), BF)


def forward_weights(w):
    w01 = jnp.concatenate([jnp.transpose(w[0]), jnp.transpose(w[1])], axis=1)
    return w01, jnp.transpose(w[2]), jnp.transpose(w[3])


def pool_matrix(pool, tile_rows):
    lane = lax.broadcasted_iota(jnp.int32, pool.shape, 1) // tile_rows
    values = pool.astype(F32)
    parts = [jnp.where(lane == r, values, 0.0) for r in range(pool.shape[1] // tile_rows)]
    return jnp.concatenate(parts, axis=0).astype(BF)


class Copies:
    def __init__(self, sems):
        self.sems = sems
        self.used = 0
        self.open = {}

    def start(self, source, target):
        copy = pltpu.make_async_copy(source, target, self.sems.at[self.used])
        self.used += 1
        copy.start()
        self.open[id(copy)] = copy
        return copy

    def wait(self, *copies):
        for copy in copies:
            if id(copy) in self.open:
                copy.wait()
                del self.open[id(copy)]

    def finish(self):
        self.wait(*list(self.open.values()))


def shape(dims, dtype=BF):
    return jax.ShapeDtypeStruct(dims, dtype)


def call(kernel, ins, outs, scratch=(), copies=0, us=3, mib=24):
    n_in, n_out = len(ins), len(outs)
    staged_in = [i for i, (_, kind) in enumerate(ins) if kind in "hs012"]
    staged_out = [i for i, (_, kind) in enumerate(outs) if kind in "hs"]
    spaces = {"h": pltpu.VMEM, "s": pltpu.SMEM}
    stage = []
    for i in staged_in:
        array, kind = ins[i]
        dims = array.shape[1:] if kind.isdigit() else array.shape
        stage.append(spaces.get(kind, pltpu.VMEM)(dims, array.dtype))
    stage += [spaces[outs[i][1]](outs[i][0].shape, outs[i][0].dtype) for i in staged_out]
    total = len(staged_in) + len(staged_out) + copies

    def body(*refs):
        in_refs, out_refs = list(refs[:n_in]), list(refs[n_in : n_in + n_out])
        rest = list(refs[n_in + n_out :])
        sems = rest.pop() if total else None
        stages, user = rest[: len(stage)], rest[len(stage) :]
        io = Copies(sems)
        pending = {}
        for i, ref in zip(staged_in, stages):
            kind = ins[i][1]
            source = in_refs[i].at[int(kind)] if kind.isdigit() else in_refs[i]
            pending[i] = io.start(source, ref)
            in_refs[i] = ref
        targets = {}
        for i, ref in zip(staged_out, stages[len(staged_in) :]):
            targets[i] = out_refs[i]
            out_refs[i] = ref

        def need(*which):
            io.wait(*[pending[i] for i in which or pending])

        def flush(*which):
            for i in which:
                io.start(out_refs[i], targets.pop(i))

        kernel(io, need, flush, in_refs, out_refs, *user)
        flush(*list(targets))
        io.finish()

    return pl.pallas_call(
        body,
        out_shape=[s for s, _ in outs],
        in_specs=[{"v": VM, "a": ANY}.get(kind, HB) for _, kind in ins],
        out_specs=[VM if kind == "v" else HB for _, kind in outs],
        scratch_shapes=stage
        + list(scratch)
        + ([pltpu.SemaphoreType.DMA((total,))] if total else []),
        compiler_params=pltpu.CompilerParams(vmem_limit_bytes=mib << 20),
        cost_estimate=pl.CostEstimate(
            flops=0, bytes_accessed=int(us * 3_000_000), transcendentals=0
        ),
    )(*[a for a, _ in ins])


def fine_tile(h_t, window_t, s, weights, pool):
    w01, w2t, w3t = weights
    agg = dot(window_t, s).astype(BF)
    first = dot(w01, jnp.concatenate([h_t, agg], axis=0))
    middle = silu(first).astype(BF)
    second = dot(w2t, middle)
    outer = silu(second).astype(BF)
    fine_out = (h_t.astype(F32) + dot(w3t, outer)).astype(BF)
    return agg, dot_nt(pool, fine_out)


def outer_tiles(tile_count, per):
    return list(range(per)) + list(range(tile_count - per, tile_count))


def inner_kernel(tile_rows, peers, cap, io, need, flush, ins, outs, feat_t, s_ref, ids, counts):
    off, ew, feat, w, pool, owner, slot, nbrs, cew, cot = ins
    so_ref, win_ref, w01_ref, w2t_ref, w3t_ref, po_ref, spread, ext_ref, agg_ref, place = outs
    rows, d = feat.shape
    block_rows = pool.shape[0]
    n2 = cot.shape[0]
    tiles = rows // TILE
    per = TILE // tile_rows
    tile_count = rows // tile_rows
    clear_corners(s_ref.at[0])
    clear_corners(s_ref.at[1])
    clear_corners(so_ref.at[0])
    clear_corners(so_ref.at[1])
    spread[...] = jnp.zeros(spread.shape, F32)
    ids[...] = jnp.full(ids.shape, -1.0, F32)
    for p in range(peers):
        counts[p] = 0
    need(5, 6)
    lane_slot = lax.broadcasted_iota(jnp.int32, (1, 128), 1) // block_rows
    first_tiles = outer_tiles(tile_count, per)
    for t in first_tiles + [t for t in range(tile_count) if t not in first_tiles]:
        o = owner[t]
        c = counts[o]
        counts[o] = c + 1
        place[t] = o * cap + c
        row = ids[pl.ds(o, 1), :]
        ids[pl.ds(o, 1), :] = jnp.where(lane_slot == c, slot[t].astype(F32), row)
    flush(9)
    need(0, 1)
    need(2)
    feat_t[...] = jnp.transpose(feat[...])
    need()
    weights = forward_weights(w)
    for i in range(1, tiles - 1):
        cols = slice(i * TILE, (i + 1) * TILE)
        s = s_ref.at[i % 2]
        fine_edges(off[:, cols], ew[:, cols], s)
        agg, blocks = fine_tile(
            feat_t[:, cols],
            feat_t[:, i * TILE - HALO : (i + 1) * TILE + HALO],
            s[...],
            weights,
            pool_matrix(pool[:, cols], tile_rows),
        )
        agg_ref[:, cols] = agg
        for j in range(per):
            at = pl.ds(pl.multiple_of(place[i * per + j] * block_rows, 8), block_rows)
            spread[at, :] = blocks[j * block_rows : (j + 1) * block_rows, :]
    for n, i in enumerate((0, tiles - 1)):
        cols = slice(i * TILE, (i + 1) * TILE)
        fine_edges(off[:, cols], ew[:, cols], so_ref.at[n])
        po_ref[n] = pool_matrix(pool[:, cols], tile_rows)
    win_ref[0] = feat_t[:, : TILE + HALO]
    win_ref[1] = feat_t[:, rows - TILE - HALO :]
    w01_ref[...], w2t_ref[...], w3t_ref[...] = weights
    nb = nbrs[...].astype(F32)
    high = jnp.floor(nb * (1.0 / 256.0))
    ce = cew[...]
    ce_high = ce.astype(BF).astype(F32)
    fields = [high, nb - high * 256.0, ce_high, ce - ce_high]
    fields.append(jnp.zeros((nb.shape[0], 128 - 4 * n2), F32))
    top = jnp.concatenate(fields, axis=1)
    sub = lax.broadcasted_iota(jnp.int32, (8, 128), 0)
    for p in range(peers):
        ext_ref[p, 0:n2, :] = cot[...]
        below = jnp.where(sub == 0, ids[p : p + 1, :], 0.0)
        ext_ref[p, n2 : n2 + 16, :] = jnp.concatenate([top, below], axis=0).astype(BF)


def outer_kernel(
    tile_rows, cap, block_rows, io, need, flush, ins, outs, agg_edge, spread, stage, counts
):
    left, right, s_in, win, w01, w2t, w3t, pool, spread_in, ext, agg_in, owner = ins
    send_ref, agg_ref = outs
    peers, chunk, d = stage.shape
    rows = agg_in.shape[1]
    per = TILE // tile_rows
    io.start(ext, send_ref.at[:, pl.ds(chunk, ext.shape[1]), :])
    inside = pl.ds(TILE, rows - 2 * TILE)
    io.start(agg_in.at[:, inside], agg_ref.at[:, inside])
    spread[...] = spread_in[...]
    for p in range(peers):
        counts[p] = 0
    weights = (w01[...], w2t[...], w3t[...])
    results = []
    for n in range(2):
        if n == 0:
            window_t = jnp.concatenate([jnp.transpose(left[...]), win[0]], axis=1)
        else:
            window_t = jnp.concatenate([win[1], jnp.transpose(right[...])], axis=1)
        agg, blocks = fine_tile(
            window_t[:, HALO : HALO + TILE], window_t, s_in[n], weights, pool[n]
        )
        agg_edge[:, n * TILE : (n + 1) * TILE] = agg
        results.append(blocks)
    io.start(agg_edge.at[:, pl.ds(0, TILE)], agg_ref.at[:, pl.ds(0, TILE)])
    io.start(agg_edge.at[:, pl.ds(TILE, TILE)], agg_ref.at[:, pl.ds(rows - TILE, TILE)])
    need()
    for j, t in enumerate(outer_tiles(rows // tile_rows, per)):
        o = owner[t]
        c = counts[o]
        counts[o] = c + 1
        at = pl.ds(pl.multiple_of((o * cap + c) * block_rows, 8), block_rows)
        blocks = results[j // per]
        spread[at, :] = blocks[j % per * block_rows : (j % per + 1) * block_rows, :]
    group = max(1, peers // 4)
    for p in range(peers):
        stage[p] = spread[p * chunk : (p + 1) * chunk, :].astype(BF)
        if p % group == group - 1:
            part = pl.ds(p + 1 - group, group)
            io.start(stage.at[part], send_ref.at[part, pl.ds(0, chunk), :])


def mid_edges(nbrs, ew, s_ref):
    nodes = nbrs.shape[1]
    for c in range(nodes // 128):
        lane = slice(128 * c, 128 * (c + 1))
        idx = nbrs[:, lane]
        weight = merged_weights(idx, ew[:, lane])
        idx = idx.astype(jnp.int16)
        for r in range(nodes // 128):
            s_ref[128 * r : 128 * (r + 1), lane] = edge_columns(idx, weight, 128 * r, 128)


def first_window_kernel(io, need, flush, ins, outs):
    nbrs, ew, w, pool_mid, _ = ins
    smid, w01_ref, w2t_ref, w3t_ref, pool_out = outs
    io.start(pool_mid, pool_out)
    need(0, 1)
    mid_edges(nbrs, ew, smid)
    need()
    w01_ref[...], w2t_ref[...], w3t_ref[...] = forward_weights(w)


def mid_kernel(block_rows, chunk, io, need, flush, ins, outs, blocks, coarse):
    got, smid, w01, w2t, w3t, pool_mid = ins
    send_ref, hid_ref, agg_ref, sel_ref, ext_ref = outs
    peers = got.shape[0]
    nodes = smid.shape[0]
    n2 = pool_mid.shape[0]
    io.start(got.at[:, pl.ds(chunk, n2 + 16), :], ext_ref)
    rows = [got[p, chunk + n2 : chunk + n2 + 16, :].astype(F32)[8:9, :] for p in range(peers)]
    keys = jnp.transpose(jnp.concatenate(rows, axis=0))
    keys = keys * block_rows
    keys = keys + (lax.broadcasted_iota(jnp.int32, keys.shape, 0) % block_rows).astype(F32)
    keys = keys.astype(jnp.int32)
    lane = lax.broadcasted_iota(jnp.int32, (chunk, nodes), 1)
    for p in range(peers):
        sel_ref[p * chunk : (p + 1) * chunk, :] = jnp.where(
            keys[0:chunk, p : p + 1] == lane, 1.0, 0.0
        ).astype(BF)
        blocks[p * chunk : (p + 1) * chunk, :] = got[p, 0:chunk, :]
    flush(3)
    hidden = dot_tn(blocks[...], sel_ref[...]).astype(BF)
    hid_ref[...] = hidden
    agg = dot(hidden, smid[...]).astype(BF)
    agg_ref[...] = agg
    flush(1, 2)
    middle = silu(dot(w01[...], jnp.concatenate([hidden, agg], axis=0))).astype(BF)
    outer = silu(dot(w2t[...], middle)).astype(BF)
    mid_out = (hidden.astype(F32) + dot(w3t[...], outer)).astype(BF)
    coarse[...] = dot_nt(pool_mid[...], mid_out).astype(BF)
    for p in range(peers):
        io.start(coarse, send_ref.at[p])


def second_window_kernel(io, need, flush, ins, outs, nb_ref, ew_ref):
    ext, hid, agg, mid_nbrs, mid_ew, mid_cot, sel_h, w_h, pool_h, cot_h, w1 = ins
    sco, cot_all, smid, mcot, sl1_ref, sl2_ref, sel, w12, pool_mid, cot_my = outs
    io.start(sel_h, sel)
    io.start(w_h.at[pl.ds(1, 2)], w12)
    io.start(pool_h, pool_mid)
    io.start(cot_h, cot_my)
    peers = ext.shape[0]
    n2 = cot_h.shape[0]
    nodes = peers * n2
    edges = mid_nbrs.shape[0]
    need()
    for p in range(peers):
        part = ext[p, n2 : n2 + 16, :].astype(F32)[0:edges, :]
        at = slice(p * n2, (p + 1) * n2)
        nb_ref[:, at] = (part[:, 0:n2] * 256.0 + part[:, n2 : 2 * n2]).astype(jnp.int32)
        ew_ref[:, at] = part[:, 2 * n2 : 3 * n2] + part[:, 3 * n2 : 4 * n2]
    cots = jnp.concatenate([ext[p, 0:n2, :] for p in range(peers)], axis=0)
    cot_all[...] = jnp.transpose(cots)
    mcot[...] = jnp.transpose(mid_cot[...])

    def column(c, _):
        lane = pl.ds(pl.multiple_of(c * 128, 128), 128)
        idx = nb_ref[:, lane]
        weight = merged_weights(idx, ew_ref[:, lane])
        idx = idx.astype(jnp.int16)
        for r in range(nodes // 128):
            sco[128 * r : 128 * (r + 1), lane] = edge_columns(idx, weight, 128 * r, 128)
        return 0

    lax.fori_loop(0, nodes // 128, column, 0)
    mid_edges(mid_nbrs, mid_ew, smid)
    w01, w2t, _ = forward_weights(w1)
    first = dot(w01, jnp.concatenate([hid[...], agg[...]], axis=0))
    s1 = 1.0 / (1.0 + jnp.exp(-first))
    second = dot(w2t, (first * s1).astype(BF))
    s2 = 1.0 / (1.0 + jnp.exp(-second))
    sl1_ref[...] = s1 * (1.0 + first * (1.0 - s1))
    sl2_ref[...] = s2 * (1.0 + second * (1.0 - s2))


def coarse_kernel(io, need, flush, ins, outs):
    got, sco, cot_all, smid, mcot, msl1, msl2, sel, w, pool_mid, cot_my = ins
    send_ref, gmid_ref, sg_ref, fg_ref, cwg_ref = outs
    nodes = got.shape[0]
    n2 = cot_my.shape[0]
    me = lax.axis_index("nodes")
    width = min(TILE, nodes)
    hidden = jnp.transpose(got[...])
    w01, w2t, _ = forward_weights(w.at[1])
    mine = pl.ds(pl.multiple_of(me * n2, 16), n2)
    spread = jnp.zeros((n2, 128), F32)
    fg_mine = jnp.zeros((n2, 128), F32)
    grads = [jnp.zeros((128, 128), F32) for _ in range(4)]
    row = lax.broadcasted_iota(jnp.int32, (n2, width), 0) + me * n2
    lane = lax.broadcasted_iota(jnp.int32, (n2, width), 1)
    for i in range(nodes // width):
        cols = slice(i * width, (i + 1) * width)
        h = hidden[:, cols]
        agg = dot(hidden, sco[:, cols]).astype(BF)
        first = dot(w01, jnp.concatenate([h, agg], axis=0))
        s1 = 1.0 / (1.0 + jnp.exp(-first))
        middle = (first * s1).astype(BF)
        second = dot(w2t, middle)
        s2 = 1.0 / (1.0 + jnp.exp(-second))
        outer = (second * s2).astype(BF)
        g = cot_all[:, cols]
        sg = (dot(w[1, 3], g) * (s2 * (1.0 + second * (1.0 - s2)))).astype(BF)
        fg = (dot(w[1, 2], sg) * (s1 * (1.0 + first * (1.0 - s1)))).astype(BF)
        spill = dot(w[1, 1], fg).astype(BF)
        spread = spread + dot_nt(sco[mine, cols], spill)
        here = jnp.where(lane + i * width == row, 1.0, 0.0).astype(BF)
        fg_mine = fg_mine + dot_nt(here, fg)
        grads = [
            grads[0] + dot_nt(h, fg),
            grads[1] + dot_nt(agg, fg),
            grads[2] + dot_nt(middle, sg),
            grads[3] + dot_nt(outer, g),
        ]
    scale = 1.0 / math.sqrt(nodes)
    for m in range(4):
        cwg_ref[m] = grads[m] * scale
    flush(4)
    direct = cot_my[...].astype(F32) + dot_nt(fg_mine.astype(BF), w[1, 0])
    coarse_grad = (direct + spread).astype(BF)
    back = dot_tn(coarse_grad, pool_mid[...])
    g = (mcot[...].astype(F32) + back).astype(BF)
    gmid_ref[...] = g
    sg = (dot(w[0, 3], g) * msl2[...]).astype(BF)
    sg_ref[...] = sg
    fg = (dot(w[0, 2], sg) * msl1[...]).astype(BF)
    fg_ref[...] = fg
    flush(1, 2, 3)
    spill = dot(w[0, 1], fg).astype(BF)
    mid_grad = (g.astype(F32) + dot(w[0, 0], fg) + dot_nt(spill, smid[...])).astype(BF)
    send_ref[...] = dot_nt(sel[...], mid_grad).astype(BF)


def third_window_kernel(tile_rows, mid_scale, io, need, flush, ins, outs):
    mhid, magg, gmid, msg, mfg, feat, fine_cot, w, pool, place, agg_h, w1 = ins
    wg_ref, hid_ref, agg, mid_ref, outer_ref, sl1_ref, sl2_ref, cot_ref, pick_ref, po_ref, w0 = outs
    d, rows = hid_ref.shape
    block_rows = pool.shape[0]
    per = TILE // tile_rows
    agg_copy = io.start(agg_h, agg)
    w_copy = io.start(w.at[0], w0)
    need()
    w01, w2t, _ = forward_weights(w1)
    middle = silu(dot(w01, jnp.concatenate([mhid[...], magg[...]], axis=0))).astype(BF)
    outer = silu(dot(w2t, middle)).astype(BF)
    wg_ref[0:d, :] = (dot_nt(mhid[...], mfg[...]) * mid_scale).astype(BF)
    wg_ref[d : 2 * d, :] = (dot_nt(magg[...], mfg[...]) * mid_scale).astype(BF)
    wg_ref[2 * d : 3 * d, :] = (dot_nt(middle, msg[...]) * mid_scale).astype(BF)
    wg_ref[3 * d : 4 * d, :] = (dot_nt(outer, gmid[...]) * mid_scale).astype(BF)
    hid_ref[...] = jnp.transpose(feat[...])
    cot_ref[...] = jnp.transpose(fine_cot[...])
    slots = pick_ref.shape[1]
    lane = lax.broadcasted_iota(jnp.int32, (block_rows, slots), 1)
    lane = lane - lax.broadcasted_iota(jnp.int32, (block_rows, slots), 0)
    for t in range(0, rows // tile_rows, 2):
        both = [jnp.where(lane == place[t + j] * block_rows, 1.0, 0.0) for j in range(2)]
        pick_ref[t * block_rows : (t + 2) * block_rows, :] = jnp.concatenate(
            both, axis=0
        ).astype(BF)
    io.wait(agg_copy, w_copy)
    w01, w2t, _ = forward_weights(w0)
    for i in range(rows // TILE):
        cols = slice(i * TILE, (i + 1) * TILE)
        first = dot(w01, jnp.concatenate([hid_ref[:, cols], agg[:, cols]], axis=0))
        s1 = 1.0 / (1.0 + jnp.exp(-first))
        middle = (first * s1).astype(BF)
        mid_ref[:, cols] = middle
        sl1_ref[:, cols] = s1 * (1.0 + first * (1.0 - s1))
        second = dot(w2t, middle)
        s2 = 1.0 / (1.0 + jnp.exp(-second))
        outer_ref[:, cols] = (second * s2).astype(BF)
        sl2_ref[:, cols] = s2 * (1.0 + second * (1.0 - s2))
        po_ref[i] = pool_matrix(pool[:, cols], tile_rows)


def fine_grad_kernel(scale, io, need, flush, ins, outs, g_ref, fg_ref):
    got, mid_wg, hid, agg, mid, outer, slope1, slope2, cot, pick, pool, w = ins
    send_ref, g_out, fg_out = outs
    d, rows = hid.shape
    send_ref[4 * d : 8 * d, :] = mid_wg[...]
    blocks = dot(pick[...], got[...]).astype(BF)
    per = pool.shape[1]
    grads = [jnp.zeros((d, d), F32) for _ in range(4)]
    for i in range(rows // TILE):
        cols = slice(i * TILE, (i + 1) * TILE)
        back = dot_tn(blocks[i * per : (i + 1) * per, :], pool[i])
        g = (cot[:, cols].astype(F32) + back).astype(BF)
        sg = (dot(w[3], g) * slope2[:, cols]).astype(BF)
        fg = (dot(w[2], sg) * slope1[:, cols]).astype(BF)
        g_ref[:, cols] = g
        fg_ref[:, cols] = fg
        grads = [
            grads[0] + dot_nt(hid[:, cols], fg),
            grads[1] + dot_nt(agg[:, cols], fg),
            grads[2] + dot_nt(mid[:, cols], sg),
            grads[3] + dot_nt(outer[:, cols], g),
        ]
    io.start(g_ref, g_out)
    io.start(fg_ref, fg_out)
    for m in range(4):
        send_ref[m * d : (m + 1) * d, :] = (grads[m] * scale).astype(BF)


def fine_spread_kernel(io, need, flush, ins, outs, s_ref, total):
    off, ew, w, g, fg = ins
    rim_l, rim_r, out_ref = outs
    rows = g.shape[1]
    clear_corners(s_ref.at[0])
    clear_corners(s_ref.at[1])
    total[...] = jnp.zeros(total.shape, F32)
    need()
    for i in range(rows // TILE):
        cols = slice(i * TILE, (i + 1) * TILE)
        s = s_ref.at[i % 2]
        fine_edges(off[:, cols], ew[:, cols], s)
        fg_tile = fg[:, cols]
        direct = g[:, cols].astype(F32) + dot(w[0], fg_tile)
        spill = dot(w[1], fg_tile).astype(BF)
        window = slice(i * TILE, (i + 1) * TILE + 2 * HALO)
        total[window, :] = total[window, :] + dot_nt(s[...], spill)
        here = slice(HALO + i * TILE, HALO + (i + 1) * TILE)
        total[here, :] = total[here, :] + jnp.transpose(direct)
    rim_l[...] = total[:HALO, :].astype(BF)
    rim_r[...] = total[HALO + rows :, :].astype(BF)
    out_ref[...] = total[HALO : HALO + rows, :]


def sum_kernel(io, need, flush, ins, outs, part):
    got, _ = ins
    send_ref = outs[0]
    peers = got.shape[0]
    part[...] = sum(got[p].astype(F32) for p in range(peers)).astype(BF)
    for p in range(peers):
        io.start(part, send_ref.at[p])


def join_kernel(io, need, flush, ins, outs):
    total, from_left, from_right = ins
    out_ref = outs[0]
    rows = total.shape[0]
    out_ref[:HALO, :] = (total[:HALO, :] + from_left[...].astype(F32)).astype(BF)
    out_ref[HALO : rows - HALO, :] = total[HALO : rows - HALO, :].astype(BF)
    out_ref[rows - HALO :, :] = (total[rows - HALO :, :] + from_right[...].astype(F32)).astype(BF)


def exchange(x):
    return lax.all_to_all(x, "nodes", split_axis=0, concat_axis=0, tiled=True)


def per_device(
    features,
    fine_cotangent,
    mid_cotangent,
    coarse_cotangent,
    weights,
    fine_offsets,
    fine_edge_w,
    pool_fine,
    owner_dev,
    coarse_slot,
    mid_nbrs,
    mid_edge_w,
    pool_mid,
    coarse_nbrs,
    coarse_edge_w,
):
    n, d = features.shape
    tile_count = owner_dev.shape[0]
    tile_rows = n // tile_count
    block_rows = pool_fine.shape[0]
    n1 = mid_cotangent.shape[0]
    n2 = coarse_cotangent.shape[0]
    edges = fine_offsets.shape[0]
    peers = lax.axis_size("nodes")
    cap = max(2, 2 * tile_count // peers)
    chunk = cap * block_rows
    window = TILE + 2 * HALO
    per = TILE // tile_rows * block_rows
    ends = peers - 1
    up = [(i, i + 1) for i in range(ends)]
    down = [(i + 1, i) for i in range(ends)]
    total2 = peers * n2

    left = lax.ppermute(features[n - HALO :], "nodes", up)
    right = lax.ppermute(features[:HALO], "nodes", down)
    owners = owner_dev.reshape(-1)
    s_out, win, w01, w2t, w3t, pool_out, spread, ext, agg_in, place = call(
        functools.partial(inner_kernel, tile_rows, peers, cap),
        [
            (fine_offsets, "h"), (fine_edge_w, "h"), (features, "h"), (weights, "0"),
            (pool_fine, "h"), (owners, "s"), (coarse_slot, "s"), (coarse_nbrs, "h"),
            (coarse_edge_w, "h"), (coarse_cotangent, "h"),
        ],
        [
            (shape((2, window, TILE)), "v"), (shape((2, d, TILE + HALO)), "v"),
            (shape((d, 2 * d)), "v"), (shape((d, d)), "v"), (shape((d, d)), "v"),
            (shape((2, per, TILE)), "v"), (shape((peers * chunk, d), F32), "v"),
            (shape((peers, n2 + 16, d)), "v"), (shape((d, n)), "v"),
            (shape((tile_count,), jnp.int32), "s"),
        ],
        scratch=(
            pltpu.VMEM((d, n), BF),
            pltpu.VMEM((2, window, TILE), BF),
            pltpu.VMEM((peers, 128), F32),
            pltpu.SMEM((peers,), jnp.int32),
        ),
        us=6,
    )
    send1, agg = call(
        functools.partial(outer_kernel, tile_rows, cap, block_rows),
        [
            (left, "v"), (right, "v"), (s_out, "v"), (win, "v"), (w01, "v"), (w2t, "v"),
            (w3t, "v"), (pool_out, "v"), (spread, "v"), (ext, "v"), (agg_in, "v"), (owners, "s"),
        ],
        [(shape((peers, chunk + n2 + 16, d)), "r"), (shape((d, n)), "r")],
        scratch=(
            pltpu.VMEM((d, 2 * TILE), BF),
            pltpu.VMEM((peers * chunk, d), F32),
            pltpu.VMEM((peers, chunk, d), BF),
            pltpu.SMEM((peers,), jnp.int32),
        ),
        copies=8,
        us=3,
    )
    got1 = exchange(send1)
    smid, m01, m2t, m3t, pool_v = call(
        first_window_kernel,
        [
            (mid_nbrs, "h"), (mid_edge_w, "h"), (weights, "1"), (pool_mid, "r"), (agg, "r"),
        ],
        [
            (shape((n1, n1)), "v"), (shape((d, 2 * d)), "v"), (shape((d, d)), "v"),
            (shape((d, d)), "v"), (shape((n2, n1)), "v"),
        ],
        copies=1,
        us=6,
    )
    send2, mhid, magg, sel, ext = call(
        functools.partial(mid_kernel, block_rows, chunk),
        [(got1, "v"), (smid, "v"), (m01, "v"), (m2t, "v"), (m3t, "v"), (pool_v, "v")],
        [
            (shape((peers, n2, d)), "r"), (shape((d, n1)), "h"), (shape((d, n1)), "h"),
            (shape((peers * chunk, n1)), "h"), (shape((peers, n2 + 16, d)), "r"),
        ],
        scratch=(pltpu.VMEM((peers * chunk, d), BF), pltpu.VMEM((n2, d), BF)),
        copies=peers + 1,
        us=3,
    )
    got2 = exchange(send2)
    second = call(
        second_window_kernel,
        [
            (ext, "h"), (mhid, "h"), (magg, "h"), (mid_nbrs, "h"), (mid_edge_w, "h"),
            (mid_cotangent, "h"), (sel, "r"), (weights, "r"), (pool_mid, "r"),
            (coarse_cotangent, "r"), (weights, "1"),
        ],
        [
            (shape((total2, total2)), "v"), (shape((d, total2)), "v"), (shape((n1, n1)), "v"),
            (shape((d, n1)), "v"), (shape((d, n1), F32), "v"), (shape((d, n1), F32), "v"),
            (shape((peers * chunk, n1)), "v"), (shape((2, 4, d, d)), "v"),
            (shape((n2, n1)), "v"), (shape((n2, d)), "v"),
        ],
        scratch=(pltpu.VMEM((edges, total2), jnp.int32), pltpu.VMEM((edges, total2), F32)),
        copies=4,
        us=6,
    )
    send3, gmid, msg, mfg, coarse_wg = call(
        coarse_kernel,
        [(got2.reshape(total2, d), "v")] + [(x, "v") for x in second],
        [
            (shape((peers * chunk, d)), "h"), (shape((d, n1)), "h"), (shape((d, n1)), "h"),
            (shape((d, n1)), "h"), (shape((4, d, d), F32), "h"),
        ],
        us=3,
    )
    got3 = exchange(send3.reshape(peers, chunk, d))
    third = call(
        functools.partial(third_window_kernel, tile_rows, 1.0 / math.sqrt(n1 * peers)),
        [
            (mhid, "h"), (magg, "h"), (gmid, "h"), (msg, "h"), (mfg, "h"), (features, "h"),
            (fine_cotangent, "h"), (weights, "r"), (pool_fine, "h"), (place, "s"), (agg, "r"),
            (weights, "1"),
        ],
        [
            (shape((4 * d, d)), "v"), (shape((d, n)), "v"), (shape((d, n)), "v"),
            (shape((d, n)), "v"), (shape((d, n)), "v"), (shape((d, n), F32), "v"),
            (shape((d, n), F32), "v"), (shape((d, n)), "v"),
            (shape((tile_count * block_rows, peers * chunk)), "v"),
            (shape((n // TILE, per, TILE)), "v"), (shape((4, d, d)), "v"),
        ],
        copies=2,
        us=6,
    )
    send4, g, fg = call(
        functools.partial(fine_grad_kernel, 1.0 / math.sqrt(n * peers)),
        [(got3.reshape(peers * chunk, d), "v")] + [(x, "v") for x in third],
        [(shape((8 * d, d)), "h"), (shape((d, n)), "r"), (shape((d, n)), "r")],
        scratch=(pltpu.VMEM((d, n), BF), pltpu.VMEM((d, n), BF)),
        copies=2,
        us=4,
    )
    got4 = exchange(send4.reshape(peers, 8 * d // peers, d))
    rim_l, rim_r, spread = call(
        fine_spread_kernel,
        [(fine_offsets, "h"), (fine_edge_w, "h"), (weights, "0"), (g, "h"), (fg, "h")],
        [(shape((HALO, d)), "v"), (shape((HALO, d)), "v"), (shape((n, d), F32), "v")],
        scratch=(pltpu.VMEM((2, window, TILE), BF), pltpu.VMEM((n + 2 * HALO, d), F32)),
        us=6,
    )
    (send5,) = call(
        sum_kernel,
        [(got4, "v"), (rim_l, "a")],
        [(shape((peers, 8 * d // peers, d)), "r")],
        scratch=(pltpu.VMEM((8 * d // peers, d), BF),),
        copies=peers,
        us=1,
    )
    got5 = exchange(send5)
    from_left = lax.ppermute(rim_r, "nodes", up)
    from_right = lax.ppermute(rim_l, "nodes", down)
    (feature_grads,) = call(
        join_kernel,
        [(spread, "v"), (from_left, "v"), (from_right, "v")],
        [(shape((n, d)), "v")],
        us=1,
    )
    weight_grads = jnp.concatenate(
        [got5.reshape(2, 4, d, d).astype(F32), coarse_wg[None]], axis=0
    )
    return (feature_grads, weight_grads)


def solution(mesh):
    rows = P(("groups", "nodes"), None)
    cols = P("groups", "nodes")
    in_specs = (
        rows, rows, rows, rows, P(), cols, cols, cols, rows, P(("groups", "nodes")),
        cols, cols, rows, cols, cols,
    )
    out_specs = (rows, P("groups", None, None, None))
    return jax.shard_map(
        per_device, mesh=mesh, in_specs=in_specs, out_specs=out_specs, check_vma=False
    )
```

time: 125 us -> 140 us (1.12)
  blocking collectives: 12.9 us -> 0 us
  waiting for transfers between devices: 8.2 us -> 18.8 us
  Pallas kernels: 25 us -> 31.9 us
  starting transfers between devices: 32.3 us -> 38.1 us
  local copies, waits for them, and re-layouts: 41.7 us -> 47.5 us
  other arithmetic: 2.62 us -> 0.97 us
    all_to_all x1 -> x0, blocking collectives: 12.9 us -> none  [exchange(): return lax.all_to_all(x, 'nodes', split_axis=0, concat_axis=0, tiled=True)]
    unnamed x128 -> x144, local copies, waits for them, and re-layouts: 36 us -> 46.6 us
    all_to_all x4 -> x5, waiting for transfers between devices: 4.55 us -> 14.4 us  [exchange(): return lax.all_to_all(x, 'nodes', split_axis=0, concat_axis=0, tiled=True)]
    pallas_call x10 -> x11, Pallas kernels: 25 us -> 31.9 us  [call(): pl.pallas_call(body, out_shape=[s for s, _ in outs], in_specs=[{'v': VM,...]
    all_to_all x4 -> x5, starting transfers between devices: 20.4 us -> 26.2 us  [exchange(): return lax.all_to_all(x, 'nodes', split_axis=0, concat_axis=0, tiled=True)]
    add x1 -> x0, other arithmetic: 1.59 us -> none  [per_device(): all_ew = extra[2] + extra[3]]
    convert_element_type x1 -> x0, local copies, waits for them, and re-layouts: 1.52 us -> none  [per_device(): all_nbrs = (extra[0] * 256.0 + extra[1]).astype(jnp.int32)]
    add x1 -> x0, local copies, waits for them, and re-layouts: 1.52 us -> none  [per_device(): all_ew = extra[2] + extra[3]]
  transfers between devices with their start and end apart: 8 -> 9, of which waited for: 4 -> 3; matrix products, arithmetic and copies ran while one was open for 4% -> 0% of each run, Pallas kernels for 9% -> 13%
where the time goes in v2:
time: 140 us; the launch traced here: 138 us
  local copies, waits for them, and re-layouts  47.5 us (34%)
  starting transfers between devices  38.1 us (27%)
  Pallas kernels  31.9 us (23%)
  waiting for transfers between devices  18.8 us (13%)
    unnamed x144, local copies, waits for them, and re-layouts  46.6 us
    pallas_call x11, Pallas kernels, call(): pl.pallas_call(body, out_shape=[s for s, _ in outs], in_specs=[{'v': VM,...  31.9 us
    all_to_all x5, starting transfers between devices, exchange(): return lax.all_to_all(x, 'nodes', split_axis=0, concat_axis=0, tiled=True)  26.2 us
    all_to_all x5, waiting for transfers between devices, exchange(): return lax.all_to_all(x, 'nodes', split_axis=0, concat_axis=0, tiled=True)  14.4 us
    ppermute x1, starting transfers between devices, per_device(): left = lax.ppermute(features[n - HALO:], 'nodes', up)  4.49 us
    ppermute x1, waiting for transfers between devices, per_device(): from_right = lax.ppermute(rim_l, 'nodes', down)  4.35 us
    ppermute x1, starting transfers between devices, per_device(): from_left = lax.ppermute(rim_r, 'nodes', up)  3.53 us
  transfers between devices with their start and end apart: 9, of which 3 were waited for; matrix products, arithmetic and copies ran while one was open for 0% of the time, Pallas kernels for 13%

profile of v2, /device:TPU:1, one launch (start us, length us, event | category | flops | bytes accessed | tf_op | source)
XLA Modules:
  0.0 138.3 jit_solution(1944498244755827915)
XLA Ops:
  1.6 2.0 %collective-permute-start.1 = (bf16[256,128]{1,0:T(8,128)(2,1)S(1)}, bf16[256,128]{1,0:T(8,128)(2,1)S(1)}, u32[]{:S(2)}, u32[]{:S(2)}) collective-permute-start(bf16[256,128]{1,0:T(8,128)(2,1)S(1)} %get-tuple-element.110), channel_id=1, source_target_pairs={{1,0},{2,1},{3,2},{4,3},{5,4},{6,5},{7,6},{8,7},{9,8},{10,9},{11,1... | collective-permute-start | bytes 196616 | tf_op jit(solution)/shard_map/ppermute | solution.py:608
  3.6 4.5 %collective-permute-start = (bf16[256,128]{1,0:T(8,128)(2,1)S(1)}, bf16[256,128]{1,0:T(8,128)(2,1)S(1)}, u32[]{:S(2)}, u32[]{:S(2)}) collective-permute-start(bf16[256,128]{1,0:T(8,128)(2,1)S(1)} %get-tuple-element.111), channel_id=1, source_target_pairs={{0,1},{1,2},{2,3},{3,4},{4,5},{5,6},{6,7},{7,8},{8,9},{9,10},{10,1... | collective-permute-start | bytes 196616 | tf_op jit(solution)/shard_map/ppermute | solution.py:607
  9.2 1.0 copy-done.2
  10.3 6.9 %shard_map.158 = (bf16[2,768,256]{2,1,0:T(8,128)(2,1)S(1)}, bf16[2,128,512]{2,1,0:T(8,128)(2,1)S(1)}, bf16[128,256]{1,0:T(8,128)(2,1)S(1)}, bf16[128,128]{1,0:T(...) custom-call(s32[8,2048]{1,0:T(8,128)S(1)} %copy-done.30, ...), custom_call_target="tpu_custom_call" | custom-call | bytes 18000000 | tf_op jit(solution)/shard_map/pallas_call | solution.py:163
  17.2 2.4 %shard_map.159 = (bf16[16,96,128]{2,1,0:T(8,128)(2,1)}, bf16[128,2048]{1,0:T(8,128)(2,1)S(1)}) custom-call(bf16[256,128]{1,0:T(8,128)(2,1)S(1)} %collective-permute-done.refs_0_, bf16[256,128]{1,0:T(8,128)(2,1)S(1)} %collective-permute-done.1.refs_1_, bf16[2,768,256]{2,1,0:T(8,128)(2,1)S(1)} %get-tuple-element.56.refs_2_, ...), custom_call_target="tpu_custom_call" | custom-call | bytes 9000000 | tf_op jit(solution)/shard_map/pallas_call | solution.py:163
  19.7 5.9 %all-to-all-start = ((bf16[16,96,128]{2,1,0:T(8,128)(2,1)}), bf16[16,96,128]{2,1,0:T(8,128)(2,1)S(1)}, u32[]{:S(2)}, u32[]{:S(2)}) async-start(bf16[16,96,128]{2,1,0:T(8,128)(2,1)} %get-tuple-element.65), calls=%async_computation | async-start | bytes 786432 | tf_op jit(solution)/shard_map/all_to_all | solution.py:570
  26.4 11.1 %all-to-all-done.refs_0_ = bf16[16,96,128]{2,1,0:T(8,128)(2,1)S(1)} async-done(((bf16[16,96,128]{2,1,0:T(8,128)(2,1)}), bf16[16,96,128]{2,1,0:T(8,128)(2,1)S(1)}, u32[]{:S(2)}, u32[]{:S(2)}) %all-to-all-start) | async-done | bytes 393248 | tf_op jit(solution)/shard_map/all_to_all | solution.py:570
  37.5 2.3 %shard_map.161 = (bf16[16,16,128]{2,1,0:T(8,128)(2,1)S(1)}, bf16[128,512]{1,0:T(8,128)(2,1)S(1)}, bf16[128,512]{1,0:T(8,128)(2,1)S(1)}, bf16[1024,512]{1,0:T(8,128)(2,1)S(1)}, bf16[16,32,128]{2,1,0:T(8,128)(2,1)S(1)}) custom-call(bf16[16,96,128]{2,1,0:T(8,128)(2,1)S(1)} %all-to-all-done.refs_0_, bf16[512,512]{1,0:T(8,128)(2,1)S(1)} %get-tuple-element.67.refs_1_, ...), custom_call_target="tpu_custom_call" | custom-call | bytes 9000000 | tf_op jit(solution)/shard_map/pallas_call | solution.py:163
  41.7 4.0 %all-to-all-start.1 = ((bf16[16,16,128]{2,1,0:T(8,128)(2,1)}), bf16[16,16,128]{2,1,0:T(8,128)(2,1)S(1)}, u32[]{:S(2)}, u32[]{:S(2)}) async-start(bf16[16,16,128]{2,1,0:T(8,128)(2,1)} %copy-done.66), calls=%async_computation.1 | async-start | bytes 131072 | tf_op jit(solution)/shard_map/all_to_all | solution.py:570
  46.6 2.2 %shard_map.162 = (bf16[256,256]{1,0:T(8,128)(2,1)S(1)}, bf16[128,256]{1,0:T(8,128)(2,1)S(1)}, bf16[512,512]{1,0:T(8,128)(2,1)S(1)}, bf16[128,512]{1,0:T(8,128)(2...) custom-call(bf16[16,32,128]{2,1,0:T(8,128)(2,1)S(1)} %copy-done.56, ...), custom_call_target="tpu_custom_call" | custom-call | bytes 18000000 | tf_op jit(solution)/shard_map/pallas_call | solution.py:163
  53.7 1.0 copy-done.27
  60.2 3.8 %shard_map.163 = (bf16[1024,128]{1,0:T(8,128)(2,1)}, bf16[128,512]{1,0:T(8,128)(2,1)S(1)}, bf16[128,512]{1,0:T(8,128)(2,1)S(1)}, bf16[128,512]{1,0:T(8,128)(2,1)S(1)}, f32[4,128,128]{2,1,0:T(8,128)S(1)}) custom-call(bf16[256,128]{1,0:T(8,128)(2,1)S(1)} %bitcast.8, bf16[256,256]{1,0:T(8,128)(2,1)S(1)} %copy-done.58, bf16[128,256]{1,0:T(8,128)(2,1)S(1)} %copy-done.65, ...), custom_call_target="tpu_custom_call" | custom-call | bytes 9000000 | tf_op jit(solution)/shard_map/pallas_call | solution.py:163
  66.7 6.1 %all-to-all-start.2 = ((bf16[16,64,128]{2,1,0:T(8,128)(2,1)}), bf16[16,64,128]{2,1,0:T(8,128)(2,1)}, u32[]{:S(2)}, u32[]{:S(2)}) async-start(bf16[16,64,128]{2,1,0:T(8,128)(2,1)} %bitcast.2), calls=%async_computation.2 | async-start | bytes 524288 | tf_op jit(solution)/shard_map/all_to_all | solution.py:570
  79.2 3.5 %shard_map.164 = (bf16[512,128]{1,0:T(8,128)(2,1)S(1)}, bf16[128,2048]{1,0:T(8,128)(2,1)S(1)}, bf16[128,2048]{1,0:T(8,128)(2,1)S(1)}, bf16[128,2048]{1,0:T(8,128...) custom-call(bf16[128,512]{1,0:T(8,128)(2,1)S(1)} %copy-done.22, ...), custom_call_target="tpu_custom_call" | custom-call | bytes 18000000 | tf_op jit(solution)/shard_map/pallas_call | solution.py:163
  89.6 1.2 copy-done.5
  91.9 1.0 copy-done.10
  98.8 4.8 %shard_map.165 = (bf16[1024,128]{1,0:T(8,128)(2,1)}, bf16[128,2048]{1,0:T(8,128)(2,1)S(1)}, bf16[128,2048]{1,0:T(8,128)(2,1)S(1)}) custom-call(bf16[1024,128]{1,0:T(8,128)(2,1)} %bitcast.3.refs_0_, bf16[512,128]{1,0:T(8,128)(2,1)S(1)} %copy-done.52, bf16[128,2048]{1,0:T(8,128)(2,1)S(1)} %copy-done.8, bf16[128,2048]{1,0:T(8,128)(2,1)S(1)} %copy-done.10, ...), custom_call_target="tpu_custom_call" | custom-call | bytes 12000000 | tf_op jit(solution)/shard_map/pallas_call | solution.py:163
  105.3 6.2 %all-to-all-start.3 = ((bf16[16,64,128]{2,1,0:T(8,128)(2,1)}), bf16[16,64,128]{2,1,0:T(8,128)(2,1)S(1)}, u32[]{:S(2)}, u32[]{:S(2)}) async-start(bf16[16,64,128]{2,1,0:T(8,128)(2,1)} %bitcast.4), calls=%async_computation.3 | async-start | bytes 524288 | tf_op jit(solution)/shard_map/all_to_all | solution.py:570
  114.1 3.5 %shard_map.166 = (bf16[256,128]{1,0:T(8,128)(2,1)S(1)}, bf16[256,128]{1,0:T(8,128)(2,1)S(1)}, f32[2048,128]{1,0:T(8,128)S(1)}) custom-call(s32[8,2048]{1,0:T(8,128)S(1)} %copy-done.31, f32[8,2048]{1,0:T(8,128)S(1)} %copy-done.33, bf16[3,4,128,128]{3,2,1,0:T(8,128)(2,1)S(1)} %copy-done.1, bf16[128,2048]{1,0:T(8,128)(2,1)S(1)} %copy-done.18, ...), custom_call_target="tpu_custom_call" | custom-call | bytes 18000000 | tf_op jit(solution)/shard_map/pallas_call | solution.py:163
  117.6 3.3 %all-to-all-done.3.refs_0_ = bf16[16,64,128]{2,1,0:T(8,128)(2,1)S(1)} async-done(((bf16[16,64,128]{2,1,0:T(8,128)(2,1)}), bf16[16,64,128]{2,1,0:T(8,128)(2,1)S(1)}, u32[]{:S(2)}, u32[]{:S(2)}) %all-to-all-start.3) | async-done | bytes 262176 | tf_op jit(solution)/shard_map/all_to_all | solution.py:570
  121.8 4.0 %all-to-all-start.4 = ((bf16[16,64,128]{2,1,0:T(8,128)(2,1)}), bf16[16,64,128]{2,1,0:T(8,128)(2,1)S(1)}, u32[]{:S(2)}, u32[]{:S(2)}) async-start(bf16[16,64,128]{2,1,0:T(8,128)(2,1)} %shard_map.168), calls=%async_computation.4 | async-start | bytes 524288 | tf_op jit(solution)/shard_map/all_to_all | solution.py:570
  125.8 3.5 %collective-permute-start.2 = (bf16[256,128]{1,0:T(8,128)(2,1)S(1)}, bf16[256,128]{1,0:T(8,128)(2,1)S(1)}, u32[]{:S(2)}, u32[]{:S(2)}) collective-permute-start(bf16[256,128]{1,0:T(8,128)(2,1)S(1)} %get-tuple-element.106), channel_id=1, source_target_pairs={{0,1},{1,2},{2,3},{3,4},{4,5},{5,6},{6,7},{7,8},{8,9},{9,10},{10,1... | collective-permute-start | bytes 196616 | tf_op jit(solution)/shard_map/ppermute | solution.py:742
  129.3 1.9 %collective-permute-start.3 = (bf16[256,128]{1,0:T(8,128)(2,1)S(1)}, bf16[256,128]{1,0:T(8,128)(2,1)S(1)}, u32[]{:S(2)}, u32[]{:S(2)}) collective-permute-start(bf16[256,128]{1,0:T(8,128)(2,1)S(1)} %get-tuple-element.107.refs_1_), channel_id=1, source_target_pairs={{1,0},{2,1},{3,2},{4,3},{5,4},{6,5},{7,6},{8,7},{9,8},{10,9},{11,1... | collective-permute-start | bytes 196616 | tf_op jit(solution)/shard_map/ppermute | solution.py:743
  131.3 4.3 %collective-permute-done.3.refs_2_ = bf16[256,128]{1,0:T(8,128)(2,1)S(1)} collective-permute-done((bf16[256,128]{1,0:T(8,128)(2,1)S(1)}, bf16[256,128]{1,0:T(8,128)(2,1)S(1)}, u32[]{:S(2)}, u32[]{:S(2)}) %collective-permute-start.3) | collective-permute-done | bytes 65568 | tf_op jit(solution)/shard_map/ppermute | solution.py:743
  (152 shorter events, 46.6 us)
Async XLA Ops:
  0.6 7.5 %copy-start.42 = (bf16[8,2048]{1,0:T(8,128)(2,1)S(1)}, bf16[8,2048]{1,0:T(8,128)(2,1)}, u32[]{:S(2)}) copy-start(bf16[8,2048]{1,0:T(8,128)(2,1)} %refs_8_.5) | copy-start | bytes 98308
  0.6 7.5 %copy-start.32 = (f32[8,2048]{1,0:T(8,128)S(1)}, f32[8,2048]{1,0:T(8,128)}, u32[]{:S(2)}) copy-start(f32[8,2048]{1,0:T(8,128)} %refs_1_.5) | copy-start | bytes 196612
  0.7 7.5 %copy-start.30 = (s32[8,2048]{1,0:T(8,128)S(1)}, s32[8,2048]{1,0:T(8,128)}, u32[]{:S(2)}) copy-start(s32[8,2048]{1,0:T(8,128)} %refs_0_.5) | copy-start | bytes 196612
  0.7 7.5 %copy-start.68 = (s32[8,16]{1,0:T(8,128)S(1)}, s32[8,16]{1,0:T(8,128)}, u32[]{:S(2)}) copy-start(s32[8,16]{1,0:T(8,128)} %refs_7_.3) | copy-start | bytes 1540
  0.7 7.5 %copy-start.69 = (f32[8,16]{1,0:T(8,128)S(1)}, f32[8,16]{1,0:T(8,128)}, u32[]{:S(2)}) copy-start(f32[8,16]{1,0:T(8,128)} %refs_8_.3) | copy-start | bytes 1540
  1.6 6.6 %copy-start.67 = (bf16[16,128]{1,0:T(8,128)(2,1)S(1)}, bf16[16,128]{1,0:T(8,128)(2,1)}, u32[]{:S(2)}) copy-start(bf16[16,128]{1,0:T(8,128)(2,1)} %refs_9_.3) | copy-start | bytes 12292
  1.6 15.5 %collective-permute-start.1 = (bf16[256,128]{1,0:T(8,128)(2,1)S(1)}, bf16[256,128]{1,0:T(8,128)(2,1)S(1)}, u32[]{:S(2)}, u32[]{:S(2)}) collective-permute-start(bf16[256,128]{1,0:T(8,128)(2,1)S(1)} %get-tuple-element.110), channel_id=1, source_target_pairs={{1,0},{2,1},{3,2},{4,3},{5,4},{6,5},{7,6},{8,7},{9,8},{10,9},{11,1... | collective-permute-start | bytes 196616 | tf_op jit(solution)/shard_map/ppermute | solution.py:608
  3.6 4.6 %copy-start.70 = (s32[64,1]{0,1:T(1,128)S(1)}, s32[64,1]{0,1:T(1,128)}, u32[]{:S(2)}) copy-start(s32[64,1]{0,1:T(1,128)} %param.23) | copy-start | bytes 772
  3.6 13.6 %collective-permute-start = (bf16[256,128]{1,0:T(8,128)(2,1)S(1)}, bf16[256,128]{1,0:T(8,128)(2,1)S(1)}, u32[]{:S(2)}, u32[]{:S(2)}) collective-permute-start(bf16[256,128]{1,0:T(8,128)(2,1)S(1)} %get-tuple-element.111), channel_id=1, source_target_pairs={{0,1},{1,2},{2,3},{3,4},{4,5},{5,6},{6,7},{7,8},{8,9},{9,10},{10,1... | collective-permute-start | bytes 196616 | tf_op jit(solution)/shard_map/ppermute | solution.py:607
  19.6 6.0 %copy-start.1 = (bf16[3,4,128,128]{3,2,1,0:T(8,128)(2,1)S(1)}, bf16[3,4,128,128]{3,2,1,0:T(8,128)(2,1)}, u32[]{:S(2)}) copy-start(bf16[3,4,128,128]{3,2,1,0:T(8,128)(2,1)} %refs_2_.5) | copy-start | bytes 1179652
  19.6 6.0 %copy-start.61 = (s32[8,512]{1,0:T(8,128)S(1)}, s32[8,512]{1,0:T(8,128)}, u32[]{:S(2)}) copy-start(s32[8,512]{1,0:T(8,128)} %refs_3_.5) | copy-start | bytes 49156
  19.7 6.0 %copy-start.62 = (f32[8,512]{1,0:T(8,128)S(1)}, f32[8,512]{1,0:T(8,128)}, u32[]{:S(2)}) copy-start(f32[8,512]{1,0:T(8,128)} %refs_4_.3) | copy-start | bytes 49156
  19.7 6.0 %copy-start.63 = (bf16[16,512]{1,0:T(8,128)(2,1)S(1)}, bf16[16,512]{1,0:T(8,128)(2,1)}, u32[]{:S(2)}) copy-start(bf16[16,512]{1,0:T(8,128)(2,1)} %refs_8_.4) | copy-start | bytes 49156
  19.7 17.8 %all-to-all-start = ((bf16[16,96,128]{2,1,0:T(8,128)(2,1)}), bf16[16,96,128]{2,1,0:T(8,128)(2,1)S(1)}, u32[]{:S(2)}, u32[]{:S(2)}) async-start(bf16[16,96,128]{2,1,0:T(8,128)(2,1)} %get-tuple-element.65), calls=%async_computation | async-start | bytes 786432 | tf_op jit(solution)/shard_map/all_to_all | solution.py:570
  37.5 8.1 %copy-start.44 = (bf16[512,128]{1,0:T(8,128)(2,1)S(1)}, bf16[512,128]{1,0:T(8,128)(2,1)}, u32[]{:S(2)}) copy-start(bf16[512,128]{1,0:T(8,128)(2,1)} %refs_5_.2) | copy-start | bytes 393220
  41.7 7.1 %copy-start.21 = (bf16[128,512]{1,0:T(8,128)(2,1)}, bf16[128,512]{1,0:T(8,128)(2,1)S(1)}, u32[]{:S(2)}) copy-start(bf16[128,512]{1,0:T(8,128)(2,1)S(1)} %get-tuple-element.74.refs_1_.refs_0_) | copy-start | bytes 393220
  41.7 12.0 %all-to-all-start.1 = ((bf16[16,16,128]{2,1,0:T(8,128)(2,1)}), bf16[16,16,128]{2,1,0:T(8,128)(2,1)S(1)}, u32[]{:S(2)}, u32[]{:S(2)}) async-start(bf16[16,16,128]{2,1,0:T(8,128)(2,1)} %copy-done.66), calls=%async_computation.1 | async-start | bytes 131072 | tf_op jit(solution)/shard_map/all_to_all | solution.py:570
  66.7 6.2 %copy-start.3 = (bf16[2048,128]{1,0:T(8,128)(2,1)S(1)}, bf16[2048,128]{1,0:T(8,128)(2,1)}, u32[]{:S(2)}) copy-start(bf16[2048,128]{1,0:T(8,128)(2,1)} %refs_5_.3) | copy-start | bytes 1572868
  66.7 22.9 %all-to-all-start.2 = ((bf16[16,64,128]{2,1,0:T(8,128)(2,1)}), bf16[16,64,128]{2,1,0:T(8,128)(2,1)}, u32[]{:S(2)}, u32[]{:S(2)}) async-start(bf16[16,64,128]{2,1,0:T(8,128)(2,1)} %bitcast.2), calls=%async_computation.2 | async-start | bytes 524288 | tf_op jit(solution)/shard_map/all_to_all | solution.py:570
  105.3 6.2 %copy-start.18 = (bf16[128,2048]{1,0:T(8,128)(2,1)S(1)}, bf16[128,2048]{1,0:T(8,128)(2,1)}, u32[]{:S(2)}) copy-start(bf16[128,2048]{1,0:T(8,128)(2,1)} %copy-done.17) | copy-start | bytes 1572868
  105.3 15.6 %all-to-all-start.3 = ((bf16[16,64,128]{2,1,0:T(8,128)(2,1)}), bf16[16,64,128]{2,1,0:T(8,128)(2,1)S(1)}, u32[]{:S(2)}, u32[]{:S(2)}) async-start(bf16[16,64,128]{2,1,0:T(8,128)(2,1)} %bitcast.4), calls=%async_computation.3 | async-start | bytes 524288 | tf_op jit(solution)/shard_map/all_to_all | solution.py:570
  121.8 14.7 %all-to-all-start.4 = ((bf16[16,64,128]{2,1,0:T(8,128)(2,1)}), bf16[16,64,128]{2,1,0:T(8,128)(2,1)S(1)}, u32[]{:S(2)}, u32[]{:S(2)}) async-start(bf16[16,64,128]{2,1,0:T(8,128)(2,1)} %shard_map.168), calls=%async_computation.4 | async-start | bytes 524288 | tf_op jit(solution)/shard_map/all_to_all | solution.py:570
  125.8 5.5 %collective-permute-start.2 = (bf16[256,128]{1,0:T(8,128)(2,1)S(1)}, bf16[256,128]{1,0:T(8,128)(2,1)S(1)}, u32[]{:S(2)}, u32[]{:S(2)}) collective-permute-start(bf16[256,128]{1,0:T(8,128)(2,1)S(1)} %get-tuple-element.106), channel_id=1, source_target_pairs={{0,1},{1,2},{2,3},{3,4},{4,5},{5,6},{6,7},{7,8},{8,9},{9,10},{10,1... | collective-permute-start | bytes 196616 | tf_op jit(solution)/shard_map/ppermute | solution.py:742
  129.3 6.3 %collective-permute-start.3 = (bf16[256,128]{1,0:T(8,128)(2,1)S(1)}, bf16[256,128]{1,0:T(8,128)(2,1)S(1)}, u32[]{:S(2)}, u32[]{:S(2)}) collective-permute-start(bf16[256,128]{1,0:T(8,128)(2,1)S(1)} %get-tuple-element.107.refs_1_), channel_id=1, source_target_pairs={{1,0},{2,1},{3,2},{4,3},{5,4},{6,5},{7,6},{8,7},{9,8},{10,9},{11,1... | collective-permute-start | bytes 196616 | tf_op jit(solution)/shard_map/ppermute | solution.py:743
  (57 other events, 55.2 us)

commit v3 on v2

--- a/solution.py
+++ b/solution.py
@@ -10,6 +10,7 @@
 
 HALO = 256
 TILE = 256
+BIG = 56
 BF = jnp.bfloat16
 F32 = jnp.float32
 
@@ -315,11 +316,11 @@
 
 
 def first_window_kernel(io, need, flush, ins, outs):
-    nbrs, ew, w, pool_mid, _ = ins
-    smid, w01_ref, w2t_ref, w3t_ref, pool_out = outs
-    io.start(pool_mid, pool_out)
+    nbrs, ew, w, _ = ins
+    smid, w01_ref, w2t_ref, w3t_ref = outs
     need(0, 1)
     mid_edges(nbrs, ew, smid)
+    flush(0)
     need()
     w01_ref[...], w2t_ref[...], w3t_ref[...] = forward_weights(w)
 
@@ -330,6 +331,7 @@
     peers = got.shape[0]
     nodes = smid.shape[0]
     n2 = pool_mid.shape[0]
+    need(0)
     io.start(got.at[:, pl.ds(chunk, n2 + 16), :], ext_ref)
     rows = [got[p, chunk + n2 : chunk + n2 + 16, :].astype(F32)[8:9, :] for p in range(peers)]
     keys = jnp.transpose(jnp.concatenate(rows, axis=0))
@@ -345,6 +347,7 @@
     flush(3)
     hidden = dot_tn(blocks[...], sel_ref[...]).astype(BF)
     hid_ref[...] = hidden
+    need()
     agg = dot(hidden, smid[...]).astype(BF)
     agg_ref[...] = agg
     flush(1, 2)
@@ -357,16 +360,12 @@
 
 
 def second_window_kernel(io, need, flush, ins, outs, nb_ref, ew_ref):
-    ext, hid, agg, mid_nbrs, mid_ew, mid_cot, sel_h, w_h, pool_h, cot_h, w1 = ins
-    sco, cot_all, smid, mcot, sl1_ref, sl2_ref, sel, w12, pool_mid, cot_my = outs
-    io.start(sel_h, sel)
-    io.start(w_h.at[pl.ds(1, 2)], w12)
-    io.start(pool_h, pool_mid)
-    io.start(cot_h, cot_my)
+    ext, hid, agg, mid_cot, w1 = ins
+    sco, cot_all, mcot, sl1_ref, sl2_ref = outs
     peers = ext.shape[0]
-    n2 = cot_h.shape[0]
+    n2 = ext.shape[1] - 16
     nodes = peers * n2
-    edges = mid_nbrs.shape[0]
+    edges = nb_ref.shape[0]
     need()
     for p in range(peers):
         part = ext[p, n2 : n2 + 16, :].astype(F32)[0:edges, :]
@@ -387,7 +386,7 @@
         return 0
 
     lax.fori_loop(0, nodes // 128, column, 0)
-    mid_edges(mid_nbrs, mid_ew, smid)
+    flush(0, 1, 2)
     w01, w2t, _ = forward_weights(w1)
     first = dot(w01, jnp.concatenate([hid[...], agg[...]], axis=0))
     s1 = 1.0 / (1.0 + jnp.exp(-first))
@@ -398,14 +397,16 @@
 
 
 def coarse_kernel(io, need, flush, ins, outs):
-    got, sco, cot_all, smid, mcot, msl1, msl2, sel, w, pool_mid, cot_my = ins
+    got, sco, w2, cot_all, cot_my, pool_mid, mcot, w1, msl2, msl1, smid, sel = ins
     send_ref, gmid_ref, sg_ref, fg_ref, cwg_ref = outs
     nodes = got.shape[0]
     n2 = cot_my.shape[0]
     me = lax.axis_index("nodes")
     width = min(TILE, nodes)
+    need(0)
     hidden = jnp.transpose(got[...])
-    w01, w2t, _ = forward_weights(w.at[1])
+    need(1, 2, 3)
+    w01, w2t, _ = forward_weights(w2)
     mine = pl.ds(pl.multiple_of(me * n2, 16), n2)
     spread = jnp.zeros((n2, 128), F32)
     fg_mine = jnp.zeros((n2, 128), F32)
@@ -423,9 +424,9 @@
         s2 = 1.0 / (1.0 + jnp.exp(-second))
         outer = (second * s2).astype(BF)
         g = cot_all[:, cols]
-        sg = (dot(w[1, 3], g) * (s2 * (1.0 + second * (1.0 - s2)))).astype(BF)
-        fg = (dot(w[1, 2], sg) * (s1 * (1.0 + first * (1.0 - s1)))).astype(BF)
-        spill = dot(w[1, 1], fg).astype(BF)
+        sg = (dot(w2[3], g) * (s2 * (1.0 + second * (1.0 - s2)))).astype(BF)
+        fg = (dot(w2[2], sg) * (s1 * (1.0 + first * (1.0 - s1)))).astype(BF)
+        spill = dot(w2[1], fg).astype(BF)
         spread = spread + dot_nt(sco[mine, cols], spill)
         here = jnp.where(lane + i * width == row, 1.0, 0.0).astype(BF)
         fg_mine = fg_mine + dot_nt(here, fg)
@@ -439,29 +440,29 @@
     for m in range(4):
         cwg_ref[m] = grads[m] * scale
     flush(4)
-    direct = cot_my[...].astype(F32) + dot_nt(fg_mine.astype(BF), w[1, 0])
+    need(4, 5, 6, 7, 8, 9)
+    direct = cot_my[...].astype(F32) + dot_nt(fg_mine.astype(BF), w2[0])
     coarse_grad = (direct + spread).astype(BF)
     back = dot_tn(coarse_grad, pool_mid[...])
     g = (mcot[...].astype(F32) + back).astype(BF)
     gmid_ref[...] = g
-    sg = (dot(w[0, 3], g) * msl2[...]).astype(BF)
+    sg = (dot(w1[3], g) * msl2[...]).astype(BF)
     sg_ref[...] = sg
-    fg = (dot(w[0, 2], sg) * msl1[...]).astype(BF)
+    fg = (dot(w1[2], sg) * msl1[...]).astype(BF)
     fg_ref[...] = fg
     flush(1, 2, 3)
-    spill = dot(w[0, 1], fg).astype(BF)
-    mid_grad = (g.astype(F32) + dot(w[0, 0], fg) + dot_nt(spill, smid[...])).astype(BF)
+    spill = dot(w1[1], fg).astype(BF)
+    need()
+    mid_grad = (g.astype(F32) + dot(w1[0], fg) + dot_nt(spill, smid[...])).astype(BF)
     send_ref[...] = dot_nt(sel[...], mid_grad).astype(BF)
 
 
 def third_window_kernel(tile_rows, mid_scale, io, need, flush, ins, outs):
-    mhid, magg, gmid, msg, mfg, feat, fine_cot, w, pool, place, agg_h, w1 = ins
-    wg_ref, hid_ref, agg, mid_ref, outer_ref, sl1_ref, sl2_ref, cot_ref, pick_ref, po_ref, w0 = outs
+    mhid, magg, gmid, msg, mfg, feat, fine_cot, w0, pool, place, agg, w1 = ins
+    wg_ref, hid_ref, mid_ref, outer_ref, sl1_ref, sl2_ref, cot_ref, pick_ref, po_ref = outs
     d, rows = hid_ref.shape
     block_rows = pool.shape[0]
     per = TILE // tile_rows
-    agg_copy = io.start(agg_h, agg)
-    w_copy = io.start(w.at[0], w0)
     need()
     w01, w2t, _ = forward_weights(w1)
     middle = silu(dot(w01, jnp.concatenate([mhid[...], magg[...]], axis=0))).astype(BF)
@@ -480,7 +481,7 @@
         pick_ref[t * block_rows : (t + 2) * block_rows, :] = jnp.concatenate(
             both, axis=0
         ).astype(BF)
-    io.wait(agg_copy, w_copy)
+    flush(0, 1, 6, 7)
     w01, w2t, _ = forward_weights(w0)
     for i in range(rows // TILE):
         cols = slice(i * TILE, (i + 1) * TILE)
@@ -497,11 +498,13 @@
 
 
 def fine_grad_kernel(scale, io, need, flush, ins, outs, g_ref, fg_ref):
-    got, mid_wg, hid, agg, mid, outer, slope1, slope2, cot, pick, pool, w = ins
+    got, pick, cot, pool, w, slope2, slope1, hid, agg, mid, outer, mid_wg = ins
     send_ref, g_out, fg_out = outs
     d, rows = hid.shape
+    need(0, 1)
+    blocks = dot(pick[...], got[...]).astype(BF)
+    need()
     send_ref[4 * d : 8 * d, :] = mid_wg[...]
-    blocks = dot(pick[...], got[...]).astype(BF)
     per = pool.shape[1]
     grads = [jnp.zeros((d, d), F32) for _ in range(4)]
     for i in range(rows // TILE):
@@ -552,6 +555,7 @@
     got, _ = ins
     send_ref = outs[0]
     peers = got.shape[0]
+    need()
     part[...] = sum(got[p].astype(F32) for p in range(peers)).astype(BF)
     for p in range(peers):
         io.start(part, send_ref.at[p])
@@ -561,6 +565,7 @@
     total, from_left, from_right = ins
     out_ref = outs[0]
     rows = total.shape[0]
+    need()
     out_ref[:HALO, :] = (total[:HALO, :] + from_left[...].astype(F32)).astype(BF)
     out_ref[HALO : rows - HALO, :] = total[HALO : rows - HALO, :].astype(BF)
     out_ref[rows - HALO :, :] = (total[rows - HALO :, :] + from_right[...].astype(F32)).astype(BF)
@@ -646,21 +651,19 @@
         us=3,
     )
     got1 = exchange(send1)
-    smid, m01, m2t, m3t, pool_v = call(
+    smid, m01, m2t, m3t = call(
         first_window_kernel,
-        [
-            (mid_nbrs, "h"), (mid_edge_w, "h"), (weights, "1"), (pool_mid, "r"), (agg, "r"),
-        ],
-        [
-            (shape((n1, n1)), "v"), (shape((d, 2 * d)), "v"), (shape((d, d)), "v"),
-            (shape((d, d)), "v"), (shape((n2, n1)), "v"),
-        ],
-        copies=1,
+        [(mid_nbrs, "h"), (mid_edge_w, "h"), (weights, "1"), (agg, "a")],
+        [
+            (shape((n1, n1)), "h"), (shape((d, 2 * d)), "h"), (shape((d, d)), "h"),
+            (shape((d, d)), "h"),
+        ],
         us=6,
+        mib=BIG,
     )
     send2, mhid, magg, sel, ext = call(
         functools.partial(mid_kernel, block_rows, chunk),
-        [(got1, "v"), (smid, "v"), (m01, "v"), (m2t, "v"), (m3t, "v"), (pool_v, "v")],
+        [(got1, "h"), (smid, "h"), (m01, "h"), (m2t, "h"), (m3t, "h"), (pool_mid, "h")],
         [
             (shape((peers, n2, d)), "r"), (shape((d, n1)), "h"), (shape((d, n1)), "h"),
             (shape((peers * chunk, n1)), "h"), (shape((peers, n2 + 16, d)), "r"),
@@ -668,67 +671,74 @@
         scratch=(pltpu.VMEM((peers * chunk, d), BF), pltpu.VMEM((n2, d), BF)),
         copies=peers + 1,
         us=3,
+        mib=BIG,
     )
     got2 = exchange(send2)
-    second = call(
+    sco, cot_all, mcot, mslope1, mslope2 = call(
         second_window_kernel,
         [
-            (ext, "h"), (mhid, "h"), (magg, "h"), (mid_nbrs, "h"), (mid_edge_w, "h"),
-            (mid_cotangent, "h"), (sel, "r"), (weights, "r"), (pool_mid, "r"),
-            (coarse_cotangent, "r"), (weights, "1"),
-        ],
-        [
-            (shape((total2, total2)), "v"), (shape((d, total2)), "v"), (shape((n1, n1)), "v"),
-            (shape((d, n1)), "v"), (shape((d, n1), F32), "v"), (shape((d, n1), F32), "v"),
-            (shape((peers * chunk, n1)), "v"), (shape((2, 4, d, d)), "v"),
-            (shape((n2, n1)), "v"), (shape((n2, d)), "v"),
+            (ext, "h"), (mhid, "h"), (magg, "h"), (mid_cotangent, "h"), (weights, "1"),
+        ],
+        [
+            (shape((total2, total2)), "h"), (shape((d, total2)), "h"), (shape((d, n1)), "h"),
+            (shape((d, n1), F32), "h"), (shape((d, n1), F32), "h"),
         ],
         scratch=(pltpu.VMEM((edges, total2), jnp.int32), pltpu.VMEM((edges, total2), F32)),
-        copies=4,
         us=6,
+        mib=BIG,
     )
     send3, gmid, msg, mfg, coarse_wg = call(
         coarse_kernel,
-        [(got2.reshape(total2, d), "v")] + [(x, "v") for x in second],
+        [
+            (got2.reshape(total2, d), "h"), (sco, "h"), (weights, "2"), (cot_all, "h"),
+            (coarse_cotangent, "h"), (pool_mid, "h"), (mcot, "h"), (weights, "1"),
+            (mslope2, "h"), (mslope1, "h"), (smid, "h"), (sel, "h"),
+        ],
         [
             (shape((peers * chunk, d)), "h"), (shape((d, n1)), "h"), (shape((d, n1)), "h"),
             (shape((d, n1)), "h"), (shape((4, d, d), F32), "h"),
         ],
         us=3,
+        mib=BIG,
     )
     got3 = exchange(send3.reshape(peers, chunk, d))
-    third = call(
+    mid_wg, hid, mid, outer, slope1, slope2, cot, pick, pool_b = call(
         functools.partial(third_window_kernel, tile_rows, 1.0 / math.sqrt(n1 * peers)),
         [
             (mhid, "h"), (magg, "h"), (gmid, "h"), (msg, "h"), (mfg, "h"), (features, "h"),
-            (fine_cotangent, "h"), (weights, "r"), (pool_fine, "h"), (place, "s"), (agg, "r"),
+            (fine_cotangent, "h"), (weights, "0"), (pool_fine, "h"), (place, "s"), (agg, "h"),
             (weights, "1"),
         ],
         [
-            (shape((4 * d, d)), "v"), (shape((d, n)), "v"), (shape((d, n)), "v"),
-            (shape((d, n)), "v"), (shape((d, n)), "v"), (shape((d, n), F32), "v"),
-            (shape((d, n), F32), "v"), (shape((d, n)), "v"),
-            (shape((tile_count * block_rows, peers * chunk)), "v"),
-            (shape((n // TILE, per, TILE)), "v"), (shape((4, d, d)), "v"),
-        ],
-        copies=2,
+            (shape((4 * d, d)), "h"), (shape((d, n)), "h"), (shape((d, n)), "h"),
+            (shape((d, n)), "h"), (shape((d, n), F32), "h"), (shape((d, n), F32), "h"),
+            (shape((d, n)), "h"), (shape((tile_count * block_rows, peers * chunk)), "h"),
+            (shape((n // TILE, per, TILE)), "h"),
+        ],
         us=6,
+        mib=BIG,
     )
     send4, g, fg = call(
         functools.partial(fine_grad_kernel, 1.0 / math.sqrt(n * peers)),
-        [(got3.reshape(peers * chunk, d), "v")] + [(x, "v") for x in third],
+        [
+            (got3.reshape(peers * chunk, d), "h"), (pick, "h"), (cot, "h"), (pool_b, "h"),
+            (weights, "0"), (slope2, "h"), (slope1, "h"), (hid, "h"), (agg, "h"), (mid, "h"),
+            (outer, "h"), (mid_wg, "h"),
+        ],
         [(shape((8 * d, d)), "h"), (shape((d, n)), "r"), (shape((d, n)), "r")],
         scratch=(pltpu.VMEM((d, n), BF), pltpu.VMEM((d, n), BF)),
         copies=2,
         us=4,
+        mib=BIG,
     )
     got4 = exchange(send4.reshape(peers, 8 * d // peers, d))
     rim_l, rim_r, spread = call(
         fine_spread_kernel,
         [(fine_offsets, "h"), (fine_edge_w, "h"), (weights, "0"), (g, "h"), (fg, "h")],
-        [(shape((HALO, d)), "v"), (shape((HALO, d)), "v"), (shape((n, d), F32), "v")],
+        [(shape((HALO, d)), "h"), (shape((HALO, d)), "h"), (shape((n, d), F32), "h")],
         scratch=(pltpu.VMEM((2, window, TILE), BF), pltpu.VMEM((n + 2 * HALO, d), F32)),
         us=6,
+        mib=BIG,
     )
     (send5,) = call(
         sum_kernel,
@@ -737,15 +747,17 @@
         scratch=(pltpu.VMEM((8 * d // peers, d), BF),),
         copies=peers,
         us=1,
+        mib=24,
     )
     got5 = exchange(send5)
     from_left = lax.ppermute(rim_r, "nodes", up)
     from_right = lax.ppermute(rim_l, "nodes", down)
     (feature_grads,) = call(
         join_kernel,
-        [(spread, "v"), (from_left, "v"), (from_right, "v")],
-        [(shape((n, d)), "v")],
+        [(spread, "h"), (from_left, "h"), (from_right, "h")],
+        [(shape((n, d)), "h")],
         us=1,
+        mib=BIG,
     )
     weight_grads = jnp.concatenate(
         [got5.reshape(2, 4, d, d).astype(F32), coarse_wg[None]], axis=0

time: 140 us -> 114 us (0.81)
  local copies, waits for them, and re-layouts: 47.5 us -> 8.74 us
  Pallas kernels: 31.9 us -> 42.3 us
  waiting for transfers between devices: 18.8 us -> 25.5 us
  starting transfers between devices: 38.1 us -> 34 us
    unnamed x144 -> x42, local copies, waits for them, and re-layouts: 46.6 us -> 7.81 us
    pallas_call x11, Pallas kernels: 31.9 us -> 42.3 us  [call(): pl.pallas_call(body, out_shape=[s for s, _ in outs], in_specs=[{'v': VM,...]
    all_to_all x5, waiting for transfers between devices: 14.4 us -> 21.2 us  [exchange(): return lax.all_to_all(x, 'nodes', split_axis=0, concat_axis=0, tiled=True)]
    all_to_all x5, starting transfers between devices: 26.2 us -> 22 us  [exchange(): return lax.all_to_all(x, 'nodes', split_axis=0, concat_axis=0, tiled=True)]
  transfers between devices with their start and end apart: 9 -> 9, of which waited for: 3 -> 5; matrix products, arithmetic and copies ran while one was open for 0% -> 0% of each run, Pallas kernels for 13% -> 22%
where the time goes in v3:
time: 114 us; the launch traced here: 112 us
  Pallas kernels  42.3 us (37%)
  starting transfers between devices  34 us (30%)
  waiting for transfers between devices  25.5 us (22%)
  local copies, waits for them, and re-layouts  8.74 us (8%)
    pallas_call x11, Pallas kernels, call(): pl.pallas_call(body, out_shape=[s for s, _ in outs], in_specs=[{'v': VM,...  42.3 us
    all_to_all x5, starting transfers between devices, exchange(): return lax.all_to_all(x, 'nodes', split_axis=0, concat_axis=0, tiled=True)  22 us
    all_to_all x5, waiting for transfers between devices, exchange(): return lax.all_to_all(x, 'nodes', split_axis=0, concat_axis=0, tiled=True)  21.2 us
    unnamed x42, local copies, waits for them, and re-layouts  7.81 us
    ppermute x1, starting transfers between devices, per_device(): left = lax.ppermute(features[n - HALO:], 'nodes', up)  4.49 us
    ppermute x1, waiting for transfers between devices, per_device(): from_right = lax.ppermute(rim_l, 'nodes', down)  4.31 us
    ppermute x1, starting transfers between devices, per_device(): from_left = lax.ppermute(rim_r, 'nodes', up)  3.55 us
  transfers between devices with their start and end apart: 9, of which 5 were waited for; matrix products, arithmetic and copies ran while one was open for 0% of the time, Pallas kernels for 22%

profile of v3, /device:TPU:1, one launch (start us, length us, event | category | flops | bytes accessed | tf_op | source)
XLA Modules:
  0.0 112.5 jit_solution(3780269178911183978)
XLA Ops:
  1.6 2.0 %collective-permute-start.1 = (bf16[256,128]{1,0:T(8,128)(2,1)S(1)}, bf16[256,128]{1,0:T(8,128)(2,1)S(1)}, u32[]{:S(2)}, u32[]{:S(2)}) collective-permute-start(bf16[256,128]{1,0:T(8,128)(2,1)S(1)} %get-tuple-element.94), channel_id=1, source_target_pairs={{1,0},{2,1},{3,2},{4,3},{5,4},{6,5},{7,6},{8,7},{9,8},{10,9},{11,1... | collective-permute-start | bytes 196616 | tf_op jit(solution)/shard_map/ppermute | solution.py:613
  3.6 4.5 %collective-permute-start = (bf16[256,128]{1,0:T(8,128)(2,1)S(1)}, bf16[256,128]{1,0:T(8,128)(2,1)S(1)}, u32[]{:S(2)}, u32[]{:S(2)}) collective-permute-start(bf16[256,128]{1,0:T(8,128)(2,1)S(1)} %get-tuple-element.95), channel_id=1, source_target_pairs={{0,1},{1,2},{2,3},{3,4},{4,5},{5,6},{6,7},{7,8},{8,9},{9,10},{10,1... | collective-permute-start | bytes 196616 | tf_op jit(solution)/shard_map/ppermute | solution.py:612
  10.3 6.9 %shard_map.158 = (bf16[2,768,256]{2,1,0:T(8,128)(2,1)S(1)}, bf16[2,128,512]{2,1,0:T(8,128)(2,1)S(1)}, bf16[128,256]{1,0:T(8,128)(2,1)S(1)}, bf16[128,128]{1,0:T(...) custom-call(s32[8,2048]{1,0:T(8,128)S(1)} %copy-done.3, ...), custom_call_target="tpu_custom_call" | custom-call | bytes 18000000 | tf_op jit(solution)/shard_map/pallas_call | solution.py:164
  17.7 2.4 %shard_map.159 = (bf16[16,96,128]{2,1,0:T(8,128)(2,1)}, bf16[128,2048]{1,0:T(8,128)(2,1)S(1)}) custom-call(bf16[256,128]{1,0:T(8,128)(2,1)S(1)} %collective-permute-done.refs_0_, bf16[256,128]{1,0:T(8,128)(2,1)S(1)} %collective-permute-done.1.refs_1_, bf16[2,768,256]{2,1,0:T(8,128)(2,1)S(1)} %get-tuple-element.48.refs_2_, ...), custom_call_target="tpu_custom_call" | custom-call | bytes 9000000 | tf_op jit(solution)/shard_map/pallas_call | solution.py:164
  21.0 5.8 %all-to-all-start = ((bf16[16,96,128]{2,1,0:T(8,128)(2,1)}), bf16[16,96,128]{2,1,0:T(8,128)(2,1)S(1)}, u32[]{:S(2)}, u32[]{:S(2)}) async-start(bf16[16,96,128]{2,1,0:T(8,128)(2,1)} %get-tuple-element.57), calls=%async_computation | async-start | bytes 786432 | tf_op jit(solution)/shard_map/all_to_all | solution.py:575
  26.7 2.0 %shard_map.160 = (bf16[512,512]{1,0:T(8,128)(2,1)}, bf16[128,256]{1,0:T(8,128)(2,1)}, bf16[128,128]{1,0:T(8,128)(2,1)}, bf16[128,128]{1,0:T(8,128)(2,1)}) custom-call(s32[8,512]{1,0:T(8,128)} %refs_0_.4, f32[8,512]{1,0:T(8,128)} %refs_1_.4, bf16[3,4,128,128]{3,2,1,0:T(8,128)(2,1)} %refs_2_.7, bf16[128,2048]{1,0:T(8,128)(2,1)} %copy-done.1), custom_call_target="tpu_custom_call" | custom-call | bytes 18000000 | tf_op jit(solution)/shard_map/pallas_call | solution.py:164
  28.7 9.9 %all-to-all-done.refs_0_ = bf16[16,96,128]{2,1,0:T(8,128)(2,1)S(1)} async-done(((bf16[16,96,128]{2,1,0:T(8,128)(2,1)}), bf16[16,96,128]{2,1,0:T(8,128)(2,1)S(1)}, u32[]{:S(2)}, u32[]{:S(2)}) %all-to-all-start) | async-done | bytes 393248 | tf_op jit(solution)/shard_map/all_to_all | solution.py:575
  39.4 3.4 %shard_map.161 = (bf16[16,16,128]{2,1,0:T(8,128)(2,1)}, bf16[128,512]{1,0:T(8,128)(2,1)}, bf16[128,512]{1,0:T(8,128)(2,1)}, bf16[1024,512]{1,0:T(8,128)(2,1)}, bf16[16,32,128]{2,1,0:T(8,128)(2,1)}) custom-call(bf16[16,96,128]{2,1,0:T(8,128)(2,1)} %copy-done.14, bf16[512,512]{1,0:T(8,128)(2,1)} %get-tuple-element.59.refs_1_.refs_10_, ...), custom_call_target="tpu_custom_call" | custom-call | bytes 9000000 | tf_op jit(solution)/shard_map/pallas_call | solution.py:164
  42.8 3.8 %all-to-all-start.1 = ((bf16[16,16,128]{2,1,0:T(8,128)(2,1)}), bf16[16,16,128]{2,1,0:T(8,128)(2,1)S(1)}, u32[]{:S(2)}, u32[]{:S(2)}) async-start(bf16[16,16,128]{2,1,0:T(8,128)(2,1)} %get-tuple-element.63), calls=%async_computation.1 | async-start | bytes 131072 | tf_op jit(solution)/shard_map/all_to_all | solution.py:575
  46.6 2.8 %shard_map.162 = (bf16[256,256]{1,0:T(8,128)(2,1)}, bf16[128,256]{1,0:T(8,128)(2,1)}, bf16[128,512]{1,0:T(8,128)(2,1)}, f32[128,512]{1,0:T(8,128)}, f32[128,512]{1,0:T(8,128)}) custom-call(bf16[16,32,128]{2,1,0:T(8,128)(2,1)} %get-tuple-element.64.refs_0_, bf16[128,512]{1,0:T(8,128)(2,1)} %get-tuple-element.65.refs_1_.refs_0_, ...), custom_call_target="tpu_custom_call" | custom-call | bytes 18000000 | tf_op jit(solution)/shard_map/pallas_call | solution.py:164
  49.5 3.2 %all-to-all-done.1 = bf16[16,16,128]{2,1,0:T(8,128)(2,1)S(1)} async-done(((bf16[16,16,128]{2,1,0:T(8,128)(2,1)}), bf16[16,16,128]{2,1,0:T(8,128)(2,1)S(1)}, u32[]{:S(2)}, u32[]{:S(2)}) %all-to-all-start.1) | async-done | bytes 65568 | tf_op jit(solution)/shard_map/all_to_all | solution.py:575
  53.3 4.5 %shard_map.163 = (bf16[1024,128]{1,0:T(8,128)(2,1)}, bf16[128,512]{1,0:T(8,128)(2,1)}, bf16[128,512]{1,0:T(8,128)(2,1)}, bf16[128,512]{1,0:T(8,128)(2,1)}, f32[4,128,128]{2,1,0:T(8,128)}) custom-call(bf16[256,128]{1,0:T(8,128)(2,1)} %bitcast.12, bf16[256,256]{1,0:T(8,128)(2,1)} %get-tuple-element.67.refs_1_, bf16[3,4,128,128]{3,2,1,0:T(8,128)(2,1)} %refs_2_.7, ...), custom_call_target="tpu_custom_call" | custom-call | bytes 9000000 | tf_op jit(solution)/shard_map/pallas_call | solution.py:164
  57.8 4.3 %all-to-all-start.2 = ((bf16[16,64,128]{2,1,0:T(8,128)(2,1)}), bf16[16,64,128]{2,1,0:T(8,128)(2,1)S(1)}, u32[]{:S(2)}, u32[]{:S(2)}) async-start(bf16[16,64,128]{2,1,0:T(8,128)(2,1)} %bitcast.13), calls=%async_computation.2 | async-start | bytes 524288 | tf_op jit(solution)/shard_map/all_to_all | solution.py:575
  62.1 5.6 %shard_map.164 = (bf16[512,128]{1,0:T(8,128)(2,1)}, bf16[128,2048]{1,0:T(8,128)(2,1)}, bf16[128,2048]{1,0:T(8,128)(2,1)}, bf16[128,2048]{1,0:T(8,128)(2,1)}, f32...) custom-call(bf16[128,512]{1,0:T(8,128)(2,1)} %get-tuple-element.65.r, ...), custom_call_target="tpu_custom_call" | custom-call | bytes 18000000 | tf_op jit(solution)/shard_map/pallas_call | solution.py:164
  67.7 3.9 %all-to-all-done.2 = bf16[16,64,128]{2,1,0:T(8,128)(2,1)S(1)} async-done(((bf16[16,64,128]{2,1,0:T(8,128)(2,1)}), bf16[16,64,128]{2,1,0:T(8,128)(2,1)S(1)}, u32[]{:S(2)}, u32[]{:S(2)}) %all-to-all-start.2) | async-done | bytes 262176 | tf_op jit(solution)/shard_map/all_to_all | solution.py:575
  72.4 6.2 %shard_map.165 = (bf16[1024,128]{1,0:T(8,128)(2,1)}, bf16[128,2048]{1,0:T(8,128)(2,1)}, bf16[128,2048]{1,0:T(8,128)(2,1)}) custom-call(bf16[1024,128]{1,0:T(8,128)(2,1)} %bitcast.11, bf16[512,1024]{1,0:T(8,128)(2,1)} %get-tuple-element.78.refs_1_, bf16[128,2048]{1,0:T(8,128)(2,1)} %get-tuple-element.79.refs_2_, ...), custom_call_target="tpu_custom_call" | custom-call | bytes 12000000 | tf_op jit(solution)/shard_map/pallas_call | solution.py:164
  78.6 4.0 %all-to-all-start.3 = ((bf16[16,64,128]{2,1,0:T(8,128)(2,1)}), bf16[16,64,128]{2,1,0:T(8,128)(2,1)S(1)}, u32[]{:S(2)}, u32[]{:S(2)}) async-start(bf16[16,64,128]{2,1,0:T(8,128)(2,1)} %bitcast.14), calls=%async_computation.3 | async-start | bytes 524288 | tf_op jit(solution)/shard_map/all_to_all | solution.py:575
  82.6 5.4 %shard_map.166 = (bf16[256,128]{1,0:T(8,128)(2,1)}, bf16[256,128]{1,0:T(8,128)(2,1)}, f32[2048,128]{1,0:T(8,128)}) custom-call(s32[8,2048]{1,0:T(8,128)} %refs_0_.5, f32[8,2048]{1,0:T(8,128)} %refs_1_.5, bf16[3,4,128,128]{3,2,1,0:T(8,128)(2,1)} %refs_2_.7, bf16[128,2048]{1,0:T(8,128)(2,1)} %get-tuple-element.87.refs_3_, ...), custom_call_target="tpu_custom_call" | custom-call | bytes 18000000 | tf_op jit(solution)/shard_map/pallas_call | solution.py:164
  88.0 4.1 %all-to-all-done.3.refs_0_ = bf16[16,64,128]{2,1,0:T(8,128)(2,1)S(1)} async-done(((bf16[16,64,128]{2,1,0:T(8,128)(2,1)}), bf16[16,64,128]{2,1,0:T(8,128)(2,1)S(1)}, u32[]{:S(2)}, u32[]{:S(2)}) %all-to-all-start.3) | async-done | bytes 262176 | tf_op jit(solution)/shard_map/all_to_all | solution.py:575
  93.9 4.1 %all-to-all-start.4 = ((bf16[16,64,128]{2,1,0:T(8,128)(2,1)}), bf16[16,64,128]{2,1,0:T(8,128)(2,1)S(1)}, u32[]{:S(2)}, u32[]{:S(2)}) async-start(bf16[16,64,128]{2,1,0:T(8,128)(2,1)} %shard_map.168), calls=%async_computation.4 | async-start | bytes 524288 | tf_op jit(solution)/shard_map/all_to_all | solution.py:575
  98.0 3.5 %collective-permute-start.2 = (bf16[256,128]{1,0:T(8,128)(2,1)S(1)}, bf16[256,128]{1,0:T(8,128)(2,1)S(1)}, u32[]{:S(2)}, u32[]{:S(2)}) collective-permute-start(bf16[256,128]{1,0:T(8,128)(2,1)S(1)} %copy-done.20), channel_id=1, source_target_pairs={{0,1},{1,2},{2,3},{3,4},{4,5},{5,6},{6,7},{7,8},{8,9},{9,10},{10,1... | collective-permute-start | bytes 196616 | tf_op jit(solution)/shard_map/ppermute | solution.py:753
  101.6 1.9 %collective-permute-start.3 = (bf16[256,128]{1,0:T(8,128)(2,1)S(1)}, bf16[256,128]{1,0:T(8,128)(2,1)S(1)}, u32[]{:S(2)}, u32[]{:S(2)}) collective-permute-start(bf16[256,128]{1,0:T(8,128)(2,1)S(1)} %copy-done.7), channel_id=1, source_target_pairs={{1,0},{2,1},{3,2},{4,3},{5,4},{6,5},{7,6},{8,7},{9,8},{10,9},{11,1... | collective-permute-start | bytes 196616 | tf_op jit(solution)/shard_map/ppermute | solution.py:754
  103.5 4.3 %collective-permute-done.3.refs_2_ = bf16[256,128]{1,0:T(8,128)(2,1)S(1)} collective-permute-done((bf16[256,128]{1,0:T(8,128)(2,1)S(1)}, bf16[256,128]{1,0:T(8,128)(2,1)S(1)}, u32[]{:S(2)}, u32[]{:S(2)}) %collective-permute-start.3) | collective-permute-done | bytes 65568 | tf_op jit(solution)/shard_map/ppermute | solution.py:754
  108.5 2.1 %shard_map.167 = bf16[2048,128]{1,0:T(8,128)(2,1)} custom-call(f32[2048,128]{1,0:T(8,128)} %get-tuple-element.89.refs_0_, bf16[256,128]{1,0:T(8,128)(2,1)} %copy-done.18, bf16[256,128]{1,0:T(8,128)(2,1)} %copy-done.19), custom_call_target="tpu_custom_call" | custom-call | bytes 3000000 | tf_op jit(solution)/shard_map/pallas_call | solution.py:164
  (50 shorter events, 10.6 us)
Async XLA Ops:
  0.6 7.5 %copy-start.5 = (bf16[8,2048]{1,0:T(8,128)(2,1)S(1)}, bf16[8,2048]{1,0:T(8,128)(2,1)}, u32[]{:S(2)}) copy-start(bf16[8,2048]{1,0:T(8,128)(2,1)} %refs_8_.3) | copy-start | bytes 98308
  0.6 7.5 %copy-start.4 = (f32[8,2048]{1,0:T(8,128)S(1)}, f32[8,2048]{1,0:T(8,128)}, u32[]{:S(2)}) copy-start(f32[8,2048]{1,0:T(8,128)} %refs_1_.5) | copy-start | bytes 196612
  0.7 7.5 %copy-start.3 = (s32[8,2048]{1,0:T(8,128)S(1)}, s32[8,2048]{1,0:T(8,128)}, u32[]{:S(2)}) copy-start(s32[8,2048]{1,0:T(8,128)} %refs_0_.5) | copy-start | bytes 196612
  0.7 7.5 %copy-start.9 = (s32[8,16]{1,0:T(8,128)S(1)}, s32[8,16]{1,0:T(8,128)}, u32[]{:S(2)}) copy-start(s32[8,16]{1,0:T(8,128)} %refs_7_.3) | copy-start | bytes 1540
  0.7 7.5 %copy-start.10 = (f32[8,16]{1,0:T(8,128)S(1)}, f32[8,16]{1,0:T(8,128)}, u32[]{:S(2)}) copy-start(f32[8,16]{1,0:T(8,128)} %refs_8_.2) | copy-start | bytes 1540
  1.6 6.6 %copy-start.8 = (bf16[16,128]{1,0:T(8,128)(2,1)S(1)}, bf16[16,128]{1,0:T(8,128)(2,1)}, u32[]{:S(2)}) copy-start(bf16[16,128]{1,0:T(8,128)(2,1)} %refs_4_.6) | copy-start | bytes 12292
  1.6 15.6 %collective-permute-start.1 = (bf16[256,128]{1,0:T(8,128)(2,1)S(1)}, bf16[256,128]{1,0:T(8,128)(2,1)S(1)}, u32[]{:S(2)}, u32[]{:S(2)}) collective-permute-start(bf16[256,128]{1,0:T(8,128)(2,1)S(1)} %get-tuple-element.94), channel_id=1, source_target_pairs={{1,0},{2,1},{3,2},{4,3},{5,4},{6,5},{7,6},{8,7},{9,8},{10,9},{11,1... | collective-permute-start | bytes 196616 | tf_op jit(solution)/shard_map/ppermute | solution.py:613
  3.6 4.6 %copy-start.11 = (s32[64,1]{0,1:T(1,128)S(1)}, s32[64,1]{0,1:T(1,128)}, u32[]{:S(2)}) copy-start(s32[64,1]{0,1:T(1,128)} %param.23) | copy-start | bytes 772
  3.6 4.6 %copy-start.12 = (s32[64]{0:T(128)S(1)}, s32[64]{0:T(128)}, u32[]{:S(2)}) copy-start(s32[64]{0:T(128)} %refs_6_.2) | copy-start | bytes 772
  3.6 13.6 %collective-permute-start = (bf16[256,128]{1,0:T(8,128)(2,1)S(1)}, bf16[256,128]{1,0:T(8,128)(2,1)S(1)}, u32[]{:S(2)}, u32[]{:S(2)}) collective-permute-start(bf16[256,128]{1,0:T(8,128)(2,1)S(1)} %get-tuple-element.95), channel_id=1, source_target_pairs={{0,1},{1,2},{2,3},{3,4},{4,5},{5,6},{6,7},{7,8},{8,9},{9,10},{10,1... | collective-permute-start | bytes 196616 | tf_op jit(solution)/shard_map/ppermute | solution.py:612
  8.2 1.0 copy-start
  9.2 1.0 copy-start.2
  21.0 17.7 %all-to-all-start = ((bf16[16,96,128]{2,1,0:T(8,128)(2,1)}), bf16[16,96,128]{2,1,0:T(8,128)(2,1)S(1)}, u32[]{:S(2)}, u32[]{:S(2)}) async-start(bf16[16,96,128]{2,1,0:T(8,128)(2,1)} %get-tuple-element.57), calls=%async_computation | async-start | bytes 786432 | tf_op jit(solution)/shard_map/all_to_all | solution.py:575
  42.8 9.9 %all-to-all-start.1 = ((bf16[16,16,128]{2,1,0:T(8,128)(2,1)}), bf16[16,16,128]{2,1,0:T(8,128)(2,1)S(1)}, u32[]{:S(2)}, u32[]{:S(2)}) async-start(bf16[16,16,128]{2,1,0:T(8,128)(2,1)} %get-tuple-element.63), calls=%async_computation.1 | async-start | bytes 131072 | tf_op jit(solution)/shard_map/all_to_all | solution.py:575
  57.8 13.8 %all-to-all-start.2 = ((bf16[16,64,128]{2,1,0:T(8,128)(2,1)}), bf16[16,64,128]{2,1,0:T(8,128)(2,1)S(1)}, u32[]{:S(2)}, u32[]{:S(2)}) async-start(bf16[16,64,128]{2,1,0:T(8,128)(2,1)} %bitcast.13), calls=%async_computation.2 | async-start | bytes 524288 | tf_op jit(solution)/shard_map/all_to_all | solution.py:575
  78.6 13.6 %all-to-all-start.3 = ((bf16[16,64,128]{2,1,0:T(8,128)(2,1)}), bf16[16,64,128]{2,1,0:T(8,128)(2,1)S(1)}, u32[]{:S(2)}, u32[]{:S(2)}) async-start(bf16[16,64,128]{2,1,0:T(8,128)(2,1)} %bitcast.14), calls=%async_computation.3 | async-start | bytes 524288 | tf_op jit(solution)/shard_map/all_to_all | solution.py:575
  92.1 0.8 copy-start.6
  93.8 4.2 %copy-start.20 = (bf16[256,128]{1,0:T(8,128)(2,1)S(1)}, bf16[256,128]{1,0:T(8,128)(2,1)}, u32[]{:S(2)}) copy-start(bf16[256,128]{1,0:T(8,128)(2,1)} %get-tuple-element.90) | copy-start | bytes 196612
  93.9 7.7 %copy-start.7 = (bf16[256,128]{1,0:T(8,128)(2,1)S(1)}, bf16[256,128]{1,0:T(8,128)(2,1)}, u32[]{:S(2)}) copy-start(bf16[256,128]{1,0:T(8,128)(2,1)} %get-tuple-element.91.refs_1_) | copy-start | bytes 196612
  93.9 16.7 %all-to-all-start.4 = ((bf16[16,64,128]{2,1,0:T(8,128)(2,1)}), bf16[16,64,128]{2,1,0:T(8,128)(2,1)S(1)}, u32[]{:S(2)}, u32[]{:S(2)}) async-start(bf16[16,64,128]{2,1,0:T(8,128)(2,1)} %shard_map.168), calls=%async_computation.4 | async-start | bytes 524288 | tf_op jit(solution)/shard_map/all_to_all | solution.py:575
  98.0 5.5 %collective-permute-start.2 = (bf16[256,128]{1,0:T(8,128)(2,1)S(1)}, bf16[256,128]{1,0:T(8,128)(2,1)S(1)}, u32[]{:S(2)}, u32[]{:S(2)}) collective-permute-start(bf16[256,128]{1,0:T(8,128)(2,1)S(1)} %copy-done.20), channel_id=1, source_target_pairs={{0,1},{1,2},{2,3},{3,4},{4,5},{5,6},{6,7},{7,8},{8,9},{9,10},{10,1... | collective-permute-start | bytes 196616 | tf_op jit(solution)/shard_map/ppermute | solution.py:753
  101.6 6.3 %collective-permute-start.3 = (bf16[256,128]{1,0:T(8,128)(2,1)S(1)}, bf16[256,128]{1,0:T(8,128)(2,1)S(1)}, u32[]{:S(2)}, u32[]{:S(2)}) collective-permute-start(bf16[256,128]{1,0:T(8,128)(2,1)S(1)} %copy-done.7), channel_id=1, source_target_pairs={{1,0},{2,1},{3,2},{4,3},{5,4},{6,5},{7,6},{8,7},{9,8},{10,9},{11,1... | collective-permute-start | bytes 196616 | tf_op jit(solution)/shard_map/ppermute | solution.py:754
  103.5 4.3 %copy-start.18 = (bf16[256,128]{1,0:T(8,128)(2,1)}, bf16[256,128]{1,0:T(8,128)(2,1)S(1)}, u32[]{:S(2)}) copy-start(bf16[256,128]{1,0:T(8,128)(2,1)S(1)} %collective-permute-done.2.refs_1_) | copy-start | bytes 196612
  110.6 1.0 copy-start.17
  (6 other events, 4.0 us)

commit v4 on v3

--- a/solution.py
+++ b/solution.py
@@ -10,13 +10,11 @@
 
 HALO = 256
 TILE = 256
-BIG = 56
 BF = jnp.bfloat16
 F32 = jnp.float32
 
 VM = pl.BlockSpec(memory_space=pltpu.VMEM)
 HB = pl.BlockSpec(memory_space=pltpu.HBM)
-ANY = pl.BlockSpec(memory_space=pl.ANY)
 
 
 def dot(a, b):
@@ -163,8 +161,10 @@
 
     return pl.pallas_call(
         body,
-        out_shape=[s for s, _ in outs],
-        in_specs=[{"v": VM, "a": ANY}.get(kind, HB) for _, kind in ins],
+        out_shape=[
+            s if kind == "v" else pltpu.HBM(s.shape, s.dtype) for s, kind in outs
+        ],
+        in_specs=[VM if kind == "v" else HB for _, kind in ins],
         out_specs=[VM if kind == "v" else HB for _, kind in outs],
         scratch_shapes=stage
         + list(scratch)
@@ -173,7 +173,10 @@
         cost_estimate=pl.CostEstimate(
             flops=0, bytes_accessed=int(us * 3_000_000), transcendentals=0
         ),
-    )(*[a for a, _ in ins])
+    )(*[
+        a if kind == "v" else pltpu.with_memory_space_constraint(a, pltpu.HBM)
+        for a, kind in ins
+    ])
 
 
 def fine_tile(h_t, window_t, s, weights, pool):
@@ -331,7 +334,6 @@
     peers = got.shape[0]
     nodes = smid.shape[0]
     n2 = pool_mid.shape[0]
-    need(0)
     io.start(got.at[:, pl.ds(chunk, n2 + 16), :], ext_ref)
     rows = [got[p, chunk + n2 : chunk + n2 + 16, :].astype(F32)[8:9, :] for p in range(peers)]
     keys = jnp.transpose(jnp.concatenate(rows, axis=0))
@@ -403,7 +405,6 @@
     n2 = cot_my.shape[0]
     me = lax.axis_index("nodes")
     width = min(TILE, nodes)
-    need(0)
     hidden = jnp.transpose(got[...])
     need(1, 2, 3)
     w01, w2t, _ = forward_weights(w2)
@@ -501,7 +502,7 @@
     got, pick, cot, pool, w, slope2, slope1, hid, agg, mid, outer, mid_wg = ins
     send_ref, g_out, fg_out = outs
     d, rows = hid.shape
-    need(0, 1)
+    need(1)
     blocks = dot(pick[...], got[...]).astype(BF)
     need()
     send_ref[4 * d : 8 * d, :] = mid_wg[...]
@@ -569,6 +570,16 @@
     out_ref[:HALO, :] = (total[:HALO, :] + from_left[...].astype(F32)).astype(BF)
     out_ref[HALO : rows - HALO, :] = total[HALO : rows - HALO, :].astype(BF)
     out_ref[rows - HALO :, :] = (total[rows - HALO :, :] + from_right[...].astype(F32)).astype(BF)
+
+
+def gather_kernel(io, need, flush, ins, outs, wide):
+    summed, coarse = ins
+    out_ref = outs[0]
+    io.start(coarse, out_ref.at[pl.ds(8, 4)])
+    for half in range(2):
+        wide[4 * half : 4 * half + 4] = summed[4 * half : 4 * half + 4].astype(F32)
+        part = pl.ds(4 * half, 4)
+        io.start(wide.at[part], out_ref.at[part])
 
 
 def exchange(x):
@@ -653,17 +664,16 @@
     got1 = exchange(send1)
     smid, m01, m2t, m3t = call(
         first_window_kernel,
-        [(mid_nbrs, "h"), (mid_edge_w, "h"), (weights, "1"), (agg, "a")],
+        [(mid_nbrs, "h"), (mid_edge_w, "h"), (weights, "1"), (agg, "r")],
         [
             (shape((n1, n1)), "h"), (shape((d, 2 * d)), "h"), (shape((d, d)), "h"),
             (shape((d, d)), "h"),
         ],
         us=6,
-        mib=BIG,
     )
     send2, mhid, magg, sel, ext = call(
         functools.partial(mid_kernel, block_rows, chunk),
-        [(got1, "h"), (smid, "h"), (m01, "h"), (m2t, "h"), (m3t, "h"), (pool_mid, "h")],
+        [(got1, "v"), (smid, "h"), (m01, "h"), (m2t, "h"), (m3t, "h"), (pool_mid, "h")],
         [
             (shape((peers, n2, d)), "r"), (shape((d, n1)), "h"), (shape((d, n1)), "h"),
             (shape((peers * chunk, n1)), "h"), (shape((peers, n2 + 16, d)), "r"),
@@ -671,7 +681,6 @@
         scratch=(pltpu.VMEM((peers * chunk, d), BF), pltpu.VMEM((n2, d), BF)),
         copies=peers + 1,
         us=3,
-        mib=BIG,
     )
     got2 = exchange(send2)
     sco, cot_all, mcot, mslope1, mslope2 = call(
@@ -685,12 +694,11 @@
         ],
         scratch=(pltpu.VMEM((edges, total2), jnp.int32), pltpu.VMEM((edges, total2), F32)),
         us=6,
-        mib=BIG,
     )
     send3, gmid, msg, mfg, coarse_wg = call(
         coarse_kernel,
         [
-            (got2.reshape(total2, d), "h"), (sco, "h"), (weights, "2"), (cot_all, "h"),
+            (got2.reshape(total2, d), "v"), (sco, "h"), (weights, "2"), (cot_all, "h"),
             (coarse_cotangent, "h"), (pool_mid, "h"), (mcot, "h"), (weights, "1"),
             (mslope2, "h"), (mslope1, "h"), (smid, "h"), (sel, "h"),
         ],
@@ -699,7 +707,6 @@
             (shape((d, n1)), "h"), (shape((4, d, d), F32), "h"),
         ],
         us=3,
-        mib=BIG,
     )
     got3 = exchange(send3.reshape(peers, chunk, d))
     mid_wg, hid, mid, outer, slope1, slope2, cot, pick, pool_b = call(
@@ -716,12 +723,11 @@
             (shape((n // TILE, per, TILE)), "h"),
         ],
         us=6,
-        mib=BIG,
     )
     send4, g, fg = call(
         functools.partial(fine_grad_kernel, 1.0 / math.sqrt(n * peers)),
         [
-            (got3.reshape(peers * chunk, d), "h"), (pick, "h"), (cot, "h"), (pool_b, "h"),
+            (got3.reshape(peers * chunk, d), "v"), (pick, "h"), (cot, "h"), (pool_b, "h"),
             (weights, "0"), (slope2, "h"), (slope1, "h"), (hid, "h"), (agg, "h"), (mid, "h"),
             (outer, "h"), (mid_wg, "h"),
         ],
@@ -729,7 +735,6 @@
         scratch=(pltpu.VMEM((d, n), BF), pltpu.VMEM((d, n), BF)),
         copies=2,
         us=4,
-        mib=BIG,
     )
     got4 = exchange(send4.reshape(peers, 8 * d // peers, d))
     rim_l, rim_r, spread = call(
@@ -738,30 +743,33 @@
         [(shape((HALO, d)), "h"), (shape((HALO, d)), "h"), (shape((n, d), F32), "h")],
         scratch=(pltpu.VMEM((2, window, TILE), BF), pltpu.VMEM((n + 2 * HALO, d), F32)),
         us=6,
-        mib=BIG,
     )
     (send5,) = call(
         sum_kernel,
-        [(got4, "v"), (rim_l, "a")],
+        [(got4, "v"), (rim_l, "r")],
         [(shape((peers, 8 * d // peers, d)), "r")],
         scratch=(pltpu.VMEM((8 * d // peers, d), BF),),
         copies=peers,
         us=1,
-        mib=24,
     )
     got5 = exchange(send5)
     from_left = lax.ppermute(rim_r, "nodes", up)
     from_right = lax.ppermute(rim_l, "nodes", down)
     (feature_grads,) = call(
         join_kernel,
-        [(spread, "h"), (from_left, "h"), (from_right, "h")],
+        [(spread, "h"), (from_left, "v"), (from_right, "v")],
         [(shape((n, d)), "h")],
         us=1,
-        mib=BIG,
-    )
-    weight_grads = jnp.concatenate(
-        [got5.reshape(2, 4, d, d).astype(F32), coarse_wg[None]], axis=0
-    )
+    )
+    (weight_grads,) = call(
+        gather_kernel,
+        [(got5.reshape(8, d, d), "v"), (coarse_wg, "r")],
+        [(shape((12, d, d), F32), "r")],
+        scratch=(pltpu.VMEM((8, d, d), F32),),
+        copies=3,
+        us=1,
+    )
+    weight_grads = weight_grads.reshape(3, 4, d, d)
     return (feature_grads, weight_grads)
 
 

time: 114 us -> 113 us (level)
  Pallas kernels: 42.3 us -> 50.3 us
  local copies, waits for them, and re-layouts: 8.74 us -> 0.89 us
    pallas_call x11 -> x12, Pallas kernels: 42.3 us -> 50.3 us  [call(): pl.pallas_call(body, out_shape=[s if kind == 'v' else pltpu.HBM(s.shape,...]
    unnamed x42 -> x4, local copies, waits for them, and re-layouts: 7.81 us -> 0.01 us
where the time goes in v4:
time: 113 us; the launch traced here: 112 us
  Pallas kernels  50.3 us (45%)
  starting transfers between devices  34.2 us (30%)
  waiting for transfers between devices  25.5 us (23%)
    pallas_call x12, Pallas kernels, call(): pl.pallas_call(body, out_shape=[s if kind == 'v' else pltpu.HBM(s.shape,...  50.3 us
    all_to_all x5, starting transfers between devices, exchange(): return lax.all_to_all(x, 'nodes', split_axis=0, concat_axis=0, tiled=True)  22.2 us
    all_to_all x5, waiting for transfers between devices, exchange(): return lax.all_to_all(x, 'nodes', split_axis=0, concat_axis=0, tiled=True)  21.2 us
    ppermute x1, starting transfers between devices, per_device(): left = lax.ppermute(features[n - HALO:], 'nodes', up)  4.49 us
    ppermute x1, waiting for transfers between devices, per_device(): from_right = lax.ppermute(rim_l, 'nodes', down)  4.32 us
    ppermute x1, starting transfers between devices, per_device(): from_left = lax.ppermute(rim_r, 'nodes', up)  3.55 us
  transfers between devices with their start and end apart: 9, of which 5 were waited for; matrix products, arithmetic and copies ran while one was open for 0% of the time, Pallas kernels for 22%

profile of v4, /device:TPU:1, one launch (start us, length us, event | category | flops | bytes accessed | tf_op | source)
XLA Modules:
  0.0 111.9 jit_solution(16850394609510874934)
XLA Ops:
  1.5 2.0 %collective-permute-start.1 = (bf16[256,128]{1,0:T(8,128)(2,1)S(1)}, bf16[256,128]{1,0:T(8,128)(2,1)S(1)}, u32[]{:S(2)}, u32[]{:S(2)}) collective-permute-start(bf16[256,128]{1,0:T(8,128)(2,1)S(1)} %get-tuple-element.94), channel_id=1, source_target_pairs={{1,0},{2,1},{3,2},{4,3},{5,4},{6,5},{7,6},{8,7},{9,8},{10,9},{11,1... | collective-permute-start | bytes 196616 | tf_op jit(solution)/shard_map/ppermute | solution.py:624
  3.5 4.5 %collective-permute-start = (bf16[256,128]{1,0:T(8,128)(2,1)S(1)}, bf16[256,128]{1,0:T(8,128)(2,1)S(1)}, u32[]{:S(2)}, u32[]{:S(2)}) collective-permute-start(bf16[256,128]{1,0:T(8,128)(2,1)S(1)} %get-tuple-element.95), channel_id=1, source_target_pairs={{0,1},{1,2},{2,3},{3,4},{4,5},{5,6},{6,7},{7,8},{8,9},{9,10},{10,1... | collective-permute-start | bytes 196616 | tf_op jit(solution)/shard_map/ppermute | solution.py:623
  8.0 6.7 %shard_map.158 = (bf16[2,768,256]{2,1,0:T(8,128)(2,1)S(1)}, bf16[2,128,512]{2,1,0:T(8,128)(2,1)S(1)}, bf16[128,256]{1,0:T(8,128)(2,1)S(1)}, bf16[128,128]{1,0:T(...) custom-call(s32[8,2048]{1,0:T(8,128)} %refs_0_.5, ...), custom_call_target="tpu_custom_call" | custom-call | bytes 18000000 | tf_op jit(solution)/shard_map/pallas_call | solution.py:162
  14.8 2.3 %shard_map.159 = (bf16[16,96,128]{2,1,0:T(8,128)(2,1)}, bf16[128,2048]{1,0:T(8,128)(2,1)}) custom-call(bf16[256,128]{1,0:T(8,128)(2,1)S(1)} %collective-permute-done.refs_0_, bf16[256,128]{1,0:T(8,128)(2,1)S(1)} %collective-permute-done.1.refs_1_, bf16[2,768,256]{2,1,0:T(8,128)(2,1)S(1)} %get-tuple-element.48.refs_2_, ...), custom_call_target="tpu_custom_call" | custom-call | bytes 9000000 | tf_op jit(solution)/shard_map/pallas_call | solution.py:162
  17.1 5.8 %all-to-all-start = ((bf16[16,96,128]{2,1,0:T(8,128)(2,1)}), bf16[16,96,128]{2,1,0:T(8,128)(2,1)S(1)}, u32[]{:S(2)}, u32[]{:S(2)}) async-start(bf16[16,96,128]{2,1,0:T(8,128)(2,1)} %get-tuple-element.57), calls=%async_computation | async-start | bytes 786432 | tf_op jit(solution)/shard_map/all_to_all | solution.py:586
  22.9 2.0 %shard_map.160 = (bf16[512,512]{1,0:T(8,128)(2,1)}, bf16[128,256]{1,0:T(8,128)(2,1)}, bf16[128,128]{1,0:T(8,128)(2,1)}, bf16[128,128]{1,0:T(8,128)(2,1)}) custom-call(s32[8,512]{1,0:T(8,128)} %refs_0_.4, f32[8,512]{1,0:T(8,128)} %refs_1_.4, bf16[3,4,128,128]{3,2,1,0:T(8,128)(2,1)} %refs_2_.7, bf16[128,2048]{1,0:T(8,128)(2,1)} %get-tuple-element.58.refs_3_.refs_10_.refs_8_), custom_call_target="tpu_custom_call" | custom-call | bytes 18000000 | tf_op jit(solution)/shard_map/pallas_call | solution.py:162
  24.9 9.9 %all-to-all-done.refs_0_ = bf16[16,96,128]{2,1,0:T(8,128)(2,1)S(1)} async-done(((bf16[16,96,128]{2,1,0:T(8,128)(2,1)}), bf16[16,96,128]{2,1,0:T(8,128)(2,1)S(1)}, u32[]{:S(2)}, u32[]{:S(2)}) %all-to-all-start) | async-done | bytes 393248 | tf_op jit(solution)/shard_map/all_to_all | solution.py:586
  34.8 2.9 %shard_map.161 = (bf16[16,16,128]{2,1,0:T(8,128)(2,1)}, bf16[128,512]{1,0:T(8,128)(2,1)}, bf16[128,512]{1,0:T(8,128)(2,1)}, bf16[1024,512]{1,0:T(8,128)(2,1)}, bf16[16,32,128]{2,1,0:T(8,128)(2,1)}) custom-call(bf16[16,96,128]{2,1,0:T(8,128)(2,1)S(1)} %all-to-all-done.refs_0_, bf16[512,512]{1,0:T(8,128)(2,1)} %get-tuple-element.59.refs_1_.refs_10_, ...), custom_call_target="tpu_custom_call" | custom-call | bytes 9000000 | tf_op jit(solution)/shard_map/pallas_call | solution.py:162
  37.7 3.8 %all-to-all-start.1 = ((bf16[16,16,128]{2,1,0:T(8,128)(2,1)}), bf16[16,16,128]{2,1,0:T(8,128)(2,1)S(1)}, u32[]{:S(2)}, u32[]{:S(2)}) async-start(bf16[16,16,128]{2,1,0:T(8,128)(2,1)} %get-tuple-element.63), calls=%async_computation.1 | async-start | bytes 131072 | tf_op jit(solution)/shard_map/all_to_all | solution.py:586
  41.5 2.8 %shard_map.162 = (bf16[256,256]{1,0:T(8,128)(2,1)}, bf16[128,256]{1,0:T(8,128)(2,1)}, bf16[128,512]{1,0:T(8,128)(2,1)}, f32[128,512]{1,0:T(8,128)}, f32[128,512]{1,0:T(8,128)}) custom-call(bf16[16,32,128]{2,1,0:T(8,128)(2,1)} %get-tuple-element.64.refs_0_, bf16[128,512]{1,0:T(8,128)(2,1)} %get-tuple-element.65.refs_1_.refs_0_, ...), custom_call_target="tpu_custom_call" | custom-call | bytes 18000000 | tf_op jit(solution)/shard_map/pallas_call | solution.py:162
  44.3 3.2 %all-to-all-done.1 = bf16[16,16,128]{2,1,0:T(8,128)(2,1)S(1)} async-done(((bf16[16,16,128]{2,1,0:T(8,128)(2,1)}), bf16[16,16,128]{2,1,0:T(8,128)(2,1)S(1)}, u32[]{:S(2)}, u32[]{:S(2)}) %all-to-all-start.1) | async-done | bytes 65568 | tf_op jit(solution)/shard_map/all_to_all | solution.py:586
  47.6 4.4 %shard_map.163 = (bf16[1024,128]{1,0:T(8,128)(2,1)}, bf16[128,512]{1,0:T(8,128)(2,1)}, bf16[128,512]{1,0:T(8,128)(2,1)}, bf16[128,512]{1,0:T(8,128)(2,1)}, f32[4,128,128]{2,1,0:T(8,128)}) custom-call(bf16[256,128]{1,0:T(8,128)(2,1)S(1)} %bitcast.9, bf16[256,256]{1,0:T(8,128)(2,1)} %get-tuple-element.67.refs_1_, bf16[3,4,128,128]{3,2,1,0:T(8,128)(2,1)} %refs_2_.7, ...), custom_call_target="tpu_custom_call" | custom-call | bytes 9000000 | tf_op jit(solution)/shard_map/pallas_call | solution.py:162
  52.0 4.3 %all-to-all-start.2 = ((bf16[16,64,128]{2,1,0:T(8,128)(2,1)}), bf16[16,64,128]{2,1,0:T(8,128)(2,1)S(1)}, u32[]{:S(2)}, u32[]{:S(2)}) async-start(bf16[16,64,128]{2,1,0:T(8,128)(2,1)} %bitcast.11), calls=%async_computation.2 | async-start | bytes 524288 | tf_op jit(solution)/shard_map/all_to_all | solution.py:586
  56.3 5.6 %shard_map.164 = (bf16[512,128]{1,0:T(8,128)(2,1)}, bf16[128,2048]{1,0:T(8,128)(2,1)}, bf16[128,2048]{1,0:T(8,128)(2,1)}, bf16[128,2048]{1,0:T(8,128)(2,1)}, f32...) custom-call(bf16[128,512]{1,0:T(8,128)(2,1)} %get-tuple-element.65.r, ...), custom_call_target="tpu_custom_call" | custom-call | bytes 18000000 | tf_op jit(solution)/shard_map/pallas_call | solution.py:162
  61.9 3.9 %all-to-all-done.2 = bf16[16,64,128]{2,1,0:T(8,128)(2,1)S(1)} async-done(((bf16[16,64,128]{2,1,0:T(8,128)(2,1)}), bf16[16,64,128]{2,1,0:T(8,128)(2,1)S(1)}, u32[]{:S(2)}, u32[]{:S(2)}) %all-to-all-start.2) | async-done | bytes 262176 | tf_op jit(solution)/shard_map/all_to_all | solution.py:586
  65.8 6.1 %shard_map.165 = (bf16[1024,128]{1,0:T(8,128)(2,1)}, bf16[128,2048]{1,0:T(8,128)(2,1)}, bf16[128,2048]{1,0:T(8,128)(2,1)}) custom-call(bf16[1024,128]{1,0:T(8,128)(2,1)S(1)} %bitcast.8, bf16[512,1024]{1,0:T(8,128)(2,1)} %get-tuple-element.78.refs_1_, bf16[128,2048]{1,0:T(8,128)(2,1)} %get-tuple-element.79.refs_2_, ...), custom_call_target="tpu_custom_call" | custom-call | bytes 12000000 | tf_op jit(solution)/shard_map/pallas_call | solution.py:162
  72.0 4.2 %all-to-all-start.3 = ((bf16[16,64,128]{2,1,0:T(8,128)(2,1)}), bf16[16,64,128]{2,1,0:T(8,128)(2,1)S(1)}, u32[]{:S(2)}, u32[]{:S(2)}) async-start(bf16[16,64,128]{2,1,0:T(8,128)(2,1)} %bitcast.12), calls=%async_computation.3 | async-start | bytes 524288 | tf_op jit(solution)/shard_map/all_to_all | solution.py:586
  76.1 5.4 %shard_map.166 = (bf16[256,128]{1,0:T(8,128)(2,1)}, bf16[256,128]{1,0:T(8,128)(2,1)}, f32[2048,128]{1,0:T(8,128)}) custom-call(s32[8,2048]{1,0:T(8,128)} %refs_0_.5, f32[8,2048]{1,0:T(8,128)} %refs_1_.5, bf16[3,4,128,128]{3,2,1,0:T(8,128)(2,1)} %refs_2_.7, bf16[128,2048]{1,0:T(8,128)(2,1)} %get-tuple-element.87.refs_3_, ...), custom_call_target="tpu_custom_call" | custom-call | bytes 18000000 | tf_op jit(solution)/shard_map/pallas_call | solution.py:162
  81.6 4.1 %all-to-all-done.3.refs_0_ = bf16[16,64,128]{2,1,0:T(8,128)(2,1)S(1)} async-done(((bf16[16,64,128]{2,1,0:T(8,128)(2,1)}), bf16[16,64,128]{2,1,0:T(8,128)(2,1)S(1)}, u32[]{:S(2)}, u32[]{:S(2)}) %all-to-all-start.3) | async-done | bytes 262176 | tf_op jit(solution)/shard_map/all_to_all | solution.py:586
  86.6 4.1 %all-to-all-start.4 = ((bf16[16,64,128]{2,1,0:T(8,128)(2,1)}), bf16[16,64,128]{2,1,0:T(8,128)(2,1)S(1)}, u32[]{:S(2)}, u32[]{:S(2)}) async-start(bf16[16,64,128]{2,1,0:T(8,128)(2,1)} %shard_map.168), calls=%async_computation.4 | async-start | bytes 524288 | tf_op jit(solution)/shard_map/all_to_all | solution.py:586
  90.7 3.5 %collective-permute-start.2 = (bf16[256,128]{1,0:T(8,128)(2,1)S(1)}, bf16[256,128]{1,0:T(8,128)(2,1)S(1)}, u32[]{:S(2)}, u32[]{:S(2)}) collective-permute-start(bf16[256,128]{1,0:T(8,128)(2,1)S(1)} %copy-done.1), channel_id=1, source_target_pairs={{0,1},{1,2},{2,3},{3,4},{4,5},{5,6},{6,7},{7,8},{8,9},{9,10},{10,1... | collective-permute-start | bytes 196616 | tf_op jit(solution)/shard_map/ppermute | solution.py:756
  96.2 4.3 %collective-permute-done.3.refs_2_ = bf16[256,128]{1,0:T(8,128)(2,1)S(1)} collective-permute-done((bf16[256,128]{1,0:T(8,128)(2,1)S(1)}, bf16[256,128]{1,0:T(8,128)(2,1)S(1)}, u32[]{:S(2)}, u32[]{:S(2)}) %collective-permute-start.3) | collective-permute-done | bytes 65568 | tf_op jit(solution)/shard_map/ppermute | solution.py:757
  100.6 2.1 %shard_map.167 = bf16[2048,128]{1,0:T(8,128)(2,1)} custom-call(f32[2048,128]{1,0:T(8,128)} %get-tuple-element.89.refs_0_, bf16[256,128]{1,0:T(8,128)(2,1)S(1)} %collective-permute-done.2.refs_1_, bf16[256,128]{1,0:T(8,128)(2,1)S(1)} %collective-permute-done.3.refs_2_), custom_call_target="tpu_custom_call" | custom-call | bytes 3000000 | tf_op jit(solution)/shard_map/pallas_call | solution.py:162
  102.7 9.1 %shard_map.169 = f32[12,128,128]{2,1,0:T(8,128)} custom-call(bf16[8,128,128]{2,1,0:T(8,128)(2,1)S(1)} %bitcast.7, f32[4,128,128]{2,1,0:T(8,128)} %get-tuple-element.93.refs_1_), custom_call_target="tpu_custom_call" | custom-call | bytes 3000000 | tf_op jit(solution)/shard_map/pallas_call | solution.py:162
  (11 shorter events, 3.7 us)
Async XLA Ops:
  1.5 13.2 %collective-permute-start.1 = (bf16[256,128]{1,0:T(8,128)(2,1)S(1)}, bf16[256,128]{1,0:T(8,128)(2,1)S(1)}, u32[]{:S(2)}, u32[]{:S(2)}) collective-permute-start(bf16[256,128]{1,0:T(8,128)(2,1)S(1)} %get-tuple-element.94), channel_id=1, source_target_pairs={{1,0},{2,1},{3,2},{4,3},{5,4},{6,5},{7,6},{8,7},{9,8},{10,9},{11,1... | collective-permute-start | bytes 196616 | tf_op jit(solution)/shard_map/ppermute | solution.py:624
  3.5 11.3 %collective-permute-start = (bf16[256,128]{1,0:T(8,128)(2,1)S(1)}, bf16[256,128]{1,0:T(8,128)(2,1)S(1)}, u32[]{:S(2)}, u32[]{:S(2)}) collective-permute-start(bf16[256,128]{1,0:T(8,128)(2,1)S(1)} %get-tuple-element.95), channel_id=1, source_target_pairs={{0,1},{1,2},{2,3},{3,4},{4,5},{5,6},{6,7},{7,8},{8,9},{9,10},{10,1... | collective-permute-start | bytes 196616 | tf_op jit(solution)/shard_map/ppermute | solution.py:623
  17.1 17.7 %all-to-all-start = ((bf16[16,96,128]{2,1,0:T(8,128)(2,1)}), bf16[16,96,128]{2,1,0:T(8,128)(2,1)S(1)}, u32[]{:S(2)}, u32[]{:S(2)}) async-start(bf16[16,96,128]{2,1,0:T(8,128)(2,1)} %get-tuple-element.57), calls=%async_computation | async-start | bytes 786432 | tf_op jit(solution)/shard_map/all_to_all | solution.py:586
  37.7 9.9 %all-to-all-start.1 = ((bf16[16,16,128]{2,1,0:T(8,128)(2,1)}), bf16[16,16,128]{2,1,0:T(8,128)(2,1)S(1)}, u32[]{:S(2)}, u32[]{:S(2)}) async-start(bf16[16,16,128]{2,1,0:T(8,128)(2,1)} %get-tuple-element.63), calls=%async_computation.1 | async-start | bytes 131072 | tf_op jit(solution)/shard_map/all_to_all | solution.py:586
  52.0 13.8 %all-to-all-start.2 = ((bf16[16,64,128]{2,1,0:T(8,128)(2,1)}), bf16[16,64,128]{2,1,0:T(8,128)(2,1)S(1)}, u32[]{:S(2)}, u32[]{:S(2)}) async-start(bf16[16,64,128]{2,1,0:T(8,128)(2,1)} %bitcast.11), calls=%async_computation.2 | async-start | bytes 524288 | tf_op jit(solution)/shard_map/all_to_all | solution.py:586
  72.0 13.7 %all-to-all-start.3 = ((bf16[16,64,128]{2,1,0:T(8,128)(2,1)}), bf16[16,64,128]{2,1,0:T(8,128)(2,1)S(1)}, u32[]{:S(2)}, u32[]{:S(2)}) async-start(bf16[16,64,128]{2,1,0:T(8,128)(2,1)} %bitcast.12), calls=%async_computation.3 | async-start | bytes 524288 | tf_op jit(solution)/shard_map/all_to_all | solution.py:586
  86.6 4.2 %copy-start.1 = (bf16[256,128]{1,0:T(8,128)(2,1)S(1)}, bf16[256,128]{1,0:T(8,128)(2,1)}, u32[]{:S(2)}) copy-start(bf16[256,128]{1,0:T(8,128)(2,1)} %get-tuple-element.90) | copy-start | bytes 196612
  86.6 7.7 %copy-start = (bf16[256,128]{1,0:T(8,128)(2,1)S(1)}, bf16[256,128]{1,0:T(8,128)(2,1)}, u32[]{:S(2)}) copy-start(bf16[256,128]{1,0:T(8,128)(2,1)} %get-tuple-element.91.refs_1_) | copy-start | bytes 196612
  86.6 16.1 %all-to-all-start.4 = ((bf16[16,64,128]{2,1,0:T(8,128)(2,1)}), bf16[16,64,128]{2,1,0:T(8,128)(2,1)S(1)}, u32[]{:S(2)}, u32[]{:S(2)}) async-start(bf16[16,64,128]{2,1,0:T(8,128)(2,1)} %shard_map.168), calls=%async_computation.4 | async-start | bytes 524288 | tf_op jit(solution)/shard_map/all_to_all | solution.py:586
  90.7 5.5 %collective-permute-start.2 = (bf16[256,128]{1,0:T(8,128)(2,1)S(1)}, bf16[256,128]{1,0:T(8,128)(2,1)S(1)}, u32[]{:S(2)}, u32[]{:S(2)}) collective-permute-start(bf16[256,128]{1,0:T(8,128)(2,1)S(1)} %copy-done.1), channel_id=1, source_target_pairs={{0,1},{1,2},{2,3},{3,4},{4,5},{5,6},{6,7},{7,8},{8,9},{9,10},{10,1... | collective-permute-start | bytes 196616 | tf_op jit(solution)/shard_map/ppermute | solution.py:756
  94.3 6.3 %collective-permute-start.3 = (bf16[256,128]{1,0:T(8,128)(2,1)S(1)}, bf16[256,128]{1,0:T(8,128)(2,1)S(1)}, u32[]{:S(2)}, u32[]{:S(2)}) collective-permute-start(bf16[256,128]{1,0:T(8,128)(2,1)S(1)} %copy-done), channel_id=1, source_target_pairs={{1,0},{2,1},{3,2},{4,3},{5,4},{6,5},{7,6},{8,7},{9,8},{10,9},{11,1... | collective-permute-start | bytes 196616 | tf_op jit(solution)/shard_map/ppermute | solution.py:757

commit v5 on v4

--- a/solution.py
+++ b/solution.py
@@ -10,6 +10,7 @@
 
 HALO = 256
 TILE = 256
+WIDE = 2048
 BF = jnp.bfloat16
 F32 = jnp.float32
 
@@ -179,15 +180,13 @@
     ])
 
 
-def fine_tile(h_t, window_t, s, weights, pool):
+def fine_forward(h_t, agg, weights):
     w01, w2t, w3t = weights
-    agg = dot(window_t, s).astype(BF)
     first = dot(w01, jnp.concatenate([h_t, agg], axis=0))
     middle = silu(first).astype(BF)
     second = dot(w2t, middle)
     outer = silu(second).astype(BF)
-    fine_out = (h_t.astype(F32) + dot(w3t, outer)).astype(BF)
-    return agg, dot_nt(pool, fine_out)
+    return (h_t.astype(F32) + dot(w3t, outer)).astype(BF)
 
 
 def outer_tiles(tile_count, per):
@@ -203,8 +202,8 @@
     tiles = rows // TILE
     per = TILE // tile_rows
     tile_count = rows // tile_rows
-    clear_corners(s_ref.at[0])
-    clear_corners(s_ref.at[1])
+    for i in range(tiles - 2):
+        clear_corners(s_ref.at[i])
     clear_corners(so_ref.at[0])
     clear_corners(so_ref.at[1])
     spread[...] = jnp.zeros(spread.shape, F32)
@@ -229,19 +228,20 @@
     weights = forward_weights(w)
     for i in range(1, tiles - 1):
         cols = slice(i * TILE, (i + 1) * TILE)
-        s = s_ref.at[i % 2]
-        fine_edges(off[:, cols], ew[:, cols], s)
-        agg, blocks = fine_tile(
-            feat_t[:, cols],
-            feat_t[:, i * TILE - HALO : (i + 1) * TILE + HALO],
-            s[...],
-            weights,
-            pool_matrix(pool[:, cols], tile_rows),
-        )
-        agg_ref[:, cols] = agg
-        for j in range(per):
-            at = pl.ds(pl.multiple_of(place[i * per + j] * block_rows, 8), block_rows)
-            spread[at, :] = blocks[j * block_rows : (j + 1) * block_rows, :]
+        fine_edges(off[:, cols], ew[:, cols], s_ref.at[i - 1])
+        around = feat_t[:, i * TILE - HALO : (i + 1) * TILE + HALO]
+        agg_ref[:, cols] = dot(around, s_ref[i - 1]).astype(BF)
+    for start in range(TILE, rows - TILE, WIDE):
+        stop = min(start + WIDE, rows - TILE)
+        cols = slice(start, stop)
+        fine_out = fine_forward(feat_t[:, cols], agg_ref[:, cols], weights)
+        for i in range(start // TILE, stop // TILE):
+            at = slice(i * TILE - start, (i + 1) * TILE - start)
+            matrix = pool_matrix(pool[:, i * TILE : (i + 1) * TILE], tile_rows)
+            blocks = dot_nt(matrix, fine_out[:, at])
+            for j in range(per):
+                at = pl.ds(pl.multiple_of(place[i * per + j] * block_rows, 8), block_rows)
+                spread[at, :] = blocks[j * block_rows : (j + 1) * block_rows, :]
     for n, i in enumerate((0, tiles - 1)):
         cols = slice(i * TILE, (i + 1) * TILE)
         fine_edges(off[:, cols], ew[:, cols], so_ref.at[n])
@@ -266,7 +266,10 @@
 def outer_kernel(
     tile_rows, cap, block_rows, io, need, flush, ins, outs, agg_edge, spread, stage, counts
 ):
-    left, right, s_in, win, w01, w2t, w3t, pool, spread_in, ext, agg_in, owner = ins
+    across, beside, s_in, win, w01, w2t, w3t, pool, spread_in, ext, agg_in, owner = ins
+    even = lax.rem(lax.axis_index("nodes"), 2) == 0
+    left = jnp.where(even, beside[...], across[...])
+    right = jnp.where(even, across[...], beside[...])
     send_ref, agg_ref = outs
     peers, chunk, d = stage.shape
     rows = agg_in.shape[1]
@@ -278,17 +281,15 @@
     for p in range(peers):
         counts[p] = 0
     weights = (w01[...], w2t[...], w3t[...])
-    results = []
     for n in range(2):
         if n == 0:
-            window_t = jnp.concatenate([jnp.transpose(left[...]), win[0]], axis=1)
+            window_t = jnp.concatenate([jnp.transpose(left), win[0]], axis=1)
         else:
-            window_t = jnp.concatenate([win[1], jnp.transpose(right[...])], axis=1)
-        agg, blocks = fine_tile(
-            window_t[:, HALO : HALO + TILE], window_t, s_in[n], weights, pool[n]
-        )
-        agg_edge[:, n * TILE : (n + 1) * TILE] = agg
-        results.append(blocks)
+            window_t = jnp.concatenate([win[1], jnp.transpose(right)], axis=1)
+        agg_edge[:, n * TILE : (n + 1) * TILE] = dot(window_t, s_in[n]).astype(BF)
+    h_t = jnp.concatenate([win[0, :, :TILE], win[1, :, HALO:]], axis=1)
+    fine_out = fine_forward(h_t, agg_edge[...], weights)
+    results = [dot_nt(pool[n], fine_out[:, n * TILE : (n + 1) * TILE]) for n in range(2)]
     io.start(agg_edge.at[:, pl.ds(0, TILE)], agg_ref.at[:, pl.ds(0, TILE)])
     io.start(agg_edge.at[:, pl.ds(TILE, TILE)], agg_ref.at[:, pl.ds(rows - TILE, TILE)])
     need()
@@ -504,33 +505,30 @@
     d, rows = hid.shape
     need(1)
     blocks = dot(pick[...], got[...]).astype(BF)
-    need()
-    send_ref[4 * d : 8 * d, :] = mid_wg[...]
+    need(2, 3)
     per = pool.shape[1]
-    grads = [jnp.zeros((d, d), F32) for _ in range(4)]
     for i in range(rows // TILE):
         cols = slice(i * TILE, (i + 1) * TILE)
         back = dot_tn(blocks[i * per : (i + 1) * per, :], pool[i])
-        g = (cot[:, cols].astype(F32) + back).astype(BF)
-        sg = (dot(w[3], g) * slope2[:, cols]).astype(BF)
-        fg = (dot(w[2], sg) * slope1[:, cols]).astype(BF)
-        g_ref[:, cols] = g
-        fg_ref[:, cols] = fg
-        grads = [
-            grads[0] + dot_nt(hid[:, cols], fg),
-            grads[1] + dot_nt(agg[:, cols], fg),
-            grads[2] + dot_nt(mid[:, cols], sg),
-            grads[3] + dot_nt(outer[:, cols], g),
-        ]
+        g_ref[:, cols] = (cot[:, cols].astype(F32) + back).astype(BF)
     io.start(g_ref, g_out)
+    g = g_ref[...]
+    need(4, 5, 6)
+    sg = (dot(w[3], g) * slope2[...]).astype(BF)
+    fg = (dot(w[2], sg) * slope1[...]).astype(BF)
+    fg_ref[...] = fg
     io.start(fg_ref, fg_out)
-    for m in range(4):
-        send_ref[m * d : (m + 1) * d, :] = (grads[m] * scale).astype(BF)
+    need()
+    send_ref[4 * d : 8 * d, :] = mid_wg[...]
+    for m, (a, b) in enumerate(
+        ((hid[...], fg), (agg[...], fg), (mid[...], sg), (outer[...], g))
+    ):
+        send_ref[m * d : (m + 1) * d, :] = (dot_nt(a, b) * scale).astype(BF)
 
 
 def fine_spread_kernel(io, need, flush, ins, outs, s_ref, total):
     off, ew, w, g, fg = ins
-    rim_l, rim_r, out_ref = outs
+    rim_near, rim_far, out_ref = outs
     rows = g.shape[1]
     clear_corners(s_ref.at[0])
     clear_corners(s_ref.at[1])
@@ -547,8 +545,10 @@
         total[window, :] = total[window, :] + dot_nt(s[...], spill)
         here = slice(HALO + i * TILE, HALO + (i + 1) * TILE)
         total[here, :] = total[here, :] + jnp.transpose(direct)
-    rim_l[...] = total[:HALO, :].astype(BF)
-    rim_r[...] = total[HALO + rows :, :].astype(BF)
+    even = lax.rem(lax.axis_index("nodes"), 2) == 0
+    low, high = total[:HALO, :].astype(BF), total[HALO + rows :, :].astype(BF)
+    rim_near[...] = jnp.where(even, high, low)
+    rim_far[...] = jnp.where(even, low, high)
     out_ref[...] = total[HALO : HALO + rows, :]
 
 
@@ -563,23 +563,27 @@
 
 
 def join_kernel(io, need, flush, ins, outs):
-    total, from_left, from_right = ins
+    total, across, beside = ins
     out_ref = outs[0]
+    even = lax.rem(lax.axis_index("nodes"), 2) == 0
+    from_left = jnp.where(even, beside[...], across[...])
+    from_right = jnp.where(even, across[...], beside[...])
     rows = total.shape[0]
     need()
-    out_ref[:HALO, :] = (total[:HALO, :] + from_left[...].astype(F32)).astype(BF)
+    out_ref[:HALO, :] = (total[:HALO, :] + from_left.astype(F32)).astype(BF)
     out_ref[HALO : rows - HALO, :] = total[HALO : rows - HALO, :].astype(BF)
-    out_ref[rows - HALO :, :] = (total[rows - HALO :, :] + from_right[...].astype(F32)).astype(BF)
+    out_ref[rows - HALO :, :] = (total[rows - HALO :, :] + from_right.astype(F32)).astype(BF)
 
 
 def gather_kernel(io, need, flush, ins, outs, wide):
     summed, coarse = ins
     out_ref = outs[0]
-    io.start(coarse, out_ref.at[pl.ds(8, 4)])
     for half in range(2):
         wide[4 * half : 4 * half + 4] = summed[4 * half : 4 * half + 4].astype(F32)
         part = pl.ds(4 * half, 4)
         io.start(wide.at[part], out_ref.at[part])
+    need()
+    io.start(coarse, out_ref.at[pl.ds(8, 4)])
 
 
 def exchange(x):
@@ -616,12 +620,15 @@
     window = TILE + 2 * HALO
     per = TILE // tile_rows * block_rows
     ends = peers - 1
-    up = [(i, i + 1) for i in range(ends)]
-    down = [(i + 1, i) for i in range(ends)]
+    inside_pairs = [(i, i ^ 1) for i in range(peers)]
+    between_pairs = [(i, ((i + 1) ^ 1) - 1) for i in range(1, ends)]
     total2 = peers * n2
 
-    left = lax.ppermute(features[n - HALO :], "nodes", up)
-    right = lax.ppermute(features[:HALO], "nodes", down)
+    odd = lax.rem(lax.axis_index("nodes"), 2)
+    near = lax.dynamic_slice_in_dim(features, (1 - odd) * (n - HALO), HALO, 0)
+    far = lax.dynamic_slice_in_dim(features, odd * (n - HALO), HALO, 0)
+    across = lax.ppermute(near, "nodes", inside_pairs)
+    beside = lax.ppermute(far, "nodes", between_pairs)
     owners = owner_dev.reshape(-1)
     s_out, win, w01, w2t, w3t, pool_out, spread, ext, agg_in, place = call(
         functools.partial(inner_kernel, tile_rows, peers, cap),
@@ -639,7 +646,7 @@
         ],
         scratch=(
             pltpu.VMEM((d, n), BF),
-            pltpu.VMEM((2, window, TILE), BF),
+            pltpu.VMEM((n // TILE - 2, window, TILE), BF),
             pltpu.VMEM((peers, 128), F32),
             pltpu.SMEM((peers,), jnp.int32),
         ),
@@ -648,7 +655,7 @@
     send1, agg = call(
         functools.partial(outer_kernel, tile_rows, cap, block_rows),
         [
-            (left, "v"), (right, "v"), (s_out, "v"), (win, "v"), (w01, "v"), (w2t, "v"),
+            (across, "v"), (beside, "v"), (s_out, "v"), (win, "v"), (w01, "v"), (w2t, "v"),
             (w3t, "v"), (pool_out, "v"), (spread, "v"), (ext, "v"), (agg_in, "v"), (owners, "s"),
         ],
         [(shape((peers, chunk + n2 + 16, d)), "r"), (shape((d, n)), "r")],
@@ -737,7 +744,7 @@
         us=4,
     )
     got4 = exchange(send4.reshape(peers, 8 * d // peers, d))
-    rim_l, rim_r, spread = call(
+    rim_near, rim_far, spread = call(
         fine_spread_kernel,
         [(fine_offsets, "h"), (fine_edge_w, "h"), (weights, "0"), (g, "h"), (fg, "h")],
         [(shape((HALO, d)), "h"), (shape((HALO, d)), "h"), (shape((n, d), F32), "h")],
@@ -746,24 +753,24 @@
     )
     (send5,) = call(
         sum_kernel,
-        [(got4, "v"), (rim_l, "r")],
+        [(got4, "v"), (rim_near, "r")],
         [(shape((peers, 8 * d // peers, d)), "r")],
         scratch=(pltpu.VMEM((8 * d // peers, d), BF),),
         copies=peers,
         us=1,
     )
     got5 = exchange(send5)
-    from_left = lax.ppermute(rim_r, "nodes", up)
-    from_right = lax.ppermute(rim_l, "nodes", down)
+    from_across = lax.ppermute(rim_near, "nodes", inside_pairs)
+    from_beside = lax.ppermute(rim_far, "nodes", between_pairs)
     (feature_grads,) = call(
         join_kernel,
-        [(spread, "h"), (from_left, "v"), (from_right, "v")],
+        [(spread, "h"), (from_across, "v"), (from_beside, "v")],
         [(shape((n, d)), "h")],
         us=1,
     )
     (weight_grads,) = call(
         gather_kernel,
-        [(got5.reshape(8, d, d), "v"), (coarse_wg, "r")],
+        [(got5.reshape(8, d, d), "v"), (coarse_wg, "h")],
         [(shape((12, d, d), F32), "r")],
         scratch=(pltpu.VMEM((8, d, d), F32),),
         copies=3,

time: 113 us -> 97.1 us (0.86)
  Pallas kernels: 50.3 us -> 38.9 us
  starting transfers between devices: 34.2 us -> 29.9 us
    pallas_call x12, Pallas kernels: 50.3 us -> 38.9 us  [call(): pl.pallas_call(body, out_shape=[s if kind == 'v' else pltpu.HBM(s.shape,...]
    ppermute x4, starting transfers between devices: 11.9 us -> 8.23 us  [the longest x1 4.54 us: per_device(): beside = lax.ppermute(far, 'nodes', between_pairs)]
    ppermute x4, waiting for transfers between devices: 4.33 us -> 2.63 us  [the longest x1 2.62 us: per_device(): from_beside = lax.ppermute(rim_far, 'nodes', between_pairs)]
    all_to_all x5, waiting for transfers between devices: 21.2 us -> 22.3 us  [exchange(): return lax.all_to_all(x, 'nodes', split_axis=0, concat_axis=0, tiled=True)]
  transfers between devices with their start and end apart: 9 -> 9, of which waited for: 5 -> 6; matrix products, arithmetic and copies ran while one was open for 0% -> 0% of each run, Pallas kernels for 22% -> 24%
where the time goes in v5:
time: 97.1 us; the launch traced here: 95.6 us
  Pallas kernels  38.9 us (40%)
  starting transfers between devices  29.9 us (31%)
  waiting for transfers between devices  25 us (26%)
    pallas_call x12, Pallas kernels, call(): pl.pallas_call(body, out_shape=[s if kind == 'v' else pltpu.HBM(s.shape,...  38.9 us
    all_to_all x5, waiting for transfers between devices, exchange(): return lax.all_to_all(x, 'nodes', split_axis=0, concat_axis=0, tiled=True)  22.3 us
    all_to_all x5, starting transfers between devices, exchange(): return lax.all_to_all(x, 'nodes', split_axis=0, concat_axis=0, tiled=True)  21.6 us
    ppermute x1, starting transfers between devices, per_device(): beside = lax.ppermute(far, 'nodes', between_pairs)  4.54 us
    ppermute x1, starting transfers between devices, per_device(): from_beside = lax.ppermute(rim_far, 'nodes', between_pairs)  3.55 us
    ppermute x1, waiting for transfers between devices, per_device(): from_beside = lax.ppermute(rim_far, 'nodes', between_pairs)  2.62 us
  transfers between devices with their start and end apart: 9, of which 6 were waited for; matrix products, arithmetic and copies ran while one was open for 0% of the time, Pallas kernels for 24%

profile of v5, /device:TPU:1, one launch (start us, length us, event | category | flops | bytes accessed | tf_op | source)
XLA Modules:
  0.0 95.6 jit_solution(8881423567293946117)
XLA Ops:
  1.5 4.5 %collective-permute-start.1 = (bf16[256,128]{1,0:T(8,128)(2,1)S(1)}, bf16[256,128]{1,0:T(8,128)(2,1)S(1)}, u32[]{:S(2)}, u32[]{:S(2)}) collective-permute-start(bf16[256,128]{1,0:T(8,128)(2,1)S(1)} %get-tuple-element.94), channel_id=1, source_target_pairs={{1,2},{2,1},{3,4},{4,3},{5,6},{6,5},{7,8},{8,7},{9,10},{10,9},{11,... | collective-permute-start | bytes 196616 | tf_op jit(solution)/shard_map/ppermute | solution.py:631
  6.2 4.7 %shard_map.158 = (bf16[2,768,256]{2,1,0:T(8,128)(2,1)S(1)}, bf16[2,128,512]{2,1,0:T(8,128)(2,1)S(1)}, bf16[128,256]{1,0:T(8,128)(2,1)S(1)}, bf16[128,128]{1,0:T(...) custom-call(s32[8,2048]{1,0:T(8,128)} %refs_0_.5, ...), custom_call_target="tpu_custom_call" | custom-call | bytes 18000000 | tf_op jit(solution)/shard_map/pallas_call | solution.py:163
  10.9 1.8 %shard_map.159 = (bf16[16,96,128]{2,1,0:T(8,128)(2,1)}, bf16[128,2048]{1,0:T(8,128)(2,1)}) custom-call(bf16[256,128]{1,0:T(8,128)(2,1)S(1)} %collective-permute-done.refs_0_, bf16[256,128]{1,0:T(8,128)(2,1)S(1)} %collective-permute-done.1.refs_1_, bf16[2,768,256]{2,1,0:T(8,128)(2,1)S(1)} %get-tuple-element.48.refs_2_, ...), custom_call_target="tpu_custom_call" | custom-call | bytes 9000000 | tf_op jit(solution)/shard_map/pallas_call | solution.py:163
  12.6 5.4 %all-to-all-start = ((bf16[16,96,128]{2,1,0:T(8,128)(2,1)}), bf16[16,96,128]{2,1,0:T(8,128)(2,1)S(1)}, u32[]{:S(2)}, u32[]{:S(2)}) async-start(bf16[16,96,128]{2,1,0:T(8,128)(2,1)} %get-tuple-element.57), calls=%async_computation | async-start | bytes 786432 | tf_op jit(solution)/shard_map/all_to_all | solution.py:590
  18.0 2.0 %shard_map.160 = (bf16[512,512]{1,0:T(8,128)(2,1)}, bf16[128,256]{1,0:T(8,128)(2,1)}, bf16[128,128]{1,0:T(8,128)(2,1)}, bf16[128,128]{1,0:T(8,128)(2,1)}) custom-call(s32[8,512]{1,0:T(8,128)} %refs_0_.4, f32[8,512]{1,0:T(8,128)} %refs_1_.4, bf16[3,4,128,128]{3,2,1,0:T(8,128)(2,1)} %refs_2_.7, bf16[128,2048]{1,0:T(8,128)(2,1)} %get-tuple-element.58.refs_3_.refs_10_.refs_8_), custom_call_target="tpu_custom_call" | custom-call | bytes 18000000 | tf_op jit(solution)/shard_map/pallas_call | solution.py:163
  20.0 9.9 %all-to-all-done.refs_0_ = bf16[16,96,128]{2,1,0:T(8,128)(2,1)S(1)} async-done(((bf16[16,96,128]{2,1,0:T(8,128)(2,1)}), bf16[16,96,128]{2,1,0:T(8,128)(2,1)S(1)}, u32[]{:S(2)}, u32[]{:S(2)}) %all-to-all-start) | async-done | bytes 393248 | tf_op jit(solution)/shard_map/all_to_all | solution.py:590
  29.9 2.9 %shard_map.161 = (bf16[16,16,128]{2,1,0:T(8,128)(2,1)}, bf16[128,512]{1,0:T(8,128)(2,1)}, bf16[128,512]{1,0:T(8,128)(2,1)}, bf16[1024,512]{1,0:T(8,128)(2,1)}, bf16[16,32,128]{2,1,0:T(8,128)(2,1)}) custom-call(bf16[16,96,128]{2,1,0:T(8,128)(2,1)S(1)} %all-to-all-done.refs_0_, bf16[512,512]{1,0:T(8,128)(2,1)} %get-tuple-element.59.refs_1_.refs_10_, ...), custom_call_target="tpu_custom_call" | custom-call | bytes 9000000 | tf_op jit(solution)/shard_map/pallas_call | solution.py:163
  32.8 3.8 %all-to-all-start.1 = ((bf16[16,16,128]{2,1,0:T(8,128)(2,1)}), bf16[16,16,128]{2,1,0:T(8,128)(2,1)S(1)}, u32[]{:S(2)}, u32[]{:S(2)}) async-start(bf16[16,16,128]{2,1,0:T(8,128)(2,1)} %get-tuple-element.63), calls=%async_computation.1 | async-start | bytes 131072 | tf_op jit(solution)/shard_map/all_to_all | solution.py:590
  36.7 2.8 %shard_map.162 = (bf16[256,256]{1,0:T(8,128)(2,1)}, bf16[128,256]{1,0:T(8,128)(2,1)}, bf16[128,512]{1,0:T(8,128)(2,1)}, f32[128,512]{1,0:T(8,128)}, f32[128,512]{1,0:T(8,128)}) custom-call(bf16[16,32,128]{2,1,0:T(8,128)(2,1)} %get-tuple-element.64.refs_0_, bf16[128,512]{1,0:T(8,128)(2,1)} %get-tuple-element.65.refs_1_.refs_0_, ...), custom_call_target="tpu_custom_call" | custom-call | bytes 18000000 | tf_op jit(solution)/shard_map/pallas_call | solution.py:163
  39.5 3.2 %all-to-all-done.1 = bf16[16,16,128]{2,1,0:T(8,128)(2,1)S(1)} async-done(((bf16[16,16,128]{2,1,0:T(8,128)(2,1)}), bf16[16,16,128]{2,1,0:T(8,128)(2,1)S(1)}, u32[]{:S(2)}, u32[]{:S(2)}) %all-to-all-start.1) | async-done | bytes 65568 | tf_op jit(solution)/shard_map/all_to_all | solution.py:590
  42.7 4.4 %shard_map.163 = (bf16[1024,128]{1,0:T(8,128)(2,1)}, bf16[128,512]{1,0:T(8,128)(2,1)}, bf16[128,512]{1,0:T(8,128)(2,1)}, bf16[128,512]{1,0:T(8,128)(2,1)}, f32[4,128,128]{2,1,0:T(8,128)}) custom-call(bf16[256,128]{1,0:T(8,128)(2,1)S(1)} %bitcast.9, bf16[256,256]{1,0:T(8,128)(2,1)} %get-tuple-element.67.refs_1_, bf16[3,4,128,128]{3,2,1,0:T(8,128)(2,1)} %refs_2_.7, ...), custom_call_target="tpu_custom_call" | custom-call | bytes 9000000 | tf_op jit(solution)/shard_map/pallas_call | solution.py:163
  47.1 4.3 %all-to-all-start.2 = ((bf16[16,64,128]{2,1,0:T(8,128)(2,1)}), bf16[16,64,128]{2,1,0:T(8,128)(2,1)S(1)}, u32[]{:S(2)}, u32[]{:S(2)}) async-start(bf16[16,64,128]{2,1,0:T(8,128)(2,1)} %bitcast.11), calls=%async_computation.2 | async-start | bytes 524288 | tf_op jit(solution)/shard_map/all_to_all | solution.py:590
  51.4 5.6 %shard_map.164 = (bf16[512,128]{1,0:T(8,128)(2,1)}, bf16[128,2048]{1,0:T(8,128)(2,1)}, bf16[128,2048]{1,0:T(8,128)(2,1)}, bf16[128,2048]{1,0:T(8,128)(2,1)}, f32...) custom-call(bf16[128,512]{1,0:T(8,128)(2,1)} %get-tuple-element.65.r, ...), custom_call_target="tpu_custom_call" | custom-call | bytes 18000000 | tf_op jit(solution)/shard_map/pallas_call | solution.py:163
  57.0 3.9 %all-to-all-done.2 = bf16[16,64,128]{2,1,0:T(8,128)(2,1)S(1)} async-done(((bf16[16,64,128]{2,1,0:T(8,128)(2,1)}), bf16[16,64,128]{2,1,0:T(8,128)(2,1)S(1)}, u32[]{:S(2)}, u32[]{:S(2)}) %all-to-all-start.2) | async-done | bytes 262176 | tf_op jit(solution)/shard_map/all_to_all | solution.py:590
  61.0 4.5 %shard_map.165 = (bf16[1024,128]{1,0:T(8,128)(2,1)}, bf16[128,2048]{1,0:T(8,128)(2,1)}, bf16[128,2048]{1,0:T(8,128)(2,1)}) custom-call(bf16[1024,128]{1,0:T(8,128)(2,1)S(1)} %bitcast.8, bf16[512,1024]{1,0:T(8,128)(2,1)} %get-tuple-element.78.refs_1_, bf16[128,2048]{1,0:T(8,128)(2,1)} %get-tuple-element.79.refs_2_, ...), custom_call_target="tpu_custom_call" | custom-call | bytes 12000000 | tf_op jit(solution)/shard_map/pallas_call | solution.py:163
  65.5 4.0 %all-to-all-start.3 = ((bf16[16,64,128]{2,1,0:T(8,128)(2,1)}), bf16[16,64,128]{2,1,0:T(8,128)(2,1)S(1)}, u32[]{:S(2)}, u32[]{:S(2)}) async-start(bf16[16,64,128]{2,1,0:T(8,128)(2,1)} %bitcast.12), calls=%async_computation.3 | async-start | bytes 524288 | tf_op jit(solution)/shard_map/all_to_all | solution.py:590
  69.5 5.5 %shard_map.166 = (bf16[256,128]{1,0:T(8,128)(2,1)}, bf16[256,128]{1,0:T(8,128)(2,1)}, f32[2048,128]{1,0:T(8,128)}) custom-call(s32[8,2048]{1,0:T(8,128)} %refs_0_.5, f32[8,2048]{1,0:T(8,128)} %refs_1_.5, bf16[3,4,128,128]{3,2,1,0:T(8,128)(2,1)} %refs_2_.7, bf16[128,2048]{1,0:T(8,128)(2,1)} %get-tuple-element.87.refs_3_, ...), custom_call_target="tpu_custom_call" | custom-call | bytes 18000000 | tf_op jit(solution)/shard_map/pallas_call | solution.py:163
  75.0 4.1 %all-to-all-done.3.refs_0_ = bf16[16,64,128]{2,1,0:T(8,128)(2,1)S(1)} async-done(((bf16[16,64,128]{2,1,0:T(8,128)(2,1)}), bf16[16,64,128]{2,1,0:T(8,128)(2,1)S(1)}, u32[]{:S(2)}, u32[]{:S(2)}) %all-to-all-start.3) | async-done | bytes 262176 | tf_op jit(solution)/shard_map/all_to_all | solution.py:590
  79.9 4.1 %all-to-all-start.4 = ((bf16[16,64,128]{2,1,0:T(8,128)(2,1)}), bf16[16,64,128]{2,1,0:T(8,128)(2,1)S(1)}, u32[]{:S(2)}, u32[]{:S(2)}) async-start(bf16[16,64,128]{2,1,0:T(8,128)(2,1)} %shard_map.168), calls=%async_computation.4 | async-start | bytes 524288 | tf_op jit(solution)/shard_map/all_to_all | solution.py:590
  84.1 3.5 %collective-permute-start.3 = (bf16[256,128]{1,0:T(8,128)(2,1)S(1)}, bf16[256,128]{1,0:T(8,128)(2,1)S(1)}, u32[]{:S(2)}, u32[]{:S(2)}) collective-permute-start(bf16[256,128]{1,0:T(8,128)(2,1)S(1)} %copy-done.1), channel_id=1, source_target_pairs={{1,2},{2,1},{3,4},{4,3},{5,6},{6,5},{7,8},{8,7},{9,10},{10,9},{11,... | collective-permute-start | bytes 196616 | tf_op jit(solution)/shard_map/ppermute | solution.py:764
  87.7 2.6 %collective-permute-done.3.refs_2_ = bf16[256,128]{1,0:T(8,128)(2,1)S(1)} collective-permute-done((bf16[256,128]{1,0:T(8,128)(2,1)S(1)}, bf16[256,128]{1,0:T(8,128)(2,1)S(1)}, u32[]{:S(2)}, u32[]{:S(2)}) %collective-permute-start.3) | collective-permute-done | bytes 65568 | tf_op jit(solution)/shard_map/ppermute | solution.py:764
  90.4 2.1 %shard_map.167 = bf16[2048,128]{1,0:T(8,128)(2,1)} custom-call(f32[2048,128]{1,0:T(8,128)} %get-tuple-element.89.refs_0_, bf16[256,128]{1,0:T(8,128)(2,1)S(1)} %collective-permute-done.2.refs_1_, bf16[256,128]{1,0:T(8,128)(2,1)S(1)} %collective-permute-done.3.refs_2_), custom_call_target="tpu_custom_call" | custom-call | bytes 3000000 | tf_op jit(solution)/shard_map/pallas_call | solution.py:163
  92.5 1.2 %all-to-all-done.4 = bf16[16,64,128]{2,1,0:T(8,128)(2,1)S(1)} async-done(((bf16[16,64,128]{2,1,0:T(8,128)(2,1)}), bf16[16,64,128]{2,1,0:T(8,128)(2,1)S(1)}, u32[]{:S(2)}, u32[]{:S(2)}) %all-to-all-start.4) | async-done | bytes 262176 | tf_op jit(solution)/shard_map/all_to_all | solution.py:590
  93.6 1.8 %shard_map.169 = f32[12,128,128]{2,1,0:T(8,128)} custom-call(bf16[8,128,128]{2,1,0:T(8,128)(2,1)S(1)} %bitcast.7, f32[4,128,128]{2,1,0:T(8,128)} %get-tuple-element.93.refs_1_), custom_call_target="tpu_custom_call" | custom-call | bytes 3000000 | tf_op jit(solution)/shard_map/pallas_call | solution.py:163
  (11 shorter events, 1.9 us)
Async XLA Ops:
  1.5 9.3 %collective-permute-start.1 = (bf16[256,128]{1,0:T(8,128)(2,1)S(1)}, bf16[256,128]{1,0:T(8,128)(2,1)S(1)}, u32[]{:S(2)}, u32[]{:S(2)}) collective-permute-start(bf16[256,128]{1,0:T(8,128)(2,1)S(1)} %get-tuple-element.94), channel_id=1, source_target_pairs={{1,2},{2,1},{3,4},{4,3},{5,6},{6,5},{7,8},{8,7},{9,10},{10,9},{11,... | collective-permute-start | bytes 196616 | tf_op jit(solution)/shard_map/ppermute | solution.py:631
  6.1 4.8 %collective-permute-start = (bf16[256,128]{1,0:T(8,128)(2,1)S(1)}, bf16[256,128]{1,0:T(8,128)(2,1)S(1)}, u32[]{:S(2)}, u32[]{:S(2)}) collective-permute-start(bf16[256,128]{1,0:T(8,128)(2,1)S(1)} %get-tuple-element.95), channel_id=1, source_target_pairs={{0,1},{1,0},{2,3},{3,2},{4,5},{5,4},{6,7},{7,6},{8,9},{9,8},{10,11... | collective-permute-start | bytes 196616 | tf_op jit(solution)/shard_map/ppermute | solution.py:630
  12.6 17.3 %all-to-all-start = ((bf16[16,96,128]{2,1,0:T(8,128)(2,1)}), bf16[16,96,128]{2,1,0:T(8,128)(2,1)S(1)}, u32[]{:S(2)}, u32[]{:S(2)}) async-start(bf16[16,96,128]{2,1,0:T(8,128)(2,1)} %get-tuple-element.57), calls=%async_computation | async-start | bytes 786432 | tf_op jit(solution)/shard_map/all_to_all | solution.py:590
  32.8 9.9 %all-to-all-start.1 = ((bf16[16,16,128]{2,1,0:T(8,128)(2,1)}), bf16[16,16,128]{2,1,0:T(8,128)(2,1)S(1)}, u32[]{:S(2)}, u32[]{:S(2)}) async-start(bf16[16,16,128]{2,1,0:T(8,128)(2,1)} %get-tuple-element.63), calls=%async_computation.1 | async-start | bytes 131072 | tf_op jit(solution)/shard_map/all_to_all | solution.py:590
  47.1 13.8 %all-to-all-start.2 = ((bf16[16,64,128]{2,1,0:T(8,128)(2,1)}), bf16[16,64,128]{2,1,0:T(8,128)(2,1)S(1)}, u32[]{:S(2)}, u32[]{:S(2)}) async-start(bf16[16,64,128]{2,1,0:T(8,128)(2,1)} %bitcast.11), calls=%async_computation.2 | async-start | bytes 524288 | tf_op jit(solution)/shard_map/all_to_all | solution.py:590
  65.5 13.6 %all-to-all-start.3 = ((bf16[16,64,128]{2,1,0:T(8,128)(2,1)}), bf16[16,64,128]{2,1,0:T(8,128)(2,1)S(1)}, u32[]{:S(2)}, u32[]{:S(2)}) async-start(bf16[16,64,128]{2,1,0:T(8,128)(2,1)} %bitcast.12), calls=%async_computation.3 | async-start | bytes 524288 | tf_op jit(solution)/shard_map/all_to_all | solution.py:590
  79.9 4.2 %copy-start.1 = (bf16[256,128]{1,0:T(8,128)(2,1)S(1)}, bf16[256,128]{1,0:T(8,128)(2,1)}, u32[]{:S(2)}) copy-start(bf16[256,128]{1,0:T(8,128)(2,1)} %get-tuple-element.91) | copy-start | bytes 196612
  79.9 7.7 %copy-start = (bf16[256,128]{1,0:T(8,128)(2,1)S(1)}, bf16[256,128]{1,0:T(8,128)(2,1)}, u32[]{:S(2)}) copy-start(bf16[256,128]{1,0:T(8,128)(2,1)} %get-tuple-element.90.refs_1_) | copy-start | bytes 196612
  79.9 13.7 %all-to-all-start.4 = ((bf16[16,64,128]{2,1,0:T(8,128)(2,1)}), bf16[16,64,128]{2,1,0:T(8,128)(2,1)S(1)}, u32[]{:S(2)}, u32[]{:S(2)}) async-start(bf16[16,64,128]{2,1,0:T(8,128)(2,1)} %shard_map.168), calls=%async_computation.4 | async-start | bytes 524288 | tf_op jit(solution)/shard_map/all_to_all | solution.py:590
  84.1 6.3 %collective-permute-start.3 = (bf16[256,128]{1,0:T(8,128)(2,1)S(1)}, bf16[256,128]{1,0:T(8,128)(2,1)S(1)}, u32[]{:S(2)}, u32[]{:S(2)}) collective-permute-start(bf16[256,128]{1,0:T(8,128)(2,1)S(1)} %copy-done.1), channel_id=1, source_target_pairs={{1,2},{2,1},{3,4},{4,3},{5,6},{6,5},{7,8},{8,7},{9,10},{10,9},{11,... | collective-permute-start | bytes 196616 | tf_op jit(solution)/shard_map/ppermute | solution.py:764
  87.7 2.7 %collective-permute-start.2 = (bf16[256,128]{1,0:T(8,128)(2,1)S(1)}, bf16[256,128]{1,0:T(8,128)(2,1)S(1)}, u32[]{:S(2)}, u32[]{:S(2)}) collective-permute-start(bf16[256,128]{1,0:T(8,128)(2,1)S(1)} %copy-done), channel_id=1, source_target_pairs={{0,1},{1,0},{2,3},{3,2},{4,5},{5,4},{6,7},{7,6},{8,9},{9,8},{10,11... | collective-permute-start | bytes 196616 | tf_op jit(solution)/shard_map/ppermute | solution.py:763

commit v6 on v5

--- a/solution.py
+++ b/solution.py
@@ -119,7 +119,7 @@
     return jax.ShapeDtypeStruct(dims, dtype)
 
 
-def call(kernel, ins, outs, scratch=(), copies=0, us=3, mib=24):
+def call(kernel, ins, outs, scratch=(), copies=0, us=3, mib=24, aliases={}):
     n_in, n_out = len(ins), len(outs)
     staged_in = [i for i, (_, kind) in enumerate(ins) if kind in "hs012"]
     staged_out = [i for i, (_, kind) in enumerate(outs) if kind in "hs"]
@@ -170,6 +170,7 @@
         scratch_shapes=stage
         + list(scratch)
         + ([pltpu.SemaphoreType.DMA((total,))] if total else []),
+        input_output_aliases=aliases,
         compiler_params=pltpu.CompilerParams(vmem_limit_bytes=mib << 20),
         cost_estimate=pl.CostEstimate(
             flops=0, bytes_accessed=int(us * 3_000_000), transcendentals=0
@@ -222,9 +223,11 @@
         ids[pl.ds(o, 1), :] = jnp.where(lane_slot == c, slot[t].astype(F32), row)
     flush(9)
     need(0, 1)
-    need(2)
+    for n, i in enumerate((0, tiles - 1)):
+        cols = slice(i * TILE, (i + 1) * TILE)
+        fine_edges(off[:, cols], ew[:, cols], so_ref.at[n])
+    need()
     feat_t[...] = jnp.transpose(feat[...])
-    need()
     weights = forward_weights(w)
     for i in range(1, tiles - 1):
         cols = slice(i * TILE, (i + 1) * TILE)
@@ -243,9 +246,7 @@
                 at = pl.ds(pl.multiple_of(place[i * per + j] * block_rows, 8), block_rows)
                 spread[at, :] = blocks[j * block_rows : (j + 1) * block_rows, :]
     for n, i in enumerate((0, tiles - 1)):
-        cols = slice(i * TILE, (i + 1) * TILE)
-        fine_edges(off[:, cols], ew[:, cols], so_ref.at[n])
-        po_ref[n] = pool_matrix(pool[:, cols], tile_rows)
+        po_ref[n] = pool_matrix(pool[:, i * TILE : (i + 1) * TILE], tile_rows)
     win_ref[0] = feat_t[:, : TILE + HALO]
     win_ref[1] = feat_t[:, rows - TILE - HALO :]
     w01_ref[...], w2t_ref[...], w3t_ref[...] = weights
@@ -363,8 +364,8 @@
 
 
 def second_window_kernel(io, need, flush, ins, outs, nb_ref, ew_ref):
-    ext, hid, agg, mid_cot, w1 = ins
-    sco, cot_all, mcot, sl1_ref, sl2_ref = outs
+    ext, hid, agg, mid_cot, w1, w2 = ins
+    sco, cot_all, back_ref, w01_ref, w2t_ref, mcot, sl1_ref, sl2_ref = outs
     peers = ext.shape[0]
     n2 = ext.shape[1] - 16
     nodes = peers * n2
@@ -389,7 +390,8 @@
         return 0
 
     lax.fori_loop(0, nodes // 128, column, 0)
-    flush(0, 1, 2)
+    w01_ref[...], w2t_ref[...], _ = forward_weights(w2)
+    back_ref[...] = dot(w2[3], cot_all[...])
     w01, w2t, _ = forward_weights(w1)
     first = dot(w01, jnp.concatenate([hid[...], agg[...]], axis=0))
     s1 = 1.0 / (1.0 + jnp.exp(-first))
@@ -400,18 +402,19 @@
 
 
 def coarse_kernel(io, need, flush, ins, outs):
-    got, sco, w2, cot_all, cot_my, pool_mid, mcot, w1, msl2, msl1, smid, sel = ins
+    got, sco, c01, c2t, cot_all, cot_back, w2, *rest = ins
+    cot_my, pool_mid, mcot, w1, msl2, msl1, smid, sel = rest
     send_ref, gmid_ref, sg_ref, fg_ref, cwg_ref = outs
     nodes = got.shape[0]
     n2 = cot_my.shape[0]
     me = lax.axis_index("nodes")
     width = min(TILE, nodes)
     hidden = jnp.transpose(got[...])
-    need(1, 2, 3)
-    w01, w2t, _ = forward_weights(w2)
+    if sco.shape[0] > 512:
+        need(1, 2, 3, 4, 5)
+    w01, w2t = c01[...], c2t[...]
     mine = pl.ds(pl.multiple_of(me * n2, 16), n2)
-    spread = jnp.zeros((n2, 128), F32)
-    fg_mine = jnp.zeros((n2, 128), F32)
+    mixed = jnp.zeros((2 * n2, 128), F32)
     grads = [jnp.zeros((128, 128), F32) for _ in range(4)]
     row = lax.broadcasted_iota(jnp.int32, (n2, width), 0) + me * n2
     lane = lax.broadcasted_iota(jnp.int32, (n2, width), 1)
@@ -426,12 +429,12 @@
         s2 = 1.0 / (1.0 + jnp.exp(-second))
         outer = (second * s2).astype(BF)
         g = cot_all[:, cols]
-        sg = (dot(w2[3], g) * (s2 * (1.0 + second * (1.0 - s2)))).astype(BF)
+        if i == 0:
+            need(6)
+        sg = (cot_back[:, cols] * (s2 * (1.0 + second * (1.0 - s2)))).astype(BF)
         fg = (dot(w2[2], sg) * (s1 * (1.0 + first * (1.0 - s1)))).astype(BF)
-        spill = dot(w2[1], fg).astype(BF)
-        spread = spread + dot_nt(sco[mine, cols], spill)
         here = jnp.where(lane + i * width == row, 1.0, 0.0).astype(BF)
-        fg_mine = fg_mine + dot_nt(here, fg)
+        mixed = mixed + dot_nt(jnp.concatenate([here, sco[mine, cols]], axis=0), fg)
         grads = [
             grads[0] + dot_nt(h, fg),
             grads[1] + dot_nt(agg, fg),
@@ -442,9 +445,11 @@
     for m in range(4):
         cwg_ref[m] = grads[m] * scale
     flush(4)
-    need(4, 5, 6, 7, 8, 9)
-    direct = cot_my[...].astype(F32) + dot_nt(fg_mine.astype(BF), w2[0])
-    coarse_grad = (direct + spread).astype(BF)
+    need(7, 8, 9, 10, 11, 12)
+    mixed = mixed.astype(BF)
+    into = jnp.concatenate([mixed[:n2], mixed[n2:]], axis=1)
+    back_weights = jnp.concatenate([w2[0], w2[1]], axis=1)
+    coarse_grad = (cot_my[...].astype(F32) + dot_nt(into, back_weights)).astype(BF)
     back = dot_tn(coarse_grad, pool_mid[...])
     g = (mcot[...].astype(F32) + back).astype(BF)
     gmid_ref[...] = g
@@ -483,7 +488,7 @@
         pick_ref[t * block_rows : (t + 2) * block_rows, :] = jnp.concatenate(
             both, axis=0
         ).astype(BF)
-    flush(0, 1, 6, 7)
+    flush(0, 1, 6)
     w01, w2t, _ = forward_weights(w0)
     for i in range(rows // TILE):
         cols = slice(i * TILE, (i + 1) * TILE)
@@ -503,7 +508,8 @@
     got, pick, cot, pool, w, slope2, slope1, hid, agg, mid, outer, mid_wg = ins
     send_ref, g_out, fg_out = outs
     d, rows = hid.shape
-    need(1)
+    if pick.shape[1] > 1024:
+        need(1)
     blocks = dot(pick[...], got[...]).astype(BF)
     need(2, 3)
     per = pool.shape[1]
@@ -563,27 +569,26 @@
 
 
 def join_kernel(io, need, flush, ins, outs):
-    total, across, beside = ins
-    out_ref = outs[0]
+    total, across, beside, coarse = ins
+    out_ref, wg_ref = outs
     even = lax.rem(lax.axis_index("nodes"), 2) == 0
     from_left = jnp.where(even, beside[...], across[...])
     from_right = jnp.where(even, across[...], beside[...])
     rows = total.shape[0]
     need()
+    io.start(coarse, wg_ref.at[pl.ds(8, 4)])
     out_ref[:HALO, :] = (total[:HALO, :] + from_left.astype(F32)).astype(BF)
     out_ref[HALO : rows - HALO, :] = total[HALO : rows - HALO, :].astype(BF)
     out_ref[rows - HALO :, :] = (total[rows - HALO :, :] + from_right.astype(F32)).astype(BF)
 
 
 def gather_kernel(io, need, flush, ins, outs, wide):
-    summed, coarse = ins
+    summed, _ = ins
     out_ref = outs[0]
     for half in range(2):
         wide[4 * half : 4 * half + 4] = summed[4 * half : 4 * half + 4].astype(F32)
         part = pl.ds(4 * half, 4)
         io.start(wide.at[part], out_ref.at[part])
-    need()
-    io.start(coarse, out_ref.at[pl.ds(8, 4)])
 
 
 def exchange(x):
@@ -690,13 +695,17 @@
         us=3,
     )
     got2 = exchange(send2)
-    sco, cot_all, mcot, mslope1, mslope2 = call(
+    near = "v" if total2 <= 512 else "h"
+    sco, cot_all, cot_back, c01, c2t, mcot, mslope1, mslope2 = call(
         second_window_kernel,
         [
             (ext, "h"), (mhid, "h"), (magg, "h"), (mid_cotangent, "h"), (weights, "1"),
-        ],
-        [
-            (shape((total2, total2)), "h"), (shape((d, total2)), "h"), (shape((d, n1)), "h"),
+            (weights, "2"),
+        ],
+        [
+            (shape((total2, total2)), near), (shape((d, total2)), near),
+            (shape((d, total2), F32), near), (shape((d, 2 * d)), near), (shape((d, d)), near),
+            (shape((d, n1)), "h"),
             (shape((d, n1), F32), "h"), (shape((d, n1), F32), "h"),
         ],
         scratch=(pltpu.VMEM((edges, total2), jnp.int32), pltpu.VMEM((edges, total2), F32)),
@@ -705,7 +714,8 @@
     send3, gmid, msg, mfg, coarse_wg = call(
         coarse_kernel,
         [
-            (got2.reshape(total2, d), "v"), (sco, "h"), (weights, "2"), (cot_all, "h"),
+            (got2.reshape(total2, d), "v"), (sco, near), (c01, near), (c2t, near),
+            (cot_all, near), (cot_back, near), (weights, "2"),
             (coarse_cotangent, "h"), (pool_mid, "h"), (mcot, "h"), (weights, "1"),
             (mslope2, "h"), (mslope1, "h"), (smid, "h"), (sel, "h"),
         ],
@@ -716,6 +726,7 @@
         us=3,
     )
     got3 = exchange(send3.reshape(peers, chunk, d))
+    pick_kind = "v" if peers * chunk <= 1024 else "h"
     mid_wg, hid, mid, outer, slope1, slope2, cot, pick, pool_b = call(
         functools.partial(third_window_kernel, tile_rows, 1.0 / math.sqrt(n1 * peers)),
         [
@@ -726,7 +737,7 @@
         [
             (shape((4 * d, d)), "h"), (shape((d, n)), "h"), (shape((d, n)), "h"),
             (shape((d, n)), "h"), (shape((d, n), F32), "h"), (shape((d, n), F32), "h"),
-            (shape((d, n)), "h"), (shape((tile_count * block_rows, peers * chunk)), "h"),
+            (shape((d, n)), "h"), (shape((tile_count * block_rows, peers * chunk)), pick_kind),
             (shape((n // TILE, per, TILE)), "h"),
         ],
         us=6,
@@ -734,7 +745,7 @@
     send4, g, fg = call(
         functools.partial(fine_grad_kernel, 1.0 / math.sqrt(n * peers)),
         [
-            (got3.reshape(peers * chunk, d), "v"), (pick, "h"), (cot, "h"), (pool_b, "h"),
+            (got3.reshape(peers * chunk, d), "v"), (pick, pick_kind), (cot, "h"), (pool_b, "h"),
             (weights, "0"), (slope2, "h"), (slope1, "h"), (hid, "h"), (agg, "h"), (mid, "h"),
             (outer, "h"), (mid_wg, "h"),
         ],
@@ -762,18 +773,20 @@
     got5 = exchange(send5)
     from_across = lax.ppermute(rim_near, "nodes", inside_pairs)
     from_beside = lax.ppermute(rim_far, "nodes", between_pairs)
-    (feature_grads,) = call(
+    feature_grads, weight_grads = call(
         join_kernel,
-        [(spread, "h"), (from_across, "v"), (from_beside, "v")],
-        [(shape((n, d)), "h")],
+        [(spread, "h"), (from_across, "v"), (from_beside, "v"), (coarse_wg, "h")],
+        [(shape((n, d)), "h"), (shape((12, d, d), F32), "r")],
+        copies=1,
         us=1,
     )
     (weight_grads,) = call(
         gather_kernel,
-        [(got5.reshape(8, d, d), "v"), (coarse_wg, "h")],
+        [(got5.reshape(8, d, d), "v"), (weight_grads, "r")],
         [(shape((12, d, d), F32), "r")],
         scratch=(pltpu.VMEM((8, d, d), F32),),
-        copies=3,
+        copies=2,
+        aliases={1: 0},
         us=1,
     )
     weight_grads = weight_grads.reshape(3, 4, d, d)

time: 97.1 us -> 95.1 us (0.979)
  Pallas kernels: 38.9 us -> 36.7 us
    pallas_call x12, Pallas kernels: 38.9 us -> 36.7 us  [call(): pl.pallas_call(body, out_shape=[s if kind == 'v' else pltpu.HBM(s.shape,...]
where the time goes in v6:
time: 95.1 us; the launch traced here: 93.6 us
  Pallas kernels  36.7 us (39%)
  starting transfers between devices  29.9 us (31%)
  waiting for transfers between devices  25.2 us (26%)
  between operations  0.97 us (1%)
    pallas_call x12, Pallas kernels, call(): pl.pallas_call(body, out_shape=[s if kind == 'v' else pltpu.HBM(s.shape,...  36.7 us
    all_to_all x5, waiting for transfers between devices, exchange(): return lax.all_to_all(x, 'nodes', split_axis=0, concat_axis=0, tiled=True)  22.6 us
    all_to_all x5, starting transfers between devices, exchange(): return lax.all_to_all(x, 'nodes', split_axis=0, concat_axis=0, tiled=True)  21.6 us
    ppermute x1, starting transfers between devices, per_device(): beside = lax.ppermute(far, 'nodes', between_pairs)  4.54 us
    ppermute x1, starting transfers between devices, per_device(): from_beside = lax.ppermute(rim_far, 'nodes', between_pairs)  3.55 us
    ppermute x1, waiting for transfers between devices, per_device(): from_beside = lax.ppermute(rim_far, 'nodes', between_pairs)  2.62 us
  transfers between devices with their start and end apart: 9, of which 6 were waited for; matrix products, arithmetic and copies ran while one was open for 0% of the time, Pallas kernels for 24%

profile of v6, /device:TPU:1, one launch (start us, length us, event | category | flops | bytes accessed | tf_op | source)
XLA Modules:
  0.0 93.6 jit_solution(9125038286443533671)
XLA Ops:
  1.5 4.5 %collective-permute-start.1 = (bf16[256,128]{1,0:T(8,128)(2,1)S(1)}, bf16[256,128]{1,0:T(8,128)(2,1)S(1)}, u32[]{:S(2)}, u32[]{:S(2)}) collective-permute-start(bf16[256,128]{1,0:T(8,128)(2,1)S(1)} %get-tuple-element.104), channel_id=1, source_target_pairs={{1,2},{2,1},{3,4},{4,3},{5,6},{6,5},{7,8},{8,7},{9,10},{10,9},{11,... | collective-permute-start | bytes 196616 | tf_op jit(solution)/shard_map/ppermute | solution.py:636
  6.2 4.3 %shard_map.158 = (bf16[2,768,256]{2,1,0:T(8,128)(2,1)S(1)}, bf16[2,128,512]{2,1,0:T(8,128)(2,1)S(1)}, bf16[128,256]{1,0:T(8,128)(2,1)S(1)}, bf16[128,128]{1,0:T(...) custom-call(s32[8,2048]{1,0:T(8,128)} %refs_0_.5, ...), custom_call_target="tpu_custom_call" | custom-call | bytes 18000000 | tf_op jit(solution)/shard_map/pallas_call | solution.py:163
  10.5 1.8 %shard_map.159 = (bf16[16,96,128]{2,1,0:T(8,128)(2,1)}, bf16[128,2048]{1,0:T(8,128)(2,1)}) custom-call(bf16[256,128]{1,0:T(8,128)(2,1)S(1)} %collective-permute-done.refs_0_, bf16[256,128]{1,0:T(8,128)(2,1)S(1)} %collective-permute-done.1.refs_1_, bf16[2,768,256]{2,1,0:T(8,128)(2,1)S(1)} %get-tuple-element.53.refs_2_, ...), custom_call_target="tpu_custom_call" | custom-call | bytes 9000000 | tf_op jit(solution)/shard_map/pallas_call | solution.py:163
  12.3 5.4 %all-to-all-start = ((bf16[16,96,128]{2,1,0:T(8,128)(2,1)}), bf16[16,96,128]{2,1,0:T(8,128)(2,1)S(1)}, u32[]{:S(2)}, u32[]{:S(2)}) async-start(bf16[16,96,128]{2,1,0:T(8,128)(2,1)} %get-tuple-element.62), calls=%async_computation | async-start | bytes 786432 | tf_op jit(solution)/shard_map/all_to_all | solution.py:595
  17.6 2.0 %shard_map.160 = (bf16[512,512]{1,0:T(8,128)(2,1)}, bf16[128,256]{1,0:T(8,128)(2,1)}, bf16[128,128]{1,0:T(8,128)(2,1)}, bf16[128,128]{1,0:T(8,128)(2,1)}) custom-call(s32[8,512]{1,0:T(8,128)} %refs_0_.4, f32[8,512]{1,0:T(8,128)} %refs_1_.4, bf16[3,4,128,128]{3,2,1,0:T(8,128)(2,1)} %refs_2_.5, bf16[128,2048]{1,0:T(8,128)(2,1)} %get-tuple-element.63.refs_3_.refs_10_.refs_8_), custom_call_target="tpu_custom_call" | custom-call | bytes 18000000 | tf_op jit(solution)/shard_map/pallas_call | solution.py:163
  19.6 9.9 %all-to-all-done.refs_0_ = bf16[16,96,128]{2,1,0:T(8,128)(2,1)S(1)} async-done(((bf16[16,96,128]{2,1,0:T(8,128)(2,1)}), bf16[16,96,128]{2,1,0:T(8,128)(2,1)S(1)}, u32[]{:S(2)}, u32[]{:S(2)}) %all-to-all-start) | async-done | bytes 393248 | tf_op jit(solution)/shard_map/all_to_all | solution.py:595
  29.6 2.9 %shard_map.161 = (bf16[16,16,128]{2,1,0:T(8,128)(2,1)}, bf16[128,512]{1,0:T(8,128)(2,1)}, bf16[128,512]{1,0:T(8,128)(2,1)}, bf16[1024,512]{1,0:T(8,128)(2,1)}, bf16[16,32,128]{2,1,0:T(8,128)(2,1)}) custom-call(bf16[16,96,128]{2,1,0:T(8,128)(2,1)S(1)} %all-to-all-done.refs_0_, bf16[512,512]{1,0:T(8,128)(2,1)} %get-tuple-element.64.refs_1_.refs_13_, ...), custom_call_target="tpu_custom_call" | custom-call | bytes 9000000 | tf_op jit(solution)/shard_map/pallas_call | solution.py:163
  32.4 3.8 %all-to-all-start.1 = ((bf16[16,16,128]{2,1,0:T(8,128)(2,1)}), bf16[16,16,128]{2,1,0:T(8,128)(2,1)S(1)}, u32[]{:S(2)}, u32[]{:S(2)}) async-start(bf16[16,16,128]{2,1,0:T(8,128)(2,1)} %get-tuple-element.68), calls=%async_computation.1 | async-start | bytes 131072 | tf_op jit(solution)/shard_map/all_to_all | solution.py:595
  36.3 2.8 %shard_map.162 = (bf16[256,256]{1,0:T(8,128)(2,1)S(1)}, bf16[128,256]{1,0:T(8,128)(2,1)S(1)}, f32[128,256]{1,0:T(8,128)S(1)}, bf16[128,256]{1,0:T(8,128)(2,1)S(1...) custom-call(bf16[16,32,128]{2,1,0:T(8,128)(2,1)} %get-tuple-element.69.ref, ...), custom_call_target="tpu_custom_call" | custom-call | bytes 18000000 | tf_op jit(solution)/shard_map/pallas_call | solution.py:163
  39.1 3.2 %all-to-all-done.1 = bf16[16,16,128]{2,1,0:T(8,128)(2,1)S(1)} async-done(((bf16[16,16,128]{2,1,0:T(8,128)(2,1)}), bf16[16,16,128]{2,1,0:T(8,128)(2,1)S(1)}, u32[]{:S(2)}, u32[]{:S(2)}) %all-to-all-start.1) | async-done | bytes 65568 | tf_op jit(solution)/shard_map/all_to_all | solution.py:595
  42.3 3.8 %shard_map.163 = (bf16[1024,128]{1,0:T(8,128)(2,1)}, bf16[128,512]{1,0:T(8,128)(2,1)}, bf16[128,512]{1,0:T(8,128)(2,1)}, bf16[128,512]{1,0:T(8,128)(2,1)}, f32[4,128,128]{2,1,0:T(8,128)}) custom-call(bf16[256,128]{1,0:T(8,128)(2,1)S(1)} %bitcast.9, bf16[256,256]{1,0:T(8,128)(2,1)S(1)} %get-tuple-element.72.refs_1_, ...), custom_call_target="tpu_custom_call" | custom-call | bytes 9000000 | tf_op jit(solution)/shard_map/pallas_call | solution.py:163
  46.1 4.3 %all-to-all-start.2 = ((bf16[16,64,128]{2,1,0:T(8,128)(2,1)}), bf16[16,64,128]{2,1,0:T(8,128)(2,1)S(1)}, u32[]{:S(2)}, u32[]{:S(2)}) async-start(bf16[16,64,128]{2,1,0:T(8,128)(2,1)} %bitcast.11), calls=%async_computation.2 | async-start | bytes 524288 | tf_op jit(solution)/shard_map/all_to_all | solution.py:595
  50.4 5.3 %shard_map.164 = (bf16[512,128]{1,0:T(8,128)(2,1)}, bf16[128,2048]{1,0:T(8,128)(2,1)}, bf16[128,2048]{1,0:T(8,128)(2,1)}, bf16[128,2048]{1,0:T(8,128)(2,1)}, f32...) custom-call(bf16[128,512]{1,0:T(8,128)(2,1)} %get-tuple-element.70.r, ...), custom_call_target="tpu_custom_call" | custom-call | bytes 18000000 | tf_op jit(solution)/shard_map/pallas_call | solution.py:163
  55.7 4.3 %all-to-all-done.2 = bf16[16,64,128]{2,1,0:T(8,128)(2,1)S(1)} async-done(((bf16[16,64,128]{2,1,0:T(8,128)(2,1)}), bf16[16,64,128]{2,1,0:T(8,128)(2,1)S(1)}, u32[]{:S(2)}, u32[]{:S(2)}) %all-to-all-start.2) | async-done | bytes 262176 | tf_op jit(solution)/shard_map/all_to_all | solution.py:595
  59.9 4.5 %shard_map.165 = (bf16[1024,128]{1,0:T(8,128)(2,1)}, bf16[128,2048]{1,0:T(8,128)(2,1)}, bf16[128,2048]{1,0:T(8,128)(2,1)}) custom-call(bf16[1024,128]{1,0:T(8,128)(2,1)S(1)} %bitcast.8, bf16[512,1024]{1,0:T(8,128)(2,1)S(1)} %get-tuple-element.86.refs_1_, bf16[128,2048]{1,0:T(8,128)(2,1)} %get-tuple-element.87.refs_2_, ...), custom_call_target="tpu_custom_call" | custom-call | bytes 12000000 | tf_op jit(solution)/shard_map/pallas_call | solution.py:163
  64.4 4.0 %all-to-all-start.3 = ((bf16[16,64,128]{2,1,0:T(8,128)(2,1)}), bf16[16,64,128]{2,1,0:T(8,128)(2,1)S(1)}, u32[]{:S(2)}, u32[]{:S(2)}) async-start(bf16[16,64,128]{2,1,0:T(8,128)(2,1)} %bitcast.12), calls=%async_computation.3 | async-start | bytes 524288 | tf_op jit(solution)/shard_map/all_to_all | solution.py:595
  68.5 5.5 %shard_map.166 = (bf16[256,128]{1,0:T(8,128)(2,1)}, bf16[256,128]{1,0:T(8,128)(2,1)}, f32[2048,128]{1,0:T(8,128)}) custom-call(s32[8,2048]{1,0:T(8,128)} %refs_0_.5, f32[8,2048]{1,0:T(8,128)} %refs_1_.5, bf16[3,4,128,128]{3,2,1,0:T(8,128)(2,1)} %refs_2_.5, bf16[128,2048]{1,0:T(8,128)(2,1)} %get-tuple-element.95.refs_3_, ...), custom_call_target="tpu_custom_call" | custom-call | bytes 18000000 | tf_op jit(solution)/shard_map/pallas_call | solution.py:163
  73.9 4.1 %all-to-all-done.3.refs_0_ = bf16[16,64,128]{2,1,0:T(8,128)(2,1)S(1)} async-done(((bf16[16,64,128]{2,1,0:T(8,128)(2,1)}), bf16[16,64,128]{2,1,0:T(8,128)(2,1)S(1)}, u32[]{:S(2)}, u32[]{:S(2)}) %all-to-all-start.3) | async-done | bytes 262176 | tf_op jit(solution)/shard_map/all_to_all | solution.py:595
  78.0 0.9 shard_map.168
  78.9 4.1 %all-to-all-start.4 = ((bf16[16,64,128]{2,1,0:T(8,128)(2,1)}), bf16[16,64,128]{2,1,0:T(8,128)(2,1)S(1)}, u32[]{:S(2)}, u32[]{:S(2)}) async-start(bf16[16,64,128]{2,1,0:T(8,128)(2,1)} %shard_map.168), calls=%async_computation.4 | async-start | bytes 524288 | tf_op jit(solution)/shard_map/all_to_all | solution.py:595
  83.1 3.5 %collective-permute-start.3 = (bf16[256,128]{1,0:T(8,128)(2,1)S(1)}, bf16[256,128]{1,0:T(8,128)(2,1)S(1)}, u32[]{:S(2)}, u32[]{:S(2)}) collective-permute-start(bf16[256,128]{1,0:T(8,128)(2,1)S(1)} %copy-done.1), channel_id=1, source_target_pairs={{1,2},{2,1},{3,4},{4,3},{5,6},{6,5},{7,8},{8,7},{9,10},{10,9},{11,... | collective-permute-start | bytes 196616 | tf_op jit(solution)/shard_map/ppermute | solution.py:775
  86.7 2.6 %collective-permute-done.3.refs_2_ = bf16[256,128]{1,0:T(8,128)(2,1)S(1)} collective-permute-done((bf16[256,128]{1,0:T(8,128)(2,1)S(1)}, bf16[256,128]{1,0:T(8,128)(2,1)S(1)}, u32[]{:S(2)}, u32[]{:S(2)}) %collective-permute-start.3) | collective-permute-done | bytes 65568 | tf_op jit(solution)/shard_map/ppermute | solution.py:775
  89.3 2.2 %shard_map.167 = (bf16[2048,128]{1,0:T(8,128)(2,1)}, f32[12,128,128]{2,1,0:T(8,128)}) custom-call(f32[2048,128]{1,0:T(8,128)} %get-tuple-element.97.refs_0_, bf16[256,128]{1,0:T(8,128)(2,1)S(1)} %collective-permute-done.2.refs_1_, bf16[256,128]{1,0:T(8,128)(2,1)S(1)} %collective-permute-done.3.refs_2_, f32[4,128,128]{2,1,0:T(8,128)} %get-tuple-element.100.refs_3_), custom_call_target="tpu_custom_call" | custom-call | bytes 3000000 | tf_op jit(solution)/shard_map/pallas_call | solution.py:163
  91.5 1.1 %all-to-all-done.4 = bf16[16,64,128]{2,1,0:T(8,128)(2,1)S(1)} async-done(((bf16[16,64,128]{2,1,0:T(8,128)(2,1)}), bf16[16,64,128]{2,1,0:T(8,128)(2,1)S(1)}, u32[]{:S(2)}, u32[]{:S(2)}) %all-to-all-start.4) | async-done | bytes 262176 | tf_op jit(solution)/shard_map/all_to_all | solution.py:595
  (11 shorter events, 1.9 us)
Async XLA Ops:
  1.5 8.9 %collective-permute-start.1 = (bf16[256,128]{1,0:T(8,128)(2,1)S(1)}, bf16[256,128]{1,0:T(8,128)(2,1)S(1)}, u32[]{:S(2)}, u32[]{:S(2)}) collective-permute-start(bf16[256,128]{1,0:T(8,128)(2,1)S(1)} %get-tuple-element.104), channel_id=1, source_target_pairs={{1,2},{2,1},{3,4},{4,3},{5,6},{6,5},{7,8},{8,7},{9,10},{10,9},{11,... | collective-permute-start | bytes 196616 | tf_op jit(solution)/shard_map/ppermute | solution.py:636
  6.1 4.4 %collective-permute-start = (bf16[256,128]{1,0:T(8,128)(2,1)S(1)}, bf16[256,128]{1,0:T(8,128)(2,1)S(1)}, u32[]{:S(2)}, u32[]{:S(2)}) collective-permute-start(bf16[256,128]{1,0:T(8,128)(2,1)S(1)} %get-tuple-element.105), channel_id=1, source_target_pairs={{0,1},{1,0},{2,3},{3,2},{4,5},{5,4},{6,7},{7,6},{8,9},{9,8},{10,11... | collective-permute-start | bytes 196616 | tf_op jit(solution)/shard_map/ppermute | solution.py:635
  12.3 17.3 %all-to-all-start = ((bf16[16,96,128]{2,1,0:T(8,128)(2,1)}), bf16[16,96,128]{2,1,0:T(8,128)(2,1)S(1)}, u32[]{:S(2)}, u32[]{:S(2)}) async-start(bf16[16,96,128]{2,1,0:T(8,128)(2,1)} %get-tuple-element.62), calls=%async_computation | async-start | bytes 786432 | tf_op jit(solution)/shard_map/all_to_all | solution.py:595
  32.4 9.9 %all-to-all-start.1 = ((bf16[16,16,128]{2,1,0:T(8,128)(2,1)}), bf16[16,16,128]{2,1,0:T(8,128)(2,1)S(1)}, u32[]{:S(2)}, u32[]{:S(2)}) async-start(bf16[16,16,128]{2,1,0:T(8,128)(2,1)} %get-tuple-element.68), calls=%async_computation.1 | async-start | bytes 131072 | tf_op jit(solution)/shard_map/all_to_all | solution.py:595
  46.1 13.8 %all-to-all-start.2 = ((bf16[16,64,128]{2,1,0:T(8,128)(2,1)}), bf16[16,64,128]{2,1,0:T(8,128)(2,1)S(1)}, u32[]{:S(2)}, u32[]{:S(2)}) async-start(bf16[16,64,128]{2,1,0:T(8,128)(2,1)} %bitcast.11), calls=%async_computation.2 | async-start | bytes 524288 | tf_op jit(solution)/shard_map/all_to_all | solution.py:595
  64.4 13.6 %all-to-all-start.3 = ((bf16[16,64,128]{2,1,0:T(8,128)(2,1)}), bf16[16,64,128]{2,1,0:T(8,128)(2,1)S(1)}, u32[]{:S(2)}, u32[]{:S(2)}) async-start(bf16[16,64,128]{2,1,0:T(8,128)(2,1)} %bitcast.12), calls=%async_computation.3 | async-start | bytes 524288 | tf_op jit(solution)/shard_map/all_to_all | solution.py:595
  78.9 4.2 %copy-start.1 = (bf16[256,128]{1,0:T(8,128)(2,1)S(1)}, bf16[256,128]{1,0:T(8,128)(2,1)}, u32[]{:S(2)}) copy-start(bf16[256,128]{1,0:T(8,128)(2,1)} %get-tuple-element.99) | copy-start | bytes 196612
  78.9 7.7 %copy-start = (bf16[256,128]{1,0:T(8,128)(2,1)S(1)}, bf16[256,128]{1,0:T(8,128)(2,1)}, u32[]{:S(2)}) copy-start(bf16[256,128]{1,0:T(8,128)(2,1)} %get-tuple-element.98.refs_1_) | copy-start | bytes 196612
  78.9 13.7 %all-to-all-start.4 = ((bf16[16,64,128]{2,1,0:T(8,128)(2,1)}), bf16[16,64,128]{2,1,0:T(8,128)(2,1)S(1)}, u32[]{:S(2)}, u32[]{:S(2)}) async-start(bf16[16,64,128]{2,1,0:T(8,128)(2,1)} %shard_map.168), calls=%async_computation.4 | async-start | bytes 524288 | tf_op jit(solution)/shard_map/all_to_all | solution.py:595
  83.1 6.3 %collective-permute-start.3 = (bf16[256,128]{1,0:T(8,128)(2,1)S(1)}, bf16[256,128]{1,0:T(8,128)(2,1)S(1)}, u32[]{:S(2)}, u32[]{:S(2)}) collective-permute-start(bf16[256,128]{1,0:T(8,128)(2,1)S(1)} %copy-done.1), channel_id=1, source_target_pairs={{1,2},{2,1},{3,4},{4,3},{5,6},{6,5},{7,8},{8,7},{9,10},{10,9},{11,... | collective-permute-start | bytes 196616 | tf_op jit(solution)/shard_map/ppermute | solution.py:775
  86.6 2.7 %collective-permute-start.2 = (bf16[256,128]{1,0:T(8,128)(2,1)S(1)}, bf16[256,128]{1,0:T(8,128)(2,1)S(1)}, u32[]{:S(2)}, u32[]{:S(2)}) collective-permute-start(bf16[256,128]{1,0:T(8,128)(2,1)S(1)} %copy-done), channel_id=1, source_target_pairs={{0,1},{1,0},{2,3},{3,2},{4,5},{5,4},{6,7},{7,6},{8,9},{9,8},{10,11... | collective-permute-start | bytes 196616 | tf_op jit(solution)/shard_map/ppermute | solution.py:774

commit v7 on v6

--- a/solution.py
+++ b/solution.py
@@ -331,7 +331,7 @@
 
 
 def mid_kernel(block_rows, chunk, io, need, flush, ins, outs, blocks, coarse):
-    got, smid, w01, w2t, w3t, pool_mid = ins
+    got, smid, w01, w2t, w3t, pool_mid, _ = ins
     send_ref, hid_ref, agg_ref, sel_ref, ext_ref = outs
     peers = got.shape[0]
     nodes = smid.shape[0]
@@ -464,34 +464,16 @@
     send_ref[...] = dot_nt(sel[...], mid_grad).astype(BF)
 
 
-def third_window_kernel(tile_rows, mid_scale, io, need, flush, ins, outs):
-    mhid, magg, gmid, msg, mfg, feat, fine_cot, w0, pool, place, agg, w1 = ins
-    wg_ref, hid_ref, mid_ref, outer_ref, sl1_ref, sl2_ref, cot_ref, pick_ref, po_ref = outs
-    d, rows = hid_ref.shape
-    block_rows = pool.shape[0]
-    per = TILE // tile_rows
-    need()
-    w01, w2t, _ = forward_weights(w1)
-    middle = silu(dot(w01, jnp.concatenate([mhid[...], magg[...]], axis=0))).astype(BF)
-    outer = silu(dot(w2t, middle)).astype(BF)
-    wg_ref[0:d, :] = (dot_nt(mhid[...], mfg[...]) * mid_scale).astype(BF)
-    wg_ref[d : 2 * d, :] = (dot_nt(magg[...], mfg[...]) * mid_scale).astype(BF)
-    wg_ref[2 * d : 3 * d, :] = (dot_nt(middle, msg[...]) * mid_scale).astype(BF)
-    wg_ref[3 * d : 4 * d, :] = (dot_nt(outer, gmid[...]) * mid_scale).astype(BF)
+def saved_kernel(tile_rows, io, need, flush, ins, outs):
+    feat, agg, w, fine_cot, pool, _ = ins
+    hid_ref, mid_ref, outer_ref, sl1_ref, sl2_ref, cot_ref, po_ref = outs
+    rows = feat.shape[0]
+    need(0, 1, 2)
     hid_ref[...] = jnp.transpose(feat[...])
-    cot_ref[...] = jnp.transpose(fine_cot[...])
-    slots = pick_ref.shape[1]
-    lane = lax.broadcasted_iota(jnp.int32, (block_rows, slots), 1)
-    lane = lane - lax.broadcasted_iota(jnp.int32, (block_rows, slots), 0)
-    for t in range(0, rows // tile_rows, 2):
-        both = [jnp.where(lane == place[t + j] * block_rows, 1.0, 0.0) for j in range(2)]
-        pick_ref[t * block_rows : (t + 2) * block_rows, :] = jnp.concatenate(
-            both, axis=0
-        ).astype(BF)
-    flush(0, 1, 6)
-    w01, w2t, _ = forward_weights(w0)
-    for i in range(rows // TILE):
-        cols = slice(i * TILE, (i + 1) * TILE)
+    flush(0)
+    w01, w2t, _ = forward_weights(w)
+    for start in range(0, rows, 512):
+        cols = slice(start, min(start + 512, rows))
         first = dot(w01, jnp.concatenate([hid_ref[:, cols], agg[:, cols]], axis=0))
         s1 = 1.0 / (1.0 + jnp.exp(-first))
         middle = (first * s1).astype(BF)
@@ -501,11 +483,42 @@
         s2 = 1.0 / (1.0 + jnp.exp(-second))
         outer_ref[:, cols] = (second * s2).astype(BF)
         sl2_ref[:, cols] = s2 * (1.0 + second * (1.0 - s2))
-        po_ref[i] = pool_matrix(pool[:, cols], tile_rows)
+    need()
+    cot_ref[...] = jnp.transpose(fine_cot[...])
+    for i in range(rows // TILE):
+        po_ref[i] = pool_matrix(pool[:, i * TILE : (i + 1) * TILE], tile_rows)
+
+
+def third_window_kernel(mid_scale, io, need, flush, ins, outs):
+    mhid, magg, gmid, msg, mfg, w1, place = ins
+    wg_ref, pick_ref = outs
+    d = mhid.shape[0]
+    block_rows = pick_ref.shape[0] // place.shape[0]
+    need()
+    w01, w2t, _ = forward_weights(w1)
+    middle = silu(dot(w01, jnp.concatenate([mhid[...], magg[...]], axis=0))).astype(BF)
+    outer = silu(dot(w2t, middle)).astype(BF)
+    wg_ref[0:d, :] = (dot_nt(mhid[...], mfg[...]) * mid_scale).astype(BF)
+    wg_ref[d : 2 * d, :] = (dot_nt(magg[...], mfg[...]) * mid_scale).astype(BF)
+    wg_ref[2 * d : 3 * d, :] = (dot_nt(middle, msg[...]) * mid_scale).astype(BF)
+    wg_ref[3 * d : 4 * d, :] = (dot_nt(outer, gmid[...]) * mid_scale).astype(BF)
+    slots = pick_ref.shape[1]
+    lane = lax.broadcasted_iota(jnp.int32, (block_rows, slots), 1)
+    lane = lane - lax.broadcasted_iota(jnp.int32, (block_rows, slots), 0)
+    for t in range(0, place.shape[0], 2):
+        both = [jnp.where(lane == place[t + j] * block_rows, 1.0, 0.0) for j in range(2)]
+        pick_ref[t * block_rows : (t + 2) * block_rows, :] = jnp.concatenate(
+            both, axis=0
+        ).astype(BF)
+
+
+def add_kernel(io, need, flush, ins, outs):
+    mine, other = ins[:2]
+    outs[0][...] = (mine[...].astype(F32) + other[...].astype(F32)).astype(BF)
 
 
 def fine_grad_kernel(scale, io, need, flush, ins, outs, g_ref, fg_ref):
-    got, pick, cot, pool, w, slope2, slope1, hid, agg, mid, outer, mid_wg = ins
+    got, pick, cot, pool, w, slope2, slope1, hid, agg, mid, outer, _ = ins
     send_ref, g_out, fg_out = outs
     d, rows = hid.shape
     if pick.shape[1] > 1024:
@@ -525,7 +538,6 @@
     fg_ref[...] = fg
     io.start(fg_ref, fg_out)
     need()
-    send_ref[4 * d : 8 * d, :] = mid_wg[...]
     for m, (a, b) in enumerate(
         ((hid[...], fg), (agg[...], fg), (mid[...], sg), (outer[...], g))
     ):
@@ -533,7 +545,7 @@
 
 
 def fine_spread_kernel(io, need, flush, ins, outs, s_ref, total):
-    off, ew, w, g, fg = ins
+    off, ew, w, g, fg, _ = ins
     rim_near, rim_far, out_ref = outs
     rows = g.shape[1]
     clear_corners(s_ref.at[0])
@@ -559,7 +571,7 @@
 
 
 def sum_kernel(io, need, flush, ins, outs, part):
-    got, _ = ins
+    got = ins[0]
     send_ref = outs[0]
     peers = got.shape[0]
     need()
@@ -583,10 +595,9 @@
 
 
 def gather_kernel(io, need, flush, ins, outs, wide):
-    summed, _ = ins
     out_ref = outs[0]
     for half in range(2):
-        wide[4 * half : 4 * half + 4] = summed[4 * half : 4 * half + 4].astype(F32)
+        wide[4 * half : 4 * half + 4] = ins[half][...].astype(F32)
         part = pl.ds(4 * half, 4)
         io.start(wide.at[part], out_ref.at[part])
 
@@ -683,9 +694,25 @@
         ],
         us=6,
     )
+    hid, mid, outer, slope1, slope2, cot, pool_b = call(
+        functools.partial(saved_kernel, tile_rows),
+        [
+            (features, "h"), (agg, "h"), (weights, "0"), (fine_cotangent, "h"),
+            (pool_fine, "h"), (m3t, "r"),
+        ],
+        [
+            (shape((d, n)), "h"), (shape((d, n)), "h"), (shape((d, n)), "h"),
+            (shape((d, n), F32), "h"), (shape((d, n), F32), "h"), (shape((d, n)), "h"),
+            (shape((n // TILE, per, TILE)), "h"),
+        ],
+        us=4,
+    )
     send2, mhid, magg, sel, ext = call(
         functools.partial(mid_kernel, block_rows, chunk),
-        [(got1, "v"), (smid, "h"), (m01, "h"), (m2t, "h"), (m3t, "h"), (pool_mid, "h")],
+        [
+            (got1, "v"), (smid, "h"), (m01, "h"), (m2t, "h"), (m3t, "h"), (pool_mid, "h"),
+            (pool_b, "r"),
+        ],
         [
             (shape((peers, n2, d)), "r"), (shape((d, n1)), "h"), (shape((d, n1)), "h"),
             (shape((peers * chunk, n1)), "h"), (shape((peers, n2 + 16, d)), "r"),
@@ -727,50 +754,61 @@
     )
     got3 = exchange(send3.reshape(peers, chunk, d))
     pick_kind = "v" if peers * chunk <= 1024 else "h"
-    mid_wg, hid, mid, outer, slope1, slope2, cot, pick, pool_b = call(
-        functools.partial(third_window_kernel, tile_rows, 1.0 / math.sqrt(n1 * peers)),
-        [
-            (mhid, "h"), (magg, "h"), (gmid, "h"), (msg, "h"), (mfg, "h"), (features, "h"),
-            (fine_cotangent, "h"), (weights, "0"), (pool_fine, "h"), (place, "s"), (agg, "h"),
-            (weights, "1"),
-        ],
-        [
-            (shape((4 * d, d)), "h"), (shape((d, n)), "h"), (shape((d, n)), "h"),
-            (shape((d, n)), "h"), (shape((d, n), F32), "h"), (shape((d, n), F32), "h"),
-            (shape((d, n)), "h"), (shape((tile_count * block_rows, peers * chunk)), pick_kind),
-            (shape((n // TILE, per, TILE)), "h"),
-        ],
-        us=6,
-    )
+    mid_wg, pick = call(
+        functools.partial(third_window_kernel, 1.0 / math.sqrt(n1 * peers)),
+        [
+            (mhid, "h"), (magg, "h"), (gmid, "h"), (msg, "h"), (mfg, "h"), (weights, "1"),
+            (place, "s"),
+        ],
+        [
+            (shape((4 * d, d)), "v"),
+            (shape((tile_count * block_rows, peers * chunk)), pick_kind),
+        ],
+        us=3,
+    )
+    reaches = [1 << i for i in range((peers - 1).bit_length())]
+    reaches = reaches[:1] + reaches[-1:] + reaches[1:-1]
+
+    def double(total, reach, *after):
+        other = lax.ppermute(total, "nodes", [(i, i ^ reach) for i in range(peers)])
+        ins = [(total, "v"), (other, "v")] + [(x, "r") for x in after]
+        return call(add_kernel, ins, [(shape((4 * d, d)), "v")], us=1)[0]
+
+    sums = [mid_wg]
+    for reach in reaches[:2]:
+        sums.append(double(sums[-1], reach))
     send4, g, fg = call(
         functools.partial(fine_grad_kernel, 1.0 / math.sqrt(n * peers)),
         [
             (got3.reshape(peers * chunk, d), "v"), (pick, pick_kind), (cot, "h"), (pool_b, "h"),
             (weights, "0"), (slope2, "h"), (slope1, "h"), (hid, "h"), (agg, "h"), (mid, "h"),
-            (outer, "h"), (mid_wg, "h"),
-        ],
-        [(shape((8 * d, d)), "h"), (shape((d, n)), "r"), (shape((d, n)), "r")],
+            (outer, "h"), (sums[1], "v"),
+        ],
+        [(shape((4 * d, d)), "h"), (shape((d, n)), "r"), (shape((d, n)), "r")],
         scratch=(pltpu.VMEM((d, n), BF), pltpu.VMEM((d, n), BF)),
         copies=2,
         us=4,
     )
-    got4 = exchange(send4.reshape(peers, 8 * d // peers, d))
+    got4 = exchange(send4.reshape(peers, 4 * d // peers, d))
     rim_near, rim_far, spread = call(
         fine_spread_kernel,
-        [(fine_offsets, "h"), (fine_edge_w, "h"), (weights, "0"), (g, "h"), (fg, "h")],
+        [(fine_offsets, "h"), (fine_edge_w, "h"), (weights, "0"), (g, "h"), (fg, "h"), (sums[2], "v")],
         [(shape((HALO, d)), "h"), (shape((HALO, d)), "h"), (shape((n, d), F32), "h")],
         scratch=(pltpu.VMEM((2, window, TILE), BF), pltpu.VMEM((n + 2 * HALO, d), F32)),
         us=6,
     )
+    sums.append(double(sums[2], reaches[2], rim_near))
     (send5,) = call(
         sum_kernel,
-        [(got4, "v"), (rim_near, "r")],
-        [(shape((peers, 8 * d // peers, d)), "r")],
-        scratch=(pltpu.VMEM((8 * d // peers, d), BF),),
+        [(got4, "v"), (rim_near, "r"), (sums[3], "v")],
+        [(shape((peers, 4 * d // peers, d)), "r")],
+        scratch=(pltpu.VMEM((4 * d // peers, d), BF),),
         copies=peers,
         us=1,
     )
     got5 = exchange(send5)
+    for reach in reaches[3:]:
+        sums.append(double(sums[-1], reach))
     from_across = lax.ppermute(rim_near, "nodes", inside_pairs)
     from_beside = lax.ppermute(rim_far, "nodes", between_pairs)
     feature_grads, weight_grads = call(
@@ -782,11 +820,13 @@
     )
     (weight_grads,) = call(
         gather_kernel,
-        [(got5.reshape(8, d, d), "v"), (weight_grads, "r")],
+        [
+            (got5.reshape(4, d, d), "v"), (sums[-1].reshape(4, d, d), "v"), (weight_grads, "r"),
+        ],
         [(shape((12, d, d), F32), "r")],
         scratch=(pltpu.VMEM((8, d, d), F32),),
         copies=2,
-        aliases={1: 0},
+        aliases={2: 0},
         us=1,
     )
     weight_grads = weight_grads.reshape(3, 4, d, d)

time: 95.1 us -> 95.4 us (level)
  waiting for transfers between devices: 25.2 us -> 15.6 us
  starting transfers between devices: 29.9 us -> 39 us
  Pallas kernels: 36.7 us -> 38 us
    all_to_all x5, waiting for transfers between devices: 22.6 us -> 12.1 us  [exchange(): return lax.all_to_all(x, 'nodes', split_axis=0, concat_axis=0, tiled=True)]
    ppermute x0 -> x4, starting transfers between devices: none -> 5.51 us  [double(): other = lax.ppermute(total, 'nodes', [(i, i ^ reach) for i in range(peers)])]
    all_to_all x5, starting transfers between devices: 21.6 us -> 25.2 us  [exchange(): return lax.all_to_all(x, 'nodes', split_axis=0, concat_axis=0, tiled=True)]
    pallas_call x12 -> x17, Pallas kernels: 36.7 us -> 38 us  [call(): pl.pallas_call(body, out_shape=[s if kind == 'v' else pltpu.HBM(s.shape,...]
    ppermute x0 -> x4, waiting for transfers between devices: none -> 1.14 us  [double(): other = lax.ppermute(total, 'nodes', [(i, i ^ reach) for i in range(peers)])]
  transfers between devices with their start and end apart: 9 -> 13, of which waited for: 6 -> 5; matrix products, arithmetic and copies ran while one was open for 0% -> 0% of each run, Pallas kernels for 24% -> 30%
where the time goes in v7:
time: 95.4 us; the launch traced here: 94.6 us
  starting transfers between devices  39 us (41%)
  Pallas kernels  38 us (40%)
  waiting for transfers between devices  15.6 us (16%)
  between operations  1.04 us (1%)
    pallas_call x17, Pallas kernels, call(): pl.pallas_call(body, out_shape=[s if kind == 'v' else pltpu.HBM(s.shape,...  38 us
    all_to_all x5, starting transfers between devices, exchange(): return lax.all_to_all(x, 'nodes', split_axis=0, concat_axis=0, tiled=True)  25.2 us
    all_to_all x5, waiting for transfers between devices, exchange(): return lax.all_to_all(x, 'nodes', split_axis=0, concat_axis=0, tiled=True)  12.1 us
    ppermute x4, starting transfers between devices, double(): other = lax.ppermute(total, 'nodes', [(i, i ^ reach) for i in range(peers)])  5.51 us
    ppermute x1, starting transfers between devices, per_device(): beside = lax.ppermute(far, 'nodes', between_pairs)  4.54 us
    ppermute x1, starting transfers between devices, per_device(): from_beside = lax.ppermute(rim_far, 'nodes', between_pairs)  3.61 us
    ppermute x1, waiting for transfers between devices, per_device(): from_beside = lax.ppermute(rim_far, 'nodes', between_pairs)  2.39 us
  transfers between devices with their start and end apart: 13, of which 5 were waited for; matrix products, arithmetic and copies ran while one was open for 0% of the time, Pallas kernels for 30%

profile of v7, /device:TPU:1, one launch (start us, length us, event | category | flops | bytes accessed | tf_op | source)
XLA Modules:
  0.0 94.6 jit_solution(16151431058197549935)
XLA Ops:
  1.5 4.5 %collective-permute-start.1 = (bf16[256,128]{1,0:T(8,128)(2,1)S(1)}, bf16[256,128]{1,0:T(8,128)(2,1)S(1)}, u32[]{:S(2)}, u32[]{:S(2)}) collective-permute-start(bf16[256,128]{1,0:T(8,128)(2,1)S(1)} %get-tuple-element.104), channel_id=1, source_target_pairs={{1,2},{2,1},{3,4},{4,3},{5,6},{6,5},{7,8},{8,7},{9,10},{10,9},{11,... | collective-permute-start | bytes 196616 | tf_op jit(solution)/shard_map/ppermute | solution.py:647
  6.2 4.3 %shard_map.158 = (bf16[2,768,256]{2,1,0:T(8,128)(2,1)S(1)}, bf16[2,128,512]{2,1,0:T(8,128)(2,1)S(1)}, bf16[128,256]{1,0:T(8,128)(2,1)S(1)}, bf16[128,128]{1,0:T(...) custom-call(s32[8,2048]{1,0:T(8,128)} %refs_0_.7, ...), custom_call_target="tpu_custom_call" | custom-call | bytes 18000000 | tf_op jit(solution)/shard_map/pallas_call | solution.py:163
  10.5 1.8 %shard_map.159 = (bf16[16,96,128]{2,1,0:T(8,128)(2,1)}, bf16[128,2048]{1,0:T(8,128)(2,1)}) custom-call(bf16[256,128]{1,0:T(8,128)(2,1)S(1)} %collective-permute-done.refs_0_, bf16[256,128]{1,0:T(8,128)(2,1)S(1)} %collective-permute-done.1.refs_1_, bf16[2,768,256]{2,1,0:T(8,128)(2,1)S(1)} %get-tuple-element.53.refs_2_, ...), custom_call_target="tpu_custom_call" | custom-call | bytes 9000000 | tf_op jit(solution)/shard_map/pallas_call | solution.py:163
  12.3 5.4 %all-to-all-start = ((bf16[16,96,128]{2,1,0:T(8,128)(2,1)}), bf16[16,96,128]{2,1,0:T(8,128)(2,1)S(1)}, u32[]{:S(2)}, u32[]{:S(2)}) async-start(bf16[16,96,128]{2,1,0:T(8,128)(2,1)} %get-tuple-element.62), calls=%async_computation | async-start | bytes 786432 | tf_op jit(solution)/shard_map/all_to_all | solution.py:606
  17.7 2.0 %shard_map.160 = (bf16[512,512]{1,0:T(8,128)(2,1)}, bf16[128,256]{1,0:T(8,128)(2,1)}, bf16[128,128]{1,0:T(8,128)(2,1)}, bf16[128,128]{1,0:T(8,128)(2,1)}) custom-call(s32[8,512]{1,0:T(8,128)} %refs_0_.5, f32[8,512]{1,0:T(8,128)} %refs_1_.4, bf16[3,4,128,128]{3,2,1,0:T(8,128)(2,1)} %refs_2_.7, bf16[128,2048]{1,0:T(8,128)(2,1)} %get-tuple-element.63.refs_3_.refs_1_.refs_8_), custom_call_target="tpu_custom_call" | custom-call | bytes 18000000 | tf_op jit(solution)/shard_map/pallas_call | solution.py:163
  19.6 4.7 %shard_map.161 = (bf16[128,2048]{1,0:T(8,128)(2,1)}, bf16[128,2048]{1,0:T(8,128)(2,1)}, bf16[128,2048]{1,0:T(8,128)(2,1)}, f32[128,2048]{1,0:T(8,128)}, f32[128,...) custom-call(bf16[2048,128]{1,0:T(8,128)(2,1)} %refs_0_.6, ...), custom_call_target="tpu_custom_call" | custom-call | bytes 12000000 | tf_op jit(solution)/shard_map/pallas_call | solution.py:163
  24.3 5.3 %all-to-all-done.refs_0_ = bf16[16,96,128]{2,1,0:T(8,128)(2,1)S(1)} async-done(((bf16[16,96,128]{2,1,0:T(8,128)(2,1)}), bf16[16,96,128]{2,1,0:T(8,128)(2,1)S(1)}, u32[]{:S(2)}, u32[]{:S(2)}) %all-to-all-start) | async-done | bytes 393248 | tf_op jit(solution)/shard_map/all_to_all | solution.py:606
  29.6 2.9 %shard_map.162 = (bf16[16,16,128]{2,1,0:T(8,128)(2,1)}, bf16[128,512]{1,0:T(8,128)(2,1)}, bf16[128,512]{1,0:T(8,128)(2,1)}, bf16[1024,512]{1,0:T(8,128)(2,1)}, bf16[16,32,128]{2,1,0:T(8,128)(2,1)}) custom-call(bf16[16,96,128]{2,1,0:T(8,128)(2,1)S(1)} %all-to-all-done.refs_0_, bf16[512,512]{1,0:T(8,128)(2,1)} %get-tuple-element.64.refs_1_.refs_13_, ...), custom_call_target="tpu_custom_call" | custom-call | bytes 9000000 | tf_op jit(solution)/shard_map/pallas_call | solution.py:163
  32.5 3.8 %all-to-all-start.1 = ((bf16[16,16,128]{2,1,0:T(8,128)(2,1)}), bf16[16,16,128]{2,1,0:T(8,128)(2,1)S(1)}, u32[]{:S(2)}, u32[]{:S(2)}) async-start(bf16[16,16,128]{2,1,0:T(8,128)(2,1)} %get-tuple-element.69), calls=%async_computation.1 | async-start | bytes 131072 | tf_op jit(solution)/shard_map/all_to_all | solution.py:606
  36.3 2.8 %shard_map.163 = (bf16[256,256]{1,0:T(8,128)(2,1)S(1)}, bf16[128,256]{1,0:T(8,128)(2,1)S(1)}, f32[128,256]{1,0:T(8,128)S(1)}, bf16[128,256]{1,0:T(8,128)(2,1)S(1...) custom-call(bf16[16,32,128]{2,1,0:T(8,128)(2,1)} %get-tuple-element.70.ref, ...), custom_call_target="tpu_custom_call" | custom-call | bytes 18000000 | tf_op jit(solution)/shard_map/pallas_call | solution.py:163
  39.1 3.2 %all-to-all-done.1 = bf16[16,16,128]{2,1,0:T(8,128)(2,1)S(1)} async-done(((bf16[16,16,128]{2,1,0:T(8,128)(2,1)}), bf16[16,16,128]{2,1,0:T(8,128)(2,1)S(1)}, u32[]{:S(2)}, u32[]{:S(2)}) %all-to-all-start.1) | async-done | bytes 65568 | tf_op jit(solution)/shard_map/all_to_all | solution.py:606
  42.3 3.8 %shard_map.164 = (bf16[1024,128]{1,0:T(8,128)(2,1)}, bf16[128,512]{1,0:T(8,128)(2,1)}, bf16[128,512]{1,0:T(8,128)(2,1)}, bf16[128,512]{1,0:T(8,128)(2,1)}, f32[4,128,128]{2,1,0:T(8,128)}) custom-call(bf16[256,128]{1,0:T(8,128)(2,1)S(1)} %bitcast.11, bf16[256,256]{1,0:T(8,128)(2,1)S(1)} %get-tuple-element.73.refs_1_, ...), custom_call_target="tpu_custom_call" | custom-call | bytes 9000000 | tf_op jit(solution)/shard_map/pallas_call | solution.py:163
  46.1 4.3 %all-to-all-start.2 = ((bf16[16,64,128]{2,1,0:T(8,128)(2,1)}), bf16[16,64,128]{2,1,0:T(8,128)(2,1)S(1)}, u32[]{:S(2)}, u32[]{:S(2)}) async-start(bf16[16,64,128]{2,1,0:T(8,128)(2,1)} %bitcast.13), calls=%async_computation.2 | async-start | bytes 524288 | tf_op jit(solution)/shard_map/all_to_all | solution.py:606
  50.4 2.0 %shard_map.165 = (bf16[512,128]{1,0:T(8,128)(2,1)S(1)}, bf16[512,1024]{1,0:T(8,128)(2,1)S(1)}) custom-call(bf16[128,512]{1,0:T(8,128)(2,1)} %get-tuple-element.71.refs_1_.refs_0_, bf16[128,512]{1,0:T(8,128)(2,1)} %get-tuple-element.72.refs_2_.refs_1_, bf16[128,512]{1,0:T(8,128)(2,1)} %get-tuple-element.83.refs_2_, ...), custom_call_target="tpu_custom_call" | custom-call | bytes 9000000 | tf_op jit(solution)/shard_map/pallas_call | solution.py:163
  53.9 2.4 %collective-permute-start.3 = (bf16[512,128]{1,0:T(8,128)(2,1)S(1)}, bf16[512,128]{1,0:T(8,128)(2,1)S(1)}, u32[]{:S(2)}, u32[]{:S(2)}) collective-permute-start(bf16[512,128]{1,0:T(8,128)(2,1)S(1)} %shard_map.166.refs_11_.refs_0_), channel_id=1, source_target_pairs={{0,8},{1,9},{2,10},{3,11},{4,12},{5,13},{6,14},{7,15},{8,0},{9,1},... | collective-permute-start | bytes 393224 | tf_op jit(solution)/shard_map/ppermute | solution.py:773
  56.3 3.6 %all-to-all-done.2 = bf16[16,64,128]{2,1,0:T(8,128)(2,1)S(1)} async-done(((bf16[16,64,128]{2,1,0:T(8,128)(2,1)}), bf16[16,64,128]{2,1,0:T(8,128)(2,1)S(1)}, u32[]{:S(2)}, u32[]{:S(2)}) %all-to-all-start.2) | async-done | bytes 262176 | tf_op jit(solution)/shard_map/all_to_all | solution.py:606
  59.9 4.4 %shard_map.167 = (bf16[512,128]{1,0:T(8,128)(2,1)}, bf16[128,2048]{1,0:T(8,128)(2,1)}, bf16[128,2048]{1,0:T(8,128)(2,1)}) custom-call(bf16[1024,128]{1,0:T(8,128)(2,1)S(1)} %bitcast.8, bf16[512,1024]{1,0:T(8,128)(2,1)S(1)} %get-tuple-element.87.refs_1_, bf16[128,2048]{1,0:T(8,128)(2,1)} %get-tuple-element.88.refs_2_, ...), custom_call_target="tpu_custom_call" | custom-call | bytes 12000000 | tf_op jit(solution)/shard_map/pallas_call | solution.py:163
  64.3 6.3 %all-to-all-start.3 = ((bf16[16,32,128]{2,1,0:T(8,128)(2,1)}), bf16[16,32,128]{2,1,0:T(8,128)(2,1)S(1)}, u32[]{:S(2)}, u32[]{:S(2)}) async-start(bf16[16,32,128]{2,1,0:T(8,128)(2,1)} %bitcast.14), calls=%async_computation.3 | async-start | bytes 262144 | tf_op jit(solution)/shard_map/all_to_all | solution.py:606
  70.6 1.5 %collective-permute-start.6 = (bf16[512,128]{1,0:T(8,128)(2,1)S(1)}, bf16[512,128]{1,0:T(8,128)(2,1)S(1)}, u32[]{:S(2)}, u32[]{:S(2)}) collective-permute-start(bf16[512,128]{1,0:T(8,128)(2,1)S(1)} %shard_map.168.refs_5_.refs_0_), channel_id=1, source_target_pairs={{0,2},{1,3},{2,0},{3,1},{4,6},{5,7},{6,4},{7,5},{8,10},{9,11},{10,... | collective-permute-start | bytes 393224 | tf_op jit(solution)/shard_map/ppermute | solution.py:773
  72.1 5.4 %shard_map.169 = (bf16[256,128]{1,0:T(8,128)(2,1)}, bf16[256,128]{1,0:T(8,128)(2,1)}, f32[2048,128]{1,0:T(8,128)}) custom-call(s32[8,2048]{1,0:T(8,128)} %refs_0_.7, f32[8,2048]{1,0:T(8,128)} %refs_1_.5, bf16[3,4,128,128]{3,2,1,0:T(8,128)(2,1)} %refs_2_.7, bf16[128,2048]{1,0:T(8,128)(2,1)} %get-tuple-element.95.refs_3_, ...), custom_call_target="tpu_custom_call" | custom-call | bytes 18000000 | tf_op jit(solution)/shard_map/pallas_call | solution.py:163
  78.4 5.4 %all-to-all-start.4 = ((bf16[16,32,128]{2,1,0:T(8,128)(2,1)}), bf16[16,32,128]{2,1,0:T(8,128)(2,1)S(1)}, u32[]{:S(2)}, u32[]{:S(2)}) async-start(bf16[16,32,128]{2,1,0:T(8,128)(2,1)} %shard_map.172), calls=%async_computation.4 | async-start | bytes 262144 | tf_op jit(solution)/shard_map/all_to_all | solution.py:606
  85.3 3.6 %collective-permute-start.5 = (bf16[256,128]{1,0:T(8,128)(2,1)S(1)}, bf16[256,128]{1,0:T(8,128)(2,1)S(1)}, u32[]{:S(2)}, u32[]{:S(2)}) collective-permute-start(bf16[256,128]{1,0:T(8,128)(2,1)S(1)} %copy-done.1), channel_id=1, source_target_pairs={{1,2},{2,1},{3,4},{4,3},{5,6},{6,5},{7,8},{8,7},{9,10},{10,9},{11,... | collective-permute-start | bytes 196616 | tf_op jit(solution)/shard_map/ppermute | solution.py:813
  89.0 2.4 %collective-permute-done.5.refs_2_ = bf16[256,128]{1,0:T(8,128)(2,1)S(1)} collective-permute-done((bf16[256,128]{1,0:T(8,128)(2,1)S(1)}, bf16[256,128]{1,0:T(8,128)(2,1)S(1)}, u32[]{:S(2)}, u32[]{:S(2)}) %collective-permute-start.5) | collective-permute-done | bytes 65568 | tf_op jit(solution)/shard_map/ppermute | solution.py:813
  91.4 2.2 %shard_map.170 = (bf16[2048,128]{1,0:T(8,128)(2,1)}, f32[12,128,128]{2,1,0:T(8,128)}) custom-call(f32[2048,128]{1,0:T(8,128)} %get-tuple-element.97.refs_0_, bf16[256,128]{1,0:T(8,128)(2,1)S(1)} %collective-permute-done.4.refs_1_, bf16[256,128]{1,0:T(8,128)(2,1)S(1)} %collective-permute-done.5.refs_2_, f32[4,128,128]{2,1,0:T(8,128)} %get-tuple-element.100.refs_3_), custom_call_target="tpu_custom_call" | custom-call | bytes 3000000 | tf_op jit(solution)/shard_map/pallas_call | solution.py:163
  (24 shorter events, 5.6 us)
Async XLA Ops:
  1.5 8.9 %collective-permute-start.1 = (bf16[256,128]{1,0:T(8,128)(2,1)S(1)}, bf16[256,128]{1,0:T(8,128)(2,1)S(1)}, u32[]{:S(2)}, u32[]{:S(2)}) collective-permute-start(bf16[256,128]{1,0:T(8,128)(2,1)S(1)} %get-tuple-element.104), channel_id=1, source_target_pairs={{1,2},{2,1},{3,4},{4,3},{5,6},{6,5},{7,8},{8,7},{9,10},{10,9},{11,... | collective-permute-start | bytes 196616 | tf_op jit(solution)/shard_map/ppermute | solution.py:647
  6.1 4.4 %collective-permute-start = (bf16[256,128]{1,0:T(8,128)(2,1)S(1)}, bf16[256,128]{1,0:T(8,128)(2,1)S(1)}, u32[]{:S(2)}, u32[]{:S(2)}) collective-permute-start(bf16[256,128]{1,0:T(8,128)(2,1)S(1)} %get-tuple-element.105), channel_id=1, source_target_pairs={{0,1},{1,0},{2,3},{3,2},{4,5},{5,4},{6,7},{7,6},{8,9},{9,8},{10,11... | collective-permute-start | bytes 196616 | tf_op jit(solution)/shard_map/ppermute | solution.py:646
  12.3 17.3 %all-to-all-start = ((bf16[16,96,128]{2,1,0:T(8,128)(2,1)}), bf16[16,96,128]{2,1,0:T(8,128)(2,1)S(1)}, u32[]{:S(2)}, u32[]{:S(2)}) async-start(bf16[16,96,128]{2,1,0:T(8,128)(2,1)} %get-tuple-element.62), calls=%async_computation | async-start | bytes 786432 | tf_op jit(solution)/shard_map/all_to_all | solution.py:606
  32.5 9.9 %all-to-all-start.1 = ((bf16[16,16,128]{2,1,0:T(8,128)(2,1)}), bf16[16,16,128]{2,1,0:T(8,128)(2,1)S(1)}, u32[]{:S(2)}, u32[]{:S(2)}) async-start(bf16[16,16,128]{2,1,0:T(8,128)(2,1)} %get-tuple-element.69), calls=%async_computation.1 | async-start | bytes 131072 | tf_op jit(solution)/shard_map/all_to_all | solution.py:606
  46.1 13.7 %all-to-all-start.2 = ((bf16[16,64,128]{2,1,0:T(8,128)(2,1)}), bf16[16,64,128]{2,1,0:T(8,128)(2,1)S(1)}, u32[]{:S(2)}, u32[]{:S(2)}) async-start(bf16[16,64,128]{2,1,0:T(8,128)(2,1)} %bitcast.13), calls=%async_computation.2 | async-start | bytes 524288 | tf_op jit(solution)/shard_map/all_to_all | solution.py:606
  52.4 1.4 %collective-permute-start.2 = (bf16[512,128]{1,0:T(8,128)(2,1)S(1)}, bf16[512,128]{1,0:T(8,128)(2,1)S(1)}, u32[]{:S(2)}, u32[]{:S(2)}) collective-permute-start(bf16[512,128]{1,0:T(8,128)(2,1)S(1)} %get-tuple-element.94.refs_0_), channel_id=1, source_target_pairs={{0,1},{1,0},{2,3},{3,2},{4,5},{5,4},{6,7},{7,6},{8,9},{9,8},{10,11... | collective-permute-start | bytes 393224 | tf_op jit(solution)/shard_map/ppermute | solution.py:773
  53.9 16.7 %collective-permute-start.3 = (bf16[512,128]{1,0:T(8,128)(2,1)S(1)}, bf16[512,128]{1,0:T(8,128)(2,1)S(1)}, u32[]{:S(2)}, u32[]{:S(2)}) collective-permute-start(bf16[512,128]{1,0:T(8,128)(2,1)S(1)} %shard_map.166.refs_11_.refs_0_), channel_id=1, source_target_pairs={{0,8},{1,9},{2,10},{3,11},{4,12},{5,13},{6,14},{7,15},{8,0},{9,1},... | collective-permute-start | bytes 393224 | tf_op jit(solution)/shard_map/ppermute | solution.py:773
  64.3 13.3 %all-to-all-start.3 = ((bf16[16,32,128]{2,1,0:T(8,128)(2,1)}), bf16[16,32,128]{2,1,0:T(8,128)(2,1)S(1)}, u32[]{:S(2)}, u32[]{:S(2)}) async-start(bf16[16,32,128]{2,1,0:T(8,128)(2,1)} %bitcast.14), calls=%async_computation.3 | async-start | bytes 262144 | tf_op jit(solution)/shard_map/all_to_all | solution.py:606
  70.6 6.9 %collective-permute-start.6 = (bf16[512,128]{1,0:T(8,128)(2,1)S(1)}, bf16[512,128]{1,0:T(8,128)(2,1)S(1)}, u32[]{:S(2)}, u32[]{:S(2)}) collective-permute-start(bf16[512,128]{1,0:T(8,128)(2,1)S(1)} %shard_map.168.refs_5_.refs_0_), channel_id=1, source_target_pairs={{0,2},{1,3},{2,0},{3,1},{4,6},{5,7},{6,4},{7,5},{8,10},{9,11},{10,... | collective-permute-start | bytes 393224 | tf_op jit(solution)/shard_map/ppermute | solution.py:773
  78.4 6.8 %copy-start.1 = (bf16[256,128]{1,0:T(8,128)(2,1)S(1)}, bf16[256,128]{1,0:T(8,128)(2,1)}, u32[]{:S(2)}) copy-start(bf16[256,128]{1,0:T(8,128)(2,1)} %get-tuple-element.99) | copy-start | bytes 196612
  78.4 10.4 %copy-start = (bf16[256,128]{1,0:T(8,128)(2,1)S(1)}, bf16[256,128]{1,0:T(8,128)(2,1)}, u32[]{:S(2)}) copy-start(bf16[256,128]{1,0:T(8,128)(2,1)} %get-tuple-element.98.refs_2_.refs_1_) | copy-start | bytes 196612
  78.4 15.1 %all-to-all-start.4 = ((bf16[16,32,128]{2,1,0:T(8,128)(2,1)}), bf16[16,32,128]{2,1,0:T(8,128)(2,1)S(1)}, u32[]{:S(2)}, u32[]{:S(2)}) async-start(bf16[16,32,128]{2,1,0:T(8,128)(2,1)} %shard_map.172), calls=%async_computation.4 | async-start | bytes 262144 | tf_op jit(solution)/shard_map/all_to_all | solution.py:606
  83.9 9.7 %collective-permute-start.7 = (bf16[512,128]{1,0:T(8,128)(2,1)S(1)}, bf16[512,128]{1,0:T(8,128)(2,1)S(1)}, u32[]{:S(2)}, u32[]{:S(2)}) collective-permute-start(bf16[512,128]{1,0:T(8,128)(2,1)S(1)} %shard_map.171.refs_2_.refs_0_), channel_id=1, source_target_pairs={{0,4},{1,5},{2,6},{3,7},{4,0},{5,1},{6,2},{7,3},{8,12},{9,13},{10,... | collective-permute-start | bytes 393224 | tf_op jit(solution)/shard_map/ppermute | solution.py:773
  85.3 6.1 %collective-permute-start.5 = (bf16[256,128]{1,0:T(8,128)(2,1)S(1)}, bf16[256,128]{1,0:T(8,128)(2,1)S(1)}, u32[]{:S(2)}, u32[]{:S(2)}) collective-permute-start(bf16[256,128]{1,0:T(8,128)(2,1)S(1)} %copy-done.1), channel_id=1, source_target_pairs={{1,2},{2,1},{3,4},{4,3},{5,6},{6,5},{7,8},{8,7},{9,10},{10,9},{11,... | collective-permute-start | bytes 196616 | tf_op jit(solution)/shard_map/ppermute | solution.py:813
  88.9 2.5 %collective-permute-start.4 = (bf16[256,128]{1,0:T(8,128)(2,1)S(1)}, bf16[256,128]{1,0:T(8,128)(2,1)S(1)}, u32[]{:S(2)}, u32[]{:S(2)}) collective-permute-start(bf16[256,128]{1,0:T(8,128)(2,1)S(1)} %copy-done), channel_id=1, source_target_pairs={{0,1},{1,0},{2,3},{3,2},{4,5},{5,4},{6,7},{7,6},{8,9},{9,8},{10,11... | collective-permute-start | bytes 196616 | tf_op jit(solution)/shard_map/ppermute | solution.py:812

commit v8 on v7

--- a/solution.py
+++ b/solution.py
@@ -403,7 +403,7 @@
 
 def coarse_kernel(io, need, flush, ins, outs):
     got, sco, c01, c2t, cot_all, cot_back, w2, *rest = ins
-    cot_my, pool_mid, mcot, w1, msl2, msl1, smid, sel = rest
+    cot_my, pool_mid, mcot, w1, msl2, msl1, smid, sel, _ = rest
     send_ref, gmid_ref, sg_ref, fg_ref, cwg_ref = outs
     nodes = got.shape[0]
     n2 = cot_my.shape[0]
@@ -544,30 +544,43 @@
         send_ref[m * d : (m + 1) * d, :] = (dot_nt(a, b) * scale).astype(BF)
 
 
-def fine_spread_kernel(io, need, flush, ins, outs, s_ref, total):
-    off, ew, w, g, fg, _ = ins
-    rim_near, rim_far, out_ref = outs
+def edge_kernel(io, need, flush, ins, outs, s_ref):
+    off, ew, _ = ins
+    tiles = s_ref.shape[0]
+    for i in range(tiles):
+        clear_corners(s_ref.at[i])
+    need()
+    for i in range(tiles):
+        cols = slice(i * TILE, (i + 1) * TILE)
+        fine_edges(off[:, cols], ew[:, cols], s_ref.at[i])
+        io.start(s_ref.at[i], outs[0].at[i])
+
+
+def fine_spread_kernel(io, need, flush, ins, outs, s_ref, total, inner):
+    w, g, fg, s_all, _ = ins
+    rim_near, rim_far, edge_ref, out_ref = outs
     rows = g.shape[1]
-    clear_corners(s_ref.at[0])
-    clear_corners(s_ref.at[1])
-    total[...] = jnp.zeros(total.shape, F32)
-    need()
+    arrive = [io.start(s_all.at[i], s_ref.at[i]) for i in range(rows // TILE)]
+    total[:HALO, :] = jnp.zeros((HALO, total.shape[1]), F32)
+    total[HALO + rows :, :] = jnp.zeros((HALO, total.shape[1]), F32)
+    need()
+    spill = dot(w[1], fg[...]).astype(BF)
+    direct = g[...].astype(F32) + dot(w[0], fg[...])
+    total[HALO : HALO + rows, :] = jnp.transpose(direct)
     for i in range(rows // TILE):
-        cols = slice(i * TILE, (i + 1) * TILE)
-        s = s_ref.at[i % 2]
-        fine_edges(off[:, cols], ew[:, cols], s)
-        fg_tile = fg[:, cols]
-        direct = g[:, cols].astype(F32) + dot(w[0], fg_tile)
-        spill = dot(w[1], fg_tile).astype(BF)
+        io.wait(arrive[i])
         window = slice(i * TILE, (i + 1) * TILE + 2 * HALO)
-        total[window, :] = total[window, :] + dot_nt(s[...], spill)
-        here = slice(HALO + i * TILE, HALO + (i + 1) * TILE)
-        total[here, :] = total[here, :] + jnp.transpose(direct)
+        part = dot_nt(s_ref[i], spill[:, i * TILE : (i + 1) * TILE])
+        total[window, :] = total[window, :] + part
     even = lax.rem(lax.axis_index("nodes"), 2) == 0
     low, high = total[:HALO, :].astype(BF), total[HALO + rows :, :].astype(BF)
     rim_near[...] = jnp.where(even, high, low)
     rim_far[...] = jnp.where(even, low, high)
-    out_ref[...] = total[HALO : HALO + rows, :]
+    edge_ref[:HALO, :] = total[HALO : 2 * HALO, :]
+    edge_ref[HALO:, :] = total[rows : rows + HALO, :]
+    flush(0, 1, 2)
+    inner[...] = total[2 * HALO : rows, :].astype(BF)
+    io.start(inner, out_ref.at[pl.ds(HALO, rows - 2 * HALO)])
 
 
 def sum_kernel(io, need, flush, ins, outs, part):
@@ -580,18 +593,20 @@
         io.start(part, send_ref.at[p])
 
 
-def join_kernel(io, need, flush, ins, outs):
-    total, across, beside, coarse = ins
+def join_kernel(io, need, flush, ins, outs, joined):
+    edge, across, beside, coarse, _ = ins
     out_ref, wg_ref = outs
+    rows = out_ref.shape[0]
     even = lax.rem(lax.axis_index("nodes"), 2) == 0
     from_left = jnp.where(even, beside[...], across[...])
     from_right = jnp.where(even, across[...], beside[...])
-    rows = total.shape[0]
+    need(0)
+    joined[:HALO, :] = (edge[:HALO, :] + from_left.astype(F32)).astype(BF)
+    joined[HALO:, :] = (edge[HALO:, :] + from_right.astype(F32)).astype(BF)
+    io.start(joined.at[pl.ds(0, HALO)], out_ref.at[pl.ds(0, HALO)])
+    io.start(joined.at[pl.ds(HALO, HALO)], out_ref.at[pl.ds(rows - HALO, HALO)])
     need()
     io.start(coarse, wg_ref.at[pl.ds(8, 4)])
-    out_ref[:HALO, :] = (total[:HALO, :] + from_left.astype(F32)).astype(BF)
-    out_ref[HALO : rows - HALO, :] = total[HALO : rows - HALO, :].astype(BF)
-    out_ref[rows - HALO :, :] = (total[rows - HALO :, :] + from_right.astype(F32)).astype(BF)
 
 
 def gather_kernel(io, need, flush, ins, outs, wide):
@@ -722,6 +737,14 @@
         us=3,
     )
     got2 = exchange(send2)
+    (s_all,) = call(
+        edge_kernel,
+        [(fine_offsets, "h"), (fine_edge_w, "h"), (mhid, "r")],
+        [(shape((n // TILE, window, TILE)), "r")],
+        scratch=(pltpu.VMEM((n // TILE, window, TILE), BF),),
+        copies=n // TILE,
+        us=3,
+    )
     near = "v" if total2 <= 512 else "h"
     sco, cot_all, cot_back, c01, c2t, mcot, mslope1, mslope2 = call(
         second_window_kernel,
@@ -745,6 +768,7 @@
             (cot_all, near), (cot_back, near), (weights, "2"),
             (coarse_cotangent, "h"), (pool_mid, "h"), (mcot, "h"), (weights, "1"),
             (mslope2, "h"), (mslope1, "h"), (smid, "h"), (sel, "h"),
+            (s_all, "r"),
         ],
         [
             (shape((peers * chunk, d)), "h"), (shape((d, n1)), "h"), (shape((d, n1)), "h"),
@@ -790,12 +814,20 @@
         us=4,
     )
     got4 = exchange(send4.reshape(peers, 4 * d // peers, d))
-    rim_near, rim_far, spread = call(
+    rim_near, rim_far, edge_sums, inner_grads = call(
         fine_spread_kernel,
-        [(fine_offsets, "h"), (fine_edge_w, "h"), (weights, "0"), (g, "h"), (fg, "h"), (sums[2], "v")],
-        [(shape((HALO, d)), "h"), (shape((HALO, d)), "h"), (shape((n, d), F32), "h")],
-        scratch=(pltpu.VMEM((2, window, TILE), BF), pltpu.VMEM((n + 2 * HALO, d), F32)),
-        us=6,
+        [(weights, "0"), (g, "h"), (fg, "h"), (s_all, "r"), (sums[2], "v")],
+        [
+            (shape((HALO, d)), "h"), (shape((HALO, d)), "h"), (shape((2 * HALO, d), F32), "h"),
+            (shape((n, d)), "r"),
+        ],
+        scratch=(
+            pltpu.VMEM((n // TILE, window, TILE), BF),
+            pltpu.VMEM((n + 2 * HALO, d), F32),
+            pltpu.VMEM((n - 2 * HALO, d), BF),
+        ),
+        copies=n // TILE + 1,
+        us=4,
     )
     sums.append(double(sums[2], reaches[2], rim_near))
     (send5,) = call(
@@ -813,9 +845,14 @@
     from_beside = lax.ppermute(rim_far, "nodes", between_pairs)
     feature_grads, weight_grads = call(
         join_kernel,
-        [(spread, "h"), (from_across, "v"), (from_beside, "v"), (coarse_wg, "h")],
-        [(shape((n, d)), "h"), (shape((12, d, d), F32), "r")],
-        copies=1,
+        [
+            (edge_sums, "h"), (from_across, "v"), (from_beside, "v"), (coarse_wg, "h"),
+            (inner_grads, "r"),
+        ],
+        [(shape((n, d)), "r"), (shape((12, d, d), F32), "r")],
+        scratch=(pltpu.VMEM((2 * HALO, d), BF),),
+        copies=3,
+        aliases={4: 0},
         us=1,
     )
     (weight_grads,) = call(

time: 95.4 us -> 97.1 us (1.018)
  waiting for transfers between devices: 15.6 us -> 12.8 us
  Pallas kernels: 38 us -> 40.8 us
  starting transfers between devices: 39 us -> 40.7 us
    all_to_all x5, waiting for transfers between devices: 12.1 us -> 8.98 us  [exchange(): return lax.all_to_all(x, 'nodes', split_axis=0, concat_axis=0, tiled=True)]
    pallas_call x17 -> x18, Pallas kernels: 38 us -> 40.8 us  [call(): pl.pallas_call(body, out_shape=[s if kind == 'v' else pltpu.HBM(s.shape,...]
    all_to_all x5, starting transfers between devices: 25.2 us -> 27.1 us  [exchange(): return lax.all_to_all(x, 'nodes', split_axis=0, concat_axis=0, tiled=True)]
  transfers between devices with their start and end apart: 13 -> 13, of which waited for: 5 -> 5; matrix products, arithmetic and copies ran while one was open for 0% -> 0% of each run, Pallas kernels for 30% -> 32%
where the time goes in v8:
time: 97.1 us; the launch traced here: 96.3 us
  Pallas kernels  40.8 us (42%)
  starting transfers between devices  40.7 us (42%)
  waiting for transfers between devices  12.8 us (13%)
  between operations  1.02 us (1%)
    pallas_call x18, Pallas kernels, call(): pl.pallas_call(body, out_shape=[s if kind == 'v' else pltpu.HBM(s.shape,...  40.8 us
    all_to_all x5, starting transfers between devices, exchange(): return lax.all_to_all(x, 'nodes', split_axis=0, concat_axis=0, tiled=True)  27.1 us
    all_to_all x5, waiting for transfers between devices, exchange(): return lax.all_to_all(x, 'nodes', split_axis=0, concat_axis=0, tiled=True)  8.98 us
    ppermute x4, starting transfers between devices, double(): other = lax.ppermute(total, 'nodes', [(i, i ^ reach) for i in range(peers)])  5.38 us
    ppermute x1, starting transfers between devices, per_device(): beside = lax.ppermute(far, 'nodes', between_pairs)  4.54 us
    ppermute x1, starting transfers between devices, per_device(): from_beside = lax.ppermute(rim_far, 'nodes', between_pairs)  3.61 us
    ppermute x1, waiting for transfers between devices, per_device(): from_beside = lax.ppermute(rim_far, 'nodes', between_pairs)  2.56 us
  transfers between devices with their start and end apart: 13, of which 5 were waited for; matrix products, arithmetic and copies ran while one was open for 0% of the time, Pallas kernels for 32%

profile of v8, /device:TPU:1, one launch (start us, length us, event | category | flops | bytes accessed | tf_op | source)
XLA Modules:
  0.0 96.3 jit_solution(10052666428726564266)
XLA Ops:
  1.5 4.5 %collective-permute-start.1 = (bf16[256,128]{1,0:T(8,128)(2,1)S(1)}, bf16[256,128]{1,0:T(8,128)(2,1)S(1)}, u32[]{:S(2)}, u32[]{:S(2)}) collective-permute-start(bf16[256,128]{1,0:T(8,128)(2,1)S(1)} %get-tuple-element.106), channel_id=1, source_target_pairs={{1,2},{2,1},{3,4},{4,3},{5,6},{6,5},{7,8},{8,7},{9,10},{10,9},{11,... | collective-permute-start | bytes 196616 | tf_op jit(solution)/shard_map/ppermute | solution.py:662
  6.2 4.3 %shard_map.158 = (bf16[2,768,256]{2,1,0:T(8,128)(2,1)S(1)}, bf16[2,128,512]{2,1,0:T(8,128)(2,1)S(1)}, bf16[128,256]{1,0:T(8,128)(2,1)S(1)}, bf16[128,128]{1,0:T(...) custom-call(s32[8,2048]{1,0:T(8,128)} %refs_0_.8, ...), custom_call_target="tpu_custom_call" | custom-call | bytes 18000000 | tf_op jit(solution)/shard_map/pallas_call | solution.py:163
  10.5 1.8 %shard_map.159 = (bf16[16,96,128]{2,1,0:T(8,128)(2,1)}, bf16[128,2048]{1,0:T(8,128)(2,1)}) custom-call(bf16[256,128]{1,0:T(8,128)(2,1)S(1)} %collective-permute-done.refs_0_, bf16[256,128]{1,0:T(8,128)(2,1)S(1)} %collective-permute-done.1.refs_1_, bf16[2,768,256]{2,1,0:T(8,128)(2,1)S(1)} %get-tuple-element.54.refs_2_, ...), custom_call_target="tpu_custom_call" | custom-call | bytes 9000000 | tf_op jit(solution)/shard_map/pallas_call | solution.py:163
  12.3 5.4 %all-to-all-start = ((bf16[16,96,128]{2,1,0:T(8,128)(2,1)}), bf16[16,96,128]{2,1,0:T(8,128)(2,1)S(1)}, u32[]{:S(2)}, u32[]{:S(2)}) async-start(bf16[16,96,128]{2,1,0:T(8,128)(2,1)} %get-tuple-element.63), calls=%async_computation | async-start | bytes 786432 | tf_op jit(solution)/shard_map/all_to_all | solution.py:621
  17.7 2.0 %shard_map.160 = (bf16[512,512]{1,0:T(8,128)(2,1)}, bf16[128,256]{1,0:T(8,128)(2,1)}, bf16[128,128]{1,0:T(8,128)(2,1)}, bf16[128,128]{1,0:T(8,128)(2,1)}) custom-call(s32[8,512]{1,0:T(8,128)} %refs_0_.6, f32[8,512]{1,0:T(8,128)} %refs_1_.4, bf16[3,4,128,128]{3,2,1,0:T(8,128)(2,1)} %refs_0_.9, bf16[128,2048]{1,0:T(8,128)(2,1)} %get-tuple-element.64.refs_3_.refs_1_.refs_8_), custom_call_target="tpu_custom_call" | custom-call | bytes 18000000 | tf_op jit(solution)/shard_map/pallas_call | solution.py:163
  19.6 4.8 %shard_map.161 = (bf16[128,2048]{1,0:T(8,128)(2,1)}, bf16[128,2048]{1,0:T(8,128)(2,1)}, bf16[128,2048]{1,0:T(8,128)(2,1)}, f32[128,2048]{1,0:T(8,128)}, f32[128,...) custom-call(bf16[2048,128]{1,0:T(8,128)(2,1)} %refs_0_.7, ...), custom_call_target="tpu_custom_call" | custom-call | bytes 12000000 | tf_op jit(solution)/shard_map/pallas_call | solution.py:163
  24.5 5.1 %all-to-all-done.refs_0_ = bf16[16,96,128]{2,1,0:T(8,128)(2,1)S(1)} async-done(((bf16[16,96,128]{2,1,0:T(8,128)(2,1)}), bf16[16,96,128]{2,1,0:T(8,128)(2,1)S(1)}, u32[]{:S(2)}, u32[]{:S(2)}) %all-to-all-start) | async-done | bytes 393248 | tf_op jit(solution)/shard_map/all_to_all | solution.py:621
  29.6 2.9 %shard_map.162 = (bf16[16,16,128]{2,1,0:T(8,128)(2,1)}, bf16[128,512]{1,0:T(8,128)(2,1)}, bf16[128,512]{1,0:T(8,128)(2,1)}, bf16[1024,512]{1,0:T(8,128)(2,1)}, bf16[16,32,128]{2,1,0:T(8,128)(2,1)}) custom-call(bf16[16,96,128]{2,1,0:T(8,128)(2,1)S(1)} %all-to-all-done.refs_0_, bf16[512,512]{1,0:T(8,128)(2,1)} %get-tuple-element.65.refs_1_.refs_13_, ...), custom_call_target="tpu_custom_call" | custom-call | bytes 9000000 | tf_op jit(solution)/shard_map/pallas_call | solution.py:163
  32.5 3.8 %all-to-all-start.1 = ((bf16[16,16,128]{2,1,0:T(8,128)(2,1)}), bf16[16,16,128]{2,1,0:T(8,128)(2,1)S(1)}, u32[]{:S(2)}, u32[]{:S(2)}) async-start(bf16[16,16,128]{2,1,0:T(8,128)(2,1)} %get-tuple-element.70), calls=%async_computation.1 | async-start | bytes 131072 | tf_op jit(solution)/shard_map/all_to_all | solution.py:621
  36.3 3.4 %shard_map.164.refs_15_.refs_3_ = bf16[8,768,256]{2,1,0:T(8,128)(2,1)} custom-call(s32[8,2048]{1,0:T(8,128)} %refs_0_.8, f32[8,2048]{1,0:T(8,128)} %refs_1_.5, bf16[128,512]{1,0:T(8,128)(2,1)} %get-tuple-element.72.refs_1_.refs_2_.refs_0_), custom_call_target="tpu_custom_call" | custom-call | bytes 9000000 | tf_op jit(solution)/shard_map/pallas_call | solution.py:163
  39.7 2.8 %shard_map.163 = (bf16[256,256]{1,0:T(8,128)(2,1)S(1)}, bf16[128,256]{1,0:T(8,128)(2,1)S(1)}, f32[128,256]{1,0:T(8,128)S(1)}, bf16[128,256]{1,0:T(8,128)(2,1)S(1...) custom-call(bf16[16,32,128]{2,1,0:T(8,128)(2,1)} %get-tuple-element.71.ref, ...), custom_call_target="tpu_custom_call" | custom-call | bytes 18000000 | tf_op jit(solution)/shard_map/pallas_call | solution.py:163
  42.6 3.8 %shard_map.165 = (bf16[1024,128]{1,0:T(8,128)(2,1)}, bf16[128,512]{1,0:T(8,128)(2,1)}, bf16[128,512]{1,0:T(8,128)(2,1)}, bf16[128,512]{1,0:T(8,128)(2,1)}, f32[4,128,128]{2,1,0:T(8,128)}) custom-call(bf16[256,128]{1,0:T(8,128)(2,1)S(1)} %bitcast.11, bf16[256,256]{1,0:T(8,128)(2,1)S(1)} %get-tuple-element.74.refs_1_, ...), custom_call_target="tpu_custom_call" | custom-call | bytes 9000000 | tf_op jit(solution)/shard_map/pallas_call | solution.py:163
  46.4 6.0 %all-to-all-start.2 = ((bf16[16,64,128]{2,1,0:T(8,128)(2,1)}), bf16[16,64,128]{2,1,0:T(8,128)(2,1)S(1)}, u32[]{:S(2)}, u32[]{:S(2)}) async-start(bf16[16,64,128]{2,1,0:T(8,128)(2,1)} %bitcast.13), calls=%async_computation.2 | async-start | bytes 524288 | tf_op jit(solution)/shard_map/all_to_all | solution.py:621
  52.4 2.0 %shard_map.166 = (bf16[512,128]{1,0:T(8,128)(2,1)S(1)}, bf16[512,1024]{1,0:T(8,128)(2,1)S(1)}) custom-call(bf16[128,512]{1,0:T(8,128)(2,1)} %get-tuple-element.72.refs_1_.refs_2_.refs_0_, bf16[128,512]{1,0:T(8,128)(2,1)} %get-tuple-element.73.refs_2_.refs_1_, bf16[128,512]{1,0:T(8,128)(2,1)} %get-tuple-element.84.refs_2_, ...), custom_call_target="tpu_custom_call" | custom-call | bytes 9000000 | tf_op jit(solution)/shard_map/pallas_call | solution.py:163
  55.9 2.4 %collective-permute-start.3 = (bf16[512,128]{1,0:T(8,128)(2,1)S(1)}, bf16[512,128]{1,0:T(8,128)(2,1)S(1)}, u32[]{:S(2)}, u32[]{:S(2)}) collective-permute-start(bf16[512,128]{1,0:T(8,128)(2,1)S(1)} %shard_map.167.refs_11_.refs_0_), channel_id=1, source_target_pairs={{0,8},{1,9},{2,10},{3,11},{4,12},{5,13},{6,14},{7,15},{8,0},{9,1},... | collective-permute-start | bytes 393224 | tf_op jit(solution)/shard_map/ppermute | solution.py:797
  58.3 3.6 %all-to-all-done.2 = bf16[16,64,128]{2,1,0:T(8,128)(2,1)S(1)} async-done(((bf16[16,64,128]{2,1,0:T(8,128)(2,1)}), bf16[16,64,128]{2,1,0:T(8,128)(2,1)S(1)}, u32[]{:S(2)}, u32[]{:S(2)}) %all-to-all-start.2) | async-done | bytes 262176 | tf_op jit(solution)/shard_map/all_to_all | solution.py:621
  61.9 4.4 %shard_map.168 = (bf16[512,128]{1,0:T(8,128)(2,1)}, bf16[128,2048]{1,0:T(8,128)(2,1)}, bf16[128,2048]{1,0:T(8,128)(2,1)}) custom-call(bf16[1024,128]{1,0:T(8,128)(2,1)S(1)} %bitcast.8, bf16[512,1024]{1,0:T(8,128)(2,1)S(1)} %get-tuple-element.88.refs_1_, bf16[128,2048]{1,0:T(8,128)(2,1)} %get-tuple-element.89.refs_2_, ...), custom_call_target="tpu_custom_call" | custom-call | bytes 12000000 | tf_op jit(solution)/shard_map/pallas_call | solution.py:163
  66.3 6.4 %all-to-all-start.3 = ((bf16[16,32,128]{2,1,0:T(8,128)(2,1)}), bf16[16,32,128]{2,1,0:T(8,128)(2,1)S(1)}, u32[]{:S(2)}, u32[]{:S(2)}) async-start(bf16[16,32,128]{2,1,0:T(8,128)(2,1)} %bitcast.14), calls=%async_computation.3 | async-start | bytes 262144 | tf_op jit(solution)/shard_map/all_to_all | solution.py:621
  72.7 1.5 %collective-permute-start.6 = (bf16[512,128]{1,0:T(8,128)(2,1)S(1)}, bf16[512,128]{1,0:T(8,128)(2,1)S(1)}, u32[]{:S(2)}, u32[]{:S(2)}) collective-permute-start(bf16[512,128]{1,0:T(8,128)(2,1)S(1)} %shard_map.169.refs_4_.refs_0_), channel_id=1, source_target_pairs={{0,2},{1,3},{2,0},{3,1},{4,6},{5,7},{6,4},{7,5},{8,10},{9,11},{10,... | collective-permute-start | bytes 393224 | tf_op jit(solution)/shard_map/ppermute | solution.py:797
  74.1 5.0 %shard_map.170 = (bf16[256,128]{1,0:T(8,128)(2,1)}, bf16[256,128]{1,0:T(8,128)(2,1)}, f32[512,128]{1,0:T(8,128)}, bf16[2048,128]{1,0:T(8,128)(2,1)}) custom-call(bf16[3,4,128,128]{3,2,1,0:T(8,128)(2,1)} %refs_0_.9, bf16[128,2048]{1,0:T(8,128)(2,1)} %get-tuple-element.96.refs_1_, bf16[128,2048]{1,0:T(8,128)(2,1)} %get-tuple-element.97.refs_2_, ...), custom_call_target="tpu_custom_call" | custom-call | bytes 12000000 | tf_op jit(solution)/shard_map/pallas_call | solution.py:163
  80.3 5.4 %all-to-all-start.4 = ((bf16[16,32,128]{2,1,0:T(8,128)(2,1)}), bf16[16,32,128]{2,1,0:T(8,128)(2,1)S(1)}, u32[]{:S(2)}, u32[]{:S(2)}) async-start(bf16[16,32,128]{2,1,0:T(8,128)(2,1)} %shard_map.173), calls=%async_computation.4 | async-start | bytes 262144 | tf_op jit(solution)/shard_map/all_to_all | solution.py:621
  87.2 3.6 %collective-permute-start.5 = (bf16[256,128]{1,0:T(8,128)(2,1)}, bf16[256,128]{1,0:T(8,128)(2,1)S(1)}, u32[]{:S(2)}, u32[]{:S(2)}) collective-permute-start(bf16[256,128]{1,0:T(8,128)(2,1)} %get-tuple-element.100), channel_id=1, source_target_pairs={{1,2},{2,1},{3,4},{4,3},{5,6},{6,5},{7,8},{8,7},{9,10},{10,9},{11,... | collective-permute-start | bytes 196616 | tf_op jit(solution)/shard_map/ppermute | solution.py:845
  90.9 2.6 %collective-permute-done.5.refs_2_ = bf16[256,128]{1,0:T(8,128)(2,1)S(1)} collective-permute-done((bf16[256,128]{1,0:T(8,128)(2,1)}, bf16[256,128]{1,0:T(8,128)(2,1)S(1)}, u32[]{:S(2)}, u32[]{:S(2)}) %collective-permute-start.5) | collective-permute-done | bytes 65568 | tf_op jit(solution)/shard_map/ppermute | solution.py:845
  93.4 1.8 %shard_map.171 = (bf16[2048,128]{1,0:T(8,128)(2,1)}, f32[12,128,128]{2,1,0:T(8,128)}) custom-call(f32[512,128]{1,0:T(8,128)} %get-tuple-element.98.refs_0_, bf16[256,128]{1,0:T(8,128)(2,1)S(1)} %collective-permute-done.4.refs_1_, bf16[256,128]{1,0:T(8,128)(2,1)S(1)} %collective-permute-done.5.refs_2_, ...), custom_call_target="tpu_custom_call", output_to_operand_aliasing={{0}: (4, {})} | custom-call | bytes 3000000 | tf_op jit(solution)/shard_map/pallas_call | solution.py:163
  (21 shorter events, 5.9 us)
Async XLA Ops:
  1.5 8.9 %collective-permute-start.1 = (bf16[256,128]{1,0:T(8,128)(2,1)S(1)}, bf16[256,128]{1,0:T(8,128)(2,1)S(1)}, u32[]{:S(2)}, u32[]{:S(2)}) collective-permute-start(bf16[256,128]{1,0:T(8,128)(2,1)S(1)} %get-tuple-element.106), channel_id=1, source_target_pairs={{1,2},{2,1},{3,4},{4,3},{5,6},{6,5},{7,8},{8,7},{9,10},{10,9},{11,... | collective-permute-start | bytes 196616 | tf_op jit(solution)/shard_map/ppermute | solution.py:662
  6.1 4.4 %collective-permute-start = (bf16[256,128]{1,0:T(8,128)(2,1)S(1)}, bf16[256,128]{1,0:T(8,128)(2,1)S(1)}, u32[]{:S(2)}, u32[]{:S(2)}) collective-permute-start(bf16[256,128]{1,0:T(8,128)(2,1)S(1)} %get-tuple-element.107), channel_id=1, source_target_pairs={{0,1},{1,0},{2,3},{3,2},{4,5},{5,4},{6,7},{7,6},{8,9},{9,8},{10,11... | collective-permute-start | bytes 196616 | tf_op jit(solution)/shard_map/ppermute | solution.py:661
  12.3 17.3 %all-to-all-start = ((bf16[16,96,128]{2,1,0:T(8,128)(2,1)}), bf16[16,96,128]{2,1,0:T(8,128)(2,1)S(1)}, u32[]{:S(2)}, u32[]{:S(2)}) async-start(bf16[16,96,128]{2,1,0:T(8,128)(2,1)} %get-tuple-element.63), calls=%async_computation | async-start | bytes 786432 | tf_op jit(solution)/shard_map/all_to_all | solution.py:621
  32.5 10.1 %all-to-all-start.1 = ((bf16[16,16,128]{2,1,0:T(8,128)(2,1)}), bf16[16,16,128]{2,1,0:T(8,128)(2,1)S(1)}, u32[]{:S(2)}, u32[]{:S(2)}) async-start(bf16[16,16,128]{2,1,0:T(8,128)(2,1)} %get-tuple-element.70), calls=%async_computation.1 | async-start | bytes 131072 | tf_op jit(solution)/shard_map/all_to_all | solution.py:621
  46.4 15.4 %all-to-all-start.2 = ((bf16[16,64,128]{2,1,0:T(8,128)(2,1)}), bf16[16,64,128]{2,1,0:T(8,128)(2,1)S(1)}, u32[]{:S(2)}, u32[]{:S(2)}) async-start(bf16[16,64,128]{2,1,0:T(8,128)(2,1)} %bitcast.13), calls=%async_computation.2 | async-start | bytes 524288 | tf_op jit(solution)/shard_map/all_to_all | solution.py:621
  54.5 1.4 %collective-permute-start.2 = (bf16[512,128]{1,0:T(8,128)(2,1)S(1)}, bf16[512,128]{1,0:T(8,128)(2,1)S(1)}, u32[]{:S(2)}, u32[]{:S(2)}) collective-permute-start(bf16[512,128]{1,0:T(8,128)(2,1)S(1)} %get-tuple-element.95.refs_0_), channel_id=1, source_target_pairs={{0,1},{1,0},{2,3},{3,2},{4,5},{5,4},{6,7},{7,6},{8,9},{9,8},{10,11... | collective-permute-start | bytes 393224 | tf_op jit(solution)/shard_map/ppermute | solution.py:797
  55.9 16.7 %collective-permute-start.3 = (bf16[512,128]{1,0:T(8,128)(2,1)S(1)}, bf16[512,128]{1,0:T(8,128)(2,1)S(1)}, u32[]{:S(2)}, u32[]{:S(2)}) collective-permute-start(bf16[512,128]{1,0:T(8,128)(2,1)S(1)} %shard_map.167.refs_11_.refs_0_), channel_id=1, source_target_pairs={{0,8},{1,9},{2,10},{3,11},{4,12},{5,13},{6,14},{7,15},{8,0},{9,1},... | collective-permute-start | bytes 393224 | tf_op jit(solution)/shard_map/ppermute | solution.py:797
  66.3 13.2 %all-to-all-start.3 = ((bf16[16,32,128]{2,1,0:T(8,128)(2,1)}), bf16[16,32,128]{2,1,0:T(8,128)(2,1)S(1)}, u32[]{:S(2)}, u32[]{:S(2)}) async-start(bf16[16,32,128]{2,1,0:T(8,128)(2,1)} %bitcast.14), calls=%async_computation.3 | async-start | bytes 262144 | tf_op jit(solution)/shard_map/all_to_all | solution.py:621
  72.7 6.5 %collective-permute-start.6 = (bf16[512,128]{1,0:T(8,128)(2,1)S(1)}, bf16[512,128]{1,0:T(8,128)(2,1)S(1)}, u32[]{:S(2)}, u32[]{:S(2)}) collective-permute-start(bf16[512,128]{1,0:T(8,128)(2,1)S(1)} %shard_map.169.refs_4_.refs_0_), channel_id=1, source_target_pairs={{0,2},{1,3},{2,0},{3,1},{4,6},{5,7},{6,4},{7,5},{8,10},{9,11},{10,... | collective-permute-start | bytes 393224 | tf_op jit(solution)/shard_map/ppermute | solution.py:797
  80.3 14.9 %all-to-all-start.4 = ((bf16[16,32,128]{2,1,0:T(8,128)(2,1)}), bf16[16,32,128]{2,1,0:T(8,128)(2,1)S(1)}, u32[]{:S(2)}, u32[]{:S(2)}) async-start(bf16[16,32,128]{2,1,0:T(8,128)(2,1)} %shard_map.173), calls=%async_computation.4 | async-start | bytes 262144 | tf_op jit(solution)/shard_map/all_to_all | solution.py:621
  85.8 9.4 %collective-permute-start.7 = (bf16[512,128]{1,0:T(8,128)(2,1)S(1)}, bf16[512,128]{1,0:T(8,128)(2,1)S(1)}, u32[]{:S(2)}, u32[]{:S(2)}) collective-permute-start(bf16[512,128]{1,0:T(8,128)(2,1)S(1)} %shard_map.172.refs_2_.refs_0_), channel_id=1, source_target_pairs={{0,4},{1,5},{2,6},{3,7},{4,0},{5,1},{6,2},{7,3},{8,12},{9,13},{10,... | collective-permute-start | bytes 393224 | tf_op jit(solution)/shard_map/ppermute | solution.py:797
  87.2 6.3 %collective-permute-start.5 = (bf16[256,128]{1,0:T(8,128)(2,1)}, bf16[256,128]{1,0:T(8,128)(2,1)S(1)}, u32[]{:S(2)}, u32[]{:S(2)}) collective-permute-start(bf16[256,128]{1,0:T(8,128)(2,1)} %get-tuple-element.100), channel_id=1, source_target_pairs={{1,2},{2,1},{3,4},{4,3},{5,6},{6,5},{7,8},{8,7},{9,10},{10,9},{11,... | collective-permute-start | bytes 196616 | tf_op jit(solution)/shard_map/ppermute | solution.py:845
  90.8 2.6 %collective-permute-start.4 = (bf16[256,128]{1,0:T(8,128)(2,1)}, bf16[256,128]{1,0:T(8,128)(2,1)S(1)}, u32[]{:S(2)}, u32[]{:S(2)}) collective-permute-start(bf16[256,128]{1,0:T(8,128)(2,1)} %get-tuple-element.99.refs_2_.refs_1_), channel_id=1, source_target_pairs={{0,1},{1,0},{2,3},{3,2},{4,5},{5,4},{6,7},{7,6},{8,9},{9,8},{10,11... | collective-permute-start | bytes 196616 | tf_op jit(solution)/shard_map/ppermute | solution.py:844

commit v9 on v8

--- a/solution.py
+++ b/solution.py
@@ -196,7 +196,7 @@
 
 def inner_kernel(tile_rows, peers, cap, io, need, flush, ins, outs, feat_t, s_ref, ids, counts):
     off, ew, feat, w, pool, owner, slot, nbrs, cew, cot = ins
-    so_ref, win_ref, w01_ref, w2t_ref, w3t_ref, po_ref, spread, ext_ref, agg_ref, place = outs
+    so_ref, win_ref, w01_ref, w2t_ref, w3t_ref, po_ref, spread, ext_ref, agg_ref, place, s_all = outs
     rows, d = feat.shape
     block_rows = pool.shape[0]
     n2 = cot.shape[0]
@@ -226,12 +226,14 @@
     for n, i in enumerate((0, tiles - 1)):
         cols = slice(i * TILE, (i + 1) * TILE)
         fine_edges(off[:, cols], ew[:, cols], so_ref.at[n])
+        io.start(so_ref.at[n], s_all.at[i])
     need()
     feat_t[...] = jnp.transpose(feat[...])
     weights = forward_weights(w)
     for i in range(1, tiles - 1):
         cols = slice(i * TILE, (i + 1) * TILE)
         fine_edges(off[:, cols], ew[:, cols], s_ref.at[i - 1])
+        io.start(s_ref.at[i - 1], s_all.at[i])
         around = feat_t[:, i * TILE - HALO : (i + 1) * TILE + HALO]
         agg_ref[:, cols] = dot(around, s_ref[i - 1]).astype(BF)
     for start in range(TILE, rows - TILE, WIDE):
@@ -403,7 +405,7 @@
 
 def coarse_kernel(io, need, flush, ins, outs):
     got, sco, c01, c2t, cot_all, cot_back, w2, *rest = ins
-    cot_my, pool_mid, mcot, w1, msl2, msl1, smid, sel, _ = rest
+    cot_my, pool_mid, mcot, w1, msl2, msl1, smid, sel = rest
     send_ref, gmid_ref, sg_ref, fg_ref, cwg_ref = outs
     nodes = got.shape[0]
     n2 = cot_my.shape[0]
@@ -544,43 +546,46 @@
         send_ref[m * d : (m + 1) * d, :] = (dot_nt(a, b) * scale).astype(BF)
 
 
-def edge_kernel(io, need, flush, ins, outs, s_ref):
-    off, ew, _ = ins
-    tiles = s_ref.shape[0]
-    for i in range(tiles):
-        clear_corners(s_ref.at[i])
-    need()
-    for i in range(tiles):
-        cols = slice(i * TILE, (i + 1) * TILE)
-        fine_edges(off[:, cols], ew[:, cols], s_ref.at[i])
-        io.start(s_ref.at[i], outs[0].at[i])
-
-
-def fine_spread_kernel(io, need, flush, ins, outs, s_ref, total, inner):
+def fine_spread_kernel(io, need, flush, ins, outs, band, spill, inner):
     w, g, fg, s_all, _ = ins
     rim_near, rim_far, edge_ref, out_ref = outs
-    rows = g.shape[1]
-    arrive = [io.start(s_all.at[i], s_ref.at[i]) for i in range(rows // TILE)]
-    total[:HALO, :] = jnp.zeros((HALO, total.shape[1]), F32)
-    total[HALO + rows :, :] = jnp.zeros((HALO, total.shape[1]), F32)
-    need()
-    spill = dot(w[1], fg[...]).astype(BF)
-    direct = g[...].astype(F32) + dot(w[0], fg[...])
-    total[HALO : HALO + rows, :] = jnp.transpose(direct)
-    for i in range(rows // TILE):
-        io.wait(arrive[i])
-        window = slice(i * TILE, (i + 1) * TILE + 2 * HALO)
-        part = dot_nt(s_ref[i], spill[:, i * TILE : (i + 1) * TILE])
-        total[window, :] = total[window, :] + part
+    d, rows = g.shape
+    tiles = rows // TILE
+    arrive = []
+    for b in range(tiles + 2):
+        arrive.append([])
+        for j in range(3):
+            lanes = pl.ds(j * TILE, TILE)
+            if 0 <= b - 2 + j < tiles:
+                source = s_all.at[b - 2 + j, pl.ds((2 - j) * TILE, TILE), :]
+                arrive[b].append(io.start(source, band.at[b, :, lanes]))
+            else:
+                band[b, :, j * TILE : (j + 1) * TILE] = jnp.zeros((TILE, TILE), BF)
+    spill[:, : 2 * TILE] = jnp.zeros((d, 2 * TILE), BF)
+    spill[:, 2 * TILE + rows :] = jnp.zeros((d, 2 * TILE), BF)
     even = lax.rem(lax.axis_index("nodes"), 2) == 0
-    low, high = total[:HALO, :].astype(BF), total[HALO + rows :, :].astype(BF)
-    rim_near[...] = jnp.where(even, high, low)
-    rim_far[...] = jnp.where(even, low, high)
-    edge_ref[:HALO, :] = total[HALO : 2 * HALO, :]
-    edge_ref[HALO:, :] = total[rows : rows + HALO, :]
-    flush(0, 1, 2)
-    inner[...] = total[2 * HALO : rows, :].astype(BF)
-    io.start(inner, out_ref.at[pl.ds(HALO, rows - 2 * HALO)])
+    need()
+    spill[:, 2 * TILE : 2 * TILE + rows] = dot(w[1], fg[...]).astype(BF)
+    rims = []
+    for b in [0, tiles + 1] + list(range(1, tiles + 1)):
+        io.wait(*arrive[b])
+        part = dot_nt(band[b], spill[:, b * TILE : (b + 3) * TILE])
+        if b in (0, tiles + 1):
+            rims.append(part.astype(BF))
+            continue
+        if b == 1:
+            rim_near[...] = jnp.where(even, rims[1], rims[0])
+            rim_far[...] = jnp.where(even, rims[0], rims[1])
+            flush(0, 1)
+        cols = slice((b - 1) * TILE, b * TILE)
+        part = part + jnp.transpose(g[:, cols].astype(F32) + dot(w[0], fg[:, cols]))
+        if b == 1:
+            edge_ref[:TILE, :] = part
+        elif b == tiles:
+            edge_ref[TILE:, :] = part
+        else:
+            inner[(b - 2) * TILE : (b - 1) * TILE, :] = part.astype(BF)
+    io.start(inner, out_ref.at[pl.ds(TILE, rows - 2 * TILE)])
 
 
 def sum_kernel(io, need, flush, ins, outs, part):
@@ -661,7 +666,7 @@
     across = lax.ppermute(near, "nodes", inside_pairs)
     beside = lax.ppermute(far, "nodes", between_pairs)
     owners = owner_dev.reshape(-1)
-    s_out, win, w01, w2t, w3t, pool_out, spread, ext, agg_in, place = call(
+    s_out, win, w01, w2t, w3t, pool_out, spread, ext, agg_in, place, s_all = call(
         functools.partial(inner_kernel, tile_rows, peers, cap),
         [
             (fine_offsets, "h"), (fine_edge_w, "h"), (features, "h"), (weights, "0"),
@@ -673,7 +678,7 @@
             (shape((d, 2 * d)), "v"), (shape((d, d)), "v"), (shape((d, d)), "v"),
             (shape((2, per, TILE)), "v"), (shape((peers * chunk, d), F32), "v"),
             (shape((peers, n2 + 16, d)), "v"), (shape((d, n)), "v"),
-            (shape((tile_count,), jnp.int32), "s"),
+            (shape((tile_count,), jnp.int32), "s"), (shape((n // TILE, window, TILE)), "r"),
         ],
         scratch=(
             pltpu.VMEM((d, n), BF),
@@ -681,6 +686,7 @@
             pltpu.VMEM((peers, 128), F32),
             pltpu.SMEM((peers,), jnp.int32),
         ),
+        copies=n // TILE,
         us=6,
     )
     send1, agg = call(
@@ -737,14 +743,6 @@
         us=3,
     )
     got2 = exchange(send2)
-    (s_all,) = call(
-        edge_kernel,
-        [(fine_offsets, "h"), (fine_edge_w, "h"), (mhid, "r")],
-        [(shape((n // TILE, window, TILE)), "r")],
-        scratch=(pltpu.VMEM((n // TILE, window, TILE), BF),),
-        copies=n // TILE,
-        us=3,
-    )
     near = "v" if total2 <= 512 else "h"
     sco, cot_all, cot_back, c01, c2t, mcot, mslope1, mslope2 = call(
         second_window_kernel,
@@ -768,7 +766,6 @@
             (cot_all, near), (cot_back, near), (weights, "2"),
             (coarse_cotangent, "h"), (pool_mid, "h"), (mcot, "h"), (weights, "1"),
             (mslope2, "h"), (mslope1, "h"), (smid, "h"), (sel, "h"),
-            (s_all, "r"),
         ],
         [
             (shape((peers * chunk, d)), "h"), (shape((d, n1)), "h"), (shape((d, n1)), "h"),
@@ -822,11 +819,11 @@
             (shape((n, d)), "r"),
         ],
         scratch=(
-            pltpu.VMEM((n // TILE, window, TILE), BF),
-            pltpu.VMEM((n + 2 * HALO, d), F32),
+            pltpu.VMEM((n // TILE + 2, TILE, window), BF),
+            pltpu.VMEM((d, n + 4 * TILE), BF),
             pltpu.VMEM((n - 2 * HALO, d), BF),
         ),
-        copies=n // TILE + 1,
+        copies=3 * (n // TILE) + 1,
         us=4,
     )
     sums.append(double(sums[2], reaches[2], rim_near))

time: 97.1 us -> 96.6 us (level)
  waiting for transfers between devices: 12.8 us -> 15.6 us
  starting transfers between devices: 40.7 us -> 38.8 us
  Pallas kernels: 40.8 us -> 39.4 us
    all_to_all x5, waiting for transfers between devices: 8.98 us -> 11.9 us  [exchange(): return lax.all_to_all(x, 'nodes', split_axis=0, concat_axis=0, tiled=True)]
    all_to_all x5, starting transfers between devices: 27.1 us -> 25 us  [exchange(): return lax.all_to_all(x, 'nodes', split_axis=0, concat_axis=0, tiled=True)]
    pallas_call x18 -> x17, Pallas kernels: 40.8 us -> 39.4 us  [call(): pl.pallas_call(body, out_shape=[s if kind == 'v' else pltpu.HBM(s.shape,...]
  transfers between devices with their start and end apart: 13 -> 13, of which waited for: 5 -> 5; matrix products, arithmetic and copies ran while one was open for 0% -> 0% of each run, Pallas kernels for 32% -> 31%
where the time goes in v9:
time: 96.6 us; the launch traced here: 95.8 us
  Pallas kernels  39.4 us (41%)
  starting transfers between devices  38.8 us (40%)
  waiting for transfers between devices  15.6 us (16%)
  between operations  1.01 us (1%)
    pallas_call x17, Pallas kernels, call(): pl.pallas_call(body, out_shape=[s if kind == 'v' else pltpu.HBM(s.shape,...  39.4 us
    all_to_all x5, starting transfers between devices, exchange(): return lax.all_to_all(x, 'nodes', split_axis=0, concat_axis=0, tiled=True)  25 us
    all_to_all x5, waiting for transfers between devices, exchange(): return lax.all_to_all(x, 'nodes', split_axis=0, concat_axis=0, tiled=True)  11.9 us
    ppermute x4, starting transfers between devices, double(): other = lax.ppermute(total, 'nodes', [(i, i ^ reach) for i in range(peers)])  5.52 us
    ppermute x1, starting transfers between devices, per_device(): beside = lax.ppermute(far, 'nodes', between_pairs)  4.54 us
    ppermute x1, starting transfers between devices, per_device(): from_beside = lax.ppermute(rim_far, 'nodes', between_pairs)  3.61 us
    ppermute x1, waiting for transfers between devices, per_device(): from_beside = lax.ppermute(rim_far, 'nodes', between_pairs)  2.56 us
  transfers between devices with their start and end apart: 13, of which 5 were waited for; matrix products, arithmetic and copies ran while one was open for 0% of the time, Pallas kernels for 31%

profile of v9, /device:TPU:1, one launch (start us, length us, event | category | flops | bytes accessed | tf_op | source)
XLA Modules:
  0.0 95.8 jit_solution(9622831117372177398)
XLA Ops:
  1.5 4.5 %collective-permute-start.1 = (bf16[256,128]{1,0:T(8,128)(2,1)S(1)}, bf16[256,128]{1,0:T(8,128)(2,1)S(1)}, u32[]{:S(2)}, u32[]{:S(2)}) collective-permute-start(bf16[256,128]{1,0:T(8,128)(2,1)S(1)} %get-tuple-element.108), channel_id=1, source_target_pairs={{1,2},{2,1},{3,4},{4,3},{5,6},{6,5},{7,8},{8,7},{9,10},{10,9},{11,... | collective-permute-start | bytes 196616 | tf_op jit(solution)/shard_map/ppermute | solution.py:667
  6.2 4.9 %shard_map.158 = (bf16[2,768,256]{2,1,0:T(8,128)(2,1)S(1)}, bf16[2,128,512]{2,1,0:T(8,128)(2,1)S(1)}, bf16[128,256]{1,0:T(8,128)(2,1)S(1)}, bf16[128,128]{1,0:T(...) custom-call(s32[8,2048]{1,0:T(8,128)} %refs_0_.4, ...), custom_call_target="tpu_custom_call" | custom-call | bytes 18000000 | tf_op jit(solution)/shard_map/pallas_call | solution.py:163
  11.0 1.8 %shard_map.159 = (bf16[16,96,128]{2,1,0:T(8,128)(2,1)}, bf16[128,2048]{1,0:T(8,128)(2,1)}) custom-call(bf16[256,128]{1,0:T(8,128)(2,1)S(1)} %collective-permute-done.refs_0_, bf16[256,128]{1,0:T(8,128)(2,1)S(1)} %collective-permute-done.1.refs_1_, bf16[2,768,256]{2,1,0:T(8,128)(2,1)S(1)} %get-tuple-element.55.refs_2_, ...), custom_call_target="tpu_custom_call" | custom-call | bytes 9000000 | tf_op jit(solution)/shard_map/pallas_call | solution.py:163
  12.8 5.4 %all-to-all-start = ((bf16[16,96,128]{2,1,0:T(8,128)(2,1)}), bf16[16,96,128]{2,1,0:T(8,128)(2,1)S(1)}, u32[]{:S(2)}, u32[]{:S(2)}) async-start(bf16[16,96,128]{2,1,0:T(8,128)(2,1)} %get-tuple-element.64), calls=%async_computation | async-start | bytes 786432 | tf_op jit(solution)/shard_map/all_to_all | solution.py:626
  18.2 2.0 %shard_map.160 = (bf16[512,512]{1,0:T(8,128)(2,1)}, bf16[128,256]{1,0:T(8,128)(2,1)}, bf16[128,128]{1,0:T(8,128)(2,1)}, bf16[128,128]{1,0:T(8,128)(2,1)}) custom-call(s32[8,512]{1,0:T(8,128)} %refs_0_.5, f32[8,512]{1,0:T(8,128)} %refs_1_.3, bf16[3,4,128,128]{3,2,1,0:T(8,128)(2,1)} %refs_0_.7, bf16[128,2048]{1,0:T(8,128)(2,1)} %get-tuple-element.65.refs_3_.refs_1_.refs_8_), custom_call_target="tpu_custom_call" | custom-call | bytes 18000000 | tf_op jit(solution)/shard_map/pallas_call | solution.py:163
  20.2 4.8 %shard_map.161 = (bf16[128,2048]{1,0:T(8,128)(2,1)}, bf16[128,2048]{1,0:T(8,128)(2,1)}, bf16[128,2048]{1,0:T(8,128)(2,1)}, f32[128,2048]{1,0:T(8,128)}, f32[128,...) custom-call(bf16[2048,128]{1,0:T(8,128)(2,1)} %refs_0_.6, ...), custom_call_target="tpu_custom_call" | custom-call | bytes 12000000 | tf_op jit(solution)/shard_map/pallas_call | solution.py:163
  25.0 5.1 %all-to-all-done.refs_0_ = bf16[16,96,128]{2,1,0:T(8,128)(2,1)S(1)} async-done(((bf16[16,96,128]{2,1,0:T(8,128)(2,1)}), bf16[16,96,128]{2,1,0:T(8,128)(2,1)S(1)}, u32[]{:S(2)}, u32[]{:S(2)}) %all-to-all-start) | async-done | bytes 393248 | tf_op jit(solution)/shard_map/all_to_all | solution.py:626
  30.1 2.9 %shard_map.162 = (bf16[16,16,128]{2,1,0:T(8,128)(2,1)}, bf16[128,512]{1,0:T(8,128)(2,1)}, bf16[128,512]{1,0:T(8,128)(2,1)}, bf16[1024,512]{1,0:T(8,128)(2,1)}, bf16[16,32,128]{2,1,0:T(8,128)(2,1)}) custom-call(bf16[16,96,128]{2,1,0:T(8,128)(2,1)S(1)} %all-to-all-done.refs_0_, bf16[512,512]{1,0:T(8,128)(2,1)} %get-tuple-element.66.refs_1_.refs_13_, ...), custom_call_target="tpu_custom_call" | custom-call | bytes 9000000 | tf_op jit(solution)/shard_map/pallas_call | solution.py:163
  33.0 3.8 %all-to-all-start.1 = ((bf16[16,16,128]{2,1,0:T(8,128)(2,1)}), bf16[16,16,128]{2,1,0:T(8,128)(2,1)S(1)}, u32[]{:S(2)}, u32[]{:S(2)}) async-start(bf16[16,16,128]{2,1,0:T(8,128)(2,1)} %get-tuple-element.71), calls=%async_computation.1 | async-start | bytes 131072 | tf_op jit(solution)/shard_map/all_to_all | solution.py:626
  36.9 2.8 %shard_map.163 = (bf16[256,256]{1,0:T(8,128)(2,1)S(1)}, bf16[128,256]{1,0:T(8,128)(2,1)S(1)}, f32[128,256]{1,0:T(8,128)S(1)}, bf16[128,256]{1,0:T(8,128)(2,1)S(1...) custom-call(bf16[16,32,128]{2,1,0:T(8,128)(2,1)} %get-tuple-element.72.ref, ...), custom_call_target="tpu_custom_call" | custom-call | bytes 18000000 | tf_op jit(solution)/shard_map/pallas_call | solution.py:163
  39.7 3.2 %all-to-all-done.1 = bf16[16,16,128]{2,1,0:T(8,128)(2,1)S(1)} async-done(((bf16[16,16,128]{2,1,0:T(8,128)(2,1)}), bf16[16,16,128]{2,1,0:T(8,128)(2,1)S(1)}, u32[]{:S(2)}, u32[]{:S(2)}) %all-to-all-start.1) | async-done | bytes 65568 | tf_op jit(solution)/shard_map/all_to_all | solution.py:626
  42.9 3.8 %shard_map.164 = (bf16[1024,128]{1,0:T(8,128)(2,1)}, bf16[128,512]{1,0:T(8,128)(2,1)}, bf16[128,512]{1,0:T(8,128)(2,1)}, bf16[128,512]{1,0:T(8,128)(2,1)}, f32[4,128,128]{2,1,0:T(8,128)}) custom-call(bf16[256,128]{1,0:T(8,128)(2,1)S(1)} %bitcast.11, bf16[256,256]{1,0:T(8,128)(2,1)S(1)} %get-tuple-element.75.refs_1_, ...), custom_call_target="tpu_custom_call" | custom-call | bytes 9000000 | tf_op jit(solution)/shard_map/pallas_call | solution.py:163
  46.7 4.3 %all-to-all-start.2 = ((bf16[16,64,128]{2,1,0:T(8,128)(2,1)}), bf16[16,64,128]{2,1,0:T(8,128)(2,1)S(1)}, u32[]{:S(2)}, u32[]{:S(2)}) async-start(bf16[16,64,128]{2,1,0:T(8,128)(2,1)} %bitcast.13), calls=%async_computation.2 | async-start | bytes 524288 | tf_op jit(solution)/shard_map/all_to_all | solution.py:626
  51.0 2.0 %shard_map.165 = (bf16[512,128]{1,0:T(8,128)(2,1)S(1)}, bf16[512,1024]{1,0:T(8,128)(2,1)S(1)}) custom-call(bf16[128,512]{1,0:T(8,128)(2,1)} %get-tuple-element.73.refs_1_.refs_0_, bf16[128,512]{1,0:T(8,128)(2,1)} %get-tuple-element.74.refs_2_.refs_1_, bf16[128,512]{1,0:T(8,128)(2,1)} %get-tuple-element.85.refs_2_, ...), custom_call_target="tpu_custom_call" | custom-call | bytes 9000000 | tf_op jit(solution)/shard_map/pallas_call | solution.py:163
  54.5 2.4 %collective-permute-start.3 = (bf16[512,128]{1,0:T(8,128)(2,1)S(1)}, bf16[512,128]{1,0:T(8,128)(2,1)S(1)}, u32[]{:S(2)}, u32[]{:S(2)}) collective-permute-start(bf16[512,128]{1,0:T(8,128)(2,1)S(1)} %shard_map.166.refs_11_.refs_0_), channel_id=1, source_target_pairs={{0,8},{1,9},{2,10},{3,11},{4,12},{5,13},{6,14},{7,15},{8,0},{9,1},... | collective-permute-start | bytes 393224 | tf_op jit(solution)/shard_map/ppermute | solution.py:794
  56.9 3.6 %all-to-all-done.2 = bf16[16,64,128]{2,1,0:T(8,128)(2,1)S(1)} async-done(((bf16[16,64,128]{2,1,0:T(8,128)(2,1)}), bf16[16,64,128]{2,1,0:T(8,128)(2,1)S(1)}, u32[]{:S(2)}, u32[]{:S(2)}) %all-to-all-start.2) | async-done | bytes 262176 | tf_op jit(solution)/shard_map/all_to_all | solution.py:626
  60.5 4.4 %shard_map.167 = (bf16[512,128]{1,0:T(8,128)(2,1)}, bf16[128,2048]{1,0:T(8,128)(2,1)}, bf16[128,2048]{1,0:T(8,128)(2,1)}) custom-call(bf16[1024,128]{1,0:T(8,128)(2,1)S(1)} %bitcast.8, bf16[512,1024]{1,0:T(8,128)(2,1)S(1)} %get-tuple-element.89.refs_1_, bf16[128,2048]{1,0:T(8,128)(2,1)} %get-tuple-element.90.refs_2_, ...), custom_call_target="tpu_custom_call" | custom-call | bytes 12000000 | tf_op jit(solution)/shard_map/pallas_call | solution.py:163
  64.9 6.3 %all-to-all-start.3 = ((bf16[16,32,128]{2,1,0:T(8,128)(2,1)}), bf16[16,32,128]{2,1,0:T(8,128)(2,1)S(1)}, u32[]{:S(2)}, u32[]{:S(2)}) async-start(bf16[16,32,128]{2,1,0:T(8,128)(2,1)} %bitcast.14), calls=%async_computation.3 | async-start | bytes 262144 | tf_op jit(solution)/shard_map/all_to_all | solution.py:626
  71.2 1.5 %collective-permute-start.6 = (bf16[512,128]{1,0:T(8,128)(2,1)S(1)}, bf16[512,128]{1,0:T(8,128)(2,1)S(1)}, u32[]{:S(2)}, u32[]{:S(2)}) collective-permute-start(bf16[512,128]{1,0:T(8,128)(2,1)S(1)} %shard_map.168.refs_4_.refs_0_), channel_id=1, source_target_pairs={{0,2},{1,3},{2,0},{3,1},{4,6},{5,7},{6,4},{7,5},{8,10},{9,11},{10,... | collective-permute-start | bytes 393224 | tf_op jit(solution)/shard_map/ppermute | solution.py:794
  72.7 6.5 %shard_map.169 = (bf16[256,128]{1,0:T(8,128)(2,1)}, bf16[256,128]{1,0:T(8,128)(2,1)}, f32[512,128]{1,0:T(8,128)}, bf16[2048,128]{1,0:T(8,128)(2,1)}) custom-call(bf16[3,4,128,128]{3,2,1,0:T(8,128)(2,1)} %refs_0_.7, bf16[128,2048]{1,0:T(8,128)(2,1)} %get-tuple-element.97.refs_1_, bf16[128,2048]{1,0:T(8,128)(2,1)} %get-tuple-element.98.refs_2_, ...), custom_call_target="tpu_custom_call" | custom-call | bytes 12000000 | tf_op jit(solution)/shard_map/pallas_call | solution.py:163
  80.1 5.2 %all-to-all-start.4 = ((bf16[16,32,128]{2,1,0:T(8,128)(2,1)}), bf16[16,32,128]{2,1,0:T(8,128)(2,1)S(1)}, u32[]{:S(2)}, u32[]{:S(2)}) async-start(bf16[16,32,128]{2,1,0:T(8,128)(2,1)} %shard_map.172), calls=%async_computation.4 | async-start | bytes 262144 | tf_op jit(solution)/shard_map/all_to_all | solution.py:626
  86.7 3.6 %collective-permute-start.5 = (bf16[256,128]{1,0:T(8,128)(2,1)}, bf16[256,128]{1,0:T(8,128)(2,1)S(1)}, u32[]{:S(2)}, u32[]{:S(2)}) collective-permute-start(bf16[256,128]{1,0:T(8,128)(2,1)} %get-tuple-element.102), channel_id=1, source_target_pairs={{1,2},{2,1},{3,4},{4,3},{5,6},{6,5},{7,8},{8,7},{9,10},{10,9},{11,... | collective-permute-start | bytes 196616 | tf_op jit(solution)/shard_map/ppermute | solution.py:842
  90.4 2.6 %collective-permute-done.5.refs_2_ = bf16[256,128]{1,0:T(8,128)(2,1)S(1)} collective-permute-done((bf16[256,128]{1,0:T(8,128)(2,1)}, bf16[256,128]{1,0:T(8,128)(2,1)S(1)}, u32[]{:S(2)}, u32[]{:S(2)}) %collective-permute-start.5) | collective-permute-done | bytes 65568 | tf_op jit(solution)/shard_map/ppermute | solution.py:842
  93.0 1.8 %shard_map.170 = (bf16[2048,128]{1,0:T(8,128)(2,1)}, f32[12,128,128]{2,1,0:T(8,128)}) custom-call(f32[512,128]{1,0:T(8,128)} %get-tuple-element.100.refs_0_, bf16[256,128]{1,0:T(8,128)(2,1)S(1)} %collective-permute-done.4.refs_1_, bf16[256,128]{1,0:T(8,128)(2,1)S(1)} %collective-permute-done.5.refs_2_, ...), custom_call_target="tpu_custom_call", output_to_operand_aliasing={{0}: (4, {})} | custom-call | bytes 3000000 | tf_op jit(solution)/shard_map/pallas_call | solution.py:163
  (20 shorter events, 5.6 us)
Async XLA Ops:
  1.5 9.5 %collective-permute-start.1 = (bf16[256,128]{1,0:T(8,128)(2,1)S(1)}, bf16[256,128]{1,0:T(8,128)(2,1)S(1)}, u32[]{:S(2)}, u32[]{:S(2)}) collective-permute-start(bf16[256,128]{1,0:T(8,128)(2,1)S(1)} %get-tuple-element.108), channel_id=1, source_target_pairs={{1,2},{2,1},{3,4},{4,3},{5,6},{6,5},{7,8},{8,7},{9,10},{10,9},{11,... | collective-permute-start | bytes 196616 | tf_op jit(solution)/shard_map/ppermute | solution.py:667
  6.1 5.0 %collective-permute-start = (bf16[256,128]{1,0:T(8,128)(2,1)S(1)}, bf16[256,128]{1,0:T(8,128)(2,1)S(1)}, u32[]{:S(2)}, u32[]{:S(2)}) collective-permute-start(bf16[256,128]{1,0:T(8,128)(2,1)S(1)} %get-tuple-element.109), channel_id=1, source_target_pairs={{0,1},{1,0},{2,3},{3,2},{4,5},{5,4},{6,7},{7,6},{8,9},{9,8},{10,11... | collective-permute-start | bytes 196616 | tf_op jit(solution)/shard_map/ppermute | solution.py:666
  12.8 17.3 %all-to-all-start = ((bf16[16,96,128]{2,1,0:T(8,128)(2,1)}), bf16[16,96,128]{2,1,0:T(8,128)(2,1)S(1)}, u32[]{:S(2)}, u32[]{:S(2)}) async-start(bf16[16,96,128]{2,1,0:T(8,128)(2,1)} %get-tuple-element.64), calls=%async_computation | async-start | bytes 786432 | tf_op jit(solution)/shard_map/all_to_all | solution.py:626
  33.0 9.9 %all-to-all-start.1 = ((bf16[16,16,128]{2,1,0:T(8,128)(2,1)}), bf16[16,16,128]{2,1,0:T(8,128)(2,1)S(1)}, u32[]{:S(2)}, u32[]{:S(2)}) async-start(bf16[16,16,128]{2,1,0:T(8,128)(2,1)} %get-tuple-element.71), calls=%async_computation.1 | async-start | bytes 131072 | tf_op jit(solution)/shard_map/all_to_all | solution.py:626
  46.7 13.7 %all-to-all-start.2 = ((bf16[16,64,128]{2,1,0:T(8,128)(2,1)}), bf16[16,64,128]{2,1,0:T(8,128)(2,1)S(1)}, u32[]{:S(2)}, u32[]{:S(2)}) async-start(bf16[16,64,128]{2,1,0:T(8,128)(2,1)} %bitcast.13), calls=%async_computation.2 | async-start | bytes 524288 | tf_op jit(solution)/shard_map/all_to_all | solution.py:626
  53.0 1.4 %collective-permute-start.2 = (bf16[512,128]{1,0:T(8,128)(2,1)S(1)}, bf16[512,128]{1,0:T(8,128)(2,1)S(1)}, u32[]{:S(2)}, u32[]{:S(2)}) collective-permute-start(bf16[512,128]{1,0:T(8,128)(2,1)S(1)} %get-tuple-element.96.refs_0_), channel_id=1, source_target_pairs={{0,1},{1,0},{2,3},{3,2},{4,5},{5,4},{6,7},{7,6},{8,9},{9,8},{10,11... | collective-permute-start | bytes 393224 | tf_op jit(solution)/shard_map/ppermute | solution.py:794
  54.5 16.7 %collective-permute-start.3 = (bf16[512,128]{1,0:T(8,128)(2,1)S(1)}, bf16[512,128]{1,0:T(8,128)(2,1)S(1)}, u32[]{:S(2)}, u32[]{:S(2)}) collective-permute-start(bf16[512,128]{1,0:T(8,128)(2,1)S(1)} %shard_map.166.refs_11_.refs_0_), channel_id=1, source_target_pairs={{0,8},{1,9},{2,10},{3,11},{4,12},{5,13},{6,14},{7,15},{8,0},{9,1},... | collective-permute-start | bytes 393224 | tf_op jit(solution)/shard_map/ppermute | solution.py:794
  64.9 14.4 %all-to-all-start.3 = ((bf16[16,32,128]{2,1,0:T(8,128)(2,1)}), bf16[16,32,128]{2,1,0:T(8,128)(2,1)S(1)}, u32[]{:S(2)}, u32[]{:S(2)}) async-start(bf16[16,32,128]{2,1,0:T(8,128)(2,1)} %bitcast.14), calls=%async_computation.3 | async-start | bytes 262144 | tf_op jit(solution)/shard_map/all_to_all | solution.py:626
  71.2 8.0 %collective-permute-start.6 = (bf16[512,128]{1,0:T(8,128)(2,1)S(1)}, bf16[512,128]{1,0:T(8,128)(2,1)S(1)}, u32[]{:S(2)}, u32[]{:S(2)}) collective-permute-start(bf16[512,128]{1,0:T(8,128)(2,1)S(1)} %shard_map.168.refs_4_.refs_0_), channel_id=1, source_target_pairs={{0,2},{1,3},{2,0},{3,1},{4,6},{5,7},{6,4},{7,5},{8,10},{9,11},{10,... | collective-permute-start | bytes 393224 | tf_op jit(solution)/shard_map/ppermute | solution.py:794
  80.1 14.7 %all-to-all-start.4 = ((bf16[16,32,128]{2,1,0:T(8,128)(2,1)}), bf16[16,32,128]{2,1,0:T(8,128)(2,1)S(1)}, u32[]{:S(2)}, u32[]{:S(2)}) async-start(bf16[16,32,128]{2,1,0:T(8,128)(2,1)} %shard_map.172), calls=%async_computation.4 | async-start | bytes 262144 | tf_op jit(solution)/shard_map/all_to_all | solution.py:626
  85.3 9.4 %collective-permute-start.7 = (bf16[512,128]{1,0:T(8,128)(2,1)S(1)}, bf16[512,128]{1,0:T(8,128)(2,1)S(1)}, u32[]{:S(2)}, u32[]{:S(2)}) collective-permute-start(bf16[512,128]{1,0:T(8,128)(2,1)S(1)} %shard_map.171.refs_2_.refs_0_), channel_id=1, source_target_pairs={{0,4},{1,5},{2,6},{3,7},{4,0},{5,1},{6,2},{7,3},{8,12},{9,13},{10,... | collective-permute-start | bytes 393224 | tf_op jit(solution)/shard_map/ppermute | solution.py:794
  86.7 6.3 %collective-permute-start.5 = (bf16[256,128]{1,0:T(8,128)(2,1)}, bf16[256,128]{1,0:T(8,128)(2,1)S(1)}, u32[]{:S(2)}, u32[]{:S(2)}) collective-permute-start(bf16[256,128]{1,0:T(8,128)(2,1)} %get-tuple-element.102), channel_id=1, source_target_pairs={{1,2},{2,1},{3,4},{4,3},{5,6},{6,5},{7,8},{8,7},{9,10},{10,9},{11,... | collective-permute-start | bytes 196616 | tf_op jit(solution)/shard_map/ppermute | solution.py:842
  90.3 2.6 %collective-permute-start.4 = (bf16[256,128]{1,0:T(8,128)(2,1)}, bf16[256,128]{1,0:T(8,128)(2,1)S(1)}, u32[]{:S(2)}, u32[]{:S(2)}) collective-permute-start(bf16[256,128]{1,0:T(8,128)(2,1)} %get-tuple-element.101.refs_2_.refs_1_), channel_id=1, source_target_pairs={{0,1},{1,0},{2,3},{3,2},{4,5},{5,4},{6,7},{7,6},{8,9},{9,8},{10,11... | collective-permute-start | bytes 196616 | tf_op jit(solution)/shard_map/ppermute | solution.py:841

commit v10 on v9

--- a/solution.py
+++ b/solution.py
@@ -196,7 +196,7 @@
 
 def inner_kernel(tile_rows, peers, cap, io, need, flush, ins, outs, feat_t, s_ref, ids, counts):
     off, ew, feat, w, pool, owner, slot, nbrs, cew, cot = ins
-    so_ref, win_ref, w01_ref, w2t_ref, w3t_ref, po_ref, spread, ext_ref, agg_ref, place, s_all = outs
+    so_ref, win_ref, w01_ref, w2t_ref, w3t_ref, po_ref, spread, ext_ref, agg_ref, place = outs
     rows, d = feat.shape
     block_rows = pool.shape[0]
     n2 = cot.shape[0]
@@ -226,14 +226,12 @@
     for n, i in enumerate((0, tiles - 1)):
         cols = slice(i * TILE, (i + 1) * TILE)
         fine_edges(off[:, cols], ew[:, cols], so_ref.at[n])
-        io.start(so_ref.at[n], s_all.at[i])
     need()
     feat_t[...] = jnp.transpose(feat[...])
     weights = forward_weights(w)
     for i in range(1, tiles - 1):
         cols = slice(i * TILE, (i + 1) * TILE)
         fine_edges(off[:, cols], ew[:, cols], s_ref.at[i - 1])
-        io.start(s_ref.at[i - 1], s_all.at[i])
         around = feat_t[:, i * TILE - HALO : (i + 1) * TILE + HALO]
         agg_ref[:, cols] = dot(around, s_ref[i - 1]).astype(BF)
     for start in range(TILE, rows - TILE, WIDE):
@@ -492,10 +490,9 @@
 
 
 def third_window_kernel(mid_scale, io, need, flush, ins, outs):
-    mhid, magg, gmid, msg, mfg, w1, place = ins
-    wg_ref, pick_ref = outs
+    mhid, magg, gmid, msg, mfg, w1 = ins
+    wg_ref = outs[0]
     d = mhid.shape[0]
-    block_rows = pick_ref.shape[0] // place.shape[0]
     need()
     w01, w2t, _ = forward_weights(w1)
     middle = silu(dot(w01, jnp.concatenate([mhid[...], magg[...]], axis=0))).astype(BF)
@@ -504,6 +501,12 @@
     wg_ref[d : 2 * d, :] = (dot_nt(magg[...], mfg[...]) * mid_scale).astype(BF)
     wg_ref[2 * d : 3 * d, :] = (dot_nt(middle, msg[...]) * mid_scale).astype(BF)
     wg_ref[3 * d : 4 * d, :] = (dot_nt(outer, gmid[...]) * mid_scale).astype(BF)
+
+
+def pick_kernel(block_rows, io, need, flush, ins, outs):
+    place = ins[0]
+    pick_ref = outs[0]
+    need()
     slots = pick_ref.shape[1]
     lane = lax.broadcasted_iota(jnp.int32, (block_rows, slots), 1)
     lane = lane - lax.broadcasted_iota(jnp.int32, (block_rows, slots), 0)
@@ -547,36 +550,51 @@
 
 
 def fine_spread_kernel(io, need, flush, ins, outs, band, spill, inner):
-    w, g, fg, s_all, _ = ins
+    off, ew, w, g, fg, _ = ins
     rim_near, rim_far, edge_ref, out_ref = outs
     d, rows = g.shape
     tiles = rows // TILE
-    arrive = []
-    for b in range(tiles + 2):
-        arrive.append([])
+
+    def piece(i, h, c):
+        row = 128 * (h + c)
+        lane = (2 - row // TILE) * TILE + 128 * h
+        return band.at[i + row // TILE, pl.ds(row % TILE, 128), pl.ds(lane, 128)]
+
+    def build(i):
+        for h in range(TILE // 128):
+            lane = slice(i * TILE + 128 * h, i * TILE + 128 * (h + 1))
+            o = off[:, lane]
+            weight = merged_weights(o, ew[:, lane])
+            rel = o + lax.broadcasted_iota(jnp.int32, o.shape, 1) + HALO
+            rel = rel.astype(jnp.int16)
+            for c in range(2 * HALO // 128 + 1):
+                piece(i, h, c)[...] = edge_columns(rel, weight, 128 * c, 128)
+
+    for i in range(tiles):
+        piece(i, 0, 5)[...] = jnp.zeros((128, 128), BF)
+        piece(i, 1, -1)[...] = jnp.zeros((128, 128), BF)
+    for b in (0, 1, tiles, tiles + 1):
         for j in range(3):
-            lanes = pl.ds(j * TILE, TILE)
-            if 0 <= b - 2 + j < tiles:
-                source = s_all.at[b - 2 + j, pl.ds((2 - j) * TILE, TILE), :]
-                arrive[b].append(io.start(source, band.at[b, :, lanes]))
-            else:
+            if not 0 <= b - 2 + j < tiles:
                 band[b, :, j * TILE : (j + 1) * TILE] = jnp.zeros((TILE, TILE), BF)
     spill[:, : 2 * TILE] = jnp.zeros((d, 2 * TILE), BF)
     spill[:, 2 * TILE + rows :] = jnp.zeros((d, 2 * TILE), BF)
     even = lax.rem(lax.axis_index("nodes"), 2) == 0
+    need(0, 1)
+    build(0)
+    build(tiles - 1)
     need()
     spill[:, 2 * TILE : 2 * TILE + rows] = dot(w[1], fg[...]).astype(BF)
-    rims = []
-    for b in [0, tiles + 1] + list(range(1, tiles + 1)):
-        io.wait(*arrive[b])
+    low, high = [
+        dot_nt(band[b], spill[:, b * TILE : (b + 3) * TILE]).astype(BF) for b in (0, tiles + 1)
+    ]
+    rim_near[...] = jnp.where(even, high, low)
+    rim_far[...] = jnp.where(even, low, high)
+    flush(0, 1)
+    for i in range(1, tiles - 1):
+        build(i)
+    for b in range(1, tiles + 1):
         part = dot_nt(band[b], spill[:, b * TILE : (b + 3) * TILE])
-        if b in (0, tiles + 1):
-            rims.append(part.astype(BF))
-            continue
-        if b == 1:
-            rim_near[...] = jnp.where(even, rims[1], rims[0])
-            rim_far[...] = jnp.where(even, rims[0], rims[1])
-            flush(0, 1)
         cols = slice((b - 1) * TILE, b * TILE)
         part = part + jnp.transpose(g[:, cols].astype(F32) + dot(w[0], fg[:, cols]))
         if b == 1:
@@ -666,7 +684,7 @@
     across = lax.ppermute(near, "nodes", inside_pairs)
     beside = lax.ppermute(far, "nodes", between_pairs)
     owners = owner_dev.reshape(-1)
-    s_out, win, w01, w2t, w3t, pool_out, spread, ext, agg_in, place, s_all = call(
+    s_out, win, w01, w2t, w3t, pool_out, spread, ext, agg_in, place = call(
         functools.partial(inner_kernel, tile_rows, peers, cap),
         [
             (fine_offsets, "h"), (fine_edge_w, "h"), (features, "h"), (weights, "0"),
@@ -678,7 +696,7 @@
             (shape((d, 2 * d)), "v"), (shape((d, d)), "v"), (shape((d, d)), "v"),
             (shape((2, per, TILE)), "v"), (shape((peers * chunk, d), F32), "v"),
             (shape((peers, n2 + 16, d)), "v"), (shape((d, n)), "v"),
-            (shape((tile_count,), jnp.int32), "s"), (shape((n // TILE, window, TILE)), "r"),
+            (shape((tile_count,), jnp.int32), "s"),
         ],
         scratch=(
             pltpu.VMEM((d, n), BF),
@@ -686,7 +704,6 @@
             pltpu.VMEM((peers, 128), F32),
             pltpu.SMEM((peers,), jnp.int32),
         ),
-        copies=n // TILE,
         us=6,
     )
     send1, agg = call(
@@ -775,20 +792,15 @@
     )
     got3 = exchange(send3.reshape(peers, chunk, d))
     pick_kind = "v" if peers * chunk <= 1024 else "h"
-    mid_wg, pick = call(
+    (mid_wg,) = call(
         functools.partial(third_window_kernel, 1.0 / math.sqrt(n1 * peers)),
         [
             (mhid, "h"), (magg, "h"), (gmid, "h"), (msg, "h"), (mfg, "h"), (weights, "1"),
-            (place, "s"),
-        ],
-        [
-            (shape((4 * d, d)), "v"),
-            (shape((tile_count * block_rows, peers * chunk)), pick_kind),
-        ],
-        us=3,
+        ],
+        [(shape((4 * d, d)), "v")],
+        us=2,
     )
     reaches = [1 << i for i in range((peers - 1).bit_length())]
-    reaches = reaches[:1] + reaches[-1:] + reaches[1:-1]
 
     def double(total, reach, *after):
         other = lax.ppermute(total, "nodes", [(i, i ^ reach) for i in range(peers)])
@@ -796,14 +808,20 @@
         return call(add_kernel, ins, [(shape((4 * d, d)), "v")], us=1)[0]
 
     sums = [mid_wg]
-    for reach in reaches[:2]:
+    for reach in reaches[:3]:
         sums.append(double(sums[-1], reach))
+    (pick,) = call(
+        functools.partial(pick_kernel, block_rows),
+        [(place, "s"), (sums[1], "v")],
+        [(shape((tile_count * block_rows, peers * chunk)), pick_kind)],
+        us=1,
+    )
     send4, g, fg = call(
         functools.partial(fine_grad_kernel, 1.0 / math.sqrt(n * peers)),
         [
             (got3.reshape(peers * chunk, d), "v"), (pick, pick_kind), (cot, "h"), (pool_b, "h"),
             (weights, "0"), (slope2, "h"), (slope1, "h"), (hid, "h"), (agg, "h"), (mid, "h"),
-            (outer, "h"), (sums[1], "v"),
+            (outer, "h"), (sums[2], "v"),
         ],
         [(shape((4 * d, d)), "h"), (shape((d, n)), "r"), (shape((d, n)), "r")],
         scratch=(pltpu.VMEM((d, n), BF), pltpu.VMEM((d, n), BF)),
@@ -813,7 +831,10 @@
     got4 = exchange(send4.reshape(peers, 4 * d // peers, d))
     rim_near, rim_far, edge_sums, inner_grads = call(
         fine_spread_kernel,
-        [(weights, "0"), (g, "h"), (fg, "h"), (s_all, "r"), (sums[2], "v")],
+        [
+            (fine_offsets, "h"), (fine_edge_w, "h"), (weights, "0"), (g, "h"), (fg, "h"),
+            (sums[3], "v"),
+        ],
         [
             (shape((HALO, d)), "h"), (shape((HALO, d)), "h"), (shape((2 * HALO, d), F32), "h"),
             (shape((n, d)), "r"),
@@ -823,20 +844,20 @@
             pltpu.VMEM((d, n + 4 * TILE), BF),
             pltpu.VMEM((n - 2 * HALO, d), BF),
         ),
-        copies=3 * (n // TILE) + 1,
-        us=4,
-    )
-    sums.append(double(sums[2], reaches[2], rim_near))
+        copies=1,
+        us=5,
+    )
+    sums.append(double(sums[3], reaches[3], rim_near))
     (send5,) = call(
         sum_kernel,
-        [(got4, "v"), (rim_near, "r"), (sums[3], "v")],
+        [(got4, "v"), (rim_near, "r"), (sums[4], "v")],
         [(shape((peers, 4 * d // peers, d)), "r")],
         scratch=(pltpu.VMEM((4 * d // peers, d), BF),),
         copies=peers,
         us=1,
     )
     got5 = exchange(send5)
-    for reach in reaches[3:]:
+    for reach in reaches[4:]:
         sums.append(double(sums[-1], reach))
     from_across = lax.ppermute(rim_near, "nodes", inside_pairs)
     from_beside = lax.ppermute(rim_far, "nodes", between_pairs)

time: 96.6 us -> 99.1 us (1.026)
  waiting for transfers between devices: 15.6 us -> 20.7 us
  Pallas kernels: 39.4 us -> 37.5 us
    ppermute x4, waiting for transfers between devices: 1.13 us -> 9.89 us  [double(): other = lax.ppermute(total, 'nodes', [(i, i ^ reach) for i in range(peers)])]
    all_to_all x5, waiting for transfers between devices: 11.9 us -> 8.47 us  [exchange(): return lax.all_to_all(x, 'nodes', split_axis=0, concat_axis=0, tiled=True)]
    pallas_call x17 -> x18, Pallas kernels: 39.4 us -> 37.5 us  [call(): pl.pallas_call(body, out_shape=[s if kind == 'v' else pltpu.HBM(s.shape,...]
    all_to_all x5, starting transfers between devices: 25 us -> 23.2 us  [exchange(): return lax.all_to_all(x, 'nodes', split_axis=0, concat_axis=0, tiled=True)]
  transfers between devices with their start and end apart: 13 -> 13, of which waited for: 5 -> 6; matrix products, arithmetic and copies ran while one was open for 0% -> 0% of each run, Pallas kernels for 31% -> 28%
where the time goes in v10:
time: 99.1 us; the launch traced here: 98 us
  starting transfers between devices  37.9 us (38%)
  Pallas kernels  37.5 us (38%)
  waiting for transfers between devices  20.7 us (21%)
  between operations  1.03 us (1%)
    pallas_call x18, Pallas kernels, call(): pl.pallas_call(body, out_shape=[s if kind == 'v' else pltpu.HBM(s.shape,...  37.5 us
    all_to_all x5, starting transfers between devices, exchange(): return lax.all_to_all(x, 'nodes', split_axis=0, concat_axis=0, tiled=True)  23.2 us
    ppermute x4, waiting for transfers between devices, double(): other = lax.ppermute(total, 'nodes', [(i, i ^ reach) for i in range(peers)])  9.89 us
    all_to_all x5, waiting for transfers between devices, exchange(): return lax.all_to_all(x, 'nodes', split_axis=0, concat_axis=0, tiled=True)  8.47 us
    ppermute x4, starting transfers between devices, double(): other = lax.ppermute(total, 'nodes', [(i, i ^ reach) for i in range(peers)])  6.49 us
    ppermute x1, starting transfers between devices, per_device(): beside = lax.ppermute(far, 'nodes', between_pairs)  4.54 us
    ppermute x1, starting transfers between devices, per_device(): from_beside = lax.ppermute(rim_far, 'nodes', between_pairs)  3.54 us
    ppermute x1, waiting for transfers between devices, per_device(): from_beside = lax.ppermute(rim_far, 'nodes', between_pairs)  2.34 us
  transfers between devices with their start and end apart: 13, of which 6 were waited for; matrix products, arithmetic and copies ran while one was open for 0% of the time, Pallas kernels for 28%

profile of v10, /device:TPU:1, one launch (start us, length us, event | category | flops | bytes accessed | tf_op | source)
XLA Modules:
  0.0 98.0 jit_solution(17410183315593925726)
XLA Ops:
  1.5 4.5 %collective-permute-start.1 = (bf16[256,128]{1,0:T(8,128)(2,1)S(1)}, bf16[256,128]{1,0:T(8,128)(2,1)S(1)}, u32[]{:S(2)}, u32[]{:S(2)}) collective-permute-start(bf16[256,128]{1,0:T(8,128)(2,1)S(1)} %get-tuple-element.102), channel_id=1, source_target_pairs={{1,2},{2,1},{3,4},{4,3},{5,6},{6,5},{7,8},{8,7},{9,10},{10,9},{11,... | collective-permute-start | bytes 196616 | tf_op jit(solution)/shard_map/ppermute | solution.py:685
  6.2 4.3 %shard_map.158 = (bf16[2,768,256]{2,1,0:T(8,128)(2,1)S(1)}, bf16[2,128,512]{2,1,0:T(8,128)(2,1)S(1)}, bf16[128,256]{1,0:T(8,128)(2,1)S(1)}, bf16[128,128]{1,0:T(...) custom-call(s32[8,2048]{1,0:T(8,128)} %refs_0_.7, ...), custom_call_target="tpu_custom_call" | custom-call | bytes 18000000 | tf_op jit(solution)/shard_map/pallas_call | solution.py:163
  12.3 5.4 %all-to-all-start = ((bf16[16,96,128]{2,1,0:T(8,128)(2,1)}), bf16[16,96,128]{2,1,0:T(8,128)(2,1)S(1)}, u32[]{:S(2)}, u32[]{:S(2)}) async-start(bf16[16,96,128]{2,1,0:T(8,128)(2,1)} %get-tuple-element.61), calls=%async_computation | async-start | bytes 786432 | tf_op jit(solution)/shard_map/all_to_all | solution.py:644
  17.7 2.0 %shard_map.160 = (bf16[512,512]{1,0:T(8,128)(2,1)}, bf16[128,256]{1,0:T(8,128)(2,1)}, bf16[128,128]{1,0:T(8,128)(2,1)}, bf16[128,128]{1,0:T(8,128)(2,1)}) custom-call(s32[8,512]{1,0:T(8,128)} %refs_0_.5, f32[8,512]{1,0:T(8,128)} %refs_1_.4, bf16[3,4,128,128]{3,2,1,0:T(8,128)(2,1)} %refs_2_.7, bf16[128,2048]{1,0:T(8,128)(2,1)} %get-tuple-element.62.refs_3_.refs_1_.refs_8_), custom_call_target="tpu_custom_call" | custom-call | bytes 18000000 | tf_op jit(solution)/shard_map/pallas_call | solution.py:163
  19.6 4.7 %shard_map.161 = (bf16[128,2048]{1,0:T(8,128)(2,1)}, bf16[128,2048]{1,0:T(8,128)(2,1)}, bf16[128,2048]{1,0:T(8,128)(2,1)}, f32[128,2048]{1,0:T(8,128)}, f32[128,...) custom-call(bf16[2048,128]{1,0:T(8,128)(2,1)} %refs_0_.6, ...), custom_call_target="tpu_custom_call" | custom-call | bytes 12000000 | tf_op jit(solution)/shard_map/pallas_call | solution.py:163
  24.3 5.3 %all-to-all-done.refs_0_ = bf16[16,96,128]{2,1,0:T(8,128)(2,1)S(1)} async-done(((bf16[16,96,128]{2,1,0:T(8,128)(2,1)}), bf16[16,96,128]{2,1,0:T(8,128)(2,1)S(1)}, u32[]{:S(2)}, u32[]{:S(2)}) %all-to-all-start) | async-done | bytes 393248 | tf_op jit(solution)/shard_map/all_to_all | solution.py:644
  29.6 2.9 %shard_map.162 = (bf16[16,16,128]{2,1,0:T(8,128)(2,1)}, bf16[128,512]{1,0:T(8,128)(2,1)}, bf16[128,512]{1,0:T(8,128)(2,1)}, bf16[1024,512]{1,0:T(8,128)(2,1)}, bf16[16,32,128]{2,1,0:T(8,128)(2,1)}) custom-call(bf16[16,96,128]{2,1,0:T(8,128)(2,1)S(1)} %all-to-all-done.refs_0_, bf16[512,512]{1,0:T(8,128)(2,1)} %get-tuple-element.63.refs_1_.refs_13_, ...), custom_call_target="tpu_custom_call" | custom-call | bytes 9000000 | tf_op jit(solution)/shard_map/pallas_call | solution.py:163
  32.4 3.8 %all-to-all-start.1 = ((bf16[16,16,128]{2,1,0:T(8,128)(2,1)}), bf16[16,16,128]{2,1,0:T(8,128)(2,1)S(1)}, u32[]{:S(2)}, u32[]{:S(2)}) async-start(bf16[16,16,128]{2,1,0:T(8,128)(2,1)} %get-tuple-element.68), calls=%async_computation.1 | async-start | bytes 131072 | tf_op jit(solution)/shard_map/all_to_all | solution.py:644
  36.3 2.8 %shard_map.163 = (bf16[256,256]{1,0:T(8,128)(2,1)S(1)}, bf16[128,256]{1,0:T(8,128)(2,1)S(1)}, f32[128,256]{1,0:T(8,128)S(1)}, bf16[128,256]{1,0:T(8,128)(2,1)S(1...) custom-call(bf16[16,32,128]{2,1,0:T(8,128)(2,1)} %get-tuple-element.69.ref, ...), custom_call_target="tpu_custom_call" | custom-call | bytes 18000000 | tf_op jit(solution)/shard_map/pallas_call | solution.py:163
  39.1 3.2 %all-to-all-done.1 = bf16[16,16,128]{2,1,0:T(8,128)(2,1)S(1)} async-done(((bf16[16,16,128]{2,1,0:T(8,128)(2,1)}), bf16[16,16,128]{2,1,0:T(8,128)(2,1)S(1)}, u32[]{:S(2)}, u32[]{:S(2)}) %all-to-all-start.1) | async-done | bytes 65568 | tf_op jit(solution)/shard_map/all_to_all | solution.py:644
  42.3 3.8 %shard_map.164 = (bf16[1024,128]{1,0:T(8,128)(2,1)}, bf16[128,512]{1,0:T(8,128)(2,1)}, bf16[128,512]{1,0:T(8,128)(2,1)}, bf16[128,512]{1,0:T(8,128)(2,1)}, f32[4,128,128]{2,1,0:T(8,128)}) custom-call(bf16[256,128]{1,0:T(8,128)(2,1)S(1)} %bitcast.11, bf16[256,256]{1,0:T(8,128)(2,1)S(1)} %get-tuple-element.72.refs_1_, ...), custom_call_target="tpu_custom_call" | custom-call | bytes 9000000 | tf_op jit(solution)/shard_map/pallas_call | solution.py:163
  46.1 4.3 %all-to-all-start.2 = ((bf16[16,64,128]{2,1,0:T(8,128)(2,1)}), bf16[16,64,128]{2,1,0:T(8,128)(2,1)S(1)}, u32[]{:S(2)}, u32[]{:S(2)}) async-start(bf16[16,64,128]{2,1,0:T(8,128)(2,1)} %bitcast.13), calls=%async_computation.2 | async-start | bytes 524288 | tf_op jit(solution)/shard_map/all_to_all | solution.py:644
  50.4 1.9 %shard_map.165.refs_0_ = bf16[512,128]{1,0:T(8,128)(2,1)S(1)} custom-call(bf16[128,512]{1,0:T(8,128)(2,1)} %get-tuple-element.70.refs_1_.refs_0_, bf16[128,512]{1,0:T(8,128)(2,1)} %get-tuple-element.71.refs_2_.refs_1_, bf16[128,512]{1,0:T(8,128)(2,1)} %get-tuple-element.83.refs_2_, bf16[128,512]{1,0:T(8,128)(2,1)} %get-tuple-element.84.refs_3_, ...), custom_call_target="tpu_custom_call" | custom-call | bytes 6000000 | tf_op jit(solution)/shard_map/pallas_call | solution.py:163
  55.2 4.1 %collective-permute-done.3.refs_1_ = bf16[512,128]{1,0:T(8,128)(2,1)S(1)} collective-permute-done((bf16[512,128]{1,0:T(8,128)(2,1)S(1)}, bf16[512,128]{1,0:T(8,128)(2,1)S(1)}, u32[]{:S(2)}, u32[]{:S(2)}) %collective-permute-start.3) | collective-permute-done | bytes 131104 | tf_op jit(solution)/shard_map/ppermute | solution.py:806
  59.3 2.4 %collective-permute-start.4 = (bf16[512,128]{1,0:T(8,128)(2,1)S(1)}, bf16[512,128]{1,0:T(8,128)(2,1)S(1)}, u32[]{:S(2)}, u32[]{:S(2)}) collective-permute-start(bf16[512,128]{1,0:T(8,128)(2,1)S(1)} %shard_map.168.refs_11_.refs_0_), channel_id=1, source_target_pairs={{0,4},{1,5},{2,6},{3,7},{4,0},{5,1},{6,2},{7,3},{8,12},{9,13},{10,... | collective-permute-start | bytes 393224 | tf_op jit(solution)/shard_map/ppermute | solution.py:806
  62.6 4.4 %shard_map.169 = (bf16[512,128]{1,0:T(8,128)(2,1)}, bf16[128,2048]{1,0:T(8,128)(2,1)}, bf16[128,2048]{1,0:T(8,128)(2,1)}) custom-call(bf16[1024,128]{1,0:T(8,128)(2,1)S(1)} %bitcast.9, bf16[512,1024]{1,0:T(8,128)(2,1)S(1)} %shard_map.167.refs_1_, bf16[128,2048]{1,0:T(8,128)(2,1)} %get-tuple-element.86.refs_2_, ...), custom_call_target="tpu_custom_call" | custom-call | bytes 12000000 | tf_op jit(solution)/shard_map/pallas_call | solution.py:163
  67.0 5.0 %all-to-all-start.3 = ((bf16[16,32,128]{2,1,0:T(8,128)(2,1)}), bf16[16,32,128]{2,1,0:T(8,128)(2,1)S(1)}, u32[]{:S(2)}, u32[]{:S(2)}) async-start(bf16[16,32,128]{2,1,0:T(8,128)(2,1)} %bitcast.14), calls=%async_computation.3 | async-start | bytes 262144 | tf_op jit(solution)/shard_map/all_to_all | solution.py:644
  72.1 2.4 %collective-permute-start.7 = (bf16[512,128]{1,0:T(8,128)(2,1)S(1)}, bf16[512,128]{1,0:T(8,128)(2,1)S(1)}, u32[]{:S(2)}, u32[]{:S(2)}) collective-permute-start(bf16[512,128]{1,0:T(8,128)(2,1)S(1)} %shard_map.170.refs_5_.refs_0_), channel_id=1, source_target_pairs={{0,8},{1,9},{2,10},{3,11},{4,12},{5,13},{6,14},{7,15},{8,0},{9,1},... | collective-permute-start | bytes 393224 | tf_op jit(solution)/shard_map/ppermute | solution.py:806
  74.4 4.6 %shard_map.171 = (bf16[256,128]{1,0:T(8,128)(2,1)}, bf16[256,128]{1,0:T(8,128)(2,1)}, f32[512,128]{1,0:T(8,128)}, bf16[2048,128]{1,0:T(8,128)(2,1)}) custom-call(s32[8,2048]{1,0:T(8,128)} %refs_0_.7, f32[8,2048]{1,0:T(8,128)} %refs_1_.5, bf16[3,4,128,128]{3,2,1,0:T(8,128)(2,1)} %refs_2_.7, bf16[128,2048]{1,0:T(8,128)(2,1)} %get-tuple-element.92.refs_3_, ...), custom_call_target="tpu_custom_call" | custom-call | bytes 15000000 | tf_op jit(solution)/shard_map/pallas_call | solution.py:163
  79.0 4.7 %collective-permute-done.7.refs_1_ = bf16[512,128]{1,0:T(8,128)(2,1)S(1)} collective-permute-done((bf16[512,128]{1,0:T(8,128)(2,1)S(1)}, bf16[512,128]{1,0:T(8,128)(2,1)S(1)}, u32[]{:S(2)}, u32[]{:S(2)}) %collective-permute-start.7) | collective-permute-done | bytes 131104 | tf_op jit(solution)/shard_map/ppermute | solution.py:806
  84.6 4.7 %all-to-all-start.4 = ((bf16[16,32,128]{2,1,0:T(8,128)(2,1)}), bf16[16,32,128]{2,1,0:T(8,128)(2,1)S(1)}, u32[]{:S(2)}, u32[]{:S(2)}) async-start(bf16[16,32,128]{2,1,0:T(8,128)(2,1)} %shard_map.174), calls=%async_computation.4 | async-start | bytes 262144 | tf_op jit(solution)/shard_map/all_to_all | solution.py:644
  89.3 3.5 %collective-permute-start.6 = (bf16[256,128]{1,0:T(8,128)(2,1)S(1)}, bf16[256,128]{1,0:T(8,128)(2,1)S(1)}, u32[]{:S(2)}, u32[]{:S(2)}) collective-permute-start(bf16[256,128]{1,0:T(8,128)(2,1)S(1)} %copy-done.1), channel_id=1, source_target_pairs={{1,2},{2,1},{3,4},{4,3},{5,6},{6,5},{7,8},{8,7},{9,10},{10,9},{11,... | collective-permute-start | bytes 196616 | tf_op jit(solution)/shard_map/ppermute | solution.py:863
  92.9 2.3 %collective-permute-done.6.refs_2_ = bf16[256,128]{1,0:T(8,128)(2,1)S(1)} collective-permute-done((bf16[256,128]{1,0:T(8,128)(2,1)S(1)}, bf16[256,128]{1,0:T(8,128)(2,1)S(1)}, u32[]{:S(2)}, u32[]{:S(2)}) %collective-permute-start.6) | collective-permute-done | bytes 65568 | tf_op jit(solution)/shard_map/ppermute | solution.py:863
  95.2 1.8 %shard_map.172 = (bf16[2048,128]{1,0:T(8,128)(2,1)}, f32[12,128,128]{2,1,0:T(8,128)}) custom-call(f32[512,128]{1,0:T(8,128)} %get-tuple-element.94.refs_0_, bf16[256,128]{1,0:T(8,128)(2,1)S(1)} %collective-permute-done.5.refs_1_, bf16[256,128]{1,0:T(8,128)(2,1)S(1)} %collective-permute-done.6.refs_2_, ...), custom_call_target="tpu_custom_call", output_to_operand_aliasing={{0}: (4, {})} | custom-call | bytes 3000000 | tf_op jit(solution)/shard_map/pallas_call | solution.py:163
  (25 shorter events, 8.3 us)
Async XLA Ops:
  1.5 8.9 %collective-permute-start.1 = (bf16[256,128]{1,0:T(8,128)(2,1)S(1)}, bf16[256,128]{1,0:T(8,128)(2,1)S(1)}, u32[]{:S(2)}, u32[]{:S(2)}) collective-permute-start(bf16[256,128]{1,0:T(8,128)(2,1)S(1)} %get-tuple-element.102), channel_id=1, source_target_pairs={{1,2},{2,1},{3,4},{4,3},{5,6},{6,5},{7,8},{8,7},{9,10},{10,9},{11,... | collective-permute-start | bytes 196616 | tf_op jit(solution)/shard_map/ppermute | solution.py:685
  6.1 4.4 %collective-permute-start = (bf16[256,128]{1,0:T(8,128)(2,1)S(1)}, bf16[256,128]{1,0:T(8,128)(2,1)S(1)}, u32[]{:S(2)}, u32[]{:S(2)}) collective-permute-start(bf16[256,128]{1,0:T(8,128)(2,1)S(1)} %get-tuple-element.103), channel_id=1, source_target_pairs={{0,1},{1,0},{2,3},{3,2},{4,5},{5,4},{6,7},{7,6},{8,9},{9,8},{10,11... | collective-permute-start | bytes 196616 | tf_op jit(solution)/shard_map/ppermute | solution.py:684
  12.3 17.3 %all-to-all-start = ((bf16[16,96,128]{2,1,0:T(8,128)(2,1)}), bf16[16,96,128]{2,1,0:T(8,128)(2,1)S(1)}, u32[]{:S(2)}, u32[]{:S(2)}) async-start(bf16[16,96,128]{2,1,0:T(8,128)(2,1)} %get-tuple-element.61), calls=%async_computation | async-start | bytes 786432 | tf_op jit(solution)/shard_map/all_to_all | solution.py:644
  32.4 9.9 %all-to-all-start.1 = ((bf16[16,16,128]{2,1,0:T(8,128)(2,1)}), bf16[16,16,128]{2,1,0:T(8,128)(2,1)S(1)}, u32[]{:S(2)}, u32[]{:S(2)}) async-start(bf16[16,16,128]{2,1,0:T(8,128)(2,1)} %get-tuple-element.68), calls=%async_computation.1 | async-start | bytes 131072 | tf_op jit(solution)/shard_map/all_to_all | solution.py:644
  46.1 16.4 %all-to-all-start.2 = ((bf16[16,64,128]{2,1,0:T(8,128)(2,1)}), bf16[16,64,128]{2,1,0:T(8,128)(2,1)S(1)}, u32[]{:S(2)}, u32[]{:S(2)}) async-start(bf16[16,64,128]{2,1,0:T(8,128)(2,1)} %bitcast.13), calls=%async_computation.2 | async-start | bytes 524288 | tf_op jit(solution)/shard_map/all_to_all | solution.py:644
  52.3 1.4 %collective-permute-start.2 = (bf16[512,128]{1,0:T(8,128)(2,1)S(1)}, bf16[512,128]{1,0:T(8,128)(2,1)S(1)}, u32[]{:S(2)}, u32[]{:S(2)}) collective-permute-start(bf16[512,128]{1,0:T(8,128)(2,1)S(1)} %shard_map.165.refs_0_), channel_id=1, source_target_pairs={{0,1},{1,0},{2,3},{3,2},{4,5},{5,4},{6,7},{7,6},{8,9},{9,8},{10,11... | collective-permute-start | bytes 393224 | tf_op jit(solution)/shard_map/ppermute | solution.py:806
  53.8 5.5 %collective-permute-start.3 = (bf16[512,128]{1,0:T(8,128)(2,1)S(1)}, bf16[512,128]{1,0:T(8,128)(2,1)S(1)}, u32[]{:S(2)}, u32[]{:S(2)}) collective-permute-start(bf16[512,128]{1,0:T(8,128)(2,1)S(1)} %shard_map.166.refs_1_.refs_0_), channel_id=1, source_target_pairs={{0,2},{1,3},{2,0},{3,1},{4,6},{5,7},{6,4},{7,5},{8,10},{9,11},{10,... | collective-permute-start | bytes 393224 | tf_op jit(solution)/shard_map/ppermute | solution.py:806
  59.3 12.7 %collective-permute-start.4 = (bf16[512,128]{1,0:T(8,128)(2,1)S(1)}, bf16[512,128]{1,0:T(8,128)(2,1)S(1)}, u32[]{:S(2)}, u32[]{:S(2)}) collective-permute-start(bf16[512,128]{1,0:T(8,128)(2,1)S(1)} %shard_map.168.refs_11_.refs_0_), channel_id=1, source_target_pairs={{0,4},{1,5},{2,6},{3,7},{4,0},{5,1},{6,2},{7,3},{8,12},{9,13},{10,... | collective-permute-start | bytes 393224 | tf_op jit(solution)/shard_map/ppermute | solution.py:806
  67.0 16.7 %all-to-all-start.3 = ((bf16[16,32,128]{2,1,0:T(8,128)(2,1)}), bf16[16,32,128]{2,1,0:T(8,128)(2,1)S(1)}, u32[]{:S(2)}, u32[]{:S(2)}) async-start(bf16[16,32,128]{2,1,0:T(8,128)(2,1)} %bitcast.14), calls=%async_computation.3 | async-start | bytes 262144 | tf_op jit(solution)/shard_map/all_to_all | solution.py:644
  72.1 11.6 %collective-permute-start.7 = (bf16[512,128]{1,0:T(8,128)(2,1)S(1)}, bf16[512,128]{1,0:T(8,128)(2,1)S(1)}, u32[]{:S(2)}, u32[]{:S(2)}) collective-permute-start(bf16[512,128]{1,0:T(8,128)(2,1)S(1)} %shard_map.170.refs_5_.refs_0_), channel_id=1, source_target_pairs={{0,8},{1,9},{2,10},{3,11},{4,12},{5,13},{6,14},{7,15},{8,0},{9,1},... | collective-permute-start | bytes 393224 | tf_op jit(solution)/shard_map/ppermute | solution.py:806
  84.6 4.7 %copy-start.1 = (bf16[256,128]{1,0:T(8,128)(2,1)S(1)}, bf16[256,128]{1,0:T(8,128)(2,1)}, u32[]{:S(2)}) copy-start(bf16[256,128]{1,0:T(8,128)(2,1)} %get-tuple-element.96) | copy-start | bytes 196612
  84.6 8.2 %copy-start = (bf16[256,128]{1,0:T(8,128)(2,1)S(1)}, bf16[256,128]{1,0:T(8,128)(2,1)}, u32[]{:S(2)}) copy-start(bf16[256,128]{1,0:T(8,128)(2,1)} %get-tuple-element.95.refs_2_.refs_1_) | copy-start | bytes 196612
  84.6 12.4 %all-to-all-start.4 = ((bf16[16,32,128]{2,1,0:T(8,128)(2,1)}), bf16[16,32,128]{2,1,0:T(8,128)(2,1)S(1)}, u32[]{:S(2)}, u32[]{:S(2)}) async-start(bf16[16,32,128]{2,1,0:T(8,128)(2,1)} %shard_map.174), calls=%async_computation.4 | async-start | bytes 262144 | tf_op jit(solution)/shard_map/all_to_all | solution.py:644
  89.3 6.0 %collective-permute-start.6 = (bf16[256,128]{1,0:T(8,128)(2,1)S(1)}, bf16[256,128]{1,0:T(8,128)(2,1)S(1)}, u32[]{:S(2)}, u32[]{:S(2)}) collective-permute-start(bf16[256,128]{1,0:T(8,128)(2,1)S(1)} %copy-done.1), channel_id=1, source_target_pairs={{1,2},{2,1},{3,4},{4,3},{5,6},{6,5},{7,8},{8,7},{9,10},{10,9},{11,... | collective-permute-start | bytes 196616 | tf_op jit(solution)/shard_map/ppermute | solution.py:863
  92.8 2.4 %collective-permute-start.5 = (bf16[256,128]{1,0:T(8,128)(2,1)S(1)}, bf16[256,128]{1,0:T(8,128)(2,1)S(1)}, u32[]{:S(2)}, u32[]{:S(2)}) collective-permute-start(bf16[256,128]{1,0:T(8,128)(2,1)S(1)} %copy-done), channel_id=1, source_target_pairs={{0,1},{1,0},{2,3},{3,2},{4,5},{5,4},{6,7},{7,6},{8,9},{9,8},{10,11... | collective-permute-start | bytes 196616 | tf_op jit(solution)/shard_map/ppermute | solution.py:862

commit v11 on v10

--- a/solution.py
+++ b/solution.py
@@ -478,11 +478,11 @@
         s1 = 1.0 / (1.0 + jnp.exp(-first))
         middle = (first * s1).astype(BF)
         mid_ref[:, cols] = middle
-        sl1_ref[:, cols] = s1 * (1.0 + first * (1.0 - s1))
+        sl1_ref[:, cols] = (s1 * (1.0 + first * (1.0 - s1))).astype(BF)
         second = dot(w2t, middle)
         s2 = 1.0 / (1.0 + jnp.exp(-second))
         outer_ref[:, cols] = (second * s2).astype(BF)
-        sl2_ref[:, cols] = s2 * (1.0 + second * (1.0 - s2))
+        sl2_ref[:, cols] = (s2 * (1.0 + second * (1.0 - s2))).astype(BF)
     need()
     cot_ref[...] = jnp.transpose(fine_cot[...])
     for i in range(rows // TILE):
@@ -538,8 +538,8 @@
     io.start(g_ref, g_out)
     g = g_ref[...]
     need(4, 5, 6)
-    sg = (dot(w[3], g) * slope2[...]).astype(BF)
-    fg = (dot(w[2], sg) * slope1[...]).astype(BF)
+    sg = (dot(w[3], g) * slope2[...].astype(F32)).astype(BF)
+    fg = (dot(w[2], sg) * slope1[...].astype(F32)).astype(BF)
     fg_ref[...] = fg
     io.start(fg_ref, fg_out)
     need()
@@ -740,7 +740,7 @@
         ],
         [
             (shape((d, n)), "h"), (shape((d, n)), "h"), (shape((d, n)), "h"),
-            (shape((d, n), F32), "h"), (shape((d, n), F32), "h"), (shape((d, n)), "h"),
+            (shape((d, n)), "h"), (shape((d, n)), "h"), (shape((d, n)), "h"),
             (shape((n // TILE, per, TILE)), "h"),
         ],
         us=4,
@@ -801,6 +801,7 @@
         us=2,
     )
     reaches = [1 << i for i in range((peers - 1).bit_length())]
+    reaches = reaches[:1] + reaches[-1:] + reaches[1:-1]
 
     def double(total, reach, *after):
         other = lax.ppermute(total, "nodes", [(i, i ^ reach) for i in range(peers)])
@@ -808,7 +809,7 @@
         return call(add_kernel, ins, [(shape((4 * d, d)), "v")], us=1)[0]
 
     sums = [mid_wg]
-    for reach in reaches[:3]:
+    for reach in reaches[:2]:
         sums.append(double(sums[-1], reach))
     (pick,) = call(
         functools.partial(pick_kernel, block_rows),
@@ -821,7 +822,7 @@
         [
             (got3.reshape(peers * chunk, d), "v"), (pick, pick_kind), (cot, "h"), (pool_b, "h"),
             (weights, "0"), (slope2, "h"), (slope1, "h"), (hid, "h"), (agg, "h"), (mid, "h"),
-            (outer, "h"), (sums[2], "v"),
+            (outer, "h"), (sums[1], "v"),
         ],
         [(shape((4 * d, d)), "h"), (shape((d, n)), "r"), (shape((d, n)), "r")],
         scratch=(pltpu.VMEM((d, n), BF), pltpu.VMEM((d, n), BF)),
@@ -833,7 +834,7 @@
         fine_spread_kernel,
         [
             (fine_offsets, "h"), (fine_edge_w, "h"), (weights, "0"), (g, "h"), (fg, "h"),
-            (sums[3], "v"),
+            (sums[2], "v"),
         ],
         [
             (shape((HALO, d)), "h"), (shape((HALO, d)), "h"), (shape((2 * HALO, d), F32), "h"),
@@ -847,17 +848,17 @@
         copies=1,
         us=5,
     )
-    sums.append(double(sums[3], reaches[3], rim_near))
+    sums.append(double(sums[2], reaches[2], rim_near))
     (send5,) = call(
         sum_kernel,
-        [(got4, "v"), (rim_near, "r"), (sums[4], "v")],
+        [(got4, "v"), (rim_near, "r"), (sums[3], "v")],
         [(shape((peers, 4 * d // peers, d)), "r")],
         scratch=(pltpu.VMEM((4 * d // peers, d), BF),),
         copies=peers,
         us=1,
     )
     got5 = exchange(send5)
-    for reach in reaches[4:]:
+    for reach in reaches[3:]:
         sums.append(double(sums[-1], reach))
     from_across = lax.ppermute(rim_near, "nodes", inside_pairs)
     from_beside = lax.ppermute(rim_far, "nodes", between_pairs)

time: 99.1 us -> 94.9 us (0.958)
  waiting for transfers between devices: 20.7 us -> 15.8 us
  starting transfers between devices: 37.9 us -> 39.3 us
    ppermute x4, waiting for transfers between devices: 9.89 us -> 1.28 us  [double(): other = lax.ppermute(total, 'nodes', [(i, i ^ reach) for i in range(peers)])]
    all_to_all x5, waiting for transfers between devices: 8.47 us -> 12.2 us  [exchange(): return lax.all_to_all(x, 'nodes', split_axis=0, concat_axis=0, tiled=True)]
    all_to_all x5, starting transfers between devices: 23.2 us -> 25.5 us  [exchange(): return lax.all_to_all(x, 'nodes', split_axis=0, concat_axis=0, tiled=True)]
  transfers between devices with their start and end apart: 13 -> 13, of which waited for: 6 -> 7; matrix products, arithmetic and copies ran while one was open for 0% -> 0% of each run, Pallas kernels for 28% -> 29%
where the time goes in v11:
time: 94.9 us; the launch traced here: 94 us
  starting transfers between devices  39.3 us (41%)
  Pallas kernels  37 us (39%)
  waiting for transfers between devices  15.8 us (17%)
  between operations  1.02 us (1%)
    pallas_call x18, Pallas kernels, call(): pl.pallas_call(body, out_shape=[s if kind == 'v' else pltpu.HBM(s.shape,...  37 us
    all_to_all x5, starting transfers between devices, exchange(): return lax.all_to_all(x, 'nodes', split_axis=0, concat_axis=0, tiled=True)  25.5 us
    all_to_all x5, waiting for transfers between devices, exchange(): return lax.all_to_all(x, 'nodes', split_axis=0, concat_axis=0, tiled=True)  12.2 us
    ppermute x4, starting transfers between devices, double(): other = lax.ppermute(total, 'nodes', [(i, i ^ reach) for i in range(peers)])  5.52 us
    ppermute x1, starting transfers between devices, per_device(): beside = lax.ppermute(far, 'nodes', between_pairs)  4.54 us
    ppermute x1, starting transfers between devices, per_device(): from_beside = lax.ppermute(rim_far, 'nodes', between_pairs)  3.61 us
    ppermute x1, waiting for transfers between devices, per_device(): from_beside = lax.ppermute(rim_far, 'nodes', between_pairs)  2.39 us
  transfers between devices with their start and end apart: 13, of which 7 were waited for; matrix products, arithmetic and copies ran while one was open for 0% of the time, Pallas kernels for 29%

profile of v11, /device:TPU:1, one launch (start us, length us, event | category | flops | bytes accessed | tf_op | source)
XLA Modules:
  0.0 94.0 jit_solution(8634803651047265061)
XLA Ops:
  1.5 4.5 %collective-permute-start.1 = (bf16[256,128]{1,0:T(8,128)(2,1)S(1)}, bf16[256,128]{1,0:T(8,128)(2,1)S(1)}, u32[]{:S(2)}, u32[]{:S(2)}) collective-permute-start(bf16[256,128]{1,0:T(8,128)(2,1)S(1)} %get-tuple-element.102), channel_id=1, source_target_pairs={{1,2},{2,1},{3,4},{4,3},{5,6},{6,5},{7,8},{8,7},{9,10},{10,9},{11,... | collective-permute-start | bytes 196616 | tf_op jit(solution)/shard_map/ppermute | solution.py:685
  6.2 4.3 %shard_map.158 = (bf16[2,768,256]{2,1,0:T(8,128)(2,1)S(1)}, bf16[2,128,512]{2,1,0:T(8,128)(2,1)S(1)}, bf16[128,256]{1,0:T(8,128)(2,1)S(1)}, bf16[128,128]{1,0:T(...) custom-call(s32[8,2048]{1,0:T(8,128)} %refs_0_.7, ...), custom_call_target="tpu_custom_call" | custom-call | bytes 18000000 | tf_op jit(solution)/shard_map/pallas_call | solution.py:163
  10.5 1.8 %shard_map.159 = (bf16[16,96,128]{2,1,0:T(8,128)(2,1)}, bf16[128,2048]{1,0:T(8,128)(2,1)}) custom-call(bf16[256,128]{1,0:T(8,128)(2,1)S(1)} %collective-permute-done.refs_0_, bf16[256,128]{1,0:T(8,128)(2,1)S(1)} %collective-permute-done.1.refs_1_, bf16[2,768,256]{2,1,0:T(8,128)(2,1)S(1)} %get-tuple-element.52.refs_2_, ...), custom_call_target="tpu_custom_call" | custom-call | bytes 9000000 | tf_op jit(solution)/shard_map/pallas_call | solution.py:163
  12.3 5.4 %all-to-all-start = ((bf16[16,96,128]{2,1,0:T(8,128)(2,1)}), bf16[16,96,128]{2,1,0:T(8,128)(2,1)S(1)}, u32[]{:S(2)}, u32[]{:S(2)}) async-start(bf16[16,96,128]{2,1,0:T(8,128)(2,1)} %get-tuple-element.61), calls=%async_computation | async-start | bytes 786432 | tf_op jit(solution)/shard_map/all_to_all | solution.py:644
  17.7 2.0 %shard_map.160 = (bf16[512,512]{1,0:T(8,128)(2,1)}, bf16[128,256]{1,0:T(8,128)(2,1)}, bf16[128,128]{1,0:T(8,128)(2,1)}, bf16[128,128]{1,0:T(8,128)(2,1)}) custom-call(s32[8,512]{1,0:T(8,128)} %refs_0_.5, f32[8,512]{1,0:T(8,128)} %refs_1_.4, bf16[3,4,128,128]{3,2,1,0:T(8,128)(2,1)} %refs_2_.7, bf16[128,2048]{1,0:T(8,128)(2,1)} %get-tuple-element.62.refs_3_.refs_1_.refs_8_), custom_call_target="tpu_custom_call" | custom-call | bytes 18000000 | tf_op jit(solution)/shard_map/pallas_call | solution.py:163
  19.6 4.4 %shard_map.161 = (bf16[128,2048]{1,0:T(8,128)(2,1)}, bf16[128,2048]{1,0:T(8,128)(2,1)}, bf16[128,2048]{1,0:T(8,128)(2,1)}, bf16[128,2048]{1,0:T(8,128)(2,1)}, bf...) custom-call(bf16[2048,128]{1,0:T(8,128)(2,1)} %refs_0_.6, ...), custom_call_target="tpu_custom_call" | custom-call | bytes 12000000 | tf_op jit(solution)/shard_map/pallas_call | solution.py:163
  24.1 5.5 %all-to-all-done.refs_0_ = bf16[16,96,128]{2,1,0:T(8,128)(2,1)S(1)} async-done(((bf16[16,96,128]{2,1,0:T(8,128)(2,1)}), bf16[16,96,128]{2,1,0:T(8,128)(2,1)S(1)}, u32[]{:S(2)}, u32[]{:S(2)}) %all-to-all-start) | async-done | bytes 393248 | tf_op jit(solution)/shard_map/all_to_all | solution.py:644
  29.6 2.9 %shard_map.162 = (bf16[16,16,128]{2,1,0:T(8,128)(2,1)}, bf16[128,512]{1,0:T(8,128)(2,1)}, bf16[128,512]{1,0:T(8,128)(2,1)}, bf16[1024,512]{1,0:T(8,128)(2,1)}, bf16[16,32,128]{2,1,0:T(8,128)(2,1)}) custom-call(bf16[16,96,128]{2,1,0:T(8,128)(2,1)S(1)} %all-to-all-done.refs_0_, bf16[512,512]{1,0:T(8,128)(2,1)} %get-tuple-element.63.refs_1_.refs_13_, ...), custom_call_target="tpu_custom_call" | custom-call | bytes 9000000 | tf_op jit(solution)/shard_map/pallas_call | solution.py:163
  32.4 3.8 %all-to-all-start.1 = ((bf16[16,16,128]{2,1,0:T(8,128)(2,1)}), bf16[16,16,128]{2,1,0:T(8,128)(2,1)S(1)}, u32[]{:S(2)}, u32[]{:S(2)}) async-start(bf16[16,16,128]{2,1,0:T(8,128)(2,1)} %get-tuple-element.68), calls=%async_computation.1 | async-start | bytes 131072 | tf_op jit(solution)/shard_map/all_to_all | solution.py:644
  36.3 2.8 %shard_map.163 = (bf16[256,256]{1,0:T(8,128)(2,1)S(1)}, bf16[128,256]{1,0:T(8,128)(2,1)S(1)}, f32[128,256]{1,0:T(8,128)S(1)}, bf16[128,256]{1,0:T(8,128)(2,1)S(1...) custom-call(bf16[16,32,128]{2,1,0:T(8,128)(2,1)} %get-tuple-element.69.ref, ...), custom_call_target="tpu_custom_call" | custom-call | bytes 18000000 | tf_op jit(solution)/shard_map/pallas_call | solution.py:163
  39.1 3.2 %all-to-all-done.1 = bf16[16,16,128]{2,1,0:T(8,128)(2,1)S(1)} async-done(((bf16[16,16,128]{2,1,0:T(8,128)(2,1)}), bf16[16,16,128]{2,1,0:T(8,128)(2,1)S(1)}, u32[]{:S(2)}, u32[]{:S(2)}) %all-to-all-start.1) | async-done | bytes 65568 | tf_op jit(solution)/shard_map/all_to_all | solution.py:644
  42.3 3.8 %shard_map.164 = (bf16[1024,128]{1,0:T(8,128)(2,1)}, bf16[128,512]{1,0:T(8,128)(2,1)}, bf16[128,512]{1,0:T(8,128)(2,1)}, bf16[128,512]{1,0:T(8,128)(2,1)}, f32[4,128,128]{2,1,0:T(8,128)}) custom-call(bf16[256,128]{1,0:T(8,128)(2,1)S(1)} %bitcast.11, bf16[256,256]{1,0:T(8,128)(2,1)S(1)} %get-tuple-element.72.refs_1_, ...), custom_call_target="tpu_custom_call" | custom-call | bytes 9000000 | tf_op jit(solution)/shard_map/pallas_call | solution.py:163
  46.1 4.3 %all-to-all-start.2 = ((bf16[16,64,128]{2,1,0:T(8,128)(2,1)}), bf16[16,64,128]{2,1,0:T(8,128)(2,1)S(1)}, u32[]{:S(2)}, u32[]{:S(2)}) async-start(bf16[16,64,128]{2,1,0:T(8,128)(2,1)} %bitcast.13), calls=%async_computation.2 | async-start | bytes 524288 | tf_op jit(solution)/shard_map/all_to_all | solution.py:644
  50.4 1.9 %shard_map.165.refs_0_ = bf16[512,128]{1,0:T(8,128)(2,1)S(1)} custom-call(bf16[128,512]{1,0:T(8,128)(2,1)} %get-tuple-element.70.refs_1_.refs_0_, bf16[128,512]{1,0:T(8,128)(2,1)} %get-tuple-element.71.refs_2_.refs_1_, bf16[128,512]{1,0:T(8,128)(2,1)} %get-tuple-element.83.refs_2_, bf16[128,512]{1,0:T(8,128)(2,1)} %get-tuple-element.84.refs_3_, ...), custom_call_target="tpu_custom_call" | custom-call | bytes 6000000 | tf_op jit(solution)/shard_map/pallas_call | solution.py:163
  53.8 2.4 %collective-permute-start.3 = (bf16[512,128]{1,0:T(8,128)(2,1)S(1)}, bf16[512,128]{1,0:T(8,128)(2,1)S(1)}, u32[]{:S(2)}, u32[]{:S(2)}) collective-permute-start(bf16[512,128]{1,0:T(8,128)(2,1)S(1)} %shard_map.166.refs_1_.refs_11_.refs_0_), channel_id=1, source_target_pairs={{0,8},{1,9},{2,10},{3,11},{4,12},{5,13},{6,14},{7,15},{8,0},{9,1},... | collective-permute-start | bytes 393224 | tf_op jit(solution)/shard_map/ppermute | solution.py:807
  57.0 2.9 %all-to-all-done.2 = bf16[16,64,128]{2,1,0:T(8,128)(2,1)S(1)} async-done(((bf16[16,64,128]{2,1,0:T(8,128)(2,1)}), bf16[16,64,128]{2,1,0:T(8,128)(2,1)S(1)}, u32[]{:S(2)}, u32[]{:S(2)}) %all-to-all-start.2) | async-done | bytes 262176 | tf_op jit(solution)/shard_map/all_to_all | solution.py:644
  59.9 4.1 %shard_map.168 = (bf16[512,128]{1,0:T(8,128)(2,1)}, bf16[128,2048]{1,0:T(8,128)(2,1)}, bf16[128,2048]{1,0:T(8,128)(2,1)}) custom-call(bf16[1024,128]{1,0:T(8,128)(2,1)S(1)} %bitcast.8, bf16[512,1024]{1,0:T(8,128)(2,1)S(1)} %shard_map.167.refs_1_, bf16[128,2048]{1,0:T(8,128)(2,1)} %get-tuple-element.86.refs_2_, ...), custom_call_target="tpu_custom_call" | custom-call | bytes 12000000 | tf_op jit(solution)/shard_map/pallas_call | solution.py:163
  64.0 6.4 %all-to-all-start.3 = ((bf16[16,32,128]{2,1,0:T(8,128)(2,1)}), bf16[16,32,128]{2,1,0:T(8,128)(2,1)S(1)}, u32[]{:S(2)}, u32[]{:S(2)}) async-start(bf16[16,32,128]{2,1,0:T(8,128)(2,1)} %bitcast.14), calls=%async_computation.3 | async-start | bytes 262144 | tf_op jit(solution)/shard_map/all_to_all | solution.py:644
  70.5 1.5 %collective-permute-start.6 = (bf16[512,128]{1,0:T(8,128)(2,1)S(1)}, bf16[512,128]{1,0:T(8,128)(2,1)S(1)}, u32[]{:S(2)}, u32[]{:S(2)}) collective-permute-start(bf16[512,128]{1,0:T(8,128)(2,1)S(1)} %shard_map.169.refs_5_.refs_0_), channel_id=1, source_target_pairs={{0,2},{1,3},{2,0},{3,1},{4,6},{5,7},{6,4},{7,5},{8,10},{9,11},{10,... | collective-permute-start | bytes 393224 | tf_op jit(solution)/shard_map/ppermute | solution.py:807
  71.9 4.6 %shard_map.170 = (bf16[256,128]{1,0:T(8,128)(2,1)}, bf16[256,128]{1,0:T(8,128)(2,1)}, f32[512,128]{1,0:T(8,128)}, bf16[2048,128]{1,0:T(8,128)(2,1)}) custom-call(s32[8,2048]{1,0:T(8,128)} %refs_0_.7, f32[8,2048]{1,0:T(8,128)} %refs_1_.5, bf16[3,4,128,128]{3,2,1,0:T(8,128)(2,1)} %refs_2_.7, bf16[128,2048]{1,0:T(8,128)(2,1)} %get-tuple-element.92.refs_3_, ...), custom_call_target="tpu_custom_call" | custom-call | bytes 15000000 | tf_op jit(solution)/shard_map/pallas_call | solution.py:163
  78.2 5.6 %all-to-all-start.4 = ((bf16[16,32,128]{2,1,0:T(8,128)(2,1)}), bf16[16,32,128]{2,1,0:T(8,128)(2,1)S(1)}, u32[]{:S(2)}, u32[]{:S(2)}) async-start(bf16[16,32,128]{2,1,0:T(8,128)(2,1)} %shard_map.173), calls=%async_computation.4 | async-start | bytes 262144 | tf_op jit(solution)/shard_map/all_to_all | solution.py:644
  85.1 3.6 %collective-permute-start.5 = (bf16[256,128]{1,0:T(8,128)(2,1)S(1)}, bf16[256,128]{1,0:T(8,128)(2,1)S(1)}, u32[]{:S(2)}, u32[]{:S(2)}) collective-permute-start(bf16[256,128]{1,0:T(8,128)(2,1)S(1)} %copy-done.1), channel_id=1, source_target_pairs={{1,2},{2,1},{3,4},{4,3},{5,6},{6,5},{7,8},{8,7},{9,10},{10,9},{11,... | collective-permute-start | bytes 196616 | tf_op jit(solution)/shard_map/ppermute | solution.py:864
  88.8 2.4 %collective-permute-done.5.refs_2_ = bf16[256,128]{1,0:T(8,128)(2,1)S(1)} collective-permute-done((bf16[256,128]{1,0:T(8,128)(2,1)S(1)}, bf16[256,128]{1,0:T(8,128)(2,1)S(1)}, u32[]{:S(2)}, u32[]{:S(2)}) %collective-permute-start.5) | collective-permute-done | bytes 65568 | tf_op jit(solution)/shard_map/ppermute | solution.py:864
  91.2 1.8 %shard_map.171 = (bf16[2048,128]{1,0:T(8,128)(2,1)}, f32[12,128,128]{2,1,0:T(8,128)}) custom-call(f32[512,128]{1,0:T(8,128)} %get-tuple-element.94.refs_0_, bf16[256,128]{1,0:T(8,128)(2,1)S(1)} %collective-permute-done.4.refs_1_, bf16[256,128]{1,0:T(8,128)(2,1)S(1)} %collective-permute-done.5.refs_2_, ...), custom_call_target="tpu_custom_call", output_to_operand_aliasing={{0}: (4, {})} | custom-call | bytes 3000000 | tf_op jit(solution)/shard_map/pallas_call | solution.py:163
  (25 shorter events, 7.2 us)
Async XLA Ops:
  1.5 8.9 %collective-permute-start.1 = (bf16[256,128]{1,0:T(8,128)(2,1)S(1)}, bf16[256,128]{1,0:T(8,128)(2,1)S(1)}, u32[]{:S(2)}, u32[]{:S(2)}) collective-permute-start(bf16[256,128]{1,0:T(8,128)(2,1)S(1)} %get-tuple-element.102), channel_id=1, source_target_pairs={{1,2},{2,1},{3,4},{4,3},{5,6},{6,5},{7,8},{8,7},{9,10},{10,9},{11,... | collective-permute-start | bytes 196616 | tf_op jit(solution)/shard_map/ppermute | solution.py:685
  6.1 4.4 %collective-permute-start = (bf16[256,128]{1,0:T(8,128)(2,1)S(1)}, bf16[256,128]{1,0:T(8,128)(2,1)S(1)}, u32[]{:S(2)}, u32[]{:S(2)}) collective-permute-start(bf16[256,128]{1,0:T(8,128)(2,1)S(1)} %get-tuple-element.103), channel_id=1, source_target_pairs={{0,1},{1,0},{2,3},{3,2},{4,5},{5,4},{6,7},{7,6},{8,9},{9,8},{10,11... | collective-permute-start | bytes 196616 | tf_op jit(solution)/shard_map/ppermute | solution.py:684
  12.3 17.3 %all-to-all-start = ((bf16[16,96,128]{2,1,0:T(8,128)(2,1)}), bf16[16,96,128]{2,1,0:T(8,128)(2,1)S(1)}, u32[]{:S(2)}, u32[]{:S(2)}) async-start(bf16[16,96,128]{2,1,0:T(8,128)(2,1)} %get-tuple-element.61), calls=%async_computation | async-start | bytes 786432 | tf_op jit(solution)/shard_map/all_to_all | solution.py:644
  32.4 9.9 %all-to-all-start.1 = ((bf16[16,16,128]{2,1,0:T(8,128)(2,1)}), bf16[16,16,128]{2,1,0:T(8,128)(2,1)S(1)}, u32[]{:S(2)}, u32[]{:S(2)}) async-start(bf16[16,16,128]{2,1,0:T(8,128)(2,1)} %get-tuple-element.68), calls=%async_computation.1 | async-start | bytes 131072 | tf_op jit(solution)/shard_map/all_to_all | solution.py:644
  46.1 13.7 %all-to-all-start.2 = ((bf16[16,64,128]{2,1,0:T(8,128)(2,1)}), bf16[16,64,128]{2,1,0:T(8,128)(2,1)S(1)}, u32[]{:S(2)}, u32[]{:S(2)}) async-start(bf16[16,64,128]{2,1,0:T(8,128)(2,1)} %bitcast.13), calls=%async_computation.2 | async-start | bytes 524288 | tf_op jit(solution)/shard_map/all_to_all | solution.py:644
  52.3 1.4 %collective-permute-start.2 = (bf16[512,128]{1,0:T(8,128)(2,1)S(1)}, bf16[512,128]{1,0:T(8,128)(2,1)S(1)}, u32[]{:S(2)}, u32[]{:S(2)}) collective-permute-start(bf16[512,128]{1,0:T(8,128)(2,1)S(1)} %shard_map.165.refs_0_), channel_id=1, source_target_pairs={{0,1},{1,0},{2,3},{3,2},{4,5},{5,4},{6,7},{7,6},{8,9},{9,8},{10,11... | collective-permute-start | bytes 393224 | tf_op jit(solution)/shard_map/ppermute | solution.py:807
  53.8 16.7 %collective-permute-start.3 = (bf16[512,128]{1,0:T(8,128)(2,1)S(1)}, bf16[512,128]{1,0:T(8,128)(2,1)S(1)}, u32[]{:S(2)}, u32[]{:S(2)}) collective-permute-start(bf16[512,128]{1,0:T(8,128)(2,1)S(1)} %shard_map.166.refs_1_.refs_11_.refs_0_), channel_id=1, source_target_pairs={{0,8},{1,9},{2,10},{3,11},{4,12},{5,13},{6,14},{7,15},{8,0},{9,1},... | collective-permute-start | bytes 393224 | tf_op jit(solution)/shard_map/ppermute | solution.py:807
  64.0 13.3 %all-to-all-start.3 = ((bf16[16,32,128]{2,1,0:T(8,128)(2,1)}), bf16[16,32,128]{2,1,0:T(8,128)(2,1)S(1)}, u32[]{:S(2)}, u32[]{:S(2)}) async-start(bf16[16,32,128]{2,1,0:T(8,128)(2,1)} %bitcast.14), calls=%async_computation.3 | async-start | bytes 262144 | tf_op jit(solution)/shard_map/all_to_all | solution.py:644
  70.5 6.2 %collective-permute-start.6 = (bf16[512,128]{1,0:T(8,128)(2,1)S(1)}, bf16[512,128]{1,0:T(8,128)(2,1)S(1)}, u32[]{:S(2)}, u32[]{:S(2)}) collective-permute-start(bf16[512,128]{1,0:T(8,128)(2,1)S(1)} %shard_map.169.refs_5_.refs_0_), channel_id=1, source_target_pairs={{0,2},{1,3},{2,0},{3,1},{4,6},{5,7},{6,4},{7,5},{8,10},{9,11},{10,... | collective-permute-start | bytes 393224 | tf_op jit(solution)/shard_map/ppermute | solution.py:807
  78.1 7.0 %copy-start.1 = (bf16[256,128]{1,0:T(8,128)(2,1)S(1)}, bf16[256,128]{1,0:T(8,128)(2,1)}, u32[]{:S(2)}) copy-start(bf16[256,128]{1,0:T(8,128)(2,1)} %get-tuple-element.96) | copy-start | bytes 196612
  78.1 10.6 %copy-start = (bf16[256,128]{1,0:T(8,128)(2,1)S(1)}, bf16[256,128]{1,0:T(8,128)(2,1)}, u32[]{:S(2)}) copy-start(bf16[256,128]{1,0:T(8,128)(2,1)} %get-tuple-element.95.refs_2_.refs_1_) | copy-start | bytes 196612
  78.2 14.9 %all-to-all-start.4 = ((bf16[16,32,128]{2,1,0:T(8,128)(2,1)}), bf16[16,32,128]{2,1,0:T(8,128)(2,1)S(1)}, u32[]{:S(2)}, u32[]{:S(2)}) async-start(bf16[16,32,128]{2,1,0:T(8,128)(2,1)} %shard_map.173), calls=%async_computation.4 | async-start | bytes 262144 | tf_op jit(solution)/shard_map/all_to_all | solution.py:644
  83.7 9.3 %collective-permute-start.7 = (bf16[512,128]{1,0:T(8,128)(2,1)S(1)}, bf16[512,128]{1,0:T(8,128)(2,1)S(1)}, u32[]{:S(2)}, u32[]{:S(2)}) collective-permute-start(bf16[512,128]{1,0:T(8,128)(2,1)S(1)} %shard_map.172.refs_2_.refs_0_), channel_id=1, source_target_pairs={{0,4},{1,5},{2,6},{3,7},{4,0},{5,1},{6,2},{7,3},{8,12},{9,13},{10,... | collective-permute-start | bytes 393224 | tf_op jit(solution)/shard_map/ppermute | solution.py:807
  85.1 6.1 %collective-permute-start.5 = (bf16[256,128]{1,0:T(8,128)(2,1)S(1)}, bf16[256,128]{1,0:T(8,128)(2,1)S(1)}, u32[]{:S(2)}, u32[]{:S(2)}) collective-permute-start(bf16[256,128]{1,0:T(8,128)(2,1)S(1)} %copy-done.1), channel_id=1, source_target_pairs={{1,2},{2,1},{3,4},{4,3},{5,6},{6,5},{7,8},{8,7},{9,10},{10,9},{11,... | collective-permute-start | bytes 196616 | tf_op jit(solution)/shard_map/ppermute | solution.py:864
  88.7 2.5 %collective-permute-start.4 = (bf16[256,128]{1,0:T(8,128)(2,1)S(1)}, bf16[256,128]{1,0:T(8,128)(2,1)S(1)}, u32[]{:S(2)}, u32[]{:S(2)}) collective-permute-start(bf16[256,128]{1,0:T(8,128)(2,1)S(1)} %copy-done), channel_id=1, source_target_pairs={{0,1},{1,0},{2,3},{3,2},{4,5},{5,4},{6,7},{7,6},{8,9},{9,8},{10,11... | collective-permute-start | bytes 196616 | tf_op jit(solution)/shard_map/ppermute | solution.py:863

commit v12 on v11

--- a/solution.py
+++ b/solution.py
@@ -331,7 +331,7 @@
 
 
 def mid_kernel(block_rows, chunk, io, need, flush, ins, outs, blocks, coarse):
-    got, smid, w01, w2t, w3t, pool_mid, _ = ins
+    got, smid, w01, w2t, w3, pool_mid, _ = ins
     send_ref, hid_ref, agg_ref, sel_ref, ext_ref = outs
     peers = got.shape[0]
     nodes = smid.shape[0]
@@ -357,8 +357,8 @@
     flush(1, 2)
     middle = silu(dot(w01[...], jnp.concatenate([hidden, agg], axis=0))).astype(BF)
     outer = silu(dot(w2t[...], middle)).astype(BF)
-    mid_out = (hidden.astype(F32) + dot(w3t[...], outer)).astype(BF)
-    coarse[...] = dot_nt(pool_mid[...], mid_out).astype(BF)
+    pooled = dot_nt(pool_mid[...], outer).astype(BF)
+    coarse[...] = (dot_nt(pool_mid[...], hidden) + dot(pooled, w3[3])).astype(BF)
     for p in range(peers):
         io.start(coarse, send_ref.at[p])
 
@@ -517,18 +517,14 @@
         ).astype(BF)
 
 
-def add_kernel(io, need, flush, ins, outs):
-    mine, other = ins[:2]
-    outs[0][...] = (mine[...].astype(F32) + other[...].astype(F32)).astype(BF)
-
-
 def fine_grad_kernel(scale, io, need, flush, ins, outs, g_ref, fg_ref):
-    got, pick, cot, pool, w, slope2, slope1, hid, agg, mid, outer, _ = ins
+    got, pick, cot, pool, w, slope2, slope1, hid, agg, mid, outer, mid_wg = ins
     send_ref, g_out, fg_out = outs
     d, rows = hid.shape
     if pick.shape[1] > 1024:
         need(1)
     blocks = dot(pick[...], got[...]).astype(BF)
+    send_ref[4 * d : 8 * d, :] = mid_wg[...]
     need(2, 3)
     per = pool.shape[1]
     for i in range(rows // TILE):
@@ -550,7 +546,7 @@
 
 
 def fine_spread_kernel(io, need, flush, ins, outs, band, spill, inner):
-    off, ew, w, g, fg, _ = ins
+    off, ew, w, g, fg = ins
     rim_near, rim_far, edge_ref, out_ref = outs
     d, rows = g.shape
     tiles = rows // TILE
@@ -635,7 +631,7 @@
 def gather_kernel(io, need, flush, ins, outs, wide):
     out_ref = outs[0]
     for half in range(2):
-        wide[4 * half : 4 * half + 4] = ins[half][...].astype(F32)
+        wide[4 * half : 4 * half + 4] = ins[0][4 * half : 4 * half + 4].astype(F32)
         part = pl.ds(4 * half, 4)
         io.start(wide.at[part], out_ref.at[part])
 
@@ -748,7 +744,7 @@
     send2, mhid, magg, sel, ext = call(
         functools.partial(mid_kernel, block_rows, chunk),
         [
-            (got1, "v"), (smid, "h"), (m01, "h"), (m2t, "h"), (m3t, "h"), (pool_mid, "h"),
+            (got1, "v"), (smid, "h"), (m01, "h"), (m2t, "h"), (weights, "1"), (pool_mid, "h"),
             (pool_b, "r"),
         ],
         [
@@ -800,20 +796,9 @@
         [(shape((4 * d, d)), "v")],
         us=2,
     )
-    reaches = [1 << i for i in range((peers - 1).bit_length())]
-    reaches = reaches[:1] + reaches[-1:] + reaches[1:-1]
-
-    def double(total, reach, *after):
-        other = lax.ppermute(total, "nodes", [(i, i ^ reach) for i in range(peers)])
-        ins = [(total, "v"), (other, "v")] + [(x, "r") for x in after]
-        return call(add_kernel, ins, [(shape((4 * d, d)), "v")], us=1)[0]
-
-    sums = [mid_wg]
-    for reach in reaches[:2]:
-        sums.append(double(sums[-1], reach))
     (pick,) = call(
         functools.partial(pick_kernel, block_rows),
-        [(place, "s"), (sums[1], "v")],
+        [(place, "s"), (mid_wg, "v")],
         [(shape((tile_count * block_rows, peers * chunk)), pick_kind)],
         us=1,
     )
@@ -822,19 +807,18 @@
         [
             (got3.reshape(peers * chunk, d), "v"), (pick, pick_kind), (cot, "h"), (pool_b, "h"),
             (weights, "0"), (slope2, "h"), (slope1, "h"), (hid, "h"), (agg, "h"), (mid, "h"),
-            (outer, "h"), (sums[1], "v"),
-        ],
-        [(shape((4 * d, d)), "h"), (shape((d, n)), "r"), (shape((d, n)), "r")],
+            (outer, "h"), (mid_wg, "v"),
+        ],
+        [(shape((8 * d, d)), "h"), (shape((d, n)), "r"), (shape((d, n)), "r")],
         scratch=(pltpu.VMEM((d, n), BF), pltpu.VMEM((d, n), BF)),
         copies=2,
         us=4,
     )
-    got4 = exchange(send4.reshape(peers, 4 * d // peers, d))
+    got4 = exchange(send4.reshape(peers, 8 * d // peers, d))
     rim_near, rim_far, edge_sums, inner_grads = call(
         fine_spread_kernel,
         [
             (fine_offsets, "h"), (fine_edge_w, "h"), (weights, "0"), (g, "h"), (fg, "h"),
-            (sums[2], "v"),
         ],
         [
             (shape((HALO, d)), "h"), (shape((HALO, d)), "h"), (shape((2 * HALO, d), F32), "h"),
@@ -848,18 +832,15 @@
         copies=1,
         us=5,
     )
-    sums.append(double(sums[2], reaches[2], rim_near))
     (send5,) = call(
         sum_kernel,
-        [(got4, "v"), (rim_near, "r"), (sums[3], "v")],
-        [(shape((peers, 4 * d // peers, d)), "r")],
-        scratch=(pltpu.VMEM((4 * d // peers, d), BF),),
+        [(got4, "v"), (rim_near, "r")],
+        [(shape((peers, 8 * d // peers, d)), "r")],
+        scratch=(pltpu.VMEM((8 * d // peers, d), BF),),
         copies=peers,
         us=1,
     )
     got5 = exchange(send5)
-    for reach in reaches[3:]:
-        sums.append(double(sums[-1], reach))
     from_across = lax.ppermute(rim_near, "nodes", inside_pairs)
     from_beside = lax.ppermute(rim_far, "nodes", between_pairs)
     feature_grads, weight_grads = call(
@@ -877,12 +858,12 @@
     (weight_grads,) = call(
         gather_kernel,
         [
-            (got5.reshape(4, d, d), "v"), (sums[-1].reshape(4, d, d), "v"), (weight_grads, "r"),
+            (got5.reshape(8, d, d), "v"), (weight_grads, "r"),
         ],
         [(shape((12, d, d), F32), "r")],
         scratch=(pltpu.VMEM((8, d, d), F32),),
         copies=2,
-        aliases={2: 0},
+        aliases={1: 0},
         us=1,
     )
     weight_grads = weight_grads.reshape(3, 4, d, d)

time: 94.9 us -> 94.8 us (level)
  starting transfers between devices: 39.3 us -> 29.9 us
  waiting for transfers between devices: 15.8 us -> 24.6 us
    all_to_all x5, waiting for transfers between devices: 12.2 us -> 22 us  [exchange(): return lax.all_to_all(x, 'nodes', split_axis=0, concat_axis=0, tiled=True)]
    ppermute x4 -> x0, starting transfers between devices: 5.52 us -> none  [double(): other = lax.ppermute(total, 'nodes', [(i, i ^ reach) for i in range(peers)])]
    all_to_all x5, starting transfers between devices: 25.5 us -> 21.6 us  [exchange(): return lax.all_to_all(x, 'nodes', split_axis=0, concat_axis=0, tiled=True)]
    ppermute x4 -> x0, waiting for transfers between devices: 1.28 us -> none  [double(): other = lax.ppermute(total, 'nodes', [(i, i ^ reach) for i in range(peers)])]
    pallas_call x18 -> x14, Pallas kernels: 37 us -> 37 us  [call(): pl.pallas_call(body, out_shape=[s if kind == 'v' else pltpu.HBM(s.shape,...]
  transfers between devices with their start and end apart: 13 -> 9, of which waited for: 7 -> 6; matrix products, arithmetic and copies ran while one was open for 0% -> 0% of each run, Pallas kernels for 29% -> 24%
where the time goes in v12:
time: 94.8 us; the launch traced here: 93.3 us
  Pallas kernels  37 us (39%)
  starting transfers between devices  29.9 us (32%)
  waiting for transfers between devices  24.6 us (26%)
  between operations  0.99 us (1%)
    pallas_call x14, Pallas kernels, call(): pl.pallas_call(body, out_shape=[s if kind == 'v' else pltpu.HBM(s.shape,...  37 us
    all_to_all x5, waiting for transfers between devices, exchange(): return lax.all_to_all(x, 'nodes', split_axis=0, concat_axis=0, tiled=True)  22 us
    all_to_all x5, starting transfers between devices, exchange(): return lax.all_to_all(x, 'nodes', split_axis=0, concat_axis=0, tiled=True)  21.6 us
    ppermute x1, starting transfers between devices, per_device(): beside = lax.ppermute(far, 'nodes', between_pairs)  4.54 us
    ppermute x1, starting transfers between devices, per_device(): from_beside = lax.ppermute(rim_far, 'nodes', between_pairs)  3.55 us
    ppermute x1, waiting for transfers between devices, per_device(): from_beside = lax.ppermute(rim_far, 'nodes', between_pairs)  2.62 us
  transfers between devices with their start and end apart: 9, of which 6 were waited for; matrix products, arithmetic and copies ran while one was open for 0% of the time, Pallas kernels for 24%

profile of v12, /device:TPU:1, one launch (start us, length us, event | category | flops | bytes accessed | tf_op | source)
XLA Modules:
  0.0 93.3 jit_solution(5313318053894676113)
XLA Ops:
  1.5 4.5 %collective-permute-start.1 = (bf16[256,128]{1,0:T(8,128)(2,1)S(1)}, bf16[256,128]{1,0:T(8,128)(2,1)S(1)}, u32[]{:S(2)}, u32[]{:S(2)}) collective-permute-start(bf16[256,128]{1,0:T(8,128)(2,1)S(1)} %get-tuple-element.102), channel_id=1, source_target_pairs={{1,2},{2,1},{3,4},{4,3},{5,6},{6,5},{7,8},{8,7},{9,10},{10,9},{11,... | collective-permute-start | bytes 196616 | tf_op jit(solution)/shard_map/ppermute | solution.py:681
  6.2 4.3 %shard_map.158 = (bf16[2,768,256]{2,1,0:T(8,128)(2,1)S(1)}, bf16[2,128,512]{2,1,0:T(8,128)(2,1)S(1)}, bf16[128,256]{1,0:T(8,128)(2,1)S(1)}, bf16[128,128]{1,0:T(...) custom-call(s32[8,2048]{1,0:T(8,128)} %refs_0_.7, ...), custom_call_target="tpu_custom_call" | custom-call | bytes 18000000 | tf_op jit(solution)/shard_map/pallas_call | solution.py:163
  10.5 1.8 %shard_map.159 = (bf16[16,96,128]{2,1,0:T(8,128)(2,1)}, bf16[128,2048]{1,0:T(8,128)(2,1)}) custom-call(bf16[256,128]{1,0:T(8,128)(2,1)S(1)} %collective-permute-done.refs_0_, bf16[256,128]{1,0:T(8,128)(2,1)S(1)} %collective-permute-done.1.refs_1_, bf16[2,768,256]{2,1,0:T(8,128)(2,1)S(1)} %get-tuple-element.52.refs_2_, ...), custom_call_target="tpu_custom_call" | custom-call | bytes 9000000 | tf_op jit(solution)/shard_map/pallas_call | solution.py:163
  12.3 5.4 %all-to-all-start = ((bf16[16,96,128]{2,1,0:T(8,128)(2,1)}), bf16[16,96,128]{2,1,0:T(8,128)(2,1)S(1)}, u32[]{:S(2)}, u32[]{:S(2)}) async-start(bf16[16,96,128]{2,1,0:T(8,128)(2,1)} %get-tuple-element.61), calls=%async_computation | async-start | bytes 786432 | tf_op jit(solution)/shard_map/all_to_all | solution.py:640
  17.6 2.0 %shard_map.160 = (bf16[512,512]{1,0:T(8,128)(2,1)}, bf16[128,256]{1,0:T(8,128)(2,1)}, bf16[128,128]{1,0:T(8,128)(2,1)}, bf16[128,128]{1,0:T(8,128)(2,1)}) custom-call(s32[8,512]{1,0:T(8,128)} %refs_0_.5, f32[8,512]{1,0:T(8,128)} %refs_1_.4, bf16[3,4,128,128]{3,2,1,0:T(8,128)(2,1)} %refs_2_.7, bf16[128,2048]{1,0:T(8,128)(2,1)} %get-tuple-element.62.refs_3_.refs_1_.refs_8_), custom_call_target="tpu_custom_call" | custom-call | bytes 18000000 | tf_op jit(solution)/shard_map/pallas_call | solution.py:163
  19.6 4.4 %shard_map.161 = (bf16[128,2048]{1,0:T(8,128)(2,1)}, bf16[128,2048]{1,0:T(8,128)(2,1)}, bf16[128,2048]{1,0:T(8,128)(2,1)}, bf16[128,2048]{1,0:T(8,128)(2,1)}, bf...) custom-call(bf16[2048,128]{1,0:T(8,128)(2,1)} %refs_0_.6, ...), custom_call_target="tpu_custom_call" | custom-call | bytes 12000000 | tf_op jit(solution)/shard_map/pallas_call | solution.py:163
  24.0 5.5 %all-to-all-done.refs_0_ = bf16[16,96,128]{2,1,0:T(8,128)(2,1)S(1)} async-done(((bf16[16,96,128]{2,1,0:T(8,128)(2,1)}), bf16[16,96,128]{2,1,0:T(8,128)(2,1)S(1)}, u32[]{:S(2)}, u32[]{:S(2)}) %all-to-all-start) | async-done | bytes 393248 | tf_op jit(solution)/shard_map/all_to_all | solution.py:640
  29.6 2.9 %shard_map.162 = (bf16[16,16,128]{2,1,0:T(8,128)(2,1)}, bf16[128,512]{1,0:T(8,128)(2,1)}, bf16[128,512]{1,0:T(8,128)(2,1)}, bf16[1024,512]{1,0:T(8,128)(2,1)}, bf16[16,32,128]{2,1,0:T(8,128)(2,1)}) custom-call(bf16[16,96,128]{2,1,0:T(8,128)(2,1)S(1)} %all-to-all-done.refs_0_, bf16[512,512]{1,0:T(8,128)(2,1)} %get-tuple-element.63.refs_1_.refs_13_, ...), custom_call_target="tpu_custom_call" | custom-call | bytes 9000000 | tf_op jit(solution)/shard_map/pallas_call | solution.py:163
  32.5 3.8 %all-to-all-start.1 = ((bf16[16,16,128]{2,1,0:T(8,128)(2,1)}), bf16[16,16,128]{2,1,0:T(8,128)(2,1)S(1)}, u32[]{:S(2)}, u32[]{:S(2)}) async-start(bf16[16,16,128]{2,1,0:T(8,128)(2,1)} %get-tuple-element.68), calls=%async_computation.1 | async-start | bytes 131072 | tf_op jit(solution)/shard_map/all_to_all | solution.py:640
  36.3 2.8 %shard_map.163 = (bf16[256,256]{1,0:T(8,128)(2,1)S(1)}, bf16[128,256]{1,0:T(8,128)(2,1)S(1)}, f32[128,256]{1,0:T(8,128)S(1)}, bf16[128,256]{1,0:T(8,128)(2,1)S(1...) custom-call(bf16[16,32,128]{2,1,0:T(8,128)(2,1)} %get-tuple-element.69.ref, ...), custom_call_target="tpu_custom_call" | custom-call | bytes 18000000 | tf_op jit(solution)/shard_map/pallas_call | solution.py:163
  39.2 3.2 %all-to-all-done.1 = bf16[16,16,128]{2,1,0:T(8,128)(2,1)S(1)} async-done(((bf16[16,16,128]{2,1,0:T(8,128)(2,1)}), bf16[16,16,128]{2,1,0:T(8,128)(2,1)S(1)}, u32[]{:S(2)}, u32[]{:S(2)}) %all-to-all-start.1) | async-done | bytes 65568 | tf_op jit(solution)/shard_map/all_to_all | solution.py:640
  42.4 3.8 %shard_map.164 = (bf16[1024,128]{1,0:T(8,128)(2,1)}, bf16[128,512]{1,0:T(8,128)(2,1)}, bf16[128,512]{1,0:T(8,128)(2,1)}, bf16[128,512]{1,0:T(8,128)(2,1)}, f32[4,128,128]{2,1,0:T(8,128)}) custom-call(bf16[256,128]{1,0:T(8,128)(2,1)S(1)} %bitcast.9, bf16[256,256]{1,0:T(8,128)(2,1)S(1)} %get-tuple-element.72.refs_1_, ...), custom_call_target="tpu_custom_call" | custom-call | bytes 9000000 | tf_op jit(solution)/shard_map/pallas_call | solution.py:163
  46.2 4.3 %all-to-all-start.2 = ((bf16[16,64,128]{2,1,0:T(8,128)(2,1)}), bf16[16,64,128]{2,1,0:T(8,128)(2,1)S(1)}, u32[]{:S(2)}, u32[]{:S(2)}) async-start(bf16[16,64,128]{2,1,0:T(8,128)(2,1)} %bitcast.11), calls=%async_computation.2 | async-start | bytes 524288 | tf_op jit(solution)/shard_map/all_to_all | solution.py:640
  50.5 1.9 %shard_map.165.refs_1_.refs_11_ = bf16[512,128]{1,0:T(8,128)(2,1)S(1)} custom-call(bf16[128,512]{1,0:T(8,128)(2,1)} %get-tuple-element.70.refs_1_.refs_0_, bf16[128,512]{1,0:T(8,128)(2,1)} %get-tuple-element.71.refs_2_.refs_1_, bf16[128,512]{1,0:T(8,128)(2,1)} %get-tuple-element.83.refs_2_, bf16[128,512]{1,0:T(8,128)(2,1)} %get-tuple-element.84.refs_3_, ...), custom_call_target="tpu_custom_call" | custom-call | bytes 6000000 | tf_op jit(solution)/shard_map/pallas_call | solution.py:163
  53.2 6.8 %all-to-all-done.2 = bf16[16,64,128]{2,1,0:T(8,128)(2,1)S(1)} async-done(((bf16[16,64,128]{2,1,0:T(8,128)(2,1)}), bf16[16,64,128]{2,1,0:T(8,128)(2,1)S(1)}, u32[]{:S(2)}, u32[]{:S(2)}) %all-to-all-start.2) | async-done | bytes 262176 | tf_op jit(solution)/shard_map/all_to_all | solution.py:640
  60.0 4.2 %shard_map.167 = (bf16[1024,128]{1,0:T(8,128)(2,1)}, bf16[128,2048]{1,0:T(8,128)(2,1)}, bf16[128,2048]{1,0:T(8,128)(2,1)}) custom-call(bf16[1024,128]{1,0:T(8,128)(2,1)S(1)} %bitcast.8, bf16[512,1024]{1,0:T(8,128)(2,1)S(1)} %shard_map.166.refs_1_, bf16[128,2048]{1,0:T(8,128)(2,1)} %get-tuple-element.86.refs_2_, ...), custom_call_target="tpu_custom_call" | custom-call | bytes 12000000 | tf_op jit(solution)/shard_map/pallas_call | solution.py:163
  64.2 4.0 %all-to-all-start.3 = ((bf16[16,64,128]{2,1,0:T(8,128)(2,1)}), bf16[16,64,128]{2,1,0:T(8,128)(2,1)S(1)}, u32[]{:S(2)}, u32[]{:S(2)}) async-start(bf16[16,64,128]{2,1,0:T(8,128)(2,1)} %bitcast.12), calls=%async_computation.3 | async-start | bytes 524288 | tf_op jit(solution)/shard_map/all_to_all | solution.py:640
  68.2 4.6 %shard_map.168 = (bf16[256,128]{1,0:T(8,128)(2,1)}, bf16[256,128]{1,0:T(8,128)(2,1)}, f32[512,128]{1,0:T(8,128)}, bf16[2048,128]{1,0:T(8,128)(2,1)}) custom-call(s32[8,2048]{1,0:T(8,128)} %refs_0_.7, f32[8,2048]{1,0:T(8,128)} %refs_1_.5, bf16[3,4,128,128]{3,2,1,0:T(8,128)(2,1)} %refs_2_.7, bf16[128,2048]{1,0:T(8,128)(2,1)} %get-tuple-element.92.refs_3_, ...), custom_call_target="tpu_custom_call" | custom-call | bytes 15000000 | tf_op jit(solution)/shard_map/pallas_call | solution.py:163
  72.8 5.0 %all-to-all-done.3.refs_0_ = bf16[16,64,128]{2,1,0:T(8,128)(2,1)S(1)} async-done(((bf16[16,64,128]{2,1,0:T(8,128)(2,1)}), bf16[16,64,128]{2,1,0:T(8,128)(2,1)S(1)}, u32[]{:S(2)}, u32[]{:S(2)}) %all-to-all-start.3) | async-done | bytes 262176 | tf_op jit(solution)/shard_map/all_to_all | solution.py:640
  78.6 4.1 %all-to-all-start.4 = ((bf16[16,64,128]{2,1,0:T(8,128)(2,1)}), bf16[16,64,128]{2,1,0:T(8,128)(2,1)S(1)}, u32[]{:S(2)}, u32[]{:S(2)}) async-start(bf16[16,64,128]{2,1,0:T(8,128)(2,1)} %shard_map.170), calls=%async_computation.4 | async-start | bytes 524288 | tf_op jit(solution)/shard_map/all_to_all | solution.py:640
  82.8 3.5 %collective-permute-start.3 = (bf16[256,128]{1,0:T(8,128)(2,1)S(1)}, bf16[256,128]{1,0:T(8,128)(2,1)S(1)}, u32[]{:S(2)}, u32[]{:S(2)}) collective-permute-start(bf16[256,128]{1,0:T(8,128)(2,1)S(1)} %copy-done.1), channel_id=1, source_target_pairs={{1,2},{2,1},{3,4},{4,3},{5,6},{6,5},{7,8},{8,7},{9,10},{10,9},{11,... | collective-permute-start | bytes 196616 | tf_op jit(solution)/shard_map/ppermute | solution.py:845
  86.4 2.6 %collective-permute-done.3.refs_2_ = bf16[256,128]{1,0:T(8,128)(2,1)S(1)} collective-permute-done((bf16[256,128]{1,0:T(8,128)(2,1)S(1)}, bf16[256,128]{1,0:T(8,128)(2,1)S(1)}, u32[]{:S(2)}, u32[]{:S(2)}) %collective-permute-start.3) | collective-permute-done | bytes 65568 | tf_op jit(solution)/shard_map/ppermute | solution.py:845
  89.1 1.8 %shard_map.169 = (bf16[2048,128]{1,0:T(8,128)(2,1)}, f32[12,128,128]{2,1,0:T(8,128)}) custom-call(f32[512,128]{1,0:T(8,128)} %get-tuple-element.94.refs_0_, bf16[256,128]{1,0:T(8,128)(2,1)S(1)} %collective-permute-done.2.refs_1_, bf16[256,128]{1,0:T(8,128)(2,1)S(1)} %collective-permute-done.3.refs_2_, ...), custom_call_target="tpu_custom_call", output_to_operand_aliasing={{0}: (4, {})} | custom-call | bytes 3000000 | tf_op jit(solution)/shard_map/pallas_call | solution.py:163
  90.8 1.5 %all-to-all-done.4 = bf16[16,64,128]{2,1,0:T(8,128)(2,1)S(1)} async-done(((bf16[16,64,128]{2,1,0:T(8,128)(2,1)}), bf16[16,64,128]{2,1,0:T(8,128)(2,1)S(1)}, u32[]{:S(2)}, u32[]{:S(2)}) %all-to-all-start.4) | async-done | bytes 262176 | tf_op jit(solution)/shard_map/all_to_all | solution.py:640
  (13 shorter events, 3.6 us)
Async XLA Ops:
  1.5 8.9 %collective-permute-start.1 = (bf16[256,128]{1,0:T(8,128)(2,1)S(1)}, bf16[256,128]{1,0:T(8,128)(2,1)S(1)}, u32[]{:S(2)}, u32[]{:S(2)}) collective-permute-start(bf16[256,128]{1,0:T(8,128)(2,1)S(1)} %get-tuple-element.102), channel_id=1, source_target_pairs={{1,2},{2,1},{3,4},{4,3},{5,6},{6,5},{7,8},{8,7},{9,10},{10,9},{11,... | collective-permute-start | bytes 196616 | tf_op jit(solution)/shard_map/ppermute | solution.py:681
  6.1 4.4 %collective-permute-start = (bf16[256,128]{1,0:T(8,128)(2,1)S(1)}, bf16[256,128]{1,0:T(8,128)(2,1)S(1)}, u32[]{:S(2)}, u32[]{:S(2)}) collective-permute-start(bf16[256,128]{1,0:T(8,128)(2,1)S(1)} %get-tuple-element.103), channel_id=1, source_target_pairs={{0,1},{1,0},{2,3},{3,2},{4,5},{5,4},{6,7},{7,6},{8,9},{9,8},{10,11... | collective-permute-start | bytes 196616 | tf_op jit(solution)/shard_map/ppermute | solution.py:680
  12.3 17.3 %all-to-all-start = ((bf16[16,96,128]{2,1,0:T(8,128)(2,1)}), bf16[16,96,128]{2,1,0:T(8,128)(2,1)S(1)}, u32[]{:S(2)}, u32[]{:S(2)}) async-start(bf16[16,96,128]{2,1,0:T(8,128)(2,1)} %get-tuple-element.61), calls=%async_computation | async-start | bytes 786432 | tf_op jit(solution)/shard_map/all_to_all | solution.py:640
  32.5 9.9 %all-to-all-start.1 = ((bf16[16,16,128]{2,1,0:T(8,128)(2,1)}), bf16[16,16,128]{2,1,0:T(8,128)(2,1)S(1)}, u32[]{:S(2)}, u32[]{:S(2)}) async-start(bf16[16,16,128]{2,1,0:T(8,128)(2,1)} %get-tuple-element.68), calls=%async_computation.1 | async-start | bytes 131072 | tf_op jit(solution)/shard_map/all_to_all | solution.py:640
  46.2 13.8 %all-to-all-start.2 = ((bf16[16,64,128]{2,1,0:T(8,128)(2,1)}), bf16[16,64,128]{2,1,0:T(8,128)(2,1)S(1)}, u32[]{:S(2)}, u32[]{:S(2)}) async-start(bf16[16,64,128]{2,1,0:T(8,128)(2,1)} %bitcast.11), calls=%async_computation.2 | async-start | bytes 524288 | tf_op jit(solution)/shard_map/all_to_all | solution.py:640
  64.2 13.6 %all-to-all-start.3 = ((bf16[16,64,128]{2,1,0:T(8,128)(2,1)}), bf16[16,64,128]{2,1,0:T(8,128)(2,1)S(1)}, u32[]{:S(2)}, u32[]{:S(2)}) async-start(bf16[16,64,128]{2,1,0:T(8,128)(2,1)} %bitcast.12), calls=%async_computation.3 | async-start | bytes 524288 | tf_op jit(solution)/shard_map/all_to_all | solution.py:640
  78.6 4.2 %copy-start.1 = (bf16[256,128]{1,0:T(8,128)(2,1)S(1)}, bf16[256,128]{1,0:T(8,128)(2,1)}, u32[]{:S(2)}) copy-start(bf16[256,128]{1,0:T(8,128)(2,1)} %get-tuple-element.96) | copy-start | bytes 196612
  78.6 7.7 %copy-start = (bf16[256,128]{1,0:T(8,128)(2,1)S(1)}, bf16[256,128]{1,0:T(8,128)(2,1)}, u32[]{:S(2)}) copy-start(bf16[256,128]{1,0:T(8,128)(2,1)} %get-tuple-element.95.refs_1_) | copy-start | bytes 196612
  78.6 13.7 %all-to-all-start.4 = ((bf16[16,64,128]{2,1,0:T(8,128)(2,1)}), bf16[16,64,128]{2,1,0:T(8,128)(2,1)S(1)}, u32[]{:S(2)}, u32[]{:S(2)}) async-start(bf16[16,64,128]{2,1,0:T(8,128)(2,1)} %shard_map.170), calls=%async_computation.4 | async-start | bytes 524288 | tf_op jit(solution)/shard_map/all_to_all | solution.py:640
  82.8 6.3 %collective-permute-start.3 = (bf16[256,128]{1,0:T(8,128)(2,1)S(1)}, bf16[256,128]{1,0:T(8,128)(2,1)S(1)}, u32[]{:S(2)}, u32[]{:S(2)}) collective-permute-start(bf16[256,128]{1,0:T(8,128)(2,1)S(1)} %copy-done.1), channel_id=1, source_target_pairs={{1,2},{2,1},{3,4},{4,3},{5,6},{6,5},{7,8},{8,7},{9,10},{10,9},{11,... | collective-permute-start | bytes 196616 | tf_op jit(solution)/shard_map/ppermute | solution.py:845
  86.4 2.7 %collective-permute-start.2 = (bf16[256,128]{1,0:T(8,128)(2,1)S(1)}, bf16[256,128]{1,0:T(8,128)(2,1)S(1)}, u32[]{:S(2)}, u32[]{:S(2)}) collective-permute-start(bf16[256,128]{1,0:T(8,128)(2,1)S(1)} %copy-done), channel_id=1, source_target_pairs={{0,1},{1,0},{2,3},{3,2},{4,5},{5,4},{6,7},{7,6},{8,9},{9,8},{10,11... | collective-permute-start | bytes 196616 | tf_op jit(solution)/shard_map/ppermute | solution.py:844

commit v13 on v12

--- a/solution.py
+++ b/solution.py
@@ -491,16 +491,19 @@
 
 def third_window_kernel(mid_scale, io, need, flush, ins, outs):
     mhid, magg, gmid, msg, mfg, w1 = ins
-    wg_ref = outs[0]
+    keep_ref, give_ref = outs
     d = mhid.shape[0]
+    even = lax.rem(lax.axis_index("nodes"), 2) == 0
     need()
     w01, w2t, _ = forward_weights(w1)
     middle = silu(dot(w01, jnp.concatenate([mhid[...], magg[...]], axis=0))).astype(BF)
     outer = silu(dot(w2t, middle)).astype(BF)
-    wg_ref[0:d, :] = (dot_nt(mhid[...], mfg[...]) * mid_scale).astype(BF)
-    wg_ref[d : 2 * d, :] = (dot_nt(magg[...], mfg[...]) * mid_scale).astype(BF)
-    wg_ref[2 * d : 3 * d, :] = (dot_nt(middle, msg[...]) * mid_scale).astype(BF)
-    wg_ref[3 * d : 4 * d, :] = (dot_nt(outer, gmid[...]) * mid_scale).astype(BF)
+    pairs = ((mhid, mfg), (magg, mfg), (middle, msg), (outer, gmid))
+    grads = [(dot_nt(x[...], y[...]) * mid_scale).astype(BF) for x, y in pairs]
+    for m in range(2):
+        rows = slice(m * d, (m + 1) * d)
+        keep_ref[rows, :] = jnp.where(even, grads[m], grads[m + 2])
+        give_ref[rows, :] = jnp.where(even, grads[m + 2], grads[m])
 
 
 def pick_kernel(block_rows, io, need, flush, ins, outs):
@@ -518,13 +521,17 @@
 
 
 def fine_grad_kernel(scale, io, need, flush, ins, outs, g_ref, fg_ref):
-    got, pick, cot, pool, w, slope2, slope1, hid, agg, mid, outer, mid_wg = ins
+    got, pick, cot, pool, w, slope2, slope1, hid, agg, mid, outer, *halves = ins
     send_ref, g_out, fg_out = outs
     d, rows = hid.shape
     if pick.shape[1] > 1024:
         need(1)
     blocks = dot(pick[...], got[...]).astype(BF)
-    send_ref[4 * d : 8 * d, :] = mid_wg[...]
+    peers, chunk, _ = send_ref.shape
+    fine_rows, mid_rows = chunk * 2 // 3, chunk // 3
+    both = (halves[0][...].astype(F32) + halves[1][...].astype(F32)).astype(BF)
+    for p in range(peers):
+        send_ref[p, fine_rows:, :] = both[p * mid_rows : (p + 1) * mid_rows, :]
     need(2, 3)
     per = pool.shape[1]
     for i in range(rows // TILE):
@@ -542,7 +549,10 @@
     for m, (a, b) in enumerate(
         ((hid[...], fg), (agg[...], fg), (mid[...], sg), (outer[...], g))
     ):
-        send_ref[m * d : (m + 1) * d, :] = (dot_nt(a, b) * scale).astype(BF)
+        grad = (dot_nt(a, b) * scale).astype(BF)
+        for q in range(d // fine_rows):
+            part = grad[q * fine_rows : (q + 1) * fine_rows, :]
+            send_ref[m * d // fine_rows + q, :fine_rows, :] = part
 
 
 def fine_spread_kernel(io, need, flush, ins, outs, band, spill, inner):
@@ -607,7 +617,13 @@
     send_ref = outs[0]
     peers = got.shape[0]
     need()
-    part[...] = sum(got[p].astype(F32) for p in range(peers)).astype(BF)
+    fine_rows, mid_rows = got.shape[1] * 2 // 3, got.shape[1] // 3
+    fine = sum(got[p, :fine_rows, :].astype(F32) for p in range(peers))
+    part[:fine_rows, :] = fine.astype(BF)
+    for core in range(2):
+        mids = sum(got[p, fine_rows:, :].astype(F32) for p in range(core, peers, 2))
+        at = fine_rows + core * mid_rows
+        part[at : at + mid_rows, :] = mids.astype(BF)
     for p in range(peers):
         io.start(part, send_ref.at[p])
 
@@ -625,15 +641,24 @@
     io.start(joined.at[pl.ds(0, HALO)], out_ref.at[pl.ds(0, HALO)])
     io.start(joined.at[pl.ds(HALO, HALO)], out_ref.at[pl.ds(rows - HALO, HALO)])
     need()
-    io.start(coarse, wg_ref.at[pl.ds(8, 4)])
+    io.start(coarse, wg_ref.at[pl.ds(2 * coarse.shape[0], coarse.shape[0])])
 
 
 def gather_kernel(io, need, flush, ins, outs, wide):
-    out_ref = outs[0]
-    for half in range(2):
-        wide[4 * half : 4 * half + 4] = ins[0][4 * half : 4 * half + 4].astype(F32)
-        part = pl.ds(4 * half, 4)
-        io.start(wide.at[part], out_ref.at[part])
+    summed, out_ref = ins[0], outs[0]
+    peers, chunk, _ = summed.shape
+    fine_rows, mid_rows = chunk // 2, chunk // 4
+    total = wide.shape[0]
+    for p in range(peers):
+        wide[p * fine_rows : (p + 1) * fine_rows, :] = summed[p, :fine_rows, :].astype(F32)
+    io.start(wide.at[pl.ds(0, total // 2)], out_ref.at[pl.ds(0, total // 2)])
+    for p in range(peers):
+        for core in range(2):
+            at = total // 2 + core * total // 4 + p * mid_rows
+            rows = slice(fine_rows + core * mid_rows, fine_rows + (core + 1) * mid_rows)
+            wide[at : at + mid_rows, :] = summed[p, rows, :].astype(F32)
+    rest = pl.ds(total // 2, total // 2)
+    io.start(wide.at[rest], out_ref.at[rest])
 
 
 def exchange(x):
@@ -788,17 +813,18 @@
     )
     got3 = exchange(send3.reshape(peers, chunk, d))
     pick_kind = "v" if peers * chunk <= 1024 else "h"
-    (mid_wg,) = call(
+    mid_keep, mid_give = call(
         functools.partial(third_window_kernel, 1.0 / math.sqrt(n1 * peers)),
         [
             (mhid, "h"), (magg, "h"), (gmid, "h"), (msg, "h"), (mfg, "h"), (weights, "1"),
         ],
-        [(shape((4 * d, d)), "v")],
+        [(shape((2 * d, d)), "v"), (shape((2 * d, d)), "v")],
         us=2,
     )
+    mid_got = lax.ppermute(mid_give, "nodes", inside_pairs)
     (pick,) = call(
         functools.partial(pick_kernel, block_rows),
-        [(place, "s"), (mid_wg, "v")],
+        [(place, "s"), (mid_keep, "v")],
         [(shape((tile_count * block_rows, peers * chunk)), pick_kind)],
         us=1,
     )
@@ -807,14 +833,16 @@
         [
             (got3.reshape(peers * chunk, d), "v"), (pick, pick_kind), (cot, "h"), (pool_b, "h"),
             (weights, "0"), (slope2, "h"), (slope1, "h"), (hid, "h"), (agg, "h"), (mid, "h"),
-            (outer, "h"), (mid_wg, "v"),
-        ],
-        [(shape((8 * d, d)), "h"), (shape((d, n)), "r"), (shape((d, n)), "r")],
+            (outer, "h"), (mid_keep, "v"), (mid_got, "v"),
+        ],
+        [
+            (shape((peers, 6 * d // peers, d)), "h"), (shape((d, n)), "r"), (shape((d, n)), "r"),
+        ],
         scratch=(pltpu.VMEM((d, n), BF), pltpu.VMEM((d, n), BF)),
         copies=2,
         us=4,
     )
-    got4 = exchange(send4.reshape(peers, 8 * d // peers, d))
+    got4 = exchange(send4)
     rim_near, rim_far, edge_sums, inner_grads = call(
         fine_spread_kernel,
         [
@@ -846,10 +874,10 @@
     feature_grads, weight_grads = call(
         join_kernel,
         [
-            (edge_sums, "h"), (from_across, "v"), (from_beside, "v"), (coarse_wg, "h"),
+            (edge_sums, "h"), (from_across, "v"), (from_beside, "v"), (coarse_wg.reshape(4 * d, d), "h"),
             (inner_grads, "r"),
         ],
-        [(shape((n, d)), "r"), (shape((12, d, d), F32), "r")],
+        [(shape((n, d)), "r"), (shape((12 * d, d), F32), "r")],
         scratch=(pltpu.VMEM((2 * HALO, d), BF),),
         copies=3,
         aliases={4: 0},
@@ -858,10 +886,10 @@
     (weight_grads,) = call(
         gather_kernel,
         [
-            (got5.reshape(8, d, d), "v"), (weight_grads, "r"),
-        ],
-        [(shape((12, d, d), F32), "r")],
-        scratch=(pltpu.VMEM((8, d, d), F32),),
+            (got5, "v"), (weight_grads, "r"),
+        ],
+        [(shape((12 * d, d), F32), "r")],
+        scratch=(pltpu.VMEM((8 * d, d), F32),),
         copies=2,
         aliases={1: 0},
         us=1,

time: 94.8 us -> 93.8 us (0.989)
  waiting for transfers between devices: 24.6 us -> 22.7 us
    all_to_all x5, waiting for transfers between devices: 22 us -> 19.9 us  [exchange(): return lax.all_to_all(x, 'nodes', split_axis=0, concat_axis=0, tiled=True)]
  transfers between devices with their start and end apart: 9 -> 10, of which waited for: 6 -> 7; matrix products, arithmetic and copies ran while one was open for 0% -> 0% of each run, Pallas kernels for 24% -> 24%
where the time goes in v13:
time: 93.8 us; the launch traced here: 92.3 us
  Pallas kernels  37 us (39%)
  starting transfers between devices  30.7 us (33%)
  waiting for transfers between devices  22.7 us (24%)
  between operations  0.99 us (1%)
    pallas_call x14, Pallas kernels, call(): pl.pallas_call(body, out_shape=[s if kind == 'v' else pltpu.HBM(s.shape,...  37 us
    all_to_all x5, starting transfers between devices, exchange(): return lax.all_to_all(x, 'nodes', split_axis=0, concat_axis=0, tiled=True)  22.2 us
    all_to_all x5, waiting for transfers between devices, exchange(): return lax.all_to_all(x, 'nodes', split_axis=0, concat_axis=0, tiled=True)  19.9 us
    ppermute x1, starting transfers between devices, per_device(): beside = lax.ppermute(far, 'nodes', between_pairs)  4.54 us
    ppermute x1, starting transfers between devices, per_device(): from_beside = lax.ppermute(rim_far, 'nodes', between_pairs)  3.55 us
    ppermute x1, waiting for transfers between devices, per_device(): from_beside = lax.ppermute(rim_far, 'nodes', between_pairs)  2.62 us
  transfers between devices with their start and end apart: 10, of which 7 were waited for; matrix products, arithmetic and copies ran while one was open for 0% of the time, Pallas kernels for 24%

profile of v13, /device:TPU:1, one launch (start us, length us, event | category | flops | bytes accessed | tf_op | source)
XLA Modules:
  0.0 92.3 jit_solution(13494463974737428255)
XLA Ops:
  1.5 4.5 %collective-permute-start.1 = (bf16[256,128]{1,0:T(8,128)(2,1)S(1)}, bf16[256,128]{1,0:T(8,128)(2,1)S(1)}, u32[]{:S(2)}, u32[]{:S(2)}) collective-permute-start(bf16[256,128]{1,0:T(8,128)(2,1)S(1)} %get-tuple-element.106), channel_id=1, source_target_pairs={{1,2},{2,1},{3,4},{4,3},{5,6},{6,5},{7,8},{8,7},{9,10},{10,9},{11,... | collective-permute-start | bytes 196616 | tf_op jit(solution)/shard_map/ppermute | solution.py:706
  6.2 4.3 %shard_map.158 = (bf16[2,768,256]{2,1,0:T(8,128)(2,1)S(1)}, bf16[2,128,512]{2,1,0:T(8,128)(2,1)S(1)}, bf16[128,256]{1,0:T(8,128)(2,1)S(1)}, bf16[128,128]{1,0:T(...) custom-call(s32[8,2048]{1,0:T(8,128)} %refs_0_.7, ...), custom_call_target="tpu_custom_call" | custom-call | bytes 18000000 | tf_op jit(solution)/shard_map/pallas_call | solution.py:163
  10.5 1.8 %shard_map.159 = (bf16[16,96,128]{2,1,0:T(8,128)(2,1)}, bf16[128,2048]{1,0:T(8,128)(2,1)}) custom-call(bf16[256,128]{1,0:T(8,128)(2,1)S(1)} %collective-permute-done.refs_0_, bf16[256,128]{1,0:T(8,128)(2,1)S(1)} %collective-permute-done.1.refs_1_, bf16[2,768,256]{2,1,0:T(8,128)(2,1)S(1)} %get-tuple-element.54.refs_2_, ...), custom_call_target="tpu_custom_call" | custom-call | bytes 9000000 | tf_op jit(solution)/shard_map/pallas_call | solution.py:163
  12.3 5.4 %all-to-all-start = ((bf16[16,96,128]{2,1,0:T(8,128)(2,1)}), bf16[16,96,128]{2,1,0:T(8,128)(2,1)S(1)}, u32[]{:S(2)}, u32[]{:S(2)}) async-start(bf16[16,96,128]{2,1,0:T(8,128)(2,1)} %get-tuple-element.63), calls=%async_computation | async-start | bytes 786432 | tf_op jit(solution)/shard_map/all_to_all | solution.py:665
  17.7 2.0 %shard_map.160 = (bf16[512,512]{1,0:T(8,128)(2,1)}, bf16[128,256]{1,0:T(8,128)(2,1)}, bf16[128,128]{1,0:T(8,128)(2,1)}, bf16[128,128]{1,0:T(8,128)(2,1)}) custom-call(s32[8,512]{1,0:T(8,128)} %refs_0_.5, f32[8,512]{1,0:T(8,128)} %refs_1_.4, bf16[3,4,128,128]{3,2,1,0:T(8,128)(2,1)} %refs_2_.7, bf16[128,2048]{1,0:T(8,128)(2,1)} %get-tuple-element.64.refs_3_.refs_1_.refs_8_), custom_call_target="tpu_custom_call" | custom-call | bytes 18000000 | tf_op jit(solution)/shard_map/pallas_call | solution.py:163
  19.7 4.4 %shard_map.161 = (bf16[128,2048]{1,0:T(8,128)(2,1)}, bf16[128,2048]{1,0:T(8,128)(2,1)}, bf16[128,2048]{1,0:T(8,128)(2,1)}, bf16[128,2048]{1,0:T(8,128)(2,1)}, bf...) custom-call(bf16[2048,128]{1,0:T(8,128)(2,1)} %refs_0_.6, ...), custom_call_target="tpu_custom_call" | custom-call | bytes 12000000 | tf_op jit(solution)/shard_map/pallas_call | solution.py:163
  24.1 5.5 %all-to-all-done.refs_0_ = bf16[16,96,128]{2,1,0:T(8,128)(2,1)S(1)} async-done(((bf16[16,96,128]{2,1,0:T(8,128)(2,1)}), bf16[16,96,128]{2,1,0:T(8,128)(2,1)S(1)}, u32[]{:S(2)}, u32[]{:S(2)}) %all-to-all-start) | async-done | bytes 393248 | tf_op jit(solution)/shard_map/all_to_all | solution.py:665
  29.6 2.9 %shard_map.162 = (bf16[16,16,128]{2,1,0:T(8,128)(2,1)}, bf16[128,512]{1,0:T(8,128)(2,1)}, bf16[128,512]{1,0:T(8,128)(2,1)}, bf16[1024,512]{1,0:T(8,128)(2,1)}, bf16[16,32,128]{2,1,0:T(8,128)(2,1)}) custom-call(bf16[16,96,128]{2,1,0:T(8,128)(2,1)S(1)} %all-to-all-done.refs_0_, bf16[512,512]{1,0:T(8,128)(2,1)} %get-tuple-element.65.refs_1_.refs_13_, ...), custom_call_target="tpu_custom_call" | custom-call | bytes 9000000 | tf_op jit(solution)/shard_map/pallas_call | solution.py:163
  32.5 3.8 %all-to-all-start.1 = ((bf16[16,16,128]{2,1,0:T(8,128)(2,1)}), bf16[16,16,128]{2,1,0:T(8,128)(2,1)S(1)}, u32[]{:S(2)}, u32[]{:S(2)}) async-start(bf16[16,16,128]{2,1,0:T(8,128)(2,1)} %get-tuple-element.70), calls=%async_computation.1 | async-start | bytes 131072 | tf_op jit(solution)/shard_map/all_to_all | solution.py:665
  36.4 2.8 %shard_map.163 = (bf16[256,256]{1,0:T(8,128)(2,1)S(1)}, bf16[128,256]{1,0:T(8,128)(2,1)S(1)}, f32[128,256]{1,0:T(8,128)S(1)}, bf16[128,256]{1,0:T(8,128)(2,1)S(1...) custom-call(bf16[16,32,128]{2,1,0:T(8,128)(2,1)} %get-tuple-element.71.ref, ...), custom_call_target="tpu_custom_call" | custom-call | bytes 18000000 | tf_op jit(solution)/shard_map/pallas_call | solution.py:163
  39.2 3.2 %all-to-all-done.1 = bf16[16,16,128]{2,1,0:T(8,128)(2,1)S(1)} async-done(((bf16[16,16,128]{2,1,0:T(8,128)(2,1)}), bf16[16,16,128]{2,1,0:T(8,128)(2,1)S(1)}, u32[]{:S(2)}, u32[]{:S(2)}) %all-to-all-start.1) | async-done | bytes 65568 | tf_op jit(solution)/shard_map/all_to_all | solution.py:665
  42.4 3.8 %shard_map.164 = (bf16[1024,128]{1,0:T(8,128)(2,1)}, bf16[128,512]{1,0:T(8,128)(2,1)}, bf16[128,512]{1,0:T(8,128)(2,1)}, bf16[128,512]{1,0:T(8,128)(2,1)}, f32[4,128,128]{2,1,0:T(8,128)}) custom-call(bf16[256,128]{1,0:T(8,128)(2,1)S(1)} %bitcast.7, bf16[256,256]{1,0:T(8,128)(2,1)S(1)} %get-tuple-element.74.refs_1_, ...), custom_call_target="tpu_custom_call" | custom-call | bytes 9000000 | tf_op jit(solution)/shard_map/pallas_call | solution.py:163
  46.2 4.3 %all-to-all-start.2 = ((bf16[16,64,128]{2,1,0:T(8,128)(2,1)}), bf16[16,64,128]{2,1,0:T(8,128)(2,1)S(1)}, u32[]{:S(2)}, u32[]{:S(2)}) async-start(bf16[16,64,128]{2,1,0:T(8,128)(2,1)} %bitcast.9), calls=%async_computation.2 | async-start | bytes 524288 | tf_op jit(solution)/shard_map/all_to_all | solution.py:665
  50.5 1.9 %shard_map.165 = (bf16[256,128]{1,0:T(8,128)(2,1)S(1)}, bf16[256,128]{1,0:T(8,128)(2,1)S(1)}) custom-call(bf16[128,512]{1,0:T(8,128)(2,1)} %get-tuple-element.72.refs_1_.refs_0_, bf16[128,512]{1,0:T(8,128)(2,1)} %get-tuple-element.73.refs_2_.refs_1_, bf16[128,512]{1,0:T(8,128)(2,1)} %get-tuple-element.85.refs_2_, ...), custom_call_target="tpu_custom_call" | custom-call | bytes 6000000 | tf_op jit(solution)/shard_map/pallas_call | solution.py:163
  53.7 6.4 %all-to-all-done.2 = bf16[16,64,128]{2,1,0:T(8,128)(2,1)S(1)} async-done(((bf16[16,64,128]{2,1,0:T(8,128)(2,1)}), bf16[16,64,128]{2,1,0:T(8,128)(2,1)S(1)}, u32[]{:S(2)}, u32[]{:S(2)}) %all-to-all-start.2) | async-done | bytes 262176 | tf_op jit(solution)/shard_map/all_to_all | solution.py:665
  60.0 4.2 %shard_map.167 = (bf16[16,48,128]{2,1,0:T(8,128)(2,1)}, bf16[128,2048]{1,0:T(8,128)(2,1)}, bf16[128,2048]{1,0:T(8,128)(2,1)}) custom-call(bf16[1024,128]{1,0:T(8,128)(2,1)S(1)} %bitcast.6, bf16[512,1024]{1,0:T(8,128)(2,1)S(1)} %shard_map.166.refs_1_, bf16[128,2048]{1,0:T(8,128)(2,1)} %get-tuple-element.89.refs_2_, ...), custom_call_target="tpu_custom_call" | custom-call | bytes 12000000 | tf_op jit(solution)/shard_map/pallas_call | solution.py:163
  64.2 4.0 %all-to-all-start.3 = ((bf16[16,48,128]{2,1,0:T(8,128)(2,1)}), bf16[16,48,128]{2,1,0:T(8,128)(2,1)S(1)}, u32[]{:S(2)}, u32[]{:S(2)}) async-start(bf16[16,48,128]{2,1,0:T(8,128)(2,1)} %get-tuple-element.104), calls=%async_computation.3 | async-start | bytes 393216 | tf_op jit(solution)/shard_map/all_to_all | solution.py:665
  68.2 4.6 %shard_map.168 = (bf16[256,128]{1,0:T(8,128)(2,1)}, bf16[256,128]{1,0:T(8,128)(2,1)}, f32[512,128]{1,0:T(8,128)}, bf16[2048,128]{1,0:T(8,128)(2,1)}) custom-call(s32[8,2048]{1,0:T(8,128)} %refs_0_.7, f32[8,2048]{1,0:T(8,128)} %refs_1_.5, bf16[3,4,128,128]{3,2,1,0:T(8,128)(2,1)} %refs_2_.7, bf16[128,2048]{1,0:T(8,128)(2,1)} %get-tuple-element.96.refs_3_, ...), custom_call_target="tpu_custom_call" | custom-call | bytes 15000000 | tf_op jit(solution)/shard_map/pallas_call | solution.py:163
  72.8 3.4 %all-to-all-done.3.refs_0_ = bf16[16,48,128]{2,1,0:T(8,128)(2,1)S(1)} async-done(((bf16[16,48,128]{2,1,0:T(8,128)(2,1)}), bf16[16,48,128]{2,1,0:T(8,128)(2,1)S(1)}, u32[]{:S(2)}, u32[]{:S(2)}) %all-to-all-start.3) | async-done | bytes 196640 | tf_op jit(solution)/shard_map/all_to_all | solution.py:665
  77.1 4.6 %all-to-all-start.4 = ((bf16[16,64,128]{2,1,0:T(8,128)(2,1)}), bf16[16,64,128]{2,1,0:T(8,128)(2,1)S(1)}, u32[]{:S(2)}, u32[]{:S(2)}) async-start(bf16[16,64,128]{2,1,0:T(8,128)(2,1)} %shard_map.170), calls=%async_computation.4 | async-start | bytes 524288 | tf_op jit(solution)/shard_map/all_to_all | solution.py:665
  81.7 3.5 %collective-permute-start.4 = (bf16[256,128]{1,0:T(8,128)(2,1)S(1)}, bf16[256,128]{1,0:T(8,128)(2,1)S(1)}, u32[]{:S(2)}, u32[]{:S(2)}) collective-permute-start(bf16[256,128]{1,0:T(8,128)(2,1)S(1)} %copy-done.1), channel_id=1, source_target_pairs={{1,2},{2,1},{3,4},{4,3},{5,6},{6,5},{7,8},{8,7},{9,10},{10,9},{11,... | collective-permute-start | bytes 196616 | tf_op jit(solution)/shard_map/ppermute | solution.py:873
  85.4 2.6 %collective-permute-done.4.refs_2_ = bf16[256,128]{1,0:T(8,128)(2,1)S(1)} collective-permute-done((bf16[256,128]{1,0:T(8,128)(2,1)S(1)}, bf16[256,128]{1,0:T(8,128)(2,1)S(1)}, u32[]{:S(2)}, u32[]{:S(2)}) %collective-permute-start.4) | collective-permute-done | bytes 65568 | tf_op jit(solution)/shard_map/ppermute | solution.py:873
  88.0 1.8 %shard_map.169 = (bf16[2048,128]{1,0:T(8,128)(2,1)}, f32[1536,128]{1,0:T(8,128)}) custom-call(f32[512,128]{1,0:T(8,128)} %get-tuple-element.98.refs_0_, bf16[256,128]{1,0:T(8,128)(2,1)S(1)} %collective-permute-done.3.refs_1_, bf16[256,128]{1,0:T(8,128)(2,1)S(1)} %collective-permute-done.4.refs_2_, ...), custom_call_target="tpu_custom_call", output_to_operand_aliasing={{0}: (4, {})} | custom-call | bytes 3000000 | tf_op jit(solution)/shard_map/pallas_call | solution.py:163
  89.8 1.5 %all-to-all-done.4.refs_0_ = bf16[16,64,128]{2,1,0:T(8,128)(2,1)S(1)} async-done(((bf16[16,64,128]{2,1,0:T(8,128)(2,1)}), bf16[16,64,128]{2,1,0:T(8,128)(2,1)S(1)}, u32[]{:S(2)}, u32[]{:S(2)}) %all-to-all-start.4) | async-done | bytes 262176 | tf_op jit(solution)/shard_map/all_to_all | solution.py:665
  (15 shorter events, 4.1 us)
Async XLA Ops:
  1.5 8.9 %collective-permute-start.1 = (bf16[256,128]{1,0:T(8,128)(2,1)S(1)}, bf16[256,128]{1,0:T(8,128)(2,1)S(1)}, u32[]{:S(2)}, u32[]{:S(2)}) collective-permute-start(bf16[256,128]{1,0:T(8,128)(2,1)S(1)} %get-tuple-element.106), channel_id=1, source_target_pairs={{1,2},{2,1},{3,4},{4,3},{5,6},{6,5},{7,8},{8,7},{9,10},{10,9},{11,... | collective-permute-start | bytes 196616 | tf_op jit(solution)/shard_map/ppermute | solution.py:706
  6.1 4.4 %collective-permute-start = (bf16[256,128]{1,0:T(8,128)(2,1)S(1)}, bf16[256,128]{1,0:T(8,128)(2,1)S(1)}, u32[]{:S(2)}, u32[]{:S(2)}) collective-permute-start(bf16[256,128]{1,0:T(8,128)(2,1)S(1)} %get-tuple-element.107), channel_id=1, source_target_pairs={{0,1},{1,0},{2,3},{3,2},{4,5},{5,4},{6,7},{7,6},{8,9},{9,8},{10,11... | collective-permute-start | bytes 196616 | tf_op jit(solution)/shard_map/ppermute | solution.py:705
  12.3 17.3 %all-to-all-start = ((bf16[16,96,128]{2,1,0:T(8,128)(2,1)}), bf16[16,96,128]{2,1,0:T(8,128)(2,1)S(1)}, u32[]{:S(2)}, u32[]{:S(2)}) async-start(bf16[16,96,128]{2,1,0:T(8,128)(2,1)} %get-tuple-element.63), calls=%async_computation | async-start | bytes 786432 | tf_op jit(solution)/shard_map/all_to_all | solution.py:665
  32.5 9.9 %all-to-all-start.1 = ((bf16[16,16,128]{2,1,0:T(8,128)(2,1)}), bf16[16,16,128]{2,1,0:T(8,128)(2,1)S(1)}, u32[]{:S(2)}, u32[]{:S(2)}) async-start(bf16[16,16,128]{2,1,0:T(8,128)(2,1)} %get-tuple-element.70), calls=%async_computation.1 | async-start | bytes 131072 | tf_op jit(solution)/shard_map/all_to_all | solution.py:665
  46.2 13.8 %all-to-all-start.2 = ((bf16[16,64,128]{2,1,0:T(8,128)(2,1)}), bf16[16,64,128]{2,1,0:T(8,128)(2,1)S(1)}, u32[]{:S(2)}, u32[]{:S(2)}) async-start(bf16[16,64,128]{2,1,0:T(8,128)(2,1)} %bitcast.9), calls=%async_computation.2 | async-start | bytes 524288 | tf_op jit(solution)/shard_map/all_to_all | solution.py:665
  52.4 1.3 %collective-permute-start.2 = (bf16[256,128]{1,0:T(8,128)(2,1)S(1)}, bf16[256,128]{1,0:T(8,128)(2,1)S(1)}, u32[]{:S(2)}, u32[]{:S(2)}) collective-permute-start(bf16[256,128]{1,0:T(8,128)(2,1)S(1)} %get-tuple-element.95), channel_id=1, source_target_pairs={{0,1},{1,0},{2,3},{3,2},{4,5},{5,4},{6,7},{7,6},{8,9},{9,8},{10,11... | collective-permute-start | bytes 196616 | tf_op jit(solution)/shard_map/ppermute | solution.py:824
  64.2 12.0 %all-to-all-start.3 = ((bf16[16,48,128]{2,1,0:T(8,128)(2,1)}), bf16[16,48,128]{2,1,0:T(8,128)(2,1)S(1)}, u32[]{:S(2)}, u32[]{:S(2)}) async-start(bf16[16,48,128]{2,1,0:T(8,128)(2,1)} %get-tuple-element.104), calls=%async_computation.3 | async-start | bytes 393216 | tf_op jit(solution)/shard_map/all_to_all | solution.py:665
  77.1 4.7 %copy-start.1 = (bf16[256,128]{1,0:T(8,128)(2,1)S(1)}, bf16[256,128]{1,0:T(8,128)(2,1)}, u32[]{:S(2)}) copy-start(bf16[256,128]{1,0:T(8,128)(2,1)} %get-tuple-element.100) | copy-start | bytes 196612
  77.1 8.2 %copy-start = (bf16[256,128]{1,0:T(8,128)(2,1)S(1)}, bf16[256,128]{1,0:T(8,128)(2,1)}, u32[]{:S(2)}) copy-start(bf16[256,128]{1,0:T(8,128)(2,1)} %get-tuple-element.99.refs_1_) | copy-start | bytes 196612
  77.1 14.2 %all-to-all-start.4 = ((bf16[16,64,128]{2,1,0:T(8,128)(2,1)}), bf16[16,64,128]{2,1,0:T(8,128)(2,1)S(1)}, u32[]{:S(2)}, u32[]{:S(2)}) async-start(bf16[16,64,128]{2,1,0:T(8,128)(2,1)} %shard_map.170), calls=%async_computation.4 | async-start | bytes 524288 | tf_op jit(solution)/shard_map/all_to_all | solution.py:665
  81.7 6.3 %collective-permute-start.4 = (bf16[256,128]{1,0:T(8,128)(2,1)S(1)}, bf16[256,128]{1,0:T(8,128)(2,1)S(1)}, u32[]{:S(2)}, u32[]{:S(2)}) collective-permute-start(bf16[256,128]{1,0:T(8,128)(2,1)S(1)} %copy-done.1), channel_id=1, source_target_pairs={{1,2},{2,1},{3,4},{4,3},{5,6},{6,5},{7,8},{8,7},{9,10},{10,9},{11,... | collective-permute-start | bytes 196616 | tf_op jit(solution)/shard_map/ppermute | solution.py:873
  85.3 2.7 %collective-permute-start.3 = (bf16[256,128]{1,0:T(8,128)(2,1)S(1)}, bf16[256,128]{1,0:T(8,128)(2,1)S(1)}, u32[]{:S(2)}, u32[]{:S(2)}) collective-permute-start(bf16[256,128]{1,0:T(8,128)(2,1)S(1)} %copy-done), channel_id=1, source_target_pairs={{0,1},{1,0},{2,3},{3,2},{4,5},{5,4},{6,7},{7,6},{8,9},{9,8},{10,11... | collective-permute-start | bytes 196616 | tf_op jit(solution)/shard_map/ppermute | solution.py:872

commit v14 on v13

--- a/solution.py
+++ b/solution.py
@@ -520,9 +520,9 @@
         ).astype(BF)
 
 
-def fine_grad_kernel(scale, io, need, flush, ins, outs, g_ref, fg_ref):
+def fine_grad_kernel(scale, io, need, flush, ins, outs, g_ref, fg_ref, send_ref):
     got, pick, cot, pool, w, slope2, slope1, hid, agg, mid, outer, *halves = ins
-    send_ref, g_out, fg_out = outs
+    send_out, g_out, fg_out = outs
     d, rows = hid.shape
     if pick.shape[1] > 1024:
         need(1)
@@ -532,6 +532,10 @@
     both = (halves[0][...].astype(F32) + halves[1][...].astype(F32)).astype(BF)
     for p in range(peers):
         send_ref[p, fine_rows:, :] = both[p * mid_rows : (p + 1) * mid_rows, :]
+    whole_tiles = mid_rows % 16 == 0
+    if whole_tiles:
+        rows_of_mid = pl.ds(fine_rows, mid_rows)
+        io.start(send_ref.at[:, rows_of_mid], send_out.at[:, rows_of_mid])
     need(2, 3)
     per = pool.shape[1]
     for i in range(rows // TILE):
@@ -553,6 +557,12 @@
         for q in range(d // fine_rows):
             part = grad[q * fine_rows : (q + 1) * fine_rows, :]
             send_ref[m * d // fine_rows + q, :fine_rows, :] = part
+        if whole_tiles:
+            to = pl.ds(m * d // fine_rows, d // fine_rows)
+            rows_of_fine = pl.ds(0, fine_rows)
+            io.start(send_ref.at[to, rows_of_fine], send_out.at[to, rows_of_fine])
+    if not whole_tiles:
+        io.start(send_ref, send_out)
 
 
 def fine_spread_kernel(io, need, flush, ins, outs, band, spill, inner):
@@ -836,10 +846,14 @@
             (outer, "h"), (mid_keep, "v"), (mid_got, "v"),
         ],
         [
-            (shape((peers, 6 * d // peers, d)), "h"), (shape((d, n)), "r"), (shape((d, n)), "r"),
-        ],
-        scratch=(pltpu.VMEM((d, n), BF), pltpu.VMEM((d, n), BF)),
-        copies=2,
+            (shape((peers, 6 * d // peers, d)), "r"), (shape((d, n)), "r"), (shape((d, n)), "r"),
+        ],
+        scratch=(
+            pltpu.VMEM((d, n), BF),
+            pltpu.VMEM((d, n), BF),
+            pltpu.VMEM((peers, 6 * d // peers, d), BF),
+        ),
+        copies=7,
         us=4,
     )
     got4 = exchange(send4)

time: 93.8 us -> 93.8 us (level)
  no operation moved by 1% of the time
where the time goes in v14:
time: 93.8 us; the launch traced here: 92.3 us
  Pallas kernels  37 us (39%)
  starting transfers between devices  30.7 us (33%)
  waiting for transfers between devices  22.7 us (24%)
  between operations  0.99 us (1%)
    pallas_call x14, Pallas kernels, call(): pl.pallas_call(body, out_shape=[s if kind == 'v' else pltpu.HBM(s.shape,...  37 us
    all_to_all x5, starting transfers between devices, exchange(): return lax.all_to_all(x, 'nodes', split_axis=0, concat_axis=0, tiled=True)  22.2 us
    all_to_all x5, waiting for transfers between devices, exchange(): return lax.all_to_all(x, 'nodes', split_axis=0, concat_axis=0, tiled=True)  19.9 us
    ppermute x1, starting transfers between devices, per_device(): beside = lax.ppermute(far, 'nodes', between_pairs)  4.54 us
    ppermute x1, starting transfers between devices, per_device(): from_beside = lax.ppermute(rim_far, 'nodes', between_pairs)  3.55 us
    ppermute x1, waiting for transfers between devices, per_device(): from_beside = lax.ppermute(rim_far, 'nodes', between_pairs)  2.62 us
  transfers between devices with their start and end apart: 10, of which 7 were waited for; matrix products, arithmetic and copies ran while one was open for 0% of the time, Pallas kernels for 24%

profile of v14, /device:TPU:1, one launch (start us, length us, event | category | flops | bytes accessed | tf_op | source)
XLA Modules:
  0.0 92.3 jit_solution(4649394248741189069)
XLA Ops:
  1.5 4.5 %collective-permute-start.1 = (bf16[256,128]{1,0:T(8,128)(2,1)S(1)}, bf16[256,128]{1,0:T(8,128)(2,1)S(1)}, u32[]{:S(2)}, u32[]{:S(2)}) collective-permute-start(bf16[256,128]{1,0:T(8,128)(2,1)S(1)} %get-tuple-element.106), channel_id=1, source_target_pairs={{1,2},{2,1},{3,4},{4,3},{5,6},{6,5},{7,8},{8,7},{9,10},{10,9},{11,... | collective-permute-start | bytes 196616 | tf_op jit(solution)/shard_map/ppermute | solution.py:716
  6.2 4.3 %shard_map.158 = (bf16[2,768,256]{2,1,0:T(8,128)(2,1)S(1)}, bf16[2,128,512]{2,1,0:T(8,128)(2,1)S(1)}, bf16[128,256]{1,0:T(8,128)(2,1)S(1)}, bf16[128,128]{1,0:T(...) custom-call(s32[8,2048]{1,0:T(8,128)} %refs_0_.7, ...), custom_call_target="tpu_custom_call" | custom-call | bytes 18000000 | tf_op jit(solution)/shard_map/pallas_call | solution.py:163
  10.5 1.8 %shard_map.159 = (bf16[16,96,128]{2,1,0:T(8,128)(2,1)}, bf16[128,2048]{1,0:T(8,128)(2,1)}) custom-call(bf16[256,128]{1,0:T(8,128)(2,1)S(1)} %collective-permute-done.refs_0_, bf16[256,128]{1,0:T(8,128)(2,1)S(1)} %collective-permute-done.1.refs_1_, bf16[2,768,256]{2,1,0:T(8,128)(2,1)S(1)} %get-tuple-element.54.refs_2_, ...), custom_call_target="tpu_custom_call" | custom-call | bytes 9000000 | tf_op jit(solution)/shard_map/pallas_call | solution.py:163
  12.3 5.4 %all-to-all-start = ((bf16[16,96,128]{2,1,0:T(8,128)(2,1)}), bf16[16,96,128]{2,1,0:T(8,128)(2,1)S(1)}, u32[]{:S(2)}, u32[]{:S(2)}) async-start(bf16[16,96,128]{2,1,0:T(8,128)(2,1)} %get-tuple-element.63), calls=%async_computation | async-start | bytes 786432 | tf_op jit(solution)/shard_map/all_to_all | solution.py:675
  17.7 2.0 %shard_map.160 = (bf16[512,512]{1,0:T(8,128)(2,1)}, bf16[128,256]{1,0:T(8,128)(2,1)}, bf16[128,128]{1,0:T(8,128)(2,1)}, bf16[128,128]{1,0:T(8,128)(2,1)}) custom-call(s32[8,512]{1,0:T(8,128)} %refs_0_.5, f32[8,512]{1,0:T(8,128)} %refs_1_.4, bf16[3,4,128,128]{3,2,1,0:T(8,128)(2,1)} %refs_2_.7, bf16[128,2048]{1,0:T(8,128)(2,1)} %get-tuple-element.64.refs_3_.refs_1_.refs_8_), custom_call_target="tpu_custom_call" | custom-call | bytes 18000000 | tf_op jit(solution)/shard_map/pallas_call | solution.py:163
  19.6 4.4 %shard_map.161 = (bf16[128,2048]{1,0:T(8,128)(2,1)}, bf16[128,2048]{1,0:T(8,128)(2,1)}, bf16[128,2048]{1,0:T(8,128)(2,1)}, bf16[128,2048]{1,0:T(8,128)(2,1)}, bf...) custom-call(bf16[2048,128]{1,0:T(8,128)(2,1)} %refs_0_.6, ...), custom_call_target="tpu_custom_call" | custom-call | bytes 12000000 | tf_op jit(solution)/shard_map/pallas_call | solution.py:163
  24.1 5.5 %all-to-all-done.refs_0_ = bf16[16,96,128]{2,1,0:T(8,128)(2,1)S(1)} async-done(((bf16[16,96,128]{2,1,0:T(8,128)(2,1)}), bf16[16,96,128]{2,1,0:T(8,128)(2,1)S(1)}, u32[]{:S(2)}, u32[]{:S(2)}) %all-to-all-start) | async-done | bytes 393248 | tf_op jit(solution)/shard_map/all_to_all | solution.py:675
  29.6 2.9 %shard_map.162 = (bf16[16,16,128]{2,1,0:T(8,128)(2,1)}, bf16[128,512]{1,0:T(8,128)(2,1)}, bf16[128,512]{1,0:T(8,128)(2,1)}, bf16[1024,512]{1,0:T(8,128)(2,1)}, bf16[16,32,128]{2,1,0:T(8,128)(2,1)}) custom-call(bf16[16,96,128]{2,1,0:T(8,128)(2,1)S(1)} %all-to-all-done.refs_0_, bf16[512,512]{1,0:T(8,128)(2,1)} %get-tuple-element.65.refs_1_.refs_13_, ...), custom_call_target="tpu_custom_call" | custom-call | bytes 9000000 | tf_op jit(solution)/shard_map/pallas_call | solution.py:163
  32.5 3.8 %all-to-all-start.1 = ((bf16[16,16,128]{2,1,0:T(8,128)(2,1)}), bf16[16,16,128]{2,1,0:T(8,128)(2,1)S(1)}, u32[]{:S(2)}, u32[]{:S(2)}) async-start(bf16[16,16,128]{2,1,0:T(8,128)(2,1)} %get-tuple-element.70), calls=%async_computation.1 | async-start | bytes 131072 | tf_op jit(solution)/shard_map/all_to_all | solution.py:675
  36.4 2.8 %shard_map.163 = (bf16[256,256]{1,0:T(8,128)(2,1)S(1)}, bf16[128,256]{1,0:T(8,128)(2,1)S(1)}, f32[128,256]{1,0:T(8,128)S(1)}, bf16[128,256]{1,0:T(8,128)(2,1)S(1...) custom-call(bf16[16,32,128]{2,1,0:T(8,128)(2,1)} %get-tuple-element.71.ref, ...), custom_call_target="tpu_custom_call" | custom-call | bytes 18000000 | tf_op jit(solution)/shard_map/pallas_call | solution.py:163
  39.2 3.2 %all-to-all-done.1 = bf16[16,16,128]{2,1,0:T(8,128)(2,1)S(1)} async-done(((bf16[16,16,128]{2,1,0:T(8,128)(2,1)}), bf16[16,16,128]{2,1,0:T(8,128)(2,1)S(1)}, u32[]{:S(2)}, u32[]{:S(2)}) %all-to-all-start.1) | async-done | bytes 65568 | tf_op jit(solution)/shard_map/all_to_all | solution.py:675
  42.4 3.8 %shard_map.164 = (bf16[1024,128]{1,0:T(8,128)(2,1)}, bf16[128,512]{1,0:T(8,128)(2,1)}, bf16[128,512]{1,0:T(8,128)(2,1)}, bf16[128,512]{1,0:T(8,128)(2,1)}, f32[4,128,128]{2,1,0:T(8,128)}) custom-call(bf16[256,128]{1,0:T(8,128)(2,1)S(1)} %bitcast.7, bf16[256,256]{1,0:T(8,128)(2,1)S(1)} %get-tuple-element.74.refs_1_, ...), custom_call_target="tpu_custom_call" | custom-call | bytes 9000000 | tf_op jit(solution)/shard_map/pallas_call | solution.py:163
  46.2 4.3 %all-to-all-start.2 = ((bf16[16,64,128]{2,1,0:T(8,128)(2,1)}), bf16[16,64,128]{2,1,0:T(8,128)(2,1)S(1)}, u32[]{:S(2)}, u32[]{:S(2)}) async-start(bf16[16,64,128]{2,1,0:T(8,128)(2,1)} %bitcast.9), calls=%async_computation.2 | async-start | bytes 524288 | tf_op jit(solution)/shard_map/all_to_all | solution.py:675
  50.5 1.9 %shard_map.165 = (bf16[256,128]{1,0:T(8,128)(2,1)S(1)}, bf16[256,128]{1,0:T(8,128)(2,1)S(1)}) custom-call(bf16[128,512]{1,0:T(8,128)(2,1)} %get-tuple-element.72.refs_1_.refs_0_, bf16[128,512]{1,0:T(8,128)(2,1)} %get-tuple-element.73.refs_2_.refs_1_, bf16[128,512]{1,0:T(8,128)(2,1)} %get-tuple-element.85.refs_2_, ...), custom_call_target="tpu_custom_call" | custom-call | bytes 6000000 | tf_op jit(solution)/shard_map/pallas_call | solution.py:163
  53.7 6.4 %all-to-all-done.2 = bf16[16,64,128]{2,1,0:T(8,128)(2,1)S(1)} async-done(((bf16[16,64,128]{2,1,0:T(8,128)(2,1)}), bf16[16,64,128]{2,1,0:T(8,128)(2,1)S(1)}, u32[]{:S(2)}, u32[]{:S(2)}) %all-to-all-start.2) | async-done | bytes 262176 | tf_op jit(solution)/shard_map/all_to_all | solution.py:675
  60.0 4.1 %shard_map.167 = (bf16[16,48,128]{2,1,0:T(8,128)(2,1)}, bf16[128,2048]{1,0:T(8,128)(2,1)}, bf16[128,2048]{1,0:T(8,128)(2,1)}) custom-call(bf16[1024,128]{1,0:T(8,128)(2,1)S(1)} %bitcast.6, bf16[512,1024]{1,0:T(8,128)(2,1)S(1)} %shard_map.166.refs_1_, bf16[128,2048]{1,0:T(8,128)(2,1)} %get-tuple-element.89.refs_2_, ...), custom_call_target="tpu_custom_call" | custom-call | bytes 12000000 | tf_op jit(solution)/shard_map/pallas_call | solution.py:163
  64.2 4.0 %all-to-all-start.3 = ((bf16[16,48,128]{2,1,0:T(8,128)(2,1)}), bf16[16,48,128]{2,1,0:T(8,128)(2,1)S(1)}, u32[]{:S(2)}, u32[]{:S(2)}) async-start(bf16[16,48,128]{2,1,0:T(8,128)(2,1)} %get-tuple-element.104), calls=%async_computation.3 | async-start | bytes 393216 | tf_op jit(solution)/shard_map/all_to_all | solution.py:675
  68.2 4.6 %shard_map.168 = (bf16[256,128]{1,0:T(8,128)(2,1)}, bf16[256,128]{1,0:T(8,128)(2,1)}, f32[512,128]{1,0:T(8,128)}, bf16[2048,128]{1,0:T(8,128)(2,1)}) custom-call(s32[8,2048]{1,0:T(8,128)} %refs_0_.7, f32[8,2048]{1,0:T(8,128)} %refs_1_.5, bf16[3,4,128,128]{3,2,1,0:T(8,128)(2,1)} %refs_2_.7, bf16[128,2048]{1,0:T(8,128)(2,1)} %get-tuple-element.96.refs_3_, ...), custom_call_target="tpu_custom_call" | custom-call | bytes 15000000 | tf_op jit(solution)/shard_map/pallas_call | solution.py:163
  72.8 3.4 %all-to-all-done.3.refs_0_ = bf16[16,48,128]{2,1,0:T(8,128)(2,1)S(1)} async-done(((bf16[16,48,128]{2,1,0:T(8,128)(2,1)}), bf16[16,48,128]{2,1,0:T(8,128)(2,1)S(1)}, u32[]{:S(2)}, u32[]{:S(2)}) %all-to-all-start.3) | async-done | bytes 196640 | tf_op jit(solution)/shard_map/all_to_all | solution.py:675
  77.1 4.6 %all-to-all-start.4 = ((bf16[16,64,128]{2,1,0:T(8,128)(2,1)}), bf16[16,64,128]{2,1,0:T(8,128)(2,1)S(1)}, u32[]{:S(2)}, u32[]{:S(2)}) async-start(bf16[16,64,128]{2,1,0:T(8,128)(2,1)} %shard_map.170), calls=%async_computation.4 | async-start | bytes 524288 | tf_op jit(solution)/shard_map/all_to_all | solution.py:675
  81.7 3.5 %collective-permute-start.4 = (bf16[256,128]{1,0:T(8,128)(2,1)S(1)}, bf16[256,128]{1,0:T(8,128)(2,1)S(1)}, u32[]{:S(2)}, u32[]{:S(2)}) collective-permute-start(bf16[256,128]{1,0:T(8,128)(2,1)S(1)} %copy-done.1), channel_id=1, source_target_pairs={{1,2},{2,1},{3,4},{4,3},{5,6},{6,5},{7,8},{8,7},{9,10},{10,9},{11,... | collective-permute-start | bytes 196616 | tf_op jit(solution)/shard_map/ppermute | solution.py:887
  85.4 2.6 %collective-permute-done.4.refs_2_ = bf16[256,128]{1,0:T(8,128)(2,1)S(1)} collective-permute-done((bf16[256,128]{1,0:T(8,128)(2,1)S(1)}, bf16[256,128]{1,0:T(8,128)(2,1)S(1)}, u32[]{:S(2)}, u32[]{:S(2)}) %collective-permute-start.4) | collective-permute-done | bytes 65568 | tf_op jit(solution)/shard_map/ppermute | solution.py:887
  88.0 1.8 %shard_map.169 = (bf16[2048,128]{1,0:T(8,128)(2,1)}, f32[1536,128]{1,0:T(8,128)}) custom-call(f32[512,128]{1,0:T(8,128)} %get-tuple-element.98.refs_0_, bf16[256,128]{1,0:T(8,128)(2,1)S(1)} %collective-permute-done.3.refs_1_, bf16[256,128]{1,0:T(8,128)(2,1)S(1)} %collective-permute-done.4.refs_2_, ...), custom_call_target="tpu_custom_call", output_to_operand_aliasing={{0}: (4, {})} | custom-call | bytes 3000000 | tf_op jit(solution)/shard_map/pallas_call | solution.py:163
  89.8 1.5 %all-to-all-done.4.refs_0_ = bf16[16,64,128]{2,1,0:T(8,128)(2,1)S(1)} async-done(((bf16[16,64,128]{2,1,0:T(8,128)(2,1)}), bf16[16,64,128]{2,1,0:T(8,128)(2,1)S(1)}, u32[]{:S(2)}, u32[]{:S(2)}) %all-to-all-start.4) | async-done | bytes 262176 | tf_op jit(solution)/shard_map/all_to_all | solution.py:675
  (15 shorter events, 4.1 us)
Async XLA Ops:
  1.5 8.9 %collective-permute-start.1 = (bf16[256,128]{1,0:T(8,128)(2,1)S(1)}, bf16[256,128]{1,0:T(8,128)(2,1)S(1)}, u32[]{:S(2)}, u32[]{:S(2)}) collective-permute-start(bf16[256,128]{1,0:T(8,128)(2,1)S(1)} %get-tuple-element.106), channel_id=1, source_target_pairs={{1,2},{2,1},{3,4},{4,3},{5,6},{6,5},{7,8},{8,7},{9,10},{10,9},{11,... | collective-permute-start | bytes 196616 | tf_op jit(solution)/shard_map/ppermute | solution.py:716
  6.1 4.4 %collective-permute-start = (bf16[256,128]{1,0:T(8,128)(2,1)S(1)}, bf16[256,128]{1,0:T(8,128)(2,1)S(1)}, u32[]{:S(2)}, u32[]{:S(2)}) collective-permute-start(bf16[256,128]{1,0:T(8,128)(2,1)S(1)} %get-tuple-element.107), channel_id=1, source_target_pairs={{0,1},{1,0},{2,3},{3,2},{4,5},{5,4},{6,7},{7,6},{8,9},{9,8},{10,11... | collective-permute-start | bytes 196616 | tf_op jit(solution)/shard_map/ppermute | solution.py:715
  12.3 17.3 %all-to-all-start = ((bf16[16,96,128]{2,1,0:T(8,128)(2,1)}), bf16[16,96,128]{2,1,0:T(8,128)(2,1)S(1)}, u32[]{:S(2)}, u32[]{:S(2)}) async-start(bf16[16,96,128]{2,1,0:T(8,128)(2,1)} %get-tuple-element.63), calls=%async_computation | async-start | bytes 786432 | tf_op jit(solution)/shard_map/all_to_all | solution.py:675
  32.5 9.9 %all-to-all-start.1 = ((bf16[16,16,128]{2,1,0:T(8,128)(2,1)}), bf16[16,16,128]{2,1,0:T(8,128)(2,1)S(1)}, u32[]{:S(2)}, u32[]{:S(2)}) async-start(bf16[16,16,128]{2,1,0:T(8,128)(2,1)} %get-tuple-element.70), calls=%async_computation.1 | async-start | bytes 131072 | tf_op jit(solution)/shard_map/all_to_all | solution.py:675
  46.2 13.8 %all-to-all-start.2 = ((bf16[16,64,128]{2,1,0:T(8,128)(2,1)}), bf16[16,64,128]{2,1,0:T(8,128)(2,1)S(1)}, u32[]{:S(2)}, u32[]{:S(2)}) async-start(bf16[16,64,128]{2,1,0:T(8,128)(2,1)} %bitcast.9), calls=%async_computation.2 | async-start | bytes 524288 | tf_op jit(solution)/shard_map/all_to_all | solution.py:675
  52.4 1.3 %collective-permute-start.2 = (bf16[256,128]{1,0:T(8,128)(2,1)S(1)}, bf16[256,128]{1,0:T(8,128)(2,1)S(1)}, u32[]{:S(2)}, u32[]{:S(2)}) collective-permute-start(bf16[256,128]{1,0:T(8,128)(2,1)S(1)} %get-tuple-element.95), channel_id=1, source_target_pairs={{0,1},{1,0},{2,3},{3,2},{4,5},{5,4},{6,7},{7,6},{8,9},{9,8},{10,11... | collective-permute-start | bytes 196616 | tf_op jit(solution)/shard_map/ppermute | solution.py:834
  64.2 12.0 %all-to-all-start.3 = ((bf16[16,48,128]{2,1,0:T(8,128)(2,1)}), bf16[16,48,128]{2,1,0:T(8,128)(2,1)S(1)}, u32[]{:S(2)}, u32[]{:S(2)}) async-start(bf16[16,48,128]{2,1,0:T(8,128)(2,1)} %get-tuple-element.104), calls=%async_computation.3 | async-start | bytes 393216 | tf_op jit(solution)/shard_map/all_to_all | solution.py:675
  77.1 4.7 %copy-start.1 = (bf16[256,128]{1,0:T(8,128)(2,1)S(1)}, bf16[256,128]{1,0:T(8,128)(2,1)}, u32[]{:S(2)}) copy-start(bf16[256,128]{1,0:T(8,128)(2,1)} %get-tuple-element.100) | copy-start | bytes 196612
  77.1 8.2 %copy-start = (bf16[256,128]{1,0:T(8,128)(2,1)S(1)}, bf16[256,128]{1,0:T(8,128)(2,1)}, u32[]{:S(2)}) copy-start(bf16[256,128]{1,0:T(8,128)(2,1)} %get-tuple-element.99.refs_1_) | copy-start | bytes 196612
  77.1 14.2 %all-to-all-start.4 = ((bf16[16,64,128]{2,1,0:T(8,128)(2,1)}), bf16[16,64,128]{2,1,0:T(8,128)(2,1)S(1)}, u32[]{:S(2)}, u32[]{:S(2)}) async-start(bf16[16,64,128]{2,1,0:T(8,128)(2,1)} %shard_map.170), calls=%async_computation.4 | async-start | bytes 524288 | tf_op jit(solution)/shard_map/all_to_all | solution.py:675
  81.7 6.3 %collective-permute-start.4 = (bf16[256,128]{1,0:T(8,128)(2,1)S(1)}, bf16[256,128]{1,0:T(8,128)(2,1)S(1)}, u32[]{:S(2)}, u32[]{:S(2)}) collective-permute-start(bf16[256,128]{1,0:T(8,128)(2,1)S(1)} %copy-done.1), channel_id=1, source_target_pairs={{1,2},{2,1},{3,4},{4,3},{5,6},{6,5},{7,8},{8,7},{9,10},{10,9},{11,... | collective-permute-start | bytes 196616 | tf_op jit(solution)/shard_map/ppermute | solution.py:887
  85.3 2.7 %collective-permute-start.3 = (bf16[256,128]{1,0:T(8,128)(2,1)S(1)}, bf16[256,128]{1,0:T(8,128)(2,1)S(1)}, u32[]{:S(2)}, u32[]{:S(2)}) collective-permute-start(bf16[256,128]{1,0:T(8,128)(2,1)S(1)} %copy-done), channel_id=1, source_target_pairs={{0,1},{1,0},{2,3},{3,2},{4,5},{5,4},{6,7},{7,6},{8,9},{9,8},{10,11... | collective-permute-start | bytes 196616 | tf_op jit(solution)/shard_map/ppermute | solution.py:886
